TPU v7x, 256 devices: a whole 4x4x8 slice. The times are simulated.
256 devices in a mesh: dp: 8 (over x_lo, y), ctx: 32 (over x_hi, z, core).
Axes of the slice: x: 4 (x_hi: 2, x_lo: 2; x = x_hi * 2 + x_lo), y: 4, z: 8, core: 2. Of those that a mesh axis runs over, the one named last changes fastest.
Arguments:
- tokens: bfloat16 [8, 16384, 1024], P('dp', 'ctx'), may hold values from -6 to 6
- starts: int32 [8, 2048], P('dp', 'ctx'), may hold values from 0 to 16383, as said below
- gain: float32 [1024], replicated, may hold values from 0.1 to 1.9
- w_query: bfloat16 [1024, 1024], P('dp')
- w_key: bfloat16 [1024, 1024], P('dp')
- w_value: bfloat16 [1024, 1024], P('dp'), may hold values from -0.1875 to 0.1875
- w_out: bfloat16 [1024, 1024], P('dp'), may hold values from -0.1875 to 0.1875
- cotangent: bfloat16 [8, 16384, 1024], P('dp', 'ctx'), may hold values from -6 to 6
Outputs:
- grad_tokens: bfloat16 [8, 16384, 1024], P('dp', 'ctx')
Inputs may be any that keep to these rules, and one draw needn't show every extreme that they name: starts[b, 0] is 0 and starts[b, j] rises strictly with j; segment j lies with the device that holds starts[b, j], and every position held by one device along ctx belongs to a segment held by that device or by one of its two neighbours along ctx; in the first sequence segment 64 - 1 starts at 513 or later and the last segment starts at 16383.
All inputs are finite; a program needn't handle non-finite values.
Results may differ from a plain program's by a relative error of at most 0.013.
Values may be sent and summed in bfloat16 or wider, within the bound.
No kernel may reach another device: no remote copies, remote signals or barrier semaphores. Data moves between devices by JAX's collectives and lax.ppermute only.
A program may use at most 128 MiB of HBM per device.

v0:
```python
import math

import jax
import jax.numpy as jnp
from jax import lax
from jax.sharding import PartitionSpec as P

HEAD = 128


def padded(cells, sides, width):
    for axis, dim in sides:
        count = lax.axis_size(axis)
        ends = count - 1
        head = lax.slice_in_dim(cells, 0, width, axis=dim)
        tail = lax.slice_in_dim(cells, cells.shape[dim] - width, cells.shape[dim], axis=dim)
        cells = jnp.concatenate(
            [
                lax.ppermute(tail, axis, [(i, (i + 1) % count) for i in range(ends)]),
                cells,
                lax.ppermute(head, axis, [((i + 1) % count, i) for i in range(ends)]),
            ],
            axis=dim,
        )
    return cells


def from_behind(value, axis, steps):
    count = lax.axis_size(axis)
    leading, last = (max(0, -steps), min(count, count - steps))
    return lax.ppermute(value, axis, [(source, source + steps) for source in range(leading, last)])


def contract_last(left, right):
    return lax.dot_general(
        left, right, (((1,), (1,)), ((), ())), preferred_element_type=jnp.float32
    )


def contract_first(left, right):
    return lax.dot_general(
        left, right, (((0,), (0,)), ((), ())), preferred_element_type=jnp.float32
    )


def per_device(tokens, starts, gain, w_query, w_key, w_value, w_out, cotangent):
    inner = w_query.shape[1]
    heads = inner // HEAD
    scale = 1.0 / math.sqrt(HEAD)
    token_rows = tokens[0]
    grad_out = cotangent[0]
    own_starts = starts[0]
    rows = token_rows.shape[0]
    seg_dev = own_starts.shape[0]
    ctx_count = lax.axis_size("ctx")
    ctx_place = lax.axis_index("ctx")
    positions = ctx_place * rows + lax.iota(jnp.int32, rows)
    start_window = padded(own_starts, (("ctx", 0),), seg_dev)
    window_slot = lax.iota(jnp.int32, 3 * seg_dev)
    missing_left = (ctx_place == 0) & (window_slot < seg_dev)
    missing_right = (ctx_place == ctx_count - 1) & (window_slot >= 2 * seg_dev)
    start_window = jnp.where(missing_left, -1, start_window)
    start_window = jnp.where(missing_right, rows * ctx_count, start_window)
    local_seg = jnp.sum((start_window[None, :] <= positions[:, None]).astype(jnp.int32), axis=1) - 1
    member = local_seg[:, None] == window_slot[None, :]
    earlier_member = (local_seg - 1)[:, None] == window_slot[None, :]
    window_sum = contract_first(member.astype(jnp.bfloat16), token_rows)
    window_grad = contract_first(earlier_member.astype(jnp.bfloat16), grad_out)
    window_count = jnp.sum(member.astype(jnp.float32), axis=0)
    lower = slice(0, seg_dev)
    middle = slice(seg_dev, 2 * seg_dev)
    upper = slice(2 * seg_dev, 3 * seg_dev)
    from_after = from_behind(
        (window_sum[lower], window_grad[lower], window_count[lower]), "ctx", -1
    )
    from_before = (
        from_behind(window_sum[upper].astype(jnp.bfloat16), "ctx", 1).astype(jnp.float32),
        from_behind(window_grad[upper].astype(jnp.bfloat16), "ctx", 1).astype(jnp.float32),
        from_behind(window_count[upper].astype(jnp.bfloat16), "ctx", 1).astype(jnp.float32),
    )
    count = window_count[middle] + from_after[2] + from_before[2]
    pooled = (window_sum[middle] + from_after[0] + from_before[0]) / count[:, None]
    dout = window_grad[middle] + from_after[1] + from_before[1]
    rms = jnp.sqrt(jnp.mean(pooled * pooled, axis=-1, keepdims=True) + 1e-06)
    normed = pooled / rms
    normin = (normed * gain).astype(jnp.bfloat16)
    dout_b = dout.astype(jnp.bfloat16)
    full_q, full_k, full_v, full_o = (
        lax.all_gather(w_query, "dp", axis=0, tiled=True),
        lax.all_gather(w_key, "dp", axis=0, tiled=True),
        lax.all_gather(w_value, "dp", axis=0, tiled=True),
        lax.all_gather(w_out, "dp", axis=0, tiled=True),
    )
    query = jnp.dot(normin, full_q, preferred_element_type=jnp.float32).astype(jnp.bfloat16)
    keys = jnp.dot(normin, full_k, preferred_element_type=jnp.float32).astype(jnp.bfloat16)
    values = jnp.dot(normin, full_v, preferred_element_type=jnp.float32).astype(jnp.bfloat16)
    dattended = contract_last(dout_b, full_o).astype(jnp.bfloat16)
    key_all, value_all = (
        lax.all_gather(keys, "ctx", axis=0, tiled=True),
        lax.all_gather(values, "ctx", axis=0, tiled=True),
    )
    total = key_all.shape[0]
    seg_iota = lax.iota(jnp.int32, seg_dev)
    query3 = query.reshape(seg_dev, heads, HEAD)
    key3 = key_all.reshape(total, heads, HEAD)
    value3 = value_all.reshape(total, heads, HEAD)
    dattended3 = dattended.reshape(seg_dev, heads, HEAD)
    query_place = ctx_place * seg_dev + seg_iota
    allowed = lax.iota(jnp.int32, total)[None, :] <= query_place[:, None]
    score = jnp.einsum("qhd,khd->hqk", query3, key3, preferred_element_type=jnp.float32) * scale
    score = jnp.where(allowed[None], score, -1e30)
    peak = jnp.max(score, axis=-1, keepdims=True)
    expo = jnp.where(allowed[None], jnp.exp(score - peak), 0.0)
    expo_total = jnp.sum(expo, axis=-1, keepdims=True)
    probs = expo / expo_total
    probs_b = probs.astype(jnp.bfloat16)
    attended3 = jnp.einsum(
        "hqk,khd->qhd", probs_b, value3, preferred_element_type=jnp.float32
    ).astype(jnp.bfloat16)
    delta = jnp.einsum("qhd,qhd->hq", dattended3.astype(jnp.float32), attended3.astype(jnp.float32))
    dprobs = jnp.einsum("qhd,khd->hqk", dattended3, value3, preferred_element_type=jnp.float32)
    dscore = (probs * (dprobs - delta[:, :, None])).astype(jnp.bfloat16)
    dquery = (
        (jnp.einsum("hqk,khd->qhd", dscore, key3, preferred_element_type=jnp.float32) * scale)
        .astype(jnp.bfloat16)
        .reshape(seg_dev, inner)
    )
    dkey_part = (
        jnp.einsum("hqk,qhd->khd", dscore, query3, preferred_element_type=jnp.float32) * scale
    )
    dvalue_part = jnp.einsum(
        "hqk,qhd->khd", probs_b, dattended3, preferred_element_type=jnp.float32
    )
    key_grad = lax.psum_scatter(
        jnp.concatenate(
            [
                dkey_part.reshape(lax.axis_size("ctx") * seg_dev, inner),
                dvalue_part.reshape(lax.axis_size("ctx") * seg_dev, inner),
            ],
            axis=1,
        ).astype(jnp.bfloat16),
        "ctx",
        scatter_dimension=0,
        tiled=True,
    ).astype(jnp.float32)
    dkey = key_grad[:, :inner].astype(jnp.bfloat16)
    dvalue = key_grad[:, inner:].astype(jnp.bfloat16)
    dnormin = (
        contract_last(dquery, full_q) + contract_last(dkey, full_k) + contract_last(dvalue, full_v)
    )
    scaled = dnormin * gain
    dpooled = dout + (scaled - normed * jnp.mean(scaled * normed, axis=-1, keepdims=True)) / rms
    per_seg = dpooled / count[:, None]
    per_window = padded(per_seg.astype(jnp.bfloat16), (("ctx", 0),), seg_dev).astype(per_seg.dtype)
    spread = jnp.dot(member.astype(jnp.float32), per_window, precision=lax.Precision.HIGHEST)
    result = grad_out.astype(jnp.float32) + spread
    return result.astype(jnp.bfloat16)[None]


def solution(mesh):
    return jax.shard_map(
        per_device,
        mesh=mesh,
        in_specs=(
            P("dp", "ctx", None),
            P("dp", "ctx"),
            P(),
            P("dp", None),
            P("dp", None),
            P("dp", None),
            P("dp", None),
            P("dp", "ctx", None),
        ),
        out_specs=P("dp", "ctx", None),
        check_vma=False,
    )
```

profile of v0, /device:TPU:6, one launch (start us, length us, event | category | flops | bytes accessed | tf_op | source)
XLA Modules:
  0.0 574.4 jit_solution(9665919457641828368)
XLA Ops:
  9.4 8.0 %collective-permute-start.1 = (s32[64]{0:T(128)}, s32[64]{0:T(128)S(1)}, u32[]{:S(2)}, u32[]{:S(2)}) collective-permute-start(s32[64]{0:T(128)} %bitcast.123), channel_id=1, source_target_pairs={{1,0},{2,1},{3,2},{4,3},{5,4},{6,5},{7,6},{8,7},{9,8},{10,9},{11,1... | collective-permute-start | bytes 776 | tf_op jit(solution)/shard_map/ppermute | solution.py:21
  19.4 6.7 %collective-permute-done = s32[64]{0:T(128)S(1)} collective-permute-done((s32[64]{0:T(128)}, s32[64]{0:T(128)S(1)}, u32[]{:S(2)}, u32[]{:S(2)}) %collective-permute-start) | collective-permute-done | bytes 288 | tf_op jit(solution)/shard_map/ppermute | solution.py:19
  33.9 3.6 collective-permute-start.5
  40.0 3.9 collective-permute-done.5
  44.3 11.1 %all-gather.7.cloned.1.call-done = bf16[1024,1024]{1,0:T(8,128)(2,1)} async-done(((bf16[128,1024]{1,0:T(8,128)(2,1)}), bf16[1024,1024]{1,0:T(8,128)(2,1)}) %all-gather.7.cloned.1.call-update) | async-done | bytes 2097168 | tf_op jit(solution)/shard_map/all_gather | solution.py:90
  55.4 2.7 convolution_convert_fusion.4
  58.2 42.8 %all-gather.15.cloned.1.call-done = bf16[1024,1024]{1,0:T(8,128)(2,1)} async-done(((bf16[128,1024]{1,0:T(8,128)(2,1)}), bf16[1024,1024]{1,0:T(8,128)(2,1)}) %all-gather.15.cloned.1.call-update) | async-done | bytes 2097168 | tf_op jit(solution)/shard_map/all_gather | solution.py:91
  101.0 2.7 convolution_convert_fusion.1
  106.4 7.3 %collective-permute-start.2 = (f32[64,1024]{1,0:T(8,128)S(1)}, f32[64,1024]{1,0:T(8,128)S(1)}, u32[]{:S(2)}, u32[]{:S(2)}) collective-permute-start(f32[64,1024]{1,0:T(8,128)S(1)} %slice.50), channel_id=1, source_target_pairs={{1,0},{2,1},{3,2},{4,3},{5,4},{6,5},{7,6},{8,7},{9,8},{10,9},{11,1... | collective-permute-start | bytes 786440 | tf_op jit(solution)/shard_map/ppermute | solution.py:31
  114.4 3.2 collective-permute-done.2
  117.6 28.6 %all-gather.13.cloned.1.call-done = bf16[1024,1024]{1,0:T(8,128)(2,1)} async-done(((bf16[128,1024]{1,0:T(8,128)(2,1)}), bf16[1024,1024]{1,0:T(8,128)(2,1)}) %all-gather.13.cloned.1.call-update) | async-done | bytes 2097168 | tf_op jit(solution)/shard_map/all_gather | solution.py:92
  148.6 42.6 %all-gather.11.cloned.1.call-done = bf16[1024,1024]{1,0:T(8,128)(2,1)} async-done(((bf16[128,1024]{1,0:T(8,128)(2,1)}), bf16[1024,1024]{1,0:T(8,128)(2,1)}) %all-gather.11.cloned.1.call-update) | async-done | bytes 2097168 | tf_op jit(solution)/shard_map/all_gather | solution.py:89
  193.3 85.9 %all-gather.9.cloned.1.call-done = bf16[2048,1024]{1,0:T(8,128)(2,1)} async-done(((bf16[64,1024]{1,0:T(8,128)(2,1)}), bf16[2048,1024]{1,0:T(8,128)(2,1)}) %all-gather.9.cloned.1.call-update) | async-done | bytes 4194320 | tf_op jit(solution)/shard_map/all_gather | solution.py:99
  279.3 6.9 %fusion.82 = (f32[8,64]{1,0:T(8,128)S(1)}, f32[8,64,2048]{2,1,0:T(8,128)}) fusion(pred[64,2048]{1,0:T(8,128)(4,1)S(1)} %iota_compare_fusion, bf16[8,8,8,128]{3,2,1,0:T(8,128)(2,1)S(1)} %fusion.34, bf16[2048,1024]{1,0:T(8,128)(2,1)} %all-gather.9.cloned.1.call-done), kind=kOutput, calls=%fused_computation.99 | convolution fusion | flops 273680384 | bytes 8652800 | tf_op jit(solution)/shard_map/sub | solution.py:113
  286.2 5.5 convolution_convert_fusion
  291.7 73.7 %all-gather.17.cloned.1.call-done = bf16[2048,1024]{1,0:T(8,128)(2,1)} async-done(((bf16[64,1024]{1,0:T(8,128)(2,1)}), bf16[2048,1024]{1,0:T(8,128)(2,1)}) %all-gather.17.cloned.1.call-update) | async-done | bytes 4194320 | tf_op jit(solution)/shard_map/all_gather | solution.py:100
  365.5 5.4 fusion.44
  371.4 2.6 multiply_convert_fusion.1
  374.0 3.2 multiply_convert_fusion
  377.2 8.3 %pad_maximum_fusion = bf16[2048,2048]{0,1:T(8,128)(2,1)} fusion(bf16[2048,1024]{0,1:T(8,128)(2,1)} %bitcast.121, bf16[2048,1024]{0,1:T(8,128)(2,1)} %bitcast.120), kind=kLoop, calls=%fused_computation.1 | loop fusion | flops 16777216 | bytes 16777216 | tf_op jit(solution)/shard_map/concatenate | solution.py:135
  385.6 12.3 %copy.48 = bf16[2048,2048]{1,0:T(8,128)(2,1)} copy(bf16[2048,2048]{0,1:T(8,128)(2,1)} %pad_maximum_fusion) | data formatting | bytes 16777216
  398.0 3.6 fusion.31
  403.2 145.7 %reduce-scatter.4.cloned.1.call-done = bf16[64,2048]{1,0:T(8,128)(2,1)} async-done(((bf16[2048,2048]{1,0:T(8,128)(2,1)}), bf16[64,2048]{1,0:T(8,128)(2,1)}) %reduce-scatter.4.cloned.1.call-update) | async-done | bytes 262160
  558.7 7.4 %collective-permute-done.8 = bf16[64,1024]{1,0:T(8,128)(2,1)S(1)} collective-permute-done((bf16[64,1024]{1,0:T(8,128)(2,1)S(1)}, bf16[64,1024]{1,0:T(8,128)(2,1)S(1)}, u32[]{:S(2)}, u32[]{:S(2)}) %collective-permute-start.8) | collective-permute-done | bytes 131104 | tf_op jit(solution)/shard_map/ppermute | solution.py:19
  (89 shorter events, 36.5 us)
Async XLA Ops:
  6.5 48.8 %all-gather.7.cloned.1.call-start = ((), (), s32[]{:S(2)}) async-start(), calls=%async_computation.1 | async-start | bytes 2359296 | tf_op jit(solution)/shard_map/all_gather | solution.py:90
  7.3 93.8 %all-gather.15.cloned.1.call-start = ((), (), s32[]{:S(2)}) async-start(), calls=%async_computation.5 | async-start | bytes 2359296 | tf_op jit(solution)/shard_map/all_gather | solution.py:91
  8.0 138.2 %all-gather.13.cloned.1.call-start = ((), (), s32[]{:S(2)}) async-start(), calls=%async_computation.4 | async-start | bytes 2359296 | tf_op jit(solution)/shard_map/all_gather | solution.py:92
  8.7 182.5 %all-gather.11.cloned.1.call-start = ((), (), s32[]{:S(2)}) async-start(), calls=%async_computation.3 | async-start | bytes 2359296 | tf_op jit(solution)/shard_map/all_gather | solution.py:89
  9.3 270.0 %all-gather.9.cloned.1.call-start = ((), (), s32[]{:S(2)}) async-start(), calls=%async_computation.2 | async-start | bytes 4325376 | tf_op jit(solution)/shard_map/all_gather | solution.py:99
  9.4 10.0 %collective-permute-start.1 = (s32[64]{0:T(128)}, s32[64]{0:T(128)S(1)}, u32[]{:S(2)}, u32[]{:S(2)}) collective-permute-start(s32[64]{0:T(128)} %bitcast.123), channel_id=1, source_target_pairs={{1,0},{2,1},{3,2},{4,3},{5,4},{6,5},{7,6},{8,7},{9,8},{10,9},{11,1... | collective-permute-start | bytes 776 | tf_op jit(solution)/shard_map/ppermute | solution.py:21
  17.4 8.6 %collective-permute-start = (s32[64]{0:T(128)}, s32[64]{0:T(128)S(1)}, u32[]{:S(2)}, u32[]{:S(2)}) collective-permute-start(s32[64]{0:T(128)} %bitcast.124), channel_id=1, source_target_pairs={{0,1},{1,2},{2,3},{3,4},{4,5},{5,6},{6,7},{7,8},{8,9},{9,10},{10,1... | collective-permute-start | bytes 776 | tf_op jit(solution)/shard_map/ppermute | solution.py:19
  27.3 76.5 %copy-start.4 = (bf16[1,512,1024]{2,1,0:T(8,128)(2,1)S(1)}, bf16[1,512,1024]{2,1,0:T(8,128)(2,1)}, u32[]{:S(2)}) copy-start(bf16[1,512,1024]{2,1,0:T(8,128)(2,1)} %param.15) | copy-start | bytes 3145732
  27.3 16.6 %collective-permute-start.4 = (f32[64,1024]{1,0:T(8,128)S(1)}, f32[64,1024]{1,0:T(8,128)S(1)}, u32[]{:S(2)}, u32[]{:S(2)}) collective-permute-start(f32[64,1024]{1,0:T(8,128)S(1)} %slice.53), channel_id=1, source_target_pairs={{1,0},{2,1},{3,2},{4,3},{5,4},{6,5},{7,6},{8,7},{9,8},{10,9},{11,1... | collective-permute-start | bytes 786440 | tf_op jit(solution)/shard_map/ppermute | solution.py:31
  29.5 10.4 %collective-permute-start.6 = (f32[64]{0:T(128)S(1)}, f32[64]{0:T(128)S(1)}, u32[]{:S(2)}, u32[]{:S(2)}) collective-permute-start(f32[64]{0:T(128)S(1)} %slice.45), channel_id=1, source_target_pairs={{1,0},{2,1},{3,2},{4,3},{5,4},{6,5},{7,6},{8,7},{9,8},{10,9},{11,1... | collective-permute-start | bytes 776 | tf_op jit(solution)/shard_map/ppermute | solution.py:31
  31.5 8.5 %collective-permute-start.7 = (bf16[64]{0:T(256)(128)(2,1)S(1)}, bf16[64]{0:T(256)(128)(2,1)S(1)}, u32[]{:S(2)}, u32[]{:S(2)}) collective-permute-start(bf16[64]{0:T(256)(128)(2,1)S(1)} %slice.46), channel_id=1, source_target_pairs={{0,1},{1,2},{2,3},{3,4},{4,5},{5,6},{6,7},{7,8},{8,9},{9,10},{10,1... | collective-permute-start | bytes 392 | tf_op jit(solution)/shard_map/ppermute | solution.py:31
  33.9 10.0 %collective-permute-start.5 = (bf16[64,1024]{1,0:T(8,128)(2,1)S(1)}, bf16[64,1024]{1,0:T(8,128)(2,1)S(1)}, u32[]{:S(2)}, u32[]{:S(2)}) collective-permute-start(bf16[64,1024]{1,0:T(8,128)(2,1)S(1)} %slice.79), channel_id=1, source_target_pairs={{0,1},{1,2},{2,3},{3,4},{4,5},{5,6},{6,7},{7,8},{8,9},{9,10},{10,1... | collective-permute-start | bytes 393224 | tf_op jit(solution)/shard_map/ppermute | solution.py:31
  58.1 307.3 %all-gather.17.cloned.1.call-start = ((), (), s32[]{:S(2)}) async-start(), calls=%async_computation.6 | async-start | bytes 4325376 | tf_op jit(solution)/shard_map/all_gather | solution.py:100
  103.8 445.1 %reduce-scatter.4.cloned.1.call-start = ((), (), s32[]{:S(2)}) async-start(), calls=%async_computation.7 | async-start | bytes 8650752
  104.4 181.8 %copy-start.3 = (f32[192,1024]{1,0:T(8,128)}, f32[192,1024]{1,0:T(8,128)S(1)}, u32[]{:S(2)}) copy-start(f32[192,1024]{1,0:T(8,128)S(1)} %fusion.49) | copy-start | bytes 2359300
  104.5 9.9 %collective-permute-start.3 = (bf16[64,1024]{1,0:T(8,128)(2,1)S(1)}, bf16[64,1024]{1,0:T(8,128)(2,1)S(1)}, u32[]{:S(2)}, u32[]{:S(2)}) collective-permute-start(bf16[64,1024]{1,0:T(8,128)(2,1)S(1)} %slice.80), channel_id=1, source_target_pairs={{0,1},{1,2},{2,3},{3,4},{4,5},{5,6},{6,7},{7,8},{8,9},{9,10},{10,1... | collective-permute-start | bytes 393224 | tf_op jit(solution)/shard_map/ppermute | solution.py:31
  106.4 11.2 %collective-permute-start.2 = (f32[64,1024]{1,0:T(8,128)S(1)}, f32[64,1024]{1,0:T(8,128)S(1)}, u32[]{:S(2)}, u32[]{:S(2)}) collective-permute-start(f32[64,1024]{1,0:T(8,128)S(1)} %slice.50), channel_id=1, source_target_pairs={{1,0},{2,1},{3,2},{4,3},{5,4},{6,5},{7,6},{8,7},{9,8},{10,9},{11,1... | collective-permute-start | bytes 786440 | tf_op jit(solution)/shard_map/ppermute | solution.py:31
  117.6 168.6 %copy-start.6 = (f32[64,1024]{1,0:T(8,128)}, f32[64,1024]{1,0:T(8,128)S(1)}, u32[]{:S(2)}) copy-start(f32[64,1024]{1,0:T(8,128)S(1)} %collective-permute-done.2) | copy-start | bytes 786436
  148.6 137.6 %copy-start.8 = (bf16[64,1024]{1,0:T(8,128)(2,1)}, bf16[64,1024]{1,0:T(8,128)(2,1)S(1)}, u32[]{:S(2)}) copy-start(bf16[64,1024]{1,0:T(8,128)(2,1)S(1)} %convolution_convert_fusion.2) | copy-start | bytes 393220
  286.2 79.3 %copy-start.15 = (f32[8,64]{1,0:T(8,128)}, f32[8,64]{1,0:T(8,128)S(1)}, u32[]{:S(2)}) copy-start(f32[8,64]{1,0:T(8,128)S(1)} %get-tuple-element.11) | copy-start | bytes 6148
  401.6 149.7 %copy-start.1 = (bf16[1024,1024]{1,0:T(8,128)(2,1)S(1)}, bf16[1024,1024]{1,0:T(8,128)(2,1)}, u32[]{:S(2)}) copy-start(bf16[1024,1024]{1,0:T(8,128)(2,1)} %all-gather.15.cloned.1.call-done) | copy-start | bytes 6291460
  401.6 151.5 %copy-start.11 = (bf16[64,1024]{1,0:T(8,128)(2,1)S(1)}, bf16[64,1024]{1,0:T(8,128)(2,1)}, u32[]{:S(2)}) copy-start(bf16[64,1024]{1,0:T(8,128)(2,1)} %copy-done.10) | copy-start | bytes 393220
  554.3 4.4 collective-permute-start.9
  556.2 9.9 %collective-permute-start.8 = (bf16[64,1024]{1,0:T(8,128)(2,1)S(1)}, bf16[64,1024]{1,0:T(8,128)(2,1)S(1)}, u32[]{:S(2)}, u32[]{:S(2)}) collective-permute-start(bf16[64,1024]{1,0:T(8,128)(2,1)S(1)} %divide_convert_fusion), channel_id=1, source_target_pairs={{0,1},{1,2},{2,3},{3,4},{4,5},{5,6},{6,7},{7,8},{8,9},{9,10},{10,1... | collective-permute-start | bytes 393224 | tf_op jit(solution)/shard_map/ppermute | solution.py:19
  (9 other events, 134.1 us)
Sparse Core Ops, SparseCore 0:
  9.1 46.1 all-gather.6
  57.2 43.8 all-gather.14
  102.8 43.3 all-gather.12
  147.8 43.3 all-gather.10
  193.9 85.3 all-gather.8
  281.9 83.4 all-gather.16
  398.1 150.7 reduce-scatter.3
where the time goes:
time: 575 us; the launch traced here: 574 us
  waiting for transfers between devices  457 us (79%)
  matrix products  45.3 us (8%)
  starting transfers between devices  33.7 us (6%)
  between operations  13.9 us (2%)
  local copies, waits for them, and re-layouts  13.1 us (2%)
  other arithmetic  11 us (2%)
    unnamed x8, waiting for transfers between devices  148 us
    all_gather x1, waiting for transfers between devices, per_device(): lax.all_gather(keys, 'ctx', axis=0, tiled=True)  85.9 us
    all_gather x1, waiting for transfers between devices, per_device(): lax.all_gather(values, 'ctx', axis=0, tiled=True)  73.7 us
    all_gather x1, waiting for transfers between devices, per_device(): lax.all_gather(w_value, 'dp', axis=0, tiled=True)  42.8 us
    all_gather x1, waiting for transfers between devices, per_device(): lax.all_gather(w_query, 'dp', axis=0, tiled=True)  42.6 us
    all_gather x1, waiting for transfers between devices, per_device(): lax.all_gather(w_out, 'dp', axis=0, tiled=True)  28.6 us
    ppermute x6, starting transfers between devices, from_behind(): lax.ppermute(value, axis, [(source, source + steps) for source in range(l...  19.2 us
    ppermute x2, waiting for transfers between devices, padded(): lax.ppermute(tail, axis, [(i, (i + 1) % count) for i in range(ends)])  14.1 us
  transfers between devices with their start and end apart: 17, of which 14 were waited for; matrix products, arithmetic and copies ran while one was open for 5% of the time, Pallas kernels for 0%

commit v1 on v0

v1 whole, which is shorter than its diff:
```python
import functools
import math

import jax
import jax.numpy as jnp
from jax import lax
from jax.experimental import pallas as pl
from jax.experimental.pallas import tpu as pltpu
from jax.sharding import PartitionSpec as P

HEAD = 128
CORES = 2
RING = 8
HALVES = 2
CTX = HALVES * RING * CORES
NEG = -1e30


def place(half, ring, core):
    return (half * RING + ring) * CORES + core


def devices():
    return [(h, r, k) for h in range(HALVES) for r in range(RING) for k in range(CORES)]


def along(value, steps):
    pairs = [(i, i + steps) for i in range(CTX) if 0 <= i + steps < CTX]
    return lax.ppermute(value, "ctx", pairs)


def around(value, steps):
    pairs = [(place(h, r, k), place(h, (r + steps) % RING, k)) for h, r, k in devices()]
    return lax.ppermute(value, "ctx", pairs)


def other_core(value):
    pairs = [(place(h, r, k), place(h, r, 1 - k)) for h, r, k in devices()]
    return lax.ppermute(value, "ctx", pairs)


def across(value, source):
    pairs = [
        (place(h, r, k), place(1 - h, r, k)) for h, r, k in devices() if h == source
    ]
    return lax.ppermute(value, "ctx", pairs)


def contract_last(left, right):
    return lax.dot_general(
        left, right, (((1,), (1,)), ((), ())), preferred_element_type=jnp.float32
    )


def contract_first(left, right):
    return lax.dot_general(
        left, right, (((0,), (0,)), ((), ())), preferred_element_type=jnp.float32
    )


def head_weights(w_query, w_key, w_value, w_out, ring, core):
    rows, width = w_query.shape
    half = rows // CORES
    at = core * half
    cut = [
        lax.dynamic_slice(w, (at, ring * HEAD), (half, HEAD)) for w in (w_query, w_key, w_value)
    ]
    cut.append(lax.dynamic_slice(w_out, (at, 0), (half, width)))
    gathered = lax.all_gather(jnp.concatenate(cut, axis=1), "dp", axis=0, tiled=False)
    mine_in = gathered[:, :, : 3 * HEAD]
    mine_out = lax.dynamic_index_in_dim(gathered[:, :, 3 * HEAD :], ring, 0, keepdims=False)
    theirs_in = other_core(mine_in)
    theirs_out = other_core(mine_out)
    first = core == 0
    w_in = jnp.stack(
        [jnp.where(first, mine_in, theirs_in), jnp.where(first, theirs_in, mine_in)], axis=1
    ).reshape(-1, 3 * HEAD)
    w_back = jnp.concatenate(
        [jnp.where(first, mine_out, theirs_out), jnp.where(first, theirs_out, mine_out)], axis=0
    )
    return w_in, w_back


def attention_kernel(tile, seg, q_ref, kv_ref, da_ref, place_ref, dq_ref, dkv_ref, dkt, dvt):
    half, ring, core = place_ref[0], place_ref[1], place_ref[2]
    queries, keys = q_ref.shape[0], kv_ref.shape[0]
    group = keys // 4
    spot = lax.broadcasted_iota(jnp.int32, (1, keys), 1)
    block = spot // group
    slot = (spot % group) // seg
    key_half = jnp.where(block < 2, half, 1 - half)
    key_core = jnp.where(block % 2 == 0, core, 1 - core)
    key_ring = (ring - slot + RING) % RING
    key_at = ((key_half * RING + key_ring) * CORES + key_core) * seg + spot % seg
    turn = math.log2(math.e) / math.sqrt(HEAD)
    scale = 1.0 / math.sqrt(HEAD)
    k = kv_ref[:, :HEAD]
    v = kv_ref[:, HEAD:]
    for step in range(queries // tile):
        rows = slice(step * tile, (step + 1) * tile)
        place_row = lax.broadcasted_iota(jnp.int32, (tile, 1), 0) + step * tile
        query_ring = (ring - place_row // seg + RING) % RING
        query_at = ((half * RING + query_ring) * CORES + core) * seg + place_row % seg
        q = q_ref[rows, :]
        da = da_ref[rows, :]
        score = jnp.where(key_at <= query_at, contract_last(q, k), NEG)
        peak = jnp.max(score, axis=1, keepdims=True)
        expo = jnp.exp2((score - peak) * turn)
        probs = expo * (1.0 / jnp.sum(expo, axis=1, keepdims=True))
        probs_b = probs.astype(jnp.bfloat16)
        attended = jnp.dot(probs_b, v, preferred_element_type=jnp.float32).astype(jnp.bfloat16)
        delta = jnp.sum(
            da.astype(jnp.float32) * attended.astype(jnp.float32), axis=1, keepdims=True
        )
        dscore = (probs * (contract_last(da, v) - delta)).astype(jnp.bfloat16)
        dq = jnp.dot(dscore, k, preferred_element_type=jnp.float32) * scale
        dq_ref[rows, :] = dq.astype(jnp.bfloat16)
        dk_part = contract_first(q, dscore)
        dv_part = contract_first(da, probs_b)
        if step == 0:
            dkt[...] = dk_part
            dvt[...] = dv_part
        else:
            dkt[...] += dk_part
            dvt[...] += dv_part
    dkv_ref[:, :HEAD] = (dkt[...] * scale).T.astype(jnp.bfloat16)
    dkv_ref[:, HEAD:] = dvt[...].T.astype(jnp.bfloat16)


def attention(q, kv, da, where, seg):
    queries, keys = q.shape[0], kv.shape[0]
    return pl.pallas_call(
        functools.partial(attention_kernel, 128, seg),
        out_shape=(
            jax.ShapeDtypeStruct((queries, HEAD), jnp.bfloat16),
            jax.ShapeDtypeStruct((keys, 2 * HEAD), jnp.bfloat16),
        ),
        in_specs=[
            pl.BlockSpec(memory_space=pltpu.VMEM),
            pl.BlockSpec(memory_space=pltpu.VMEM),
            pl.BlockSpec(memory_space=pltpu.VMEM),
            pl.BlockSpec(memory_space=pltpu.SMEM),
        ],
        out_specs=(
            pl.BlockSpec(memory_space=pltpu.VMEM),
            pl.BlockSpec(memory_space=pltpu.VMEM),
        ),
        scratch_shapes=[
            pltpu.VMEM((HEAD, keys), jnp.float32),
            pltpu.VMEM((HEAD, keys), jnp.float32),
        ],
        compiler_params=pltpu.CompilerParams(vmem_limit_bytes=48 * 1024 * 1024),
        cost_estimate=pl.CostEstimate(
            flops=12 * queries * keys * HEAD,
            bytes_accessed=2 * HEAD * (3 * queries + 4 * keys),
            transcendentals=queries * keys,
        ),
    )(q, kv, da, where)


def gather_ring(shard):
    rows = shard.shape[0]
    right, left = [shard], [shard]
    for _ in range(RING // 2 - 1):
        right.append(around(right[-1], 1))
        left.append(around(left[-1], -1))
    far = jnp.concatenate(
        [around(right[-1][: rows // 2], 1), around(left[-1][rows // 2 :], -1)], axis=0
    )
    return right + [far] + left[:0:-1]


def scatter_ring(parts):
    wire = jnp.bfloat16
    middle = RING // 2
    cut = parts[0].shape[0] // 2
    right = around(parts[middle][:cut].astype(wire), 1)
    left = around(parts[middle][cut:].astype(wire), -1)
    right = jnp.concatenate(
        [parts[middle + 1][:cut] + right.astype(jnp.float32), parts[middle + 1][cut:]], axis=0
    )
    left = jnp.concatenate(
        [parts[middle - 1][:cut], parts[middle - 1][cut:] + left.astype(jnp.float32)], axis=0
    )
    for step in range(1, middle):
        right = around(right.astype(wire), 1).astype(jnp.float32)
        left = around(left.astype(wire), -1).astype(jnp.float32)
        if step < middle - 1:
            right = parts[middle + 1 + step] + right
            left = parts[middle - 1 - step] + left
    return parts[0] + right + left


def per_device(tokens, starts, gain, w_query, w_key, w_value, w_out, cotangent):
    token_rows = tokens[0]
    grad_out = cotangent[0]
    own_starts = starts[0]
    rows, width = token_rows.shape
    seg = own_starts.shape[0]
    length = rows * CTX
    ctx = lax.axis_index("ctx")
    half, ring, core = ctx // (RING * CORES), (ctx // CORES) % RING, ctx % CORES
    w_in, w_back = head_weights(w_query, w_key, w_value, w_out, ring, core)

    before = jnp.where(ctx == 0, -1, along(own_starts, 1))
    after = jnp.where(ctx == CTX - 1, length, along(own_starts, -1))
    window = jnp.concatenate([before, own_starts, after])
    positions = ctx * rows + lax.iota(jnp.int32, rows)
    ends = jnp.concatenate([window[1:], jnp.full((1,), length, jnp.int32)])
    member = (
        (window[None, :] <= positions[:, None]) & (positions[:, None] < ends[None, :])
    ).astype(jnp.bfloat16)
    token_sum = contract_first(member, token_rows)
    grad_sum = contract_first(member, grad_out)
    wire = jnp.bfloat16
    lower = jnp.concatenate([token_sum[:seg], grad_sum[1 : seg + 1]], axis=1).astype(wire)
    tail = jnp.concatenate([grad_sum[2 * seg + 1 :], jnp.zeros((1, width), jnp.float32)], axis=0)
    upper = jnp.concatenate([token_sum[2 * seg :], tail], axis=1).astype(wire)
    from_after = along(lower, -1).astype(jnp.float32)
    from_before = along(upper, 1).astype(jnp.float32)
    from_second = along(grad_sum[:1].astype(wire), -2).astype(jnp.float32)
    count = (ends - window)[seg : 2 * seg].astype(jnp.float32)
    pooled = token_sum[seg : 2 * seg] + from_after[:, :width] + from_before[:, :width]
    pooled = pooled / count[:, None]
    last = lax.broadcasted_iota(jnp.int32, (seg, 1), 0) == seg - 1
    dout = grad_sum[seg + 1 : 2 * seg + 1] + from_after[:, width:] + from_before[:, width:]
    dout = dout + jnp.where(last, from_second, 0.0)
    rms = jnp.sqrt(jnp.mean(pooled * pooled, axis=-1, keepdims=True) + 1e-06)
    normed = pooled / rms
    normin = (normed * gain).astype(jnp.bfloat16)

    both = jnp.concatenate(
        gather_ring(jnp.concatenate([normin, dout.astype(jnp.bfloat16)], axis=1)), axis=0
    )
    qkv = jnp.dot(both[:, :width], w_in, preferred_element_type=jnp.float32).astype(jnp.bfloat16)
    kv_own = qkv[:, HEAD:]
    kv_far = across(kv_own, 0)
    da = contract_last(both[:, width:], w_back).astype(jnp.bfloat16)
    kv = jnp.concatenate([kv_own, other_core(kv_own), kv_far, other_core(kv_far)], axis=0)
    dq, dkv = attention(qkv[:, :HEAD], kv, da, jnp.stack([half, ring, core]), seg)
    group = qkv.shape[0]
    parts = [dkv[i * group : (i + 1) * group] for i in range(4)]
    far = parts[2].astype(jnp.float32) + other_core(parts[3]).astype(jnp.float32)
    far = across(far.astype(wire), 1).astype(jnp.float32)
    near = parts[0].astype(jnp.float32) + other_core(parts[1]).astype(jnp.float32)
    dkv_own = (near + far).astype(jnp.bfloat16)
    partial = contract_last(jnp.concatenate([dq, dkv_own], axis=1), w_in)
    dnormin = scatter_ring([partial[i * seg : (i + 1) * seg] for i in range(RING)])

    scaled = dnormin * gain
    dpooled = dout + (scaled - normed * jnp.mean(scaled * normed, axis=-1, keepdims=True)) / rms
    per_seg = (dpooled / count[:, None]).astype(wire)
    per_window = jnp.concatenate([along(per_seg, 1), per_seg, along(per_seg, -1)], axis=0)
    spread = jnp.dot(member, per_window, preferred_element_type=jnp.float32)
    return (grad_out.astype(jnp.float32) + spread).astype(jnp.bfloat16)[None]


def solution(mesh):
    return jax.shard_map(
        per_device,
        mesh=mesh,
        in_specs=(
            P("dp", "ctx", None),
            P("dp", "ctx"),
            P(),
            P("dp", None),
            P("dp", None),
            P("dp", None),
            P("dp", None),
            P("dp", "ctx", None),
        ),
        out_specs=P("dp", "ctx", None),
        check_vma=False,
    )
```

time: 575 us -> 168 us (0.29)
  waiting for transfers between devices: 457 us -> 60.8 us
  matrix products: 45.3 us -> 6.91 us
  starting transfers between devices: 33.7 us -> 57.6 us
  Pallas kernels: 0 us -> 6.32 us
    all_gather x6 -> x1, waiting for transfers between devices: 285 us -> 0.01 us  [head_weights(): lax.all_gather(jnp.concatenate(cut, axis=1), 'dp', axis=0, tiled=False)]
    unnamed x8 -> x1, waiting for transfers between devices: 148 us -> 0.02 us
    ppermute x10 -> x31, waiting for transfers between devices: 24.2 us -> 60.8 us  [the longest x16 31.7 us: around(): return lax.ppermute(value, 'ctx', pairs)]
    dot_general x9 -> x2, matrix products: 29.3 us -> 2.16 us  [the longest x1 1.45 us: per_device(): spread = jnp.dot(member, per_window, preferred_element_type=jnp.float32)]
    ppermute x10 -> x31, starting transfers between devices: 33.5 us -> 57.6 us  [the longest x7 28 us: along(): return lax.ppermute(value, 'ctx', pairs)]
    sub x1 -> x0, matrix products: 6.91 us -> none  [per_device(): expo = jnp.where(allowed[None], jnp.exp(score - peak), 0.0)]
    pallas_call x0 -> x1, Pallas kernels: none -> 6.32 us  [attention(): pl.pallas_call(functools.partial(attention_kernel, 128, seg), out_shape=(...]
    unnamed x34 -> x29, local copies, waits for them, and re-layouts: 13 us -> 7.86 us
  transfers between devices with their start and end apart: 17 -> 32, of which waited for: 14 -> 18; matrix products, arithmetic and copies ran while one was open for 5% -> 11% of each run, Pallas kernels for 0% -> 0%
where the time goes in v1:
time: 168 us; the launch traced here: 167 us
  waiting for transfers between devices  60.8 us (36%)
  starting transfers between devices  57.6 us (34%)
  local copies, waits for them, and re-layouts  14.8 us (9%)
  between operations  14 us (8%)
  other arithmetic  6.96 us (4%)
  matrix products  6.91 us (4%)
  Pallas kernels  6.32 us (4%)
    ppermute x16, waiting for transfers between devices, around(): return lax.ppermute(value, 'ctx', pairs)  31.7 us
    ppermute x7, starting transfers between devices, along(): return lax.ppermute(value, 'ctx', pairs)  28 us
    ppermute x16, starting transfers between devices, around(): return lax.ppermute(value, 'ctx', pairs)  25.4 us
    ppermute x2, waiting for transfers between devices, across(): return lax.ppermute(value, 'ctx', pairs)  15.4 us
    ppermute x7, waiting for transfers between devices, along(): return lax.ppermute(value, 'ctx', pairs)  12.3 us
    unnamed x29, local copies, waits for them, and re-layouts  7.86 us
    pallas_call x1, Pallas kernels, attention(): pl.pallas_call(functools.partial(attention_kernel, 128, seg), out_shape=(...  6.32 us
  transfers between devices with their start and end apart: 32, of which 18 were waited for; matrix products, arithmetic and copies ran while one was open for 11% of the time, Pallas kernels for 0%

profile of v1, /device:TPU:6, one launch (start us, length us, event | category | flops | bytes accessed | tf_op | source)
XLA Modules:
  0.0 167.3 jit_solution(16951008171391393233)
XLA Ops:
  6.5 8.2 %collective-permute-start.1 = (s32[64]{0:T(128)}, s32[64]{0:T(128)S(1)}, u32[]{:S(2)}, u32[]{:S(2)}) collective-permute-start(s32[64]{0:T(128)} %bitcast.38), channel_id=1, source_target_pairs={{1,0},{2,1},{3,2},{4,3},{5,4},{6,5},{7,6},{8,7},{9,8},{10,9},{11,1... | collective-permute-start | bytes 776 | tf_op jit(solution)/shard_map/ppermute | solution.py:29
  20.5 2.8 %collective-permute-done = s32[64]{0:T(128)S(1)} collective-permute-done((s32[64]{0:T(128)}, s32[64]{0:T(128)S(1)}, u32[]{:S(2)}, u32[]{:S(2)}) %collective-permute-start) | collective-permute-done | bytes 288 | tf_op jit(solution)/shard_map/ppermute | solution.py:29
  26.7 4.5 %collective-permute-start.2 = (bf16[64,2048]{1,0:T(8,128)(2,1)S(1)}, bf16[64,2048]{1,0:T(8,128)(2,1)S(1)}, u32[]{:S(2)}, u32[]{:S(2)}) collective-permute-start(bf16[64,2048]{1,0:T(8,128)(2,1)S(1)} %pad_maximum_fusion.2), channel_id=1, source_target_pairs={{1,0},{2,1},{3,2},{4,3},{5,4},{6,5},{7,6},{8,7},{9,8},{10,9},{11,1... | collective-permute-start | bytes 786440 | tf_op jit(solution)/shard_map/ppermute | solution.py:29
  33.2 2.3 %collective-permute-start.4 = (bf16[1,1024]{1,0:T(2,128)(2,1)S(1)}, bf16[1,1024]{1,0:T(2,128)(2,1)S(1)}, u32[]{:S(2)}, u32[]{:S(2)}) collective-permute-start(bf16[1,1024]{1,0:T(2,128)(2,1)S(1)} %slice.169), channel_id=1, source_target_pairs={{2,0},{3,1},{4,2},{5,3},{6,4},{7,5},{8,6},{9,7},{10,8},{11,9},{12,... | collective-permute-start | bytes 6152 | tf_op jit(solution)/shard_map/ppermute | solution.py:29
  35.6 3.1 %collective-permute-done.4 = bf16[1,1024]{1,0:T(2,128)(2,1)S(1)} collective-permute-done((bf16[1,1024]{1,0:T(2,128)(2,1)S(1)}, bf16[1,1024]{1,0:T(2,128)(2,1)S(1)}, u32[]{:S(2)}, u32[]{:S(2)}) %collective-permute-start.4) | collective-permute-done | bytes 2080 | tf_op jit(solution)/shard_map/ppermute | solution.py:29
  38.8 3.9 %collective-permute-done.3 = bf16[64,2048]{1,0:T(8,128)(2,1)S(1)} collective-permute-done((bf16[64,2048]{1,0:T(8,128)(2,1)S(1)}, bf16[64,2048]{1,0:T(8,128)(2,1)S(1)}, u32[]{:S(2)}, u32[]{:S(2)}) %collective-permute-start.3) | collective-permute-done | bytes 262176 | tf_op jit(solution)/shard_map/ppermute | solution.py:29
  45.0 3.2 %collective-permute-start.9 = (bf16[64,2048]{1,0:T(8,128)(2,1)S(1)}, bf16[64,2048]{1,0:T(8,128)(2,1)S(1)}, u32[]{:S(2)}, u32[]{:S(2)}) collective-permute-start(bf16[64,2048]{1,0:T(8,128)(2,1)S(1)} %get-tuple-element.31), channel_id=1, source_target_pairs={{0,14},{1,15},{2,0},{3,1},{4,2},{5,3},{6,4},{7,5},{8,6},{9,7},{10,... | collective-permute-start | bytes 786440 | tf_op jit(solution)/shard_map/ppermute | solution.py:34
  48.3 4.9 %collective-permute-done.5 = bf16[64,2048]{1,0:T(8,128)(2,1)S(1)} collective-permute-done((bf16[64,2048]{1,0:T(8,128)(2,1)S(1)}, bf16[64,2048]{1,0:T(8,128)(2,1)S(1)}, u32[]{:S(2)}, u32[]{:S(2)}) %collective-permute-start.5) | collective-permute-done | bytes 262176 | tf_op jit(solution)/shard_map/ppermute | solution.py:34
  53.2 3.2 %collective-permute-start.10 = (bf16[64,2048]{1,0:T(8,128)(2,1)S(1)}, bf16[64,2048]{1,0:T(8,128)(2,1)S(1)}, u32[]{:S(2)}, u32[]{:S(2)}) collective-permute-start(bf16[64,2048]{1,0:T(8,128)(2,1)S(1)} %collective-permute-done.9), channel_id=1, source_target_pairs={{0,14},{1,15},{2,0},{3,1},{4,2},{5,3},{6,4},{7,5},{8,6},{9,7},{10,... | collective-permute-start | bytes 786440 | tf_op jit(solution)/shard_map/ppermute | solution.py:34
  56.4 4.3 %collective-permute-done.6 = bf16[64,2048]{1,0:T(8,128)(2,1)S(1)} collective-permute-done((bf16[64,2048]{1,0:T(8,128)(2,1)S(1)}, bf16[64,2048]{1,0:T(8,128)(2,1)S(1)}, u32[]{:S(2)}, u32[]{:S(2)}) %collective-permute-start.6) | collective-permute-done | bytes 262176 | tf_op jit(solution)/shard_map/ppermute | solution.py:34
  60.8 3.2 %collective-permute-start.11 = (bf16[64,2048]{1,0:T(8,128)(2,1)S(1)}, bf16[64,2048]{1,0:T(8,128)(2,1)S(1)}, u32[]{:S(2)}, u32[]{:S(2)}) collective-permute-start(bf16[64,2048]{1,0:T(8,128)(2,1)S(1)} %collective-permute-done.10), channel_id=1, source_target_pairs={{0,14},{1,15},{2,0},{3,1},{4,2},{5,3},{6,4},{7,5},{8,6},{9,7},{10,... | collective-permute-start | bytes 786440 | tf_op jit(solution)/shard_map/ppermute | solution.py:34
  65.4 3.0 %collective-permute-done.7 = bf16[64,2048]{1,0:T(8,128)(2,1)S(1)} collective-permute-done((bf16[64,2048]{1,0:T(8,128)(2,1)S(1)}, bf16[64,2048]{1,0:T(8,128)(2,1)S(1)}, u32[]{:S(2)}, u32[]{:S(2)}) %collective-permute-start.7) | collective-permute-done | bytes 262176 | tf_op jit(solution)/shard_map/ppermute | solution.py:34
  68.6 3.3 %collective-permute-start.12 = (bf16[32,2048]{1,0:T(8,128)(2,1)S(1)}, bf16[32,2048]{1,0:T(8,128)(2,1)S(1)}, u32[]{:S(2)}, u32[]{:S(2)}) collective-permute-start(bf16[32,2048]{1,0:T(8,128)(2,1)S(1)} %slice.174), channel_id=1, source_target_pairs={{0,14},{1,15},{2,0},{3,1},{4,2},{5,3},{6,4},{7,5},{8,6},{9,7},{10,... | collective-permute-start | bytes 393224 | tf_op jit(solution)/shard_map/ppermute | solution.py:34
  86.4 9.3 %collective-permute-done.15 = bf16[512,256]{1,0:T(8,128)(2,1)} collective-permute-done((bf16[512,256]{1,0:T(8,128)(2,1)}, bf16[512,256]{1,0:T(8,128)(2,1)}, u32[]{:S(2)}, u32[]{:S(2)}) %collective-permute-start.15) | collective-permute-done | bytes 262176 | tf_op jit(solution)/shard_map/ppermute | solution.py:46
  100.4 6.3 %shard_map.82 = (bf16[512,128]{1,0:T(8,128)(2,1)S(1)}, bf16[2048,256]{1,0:T(8,128)(2,1)S(1)}) custom-call(bf16[512,128]{1,0:T(8,128)(2,1)S(1)} %slice.177.q_ref, bf16[2048,256]{1,0:T(8,128)(2,1)S(1)} %pad_maximum_fusion.kv_ref, bf16[512,128]{1,0:T(8,128)(2,1)S(1)} %convolution_convert_fusion.1.da_ref, s32[3]{0:T(128)S(1)} %pad_add_fusion.2.place_ref), custom_call_target="tpu_custom_call" | custom-call | flops 1610612736 | bytes 2490368 | tf_op jit(solution)/shard_map/pallas_call | solution.py:132
  110.0 6.2 %collective-permute-done.20 = bf16[512,256]{1,0:T(8,128)(2,1)S(1)} collective-permute-done((bf16[512,256]{1,0:T(8,128)(2,1)S(1)}, bf16[512,256]{1,0:T(8,128)(2,1)S(1)}, u32[]{:S(2)}, u32[]{:S(2)}) %collective-permute-start.20) | collective-permute-done | bytes 262176 | tf_op jit(solution)/shard_map/ppermute | solution.py:46
  117.2 3.2 %collective-permute-start.25 = (bf16[32,1024]{1,0:T(8,128)(2,1)S(1)}, bf16[32,1024]{1,0:T(8,128)(2,1)S(1)}, u32[]{:S(2)}, u32[]{:S(2)}) collective-permute-start(bf16[32,1024]{1,0:T(8,128)(2,1)S(1)} %get-tuple-element.20), channel_id=1, source_target_pairs={{0,14},{1,15},{2,0},{3,1},{4,2},{5,3},{6,4},{7,5},{8,6},{9,7},{10,... | collective-permute-start | bytes 196616 | tf_op jit(solution)/shard_map/ppermute | solution.py:34
  122.8 3.3 %collective-permute-start.26 = (bf16[64,1024]{1,0:T(8,128)(2,1)S(1)}, bf16[64,1024]{1,0:T(8,128)(2,1)S(1)}, u32[]{:S(2)}, u32[]{:S(2)}) collective-permute-start(bf16[64,1024]{1,0:T(8,128)(2,1)S(1)} %pad_maximum_fusion.6), channel_id=1, source_target_pairs={{0,14},{1,15},{2,0},{3,1},{4,2},{5,3},{6,4},{7,5},{8,6},{9,7},{10,... | collective-permute-start | bytes 393224 | tf_op jit(solution)/shard_map/ppermute | solution.py:34
  126.2 2.8 %collective-permute-done.22 = bf16[64,1024]{1,0:T(8,128)(2,1)S(1)} collective-permute-done((bf16[64,1024]{1,0:T(8,128)(2,1)S(1)}, bf16[64,1024]{1,0:T(8,128)(2,1)S(1)}, u32[]{:S(2)}, u32[]{:S(2)}) %collective-permute-start.22) | collective-permute-done | bytes 131104 | tf_op jit(solution)/shard_map/ppermute | solution.py:34
  129.1 6.2 %collective-permute-done.23 = bf16[64,1024]{1,0:T(8,128)(2,1)S(1)} collective-permute-done((bf16[64,1024]{1,0:T(8,128)(2,1)S(1)}, bf16[64,1024]{1,0:T(8,128)(2,1)S(1)}, u32[]{:S(2)}, u32[]{:S(2)}) %collective-permute-start.23) | collective-permute-done | bytes 131104 | tf_op jit(solution)/shard_map/ppermute | solution.py:34
  137.5 3.6 %collective-permute-done.27 = bf16[64,1024]{1,0:T(8,128)(2,1)S(1)} collective-permute-done((bf16[64,1024]{1,0:T(8,128)(2,1)S(1)}, bf16[64,1024]{1,0:T(8,128)(2,1)S(1)}, u32[]{:S(2)}, u32[]{:S(2)}) %collective-permute-start.27) | collective-permute-done | bytes 131104 | tf_op jit(solution)/shard_map/ppermute | solution.py:34
  141.0 3.4 %collective-permute-start.28 = (bf16[64,1024]{1,0:T(8,128)(2,1)S(1)}, bf16[64,1024]{1,0:T(8,128)(2,1)S(1)}, u32[]{:S(2)}, u32[]{:S(2)}) collective-permute-start(bf16[64,1024]{1,0:T(8,128)(2,1)S(1)} %fusion.19), channel_id=1, source_target_pairs={{0,14},{1,15},{2,0},{3,1},{4,2},{5,3},{6,4},{7,5},{8,6},{9,7},{10,... | collective-permute-start | bytes 393224 | tf_op jit(solution)/shard_map/ppermute | solution.py:34
  144.5 2.5 %collective-permute-done.28 = bf16[64,1024]{1,0:T(8,128)(2,1)S(1)} collective-permute-done((bf16[64,1024]{1,0:T(8,128)(2,1)S(1)}, bf16[64,1024]{1,0:T(8,128)(2,1)S(1)}, u32[]{:S(2)}, u32[]{:S(2)}) %collective-permute-start.28) | collective-permute-done | bytes 131104 | tf_op jit(solution)/shard_map/ppermute | solution.py:34
  149.3 7.3 %collective-permute-start.30 = (bf16[64,1024]{1,0:T(8,128)(2,1)S(1)}, bf16[64,1024]{1,0:T(8,128)(2,1)S(1)}, u32[]{:S(2)}, u32[]{:S(2)}) collective-permute-start(bf16[64,1024]{1,0:T(8,128)(2,1)S(1)} %divide_convert_fusion), channel_id=1, source_target_pairs={{1,0},{2,1},{3,2},{4,3},{5,4},{6,5},{7,6},{8,7},{9,8},{10,9},{11,1... | collective-permute-start | bytes 393224 | tf_op jit(solution)/shard_map/ppermute | solution.py:29
  (129 shorter events, 49.3 us)
Async XLA Ops:
  6.5 70.3 %all-gather.3.cloned.1.call-start = ((), (), s32[]{:S(2)}) async-start(), calls=%async_computation | async-start | bytes 1622016 | tf_op jit(solution)/shard_map/all_gather | solution.py:69
  6.5 14.0 %collective-permute-start.1 = (s32[64]{0:T(128)}, s32[64]{0:T(128)S(1)}, u32[]{:S(2)}, u32[]{:S(2)}) collective-permute-start(s32[64]{0:T(128)} %bitcast.38), channel_id=1, source_target_pairs={{1,0},{2,1},{3,2},{4,3},{5,4},{6,5},{7,6},{8,7},{9,8},{10,9},{11,1... | collective-permute-start | bytes 776 | tf_op jit(solution)/shard_map/ppermute | solution.py:29
  14.7 8.6 %collective-permute-start = (s32[64]{0:T(128)}, s32[64]{0:T(128)S(1)}, u32[]{:S(2)}, u32[]{:S(2)}) collective-permute-start(s32[64]{0:T(128)} %bitcast.39), channel_id=1, source_target_pairs={{0,1},{1,2},{2,3},{3,4},{4,5},{5,6},{6,7},{7,8},{8,9},{9,10},{10,1... | collective-permute-start | bytes 776 | tf_op jit(solution)/shard_map/ppermute | solution.py:29
  26.7 12.0 %collective-permute-start.2 = (bf16[64,2048]{1,0:T(8,128)(2,1)S(1)}, bf16[64,2048]{1,0:T(8,128)(2,1)S(1)}, u32[]{:S(2)}, u32[]{:S(2)}) collective-permute-start(bf16[64,2048]{1,0:T(8,128)(2,1)S(1)} %pad_maximum_fusion.2), channel_id=1, source_target_pairs={{1,0},{2,1},{3,2},{4,3},{5,4},{6,5},{7,6},{8,7},{9,8},{10,9},{11,1... | collective-permute-start | bytes 786440 | tf_op jit(solution)/shard_map/ppermute | solution.py:29
  31.3 11.4 %collective-permute-start.3 = (bf16[64,2048]{1,0:T(8,128)(2,1)S(1)}, bf16[64,2048]{1,0:T(8,128)(2,1)S(1)}, u32[]{:S(2)}, u32[]{:S(2)}) collective-permute-start(bf16[64,2048]{1,0:T(8,128)(2,1)S(1)} %fusion.17), channel_id=1, source_target_pairs={{0,1},{1,2},{2,3},{3,4},{4,5},{5,6},{6,7},{7,8},{8,9},{9,10},{10,1... | collective-permute-start | bytes 786440 | tf_op jit(solution)/shard_map/ppermute | solution.py:29
  45.0 8.1 %collective-permute-start.5 = (bf16[64,2048]{1,0:T(8,128)(2,1)S(1)}, bf16[64,2048]{1,0:T(8,128)(2,1)S(1)}, u32[]{:S(2)}, u32[]{:S(2)}) collective-permute-start(bf16[64,2048]{1,0:T(8,128)(2,1)S(1)} %get-tuple-element.31), channel_id=1, source_target_pairs={{0,2},{1,3},{2,4},{3,5},{4,6},{5,7},{6,8},{7,9},{8,10},{9,11},{10,... | collective-permute-start | bytes 786440 | tf_op jit(solution)/shard_map/ppermute | solution.py:34
  45.0 8.2 %collective-permute-start.9 = (bf16[64,2048]{1,0:T(8,128)(2,1)S(1)}, bf16[64,2048]{1,0:T(8,128)(2,1)S(1)}, u32[]{:S(2)}, u32[]{:S(2)}) collective-permute-start(bf16[64,2048]{1,0:T(8,128)(2,1)S(1)} %get-tuple-element.31), channel_id=1, source_target_pairs={{0,14},{1,15},{2,0},{3,1},{4,2},{5,3},{6,4},{7,5},{8,6},{9,7},{10,... | collective-permute-start | bytes 786440 | tf_op jit(solution)/shard_map/ppermute | solution.py:34
  53.2 7.6 %collective-permute-start.6 = (bf16[64,2048]{1,0:T(8,128)(2,1)S(1)}, bf16[64,2048]{1,0:T(8,128)(2,1)S(1)}, u32[]{:S(2)}, u32[]{:S(2)}) collective-permute-start(bf16[64,2048]{1,0:T(8,128)(2,1)S(1)} %collective-permute-done.5), channel_id=1, source_target_pairs={{0,2},{1,3},{2,4},{3,5},{4,6},{5,7},{6,8},{7,9},{8,10},{9,11},{10,... | collective-permute-start | bytes 786440 | tf_op jit(solution)/shard_map/ppermute | solution.py:34
  53.2 7.6 %collective-permute-start.10 = (bf16[64,2048]{1,0:T(8,128)(2,1)S(1)}, bf16[64,2048]{1,0:T(8,128)(2,1)S(1)}, u32[]{:S(2)}, u32[]{:S(2)}) collective-permute-start(bf16[64,2048]{1,0:T(8,128)(2,1)S(1)} %collective-permute-done.9), channel_id=1, source_target_pairs={{0,14},{1,15},{2,0},{3,1},{4,2},{5,3},{6,4},{7,5},{8,6},{9,7},{10,... | collective-permute-start | bytes 786440 | tf_op jit(solution)/shard_map/ppermute | solution.py:34
  60.8 7.7 %collective-permute-start.7 = (bf16[64,2048]{1,0:T(8,128)(2,1)S(1)}, bf16[64,2048]{1,0:T(8,128)(2,1)S(1)}, u32[]{:S(2)}, u32[]{:S(2)}) collective-permute-start(bf16[64,2048]{1,0:T(8,128)(2,1)S(1)} %collective-permute-done.6), channel_id=1, source_target_pairs={{0,2},{1,3},{2,4},{3,5},{4,6},{5,7},{6,8},{7,9},{8,10},{9,11},{10,... | collective-permute-start | bytes 786440 | tf_op jit(solution)/shard_map/ppermute | solution.py:34
  60.8 7.8 %collective-permute-start.11 = (bf16[64,2048]{1,0:T(8,128)(2,1)S(1)}, bf16[64,2048]{1,0:T(8,128)(2,1)S(1)}, u32[]{:S(2)}, u32[]{:S(2)}) collective-permute-start(bf16[64,2048]{1,0:T(8,128)(2,1)S(1)} %collective-permute-done.10), channel_id=1, source_target_pairs={{0,14},{1,15},{2,0},{3,1},{4,2},{5,3},{6,4},{7,5},{8,6},{9,7},{10,... | collective-permute-start | bytes 786440 | tf_op jit(solution)/shard_map/ppermute | solution.py:34
  68.5 6.3 %collective-permute-start.8 = (bf16[32,2048]{1,0:T(8,128)(2,1)S(1)}, bf16[32,2048]{1,0:T(8,128)(2,1)S(1)}, u32[]{:S(2)}, u32[]{:S(2)}) collective-permute-start(bf16[32,2048]{1,0:T(8,128)(2,1)S(1)} %slice.173), channel_id=1, source_target_pairs={{0,2},{1,3},{2,4},{3,5},{4,6},{5,7},{6,8},{7,9},{8,10},{9,11},{10,... | collective-permute-start | bytes 393224 | tf_op jit(solution)/shard_map/ppermute | solution.py:34
  68.6 6.8 %collective-permute-start.12 = (bf16[32,2048]{1,0:T(8,128)(2,1)S(1)}, bf16[32,2048]{1,0:T(8,128)(2,1)S(1)}, u32[]{:S(2)}, u32[]{:S(2)}) collective-permute-start(bf16[32,2048]{1,0:T(8,128)(2,1)S(1)} %slice.174), channel_id=1, source_target_pairs={{0,14},{1,15},{2,0},{3,1},{4,2},{5,3},{6,4},{7,5},{8,6},{9,7},{10,... | collective-permute-start | bytes 393224 | tf_op jit(solution)/shard_map/ppermute | solution.py:34
  83.3 12.4 %collective-permute-start.15 = (bf16[512,256]{1,0:T(8,128)(2,1)}, bf16[512,256]{1,0:T(8,128)(2,1)}, u32[]{:S(2)}, u32[]{:S(2)}) collective-permute-start(bf16[512,256]{1,0:T(8,128)(2,1)} %slice.178), channel_id=1, source_target_pairs={{0,16},{1,17},{2,18},{3,19},{4,20},{5,21},{6,22},{7,23},{8,24},{9,... | collective-permute-start | bytes 786440 | tf_op jit(solution)/shard_map/ppermute | solution.py:46
  85.7 10.0 %collective-permute-start.17 = (bf16[64,1024]{1,0:T(8,128)(2,1)S(1)}, bf16[64,1024]{1,0:T(8,128)(2,1)S(1)}, u32[]{:S(2)}, u32[]{:S(2)}) collective-permute-start(bf16[64,1024]{1,0:T(8,128)(2,1)S(1)} %dynamic-slice_bitcast_fusion), channel_id=1, source_target_pairs={{0,1},{1,0},{2,3},{3,2},{4,5},{5,4},{6,7},{7,6},{8,9},{9,8},{10,11... | collective-permute-start | bytes 393224 | tf_op jit(solution)/shard_map/ppermute | solution.py:39
  86.4 12.8 %collective-permute-start.14 = (bf16[512,256]{1,0:T(8,128)(2,1)}, bf16[512,256]{1,0:T(8,128)(2,1)S(1)}, u32[]{:S(2)}, u32[]{:S(2)}) collective-permute-start(bf16[512,256]{1,0:T(8,128)(2,1)} %slice.178), channel_id=1, source_target_pairs={{0,1},{1,0},{2,3},{3,2},{4,5},{5,4},{6,7},{7,6},{8,9},{9,8},{10,11... | collective-permute-start | bytes 786440 | tf_op jit(solution)/shard_map/ppermute | solution.py:39
  108.5 7.7 %collective-permute-start.20 = (bf16[512,256]{1,0:T(8,128)(2,1)S(1)}, bf16[512,256]{1,0:T(8,128)(2,1)S(1)}, u32[]{:S(2)}, u32[]{:S(2)}) collective-permute-start(bf16[512,256]{1,0:T(8,128)(2,1)S(1)} %add_convert_fusion.2), channel_id=1, source_target_pairs={{16,0},{17,1},{18,2},{19,3},{20,4},{21,5},{22,6},{23,7},{24,8},{25... | collective-permute-start | bytes 786440 | tf_op jit(solution)/shard_map/ppermute | solution.py:46
  122.7 6.3 %collective-permute-start.22 = (bf16[64,1024]{1,0:T(8,128)(2,1)S(1)}, bf16[64,1024]{1,0:T(8,128)(2,1)S(1)}, u32[]{:S(2)}, u32[]{:S(2)}) collective-permute-start(bf16[64,1024]{1,0:T(8,128)(2,1)S(1)} %pad_maximum_fusion.5), channel_id=1, source_target_pairs={{0,2},{1,3},{2,4},{3,5},{4,6},{5,7},{6,8},{7,9},{8,10},{9,11},{10,... | collective-permute-start | bytes 393224 | tf_op jit(solution)/shard_map/ppermute | solution.py:34
  122.8 6.3 %collective-permute-start.26 = (bf16[64,1024]{1,0:T(8,128)(2,1)S(1)}, bf16[64,1024]{1,0:T(8,128)(2,1)S(1)}, u32[]{:S(2)}, u32[]{:S(2)}) collective-permute-start(bf16[64,1024]{1,0:T(8,128)(2,1)S(1)} %pad_maximum_fusion.6), channel_id=1, source_target_pairs={{0,14},{1,15},{2,0},{3,1},{4,2},{5,3},{6,4},{7,5},{8,6},{9,7},{10,... | collective-permute-start | bytes 393224 | tf_op jit(solution)/shard_map/ppermute | solution.py:34
  129.0 6.3 %collective-permute-start.23 = (bf16[64,1024]{1,0:T(8,128)(2,1)S(1)}, bf16[64,1024]{1,0:T(8,128)(2,1)S(1)}, u32[]{:S(2)}, u32[]{:S(2)}) collective-permute-start(bf16[64,1024]{1,0:T(8,128)(2,1)S(1)} %fusion.20), channel_id=1, source_target_pairs={{0,2},{1,3},{2,4},{3,5},{4,6},{5,7},{6,8},{7,9},{8,10},{9,11},{10,... | collective-permute-start | bytes 393224 | tf_op jit(solution)/shard_map/ppermute | solution.py:34
  137.4 7.1 %collective-permute-start.24 = (bf16[64,1024]{1,0:T(8,128)(2,1)S(1)}, bf16[64,1024]{1,0:T(8,128)(2,1)S(1)}, u32[]{:S(2)}, u32[]{:S(2)}) collective-permute-start(bf16[64,1024]{1,0:T(8,128)(2,1)S(1)} %get-tuple-element.13), channel_id=1, source_target_pairs={{0,2},{1,3},{2,4},{3,5},{4,6},{5,7},{6,8},{7,9},{8,10},{9,11},{10,... | collective-permute-start | bytes 393224 | tf_op jit(solution)/shard_map/ppermute | solution.py:34
  141.0 5.9 %collective-permute-start.28 = (bf16[64,1024]{1,0:T(8,128)(2,1)S(1)}, bf16[64,1024]{1,0:T(8,128)(2,1)S(1)}, u32[]{:S(2)}, u32[]{:S(2)}) collective-permute-start(bf16[64,1024]{1,0:T(8,128)(2,1)S(1)} %fusion.19), channel_id=1, source_target_pairs={{0,14},{1,15},{2,0},{3,1},{4,2},{5,3},{6,4},{7,5},{8,6},{9,7},{10,... | collective-permute-start | bytes 393224 | tf_op jit(solution)/shard_map/ppermute | solution.py:34
  147.4 9.9 %collective-permute-start.29 = (bf16[64,1024]{1,0:T(8,128)(2,1)S(1)}, bf16[64,1024]{1,0:T(8,128)(2,1)S(1)}, u32[]{:S(2)}, u32[]{:S(2)}) collective-permute-start(bf16[64,1024]{1,0:T(8,128)(2,1)S(1)} %divide_convert_fusion), channel_id=1, source_target_pairs={{0,1},{1,2},{2,3},{3,4},{4,5},{5,6},{6,7},{7,8},{8,9},{9,10},{10,1... | collective-permute-start | bytes 393224 | tf_op jit(solution)/shard_map/ppermute | solution.py:29
  149.3 9.8 %collective-permute-start.30 = (bf16[64,1024]{1,0:T(8,128)(2,1)S(1)}, bf16[64,1024]{1,0:T(8,128)(2,1)S(1)}, u32[]{:S(2)}, u32[]{:S(2)}) collective-permute-start(bf16[64,1024]{1,0:T(8,128)(2,1)S(1)} %divide_convert_fusion), channel_id=1, source_target_pairs={{1,0},{2,1},{3,2},{4,3},{5,4},{6,5},{7,6},{8,7},{9,8},{10,9},{11,1... | collective-permute-start | bytes 393224 | tf_op jit(solution)/shard_map/ppermute | solution.py:29
  (19 other events, 208.9 us)
Sparse Core Ops, SparseCore 0:
  20.6 40.8 all-gather.2

commit v2 on v1

v2 whole, which is shorter than its diff:
```python
import functools
import math

import jax
import jax.numpy as jnp
from jax import lax
from jax.experimental import pallas as pl
from jax.experimental.pallas import tpu as pltpu
from jax.sharding import PartitionSpec as P

HEAD = 128
HALVES, TURNS, PAIR, CORES = 2, 4, 2, 2
CTX = HALVES * TURNS * PAIR * CORES
ROWS_X, ROWS_Y = 2, 4
NEG = -1e30
WIRE = jnp.bfloat16
F32 = jnp.float32
VMEM = pl.BlockSpec(memory_space=pltpu.VMEM)
SMEM = pl.BlockSpec(memory_space=pltpu.SMEM)
PARAMS = pltpu.CompilerParams(vmem_limit_bytes=48 * 1024 * 1024)


def place(half, turn, pair, core):
    return ((half * TURNS + turn % TURNS) * PAIR + pair) * CORES + core


def moved(value, to):
    spots = [
        (h, t, p, k)
        for h in range(HALVES)
        for t in range(TURNS)
        for p in range(PAIR)
        for k in range(CORES)
    ]
    pairs = [(place(*s), place(*to(*s))) for s in spots if to(*s) is not None]
    return lax.ppermute(value, "ctx", pairs)


def along(value, steps):
    pairs = [(i, i + steps) for i in range(CTX) if 0 <= i + steps < CTX]
    return lax.ppermute(value, "ctx", pairs)


def other_core(value):
    return moved(value, lambda h, t, p, k: (h, t, p, 1 - k))


def other_pair(value):
    return moved(value, lambda h, t, p, k: (h, t, 1 - p, k))


def across(value, source):
    return moved(value, lambda h, t, p, k: (1 - h, t, p, k) if h == source else None)


def turned(value, way):
    return moved(value, lambda h, t, p, k: (h, t + way * (1 - 2 * k), p, k))


def contract_last(left, right):
    return lax.dot_general(left, right, (((1,), (1,)), ((), ())), preferred_element_type=F32)


def contract_first(left, right):
    return lax.dot_general(left, right, (((0,), (0,)), ((), ())), preferred_element_type=F32)


def cut_kernel(head_ref, q_ref, k_ref, v_ref, out_ref):
    out_ref[:, :HEAD] = q_ref[...]
    out_ref[:, HEAD : 2 * HEAD] = k_ref[...]
    out_ref[:, 2 * HEAD :] = v_ref[...]


def columns_in(w_query, w_key, w_value, head):
    rows = w_query.shape[0]
    block = pl.BlockSpec((rows, HEAD), lambda i, h: (0, h[0]))
    mine = pl.pallas_call(
        cut_kernel,
        grid_spec=pltpu.PrefetchScalarGridSpec(
            num_scalar_prefetch=1,
            grid=(1,),
            in_specs=[block] * 3,
            out_specs=pl.BlockSpec((rows, 3 * HEAD), lambda i, h: (0, 0)),
        ),
        out_shape=jax.ShapeDtypeStruct((rows, 3 * HEAD), w_query.dtype),
    )(head[None], w_query, w_key, w_value)
    count = ROWS_X * ROWS_Y
    swap = [(d, (d + ROWS_Y) % count) for d in range(count)]
    both = jnp.concatenate([mine, lax.ppermute(mine, "dp", swap)], axis=0)

    def shifted(step):
        pairs = [(d, d // ROWS_Y * ROWS_Y + (d + step) % ROWS_Y) for d in range(count)]
        return lax.ppermute(both, "dp", pairs)

    return [both, shifted(1), shifted(-1), shifted(2)]


def rows_out(w_out, turn, core):
    rows = w_out.shape[0] // CORES
    half = lax.dynamic_slice(w_out, (core * rows, 0), (rows, w_out.shape[1]))
    gathered = lax.all_gather(half, "dp", axis=0, tiled=False)
    mine = lax.dynamic_index_in_dim(gathered, turn * CORES + core, 0, keepdims=False)
    theirs = lax.dynamic_index_in_dim(gathered, turn * CORES + 1 - core, 0, keepdims=False)
    return mine, other_core(theirs)


def gathered_rows(shard):
    swapped = other_core(shard)
    near = turned(jnp.concatenate([shard, swapped], axis=0), 1)
    far = turned(near[: shard.shape[0]], 1)
    return [shard, swapped, near, other_core(near), far, other_core(far)]


def rows_at(row, half, turn, pair, core, seg):
    slot = row // seg
    two = slot // 2
    way = 1 - 2 * core
    step = jnp.where(two == 0, 0, jnp.where(two == 1, way, jnp.where(two == 2, -way, 2)))
    flip = jnp.where(two == 2, 1 - slot % 2, slot % 2)
    its_core = jnp.where(flip == 1, 1 - core, core)
    its_turn = (turn - step + TURNS) % TURNS
    return place(half, its_turn, pair, its_core) * seg + row % seg


def fill(out_ref, pieces):
    at = 0
    for piece in pieces:
        out_ref[at : at + piece.shape[0], :] = piece[...]
        at += piece.shape[0]


def project_kernel(*refs):
    place_ref, pieces, weights = refs[0], refs[1:7], refs[7:11]
    q_ref, top_ref, bottom_ref, w_ref, rows = refs[11:]
    fill(rows, pieces)
    dp = place_ref[4]
    x, y = dp // ROWS_Y, dp % ROWS_Y
    depth = weights[0].shape[0] // ROWS_X
    for weight, step in zip(weights, (0, 1, -1, 2)):
        its_y = (y - step + ROWS_Y) % ROWS_Y
        for i in range(ROWS_X):
            its_x = x if i == 0 else 1 - x
            at = pl.multiple_of((its_x * ROWS_Y + its_y) * depth, depth)
            w_ref[pl.ds(at, depth), :] = weight[i * depth : (i + 1) * depth, :]
    out = jnp.dot(rows[...], w_ref[...], preferred_element_type=F32).astype(jnp.bfloat16)
    cut = out.shape[0] // 2
    q_ref[...] = out[:, :HEAD]
    top_ref[...] = out[:cut, HEAD:]
    bottom_ref[...] = out[cut:, HEAD:]


def project(where, pieces, weights):
    rows = sum(piece.shape[0] for piece in pieces)
    width = pieces[0].shape[1]
    bf16 = lambda *shape: jax.ShapeDtypeStruct(shape, jnp.bfloat16)
    return pl.pallas_call(
        project_kernel,
        out_shape=(
            bf16(rows, HEAD),
            bf16(rows // 2, 2 * HEAD),
            bf16(rows // 2, 2 * HEAD),
            bf16(width, 3 * HEAD),
        ),
        in_specs=[SMEM] + [VMEM] * 10,
        out_specs=(VMEM,) * 4,
        scratch_shapes=[pltpu.VMEM((rows, width), jnp.bfloat16)],
        compiler_params=PARAMS,
    )(where, *pieces, *weights)


def dattended_kernel(*refs):
    place_ref, pieces, mine, theirs, da_ref, rows, weight = (
        refs[0],
        refs[1:7],
        refs[7],
        refs[8],
        refs[9],
        refs[10],
        refs[11],
    )
    core = place_ref[3]
    half = mine.shape[0]
    fill(rows, pieces)
    weight[pl.ds(pl.multiple_of(core * half, half), half), :] = mine[...]
    weight[pl.ds(pl.multiple_of((1 - core) * half, half), half), :] = theirs[...]
    da_ref[...] = contract_last(rows[...], weight[...]).astype(jnp.bfloat16)


def dattended(where, pieces, mine, theirs):
    rows = sum(piece.shape[0] for piece in pieces)
    width = pieces[0].shape[1]
    return pl.pallas_call(
        dattended_kernel,
        out_shape=jax.ShapeDtypeStruct((rows, HEAD), jnp.bfloat16),
        in_specs=[SMEM] + [VMEM] * 8,
        out_specs=VMEM,
        scratch_shapes=[
            pltpu.VMEM((rows, width), jnp.bfloat16),
            pltpu.VMEM((HEAD, width), jnp.bfloat16),
        ],
        compiler_params=PARAMS,
    )(where, *pieces, mine, theirs)


def attention_kernel(tile, seg, *refs):
    place_ref, q_ref, da_ref, blocks = refs[0], refs[1], refs[2], refs[3:11]
    dq_ref, outs, kv, dkt, dvt = refs[11], refs[12:20], refs[20], refs[21], refs[22]
    half, turn, pair, core = place_ref[0], place_ref[1], place_ref[2], place_ref[3]
    queries, keys = q_ref.shape[0], kv.shape[0]
    fill(kv, blocks)
    spot = lax.broadcasted_iota(jnp.int32, (1, keys), 1)
    block = spot // queries
    key_half = jnp.where(block < 2, half, 1 - half)
    key_pair = jnp.where(block % 2 == 0, pair, 1 - pair)
    key_at = rows_at(spot % queries, key_half, turn, key_pair, core, seg)
    turn_up = math.log2(math.e) / math.sqrt(HEAD)
    scale = 1.0 / math.sqrt(HEAD)
    k = kv[:, :HEAD]
    v = kv[:, HEAD:]
    for step in range(queries // tile):
        rows = slice(step * tile, (step + 1) * tile)
        query = lax.broadcasted_iota(jnp.int32, (tile, 1), 0) + step * tile
        query_at = rows_at(query, half, turn, pair, core, seg)
        q = q_ref[rows, :]
        da = da_ref[rows, :]
        score = jnp.where(key_at <= query_at, contract_last(q, k), NEG)
        peak = jnp.max(score, axis=1, keepdims=True)
        expo = jnp.exp2((score - peak) * turn_up)
        probs = expo * (1.0 / jnp.sum(expo, axis=1, keepdims=True))
        probs_b = probs.astype(jnp.bfloat16)
        attended = jnp.dot(probs_b, v, preferred_element_type=F32).astype(jnp.bfloat16)
        delta = jnp.sum(da.astype(F32) * attended.astype(F32), axis=1, keepdims=True)
        dscore = (probs * (contract_last(da, v) - delta)).astype(jnp.bfloat16)
        dq = jnp.dot(dscore, k, preferred_element_type=F32) * scale
        dq_ref[rows, :] = dq.astype(jnp.bfloat16)
        dk_part = contract_first(q, dscore)
        dv_part = contract_first(da, probs_b)
        if step == 0:
            dkt[...] = dk_part
            dvt[...] = dv_part
        else:
            dkt[...] += dk_part
            dvt[...] += dv_part
    part = keys // len(outs)
    for i, out in enumerate(outs):
        lanes = slice(i * part, (i + 1) * part)
        out[:, :HEAD] = (dkt[:, lanes] * scale).T.astype(jnp.bfloat16)
        out[:, HEAD:] = dvt[:, lanes].T.astype(jnp.bfloat16)


def attention(where, q, da, blocks, seg):
    queries = q.shape[0]
    keys = sum(block.shape[0] for block in blocks)
    part = jax.ShapeDtypeStruct(blocks[0].shape, jnp.bfloat16)
    return pl.pallas_call(
        functools.partial(attention_kernel, 128, seg),
        out_shape=(jax.ShapeDtypeStruct((queries, HEAD), jnp.bfloat16),) + (part,) * 8,
        in_specs=[SMEM] + [VMEM] * 10,
        out_specs=(VMEM,) * 9,
        scratch_shapes=[
            pltpu.VMEM((keys, 2 * HEAD), jnp.bfloat16),
            pltpu.VMEM((HEAD, keys), F32),
            pltpu.VMEM((HEAD, keys), F32),
        ],
        compiler_params=PARAMS,
        cost_estimate=pl.CostEstimate(
            flops=12 * queries * keys * HEAD,
            bytes_accessed=2 * HEAD * (3 * queries + 4 * keys),
            transcendentals=queries * keys,
        ),
    )(where, q, da, *blocks)


def unproject_kernel(seg, dq_ref, *refs):
    dkv_parts, w_ref = refs[:6], refs[6]
    swap_ref, far_ref, near_ref, own_ref = refs[7:11]
    top = sum(ref[...].astype(F32) for ref in dkv_parts[0::2])
    bottom = sum(ref[...].astype(F32) for ref in dkv_parts[1::2])
    dkv = jnp.concatenate([top, bottom], axis=0).astype(jnp.bfloat16)
    left = jnp.concatenate([dq_ref[...], dkv], axis=1)
    out = contract_last(left, w_ref[...])
    own_ref[...] = out[: 2 * seg]
    near_ref[...] = out[2 * seg : 4 * seg]
    swap_ref[: 2 * seg, :] = out[4 * seg : 6 * seg].astype(WIRE)
    far_ref[...] = out[6 * seg : 7 * seg]
    swap_ref[2 * seg :, :] = out[7 * seg :].astype(WIRE)


def unproject(dq, dkv_parts, w_full, seg):
    width = w_full.shape[0]
    return pl.pallas_call(
        functools.partial(unproject_kernel, seg),
        out_shape=(
            jax.ShapeDtypeStruct((3 * seg, width), WIRE),
            jax.ShapeDtypeStruct((seg, width), F32),
            jax.ShapeDtypeStruct((2 * seg, width), F32),
            jax.ShapeDtypeStruct((2 * seg, width), F32),
        ),
        in_specs=[VMEM] * 8,
        out_specs=(VMEM,) * 4,
        compiler_params=PARAMS,
    )(dq, *dkv_parts, w_full)


def summed_rows(swap, far, near, own, seg):
    swapped = other_core(swap).astype(F32)
    back = turned((far + swapped[2 * seg :]).astype(WIRE), -1).astype(F32)
    near = near + swapped[: 2 * seg] + jnp.pad(back, ((0, seg), (0, 0)))
    own = own + turned(near.astype(WIRE), -1).astype(F32)
    return own[:seg] + other_core(own[seg:].astype(WIRE)).astype(F32)


def per_device(tokens, starts, gain, w_query, w_key, w_value, w_out, cotangent):
    token_rows = tokens[0]
    grad_out = cotangent[0]
    own_starts = starts[0]
    rows, width = token_rows.shape
    seg = own_starts.shape[0]
    length = rows * CTX
    ctx = lax.axis_index("ctx")
    core, pair = ctx % CORES, ctx // CORES % PAIR
    turn, half = ctx // (CORES * PAIR) % TURNS, ctx // (CORES * PAIR * TURNS)
    where = jnp.stack([half, turn, pair, core, lax.axis_index("dp")])

    before = jnp.where(ctx == 0, -1, along(own_starts, 1))
    after = jnp.where(ctx == CTX - 1, length, along(own_starts, -1))
    weights = columns_in(w_query, w_key, w_value, turn * CORES + core)
    out_mine, out_theirs = rows_out(w_out, turn, core)
    window = jnp.concatenate([before, own_starts, after])
    positions = ctx * rows + lax.iota(jnp.int32, rows)
    ends = jnp.concatenate([window[1:], jnp.full((1,), length, jnp.int32)])
    member = (
        (window[None, :] <= positions[:, None]) & (positions[:, None] < ends[None, :])
    ).astype(jnp.bfloat16)
    token_sum = contract_first(member, token_rows)
    grad_sum = contract_first(member, grad_out)
    lower = jnp.concatenate([token_sum[:seg], grad_sum[1 : seg + 1]], axis=1).astype(WIRE)
    tail = jnp.concatenate([grad_sum[2 * seg + 1 :], jnp.zeros((1, width), F32)], axis=0)
    upper = jnp.concatenate([token_sum[2 * seg :], tail], axis=1).astype(WIRE)
    from_after = along(lower, -1).astype(F32)
    from_before = along(upper, 1).astype(F32)
    from_second = along(grad_sum[:1].astype(WIRE), -2).astype(F32)
    count = (ends - window)[seg : 2 * seg].astype(F32)
    pooled = token_sum[seg : 2 * seg] + from_after[:, :width] + from_before[:, :width]
    pooled = pooled / count[:, None]
    last = lax.broadcasted_iota(jnp.int32, (seg, 1), 0) == seg - 1
    dout = grad_sum[seg + 1 : 2 * seg + 1] + from_after[:, width:] + from_before[:, width:]
    dout = dout + jnp.where(last, from_second, 0.0)
    rms = jnp.sqrt(jnp.mean(pooled * pooled, axis=-1, keepdims=True) + 1e-06)
    normed = pooled / rms
    normin = (normed * gain).astype(jnp.bfloat16)

    pieces = gathered_rows(normin)
    q, own_top, own_bottom, w_full = project(where, pieces, weights)
    dout_b, _ = lax.optimization_barrier((dout.astype(jnp.bfloat16), pieces[4]))
    da = dattended(where, gathered_rows(dout_b), out_mine, out_theirs)
    pair_top, far_bottom = other_pair(own_top), across(own_bottom, 0)
    pair_bottom, far_top = other_pair(own_bottom), across(own_top, 0)
    cross_top, cross_bottom = across(pair_top, 0), other_pair(far_bottom)
    blocks = (
        own_top,
        own_bottom,
        pair_top,
        pair_bottom,
        far_top,
        far_bottom,
        cross_top,
        cross_bottom,
    )
    dq, *grads = attention(where, q, da, blocks, seg)
    own_top, own_bottom, pair_top, pair_bottom, far_top, far_bottom, cross_top, cross_bottom = grads
    add = lambda a, b: (a.astype(F32) + b.astype(F32)).astype(WIRE)
    back_top, back_bottom = across(cross_top, 1), other_pair(cross_bottom)
    got_bottom, got_far_top = other_pair(pair_bottom), across(far_top, 1)
    got_top = other_pair(add(pair_top, back_top))
    got_far_bottom = across(add(far_bottom, back_bottom), 1)
    parts = (own_top, own_bottom, got_top, got_bottom, got_far_top, got_far_bottom)
    dnormin = summed_rows(*unproject(dq, parts, w_full, seg), seg)

    scaled = dnormin * gain
    dpooled = dout + (scaled - normed * jnp.mean(scaled * normed, axis=-1, keepdims=True)) / rms
    per_seg = (dpooled / count[:, None]).astype(WIRE)
    per_window = jnp.concatenate([along(per_seg, 1), per_seg, along(per_seg, -1)], axis=0)
    spread = jnp.dot(member, per_window, preferred_element_type=F32)
    return (grad_out.astype(F32) + spread).astype(jnp.bfloat16)[None]


def solution(mesh):
    return jax.shard_map(
        per_device,
        mesh=mesh,
        in_specs=(
            P("dp", "ctx", None),
            P("dp", "ctx"),
            P(),
            P("dp", None),
            P("dp", None),
            P("dp", None),
            P("dp", None),
            P("dp", "ctx", None),
        ),
        out_specs=P("dp", "ctx", None),
        check_vma=False,
    )
```

time: 168 us -> 177 us (1.054)
  waiting for transfers between devices: 60.8 us -> 72.6 us
  Pallas kernels: 6.32 us -> 12.4 us
  local copies, waits for them, and re-layouts: 14.8 us -> 11.5 us
  matrix products: 6.91 us -> 3.81 us
  other arithmetic: 6.96 us -> 4.25 us
    ppermute x24 -> x31, waiting for transfers between devices: 48.5 us -> 58.1 us  [the longest x27 46.4 us: moved(): return lax.ppermute(value, 'ctx', pairs)]
    pallas_call x0 -> x4, Pallas kernels: none -> 5.59 us  [the longest x1 1.98 us: project(): pl.pallas_call(project_kernel, out_shape=(bf16(rows, HEAD), bf16(rows //...]
    dot_general x4 -> x1, matrix products: 4.56 us -> 1.46 us  [per_device(): spread = jnp.dot(member, per_window, preferred_element_type=F32)]
    slice x9 -> x4, local copies, waits for them, and re-layouts: 2.99 us -> 0.69 us  [the longest x2 0.67 us: gathered_rows(): far = turned(near[:shard.shape[0]], 1)]
    ppermute x7, starting transfers between devices: 28 us -> 25.7 us  [along(): return lax.ppermute(value, 'ctx', pairs)]
    ppermute x7, waiting for transfers between devices: 12.3 us -> 14.5 us  [along(): return lax.ppermute(value, 'ctx', pairs)]
    ppermute x24 -> x31, starting transfers between devices: 29.6 us -> 30.4 us  [the longest x27 25.3 us: moved(): return lax.ppermute(value, 'ctx', pairs)]
    unnamed x29 -> x44, local copies, waits for them, and re-layouts: 7.86 us -> 8 us
  transfers between devices with their start and end apart: 32 -> 39, of which waited for: 18 -> 22; matrix products, arithmetic and copies ran while one was open for 11% -> 5% of each run, Pallas kernels for 0% -> 3%
where the time goes in v2:
time: 177 us; the launch traced here: 175 us
  waiting for transfers between devices  72.6 us (41%)
  starting transfers between devices  56.2 us (32%)
  between operations  13.9 us (8%)
  Pallas kernels  12.4 us (7%)
  local copies, waits for them, and re-layouts  11.5 us (6%)
  other arithmetic  4.25 us (2%)
  matrix products  3.81 us (2%)
    ppermute x27, waiting for transfers between devices, moved(): return lax.ppermute(value, 'ctx', pairs)  46.4 us
    ppermute x7, starting transfers between devices, along(): return lax.ppermute(value, 'ctx', pairs)  25.7 us
    ppermute x27, starting transfers between devices, moved(): return lax.ppermute(value, 'ctx', pairs)  25.3 us
    ppermute x7, waiting for transfers between devices, along(): return lax.ppermute(value, 'ctx', pairs)  14.5 us
    unnamed x44, local copies, waits for them, and re-layouts  8 us
    pallas_call x1, Pallas kernels, attention(): pl.pallas_call(functools.partial(attention_kernel, 128, seg), out_shape=(...  6.78 us
    ppermute x3, waiting for transfers between devices, shifted(): return lax.ppermute(both, 'dp', pairs)  6.37 us
    ppermute x1, waiting for transfers between devices, columns_in(): both = jnp.concatenate([mine, lax.ppermute(mine, 'dp', swap)], axis=0)  5.26 us
  transfers between devices with their start and end apart: 39, of which 22 were waited for; matrix products, arithmetic and copies ran while one was open for 5% of the time, Pallas kernels for 3%

profile of v2, /device:TPU:6, one launch (start us, length us, event | category | flops | bytes accessed | tf_op | source)
XLA Modules:
  0.0 174.7 jit_solution(217925654987888142)
XLA Ops:
  6.5 8.2 %collective-permute-start.1 = (s32[64]{0:T(128)}, s32[64]{0:T(128)S(1)}, u32[]{:S(2)}, u32[]{:S(2)}) collective-permute-start(s32[64]{0:T(128)} %bitcast.28), channel_id=1, source_target_pairs={{1,0},{2,1},{3,2},{4,3},{5,4},{6,5},{7,6},{8,7},{9,8},{10,9},{11,1... | collective-permute-start | bytes 776 | tf_op jit(solution)/shard_map/ppermute | solution.py:41
  18.3 5.0 %collective-permute-done = s32[64]{0:T(128)S(1)} collective-permute-done((s32[64]{0:T(128)}, s32[64]{0:T(128)S(1)}, u32[]{:S(2)}, u32[]{:S(2)}) %collective-permute-start) | collective-permute-done | bytes 288 | tf_op jit(solution)/shard_map/ppermute | solution.py:41
  26.7 2.3 %collective-permute-start.2 = (bf16[64,2048]{1,0:T(8,128)(2,1)S(1)}, bf16[64,2048]{1,0:T(8,128)(2,1)S(1)}, u32[]{:S(2)}, u32[]{:S(2)}) collective-permute-start(bf16[64,2048]{1,0:T(8,128)(2,1)S(1)} %pad_maximum_fusion), channel_id=1, source_target_pairs={{1,0},{2,1},{3,2},{4,3},{5,4},{6,5},{7,6},{8,7},{9,8},{10,9},{11,1... | collective-permute-start | bytes 786440 | tf_op jit(solution)/shard_map/ppermute | solution.py:41
  29.0 2.1 %collective-permute-start.3 = (bf16[64,2048]{1,0:T(8,128)(2,1)S(1)}, bf16[64,2048]{1,0:T(8,128)(2,1)S(1)}, u32[]{:S(2)}, u32[]{:S(2)}) collective-permute-start(bf16[64,2048]{1,0:T(8,128)(2,1)S(1)} %fusion.13), channel_id=1, source_target_pairs={{0,1},{1,2},{2,3},{3,4},{4,5},{5,6},{6,7},{7,8},{8,9},{9,10},{10,1... | collective-permute-start | bytes 786440 | tf_op jit(solution)/shard_map/ppermute | solution.py:41
  31.1 2.2 %collective-permute-start.4 = (bf16[1,1024]{1,0:T(2,128)(2,1)S(1)}, bf16[1,1024]{1,0:T(2,128)(2,1)S(1)}, u32[]{:S(2)}, u32[]{:S(2)}) collective-permute-start(bf16[1,1024]{1,0:T(2,128)(2,1)S(1)} %slice.89), channel_id=1, source_target_pairs={{2,0},{3,1},{4,2},{5,3},{6,4},{7,5},{8,6},{9,7},{10,8},{11,9},{12,... | collective-permute-start | bytes 6152 | tf_op jit(solution)/shard_map/ppermute | solution.py:41
  33.4 3.3 %collective-permute-done.4 = bf16[1,1024]{1,0:T(2,128)(2,1)S(1)} collective-permute-done((bf16[1,1024]{1,0:T(2,128)(2,1)S(1)}, bf16[1,1024]{1,0:T(2,128)(2,1)S(1)}, u32[]{:S(2)}, u32[]{:S(2)}) %collective-permute-start.4) | collective-permute-done | bytes 2080 | tf_op jit(solution)/shard_map/ppermute | solution.py:41
  36.7 3.7 %collective-permute-done.3 = bf16[64,2048]{1,0:T(8,128)(2,1)S(1)} collective-permute-done((bf16[64,2048]{1,0:T(8,128)(2,1)S(1)}, bf16[64,2048]{1,0:T(8,128)(2,1)S(1)}, u32[]{:S(2)}, u32[]{:S(2)}) %collective-permute-start.3) | collective-permute-done | bytes 262176 | tf_op jit(solution)/shard_map/ppermute | solution.py:41
  43.7 9.9 %collective-permute-done.6.refs_3_ = bf16[128,1024]{1,0:T(8,128)(2,1)S(1)} collective-permute-done((bf16[128,1024]{1,0:T(8,128)(2,1)S(1)}, bf16[128,1024]{1,0:T(8,128)(2,1)S(1)}, u32[]{:S(2)}, u32[]{:S(2)}) %collective-permute-start.6) | collective-permute-done | bytes 262176 | tf_op jit(solution)/shard_map/ppermute | solution.py:36
  53.7 10.0 %collective-permute-done.8.refs_5_ = bf16[64,1024]{1,0:T(8,128)(2,1)S(1)} collective-permute-done((bf16[64,1024]{1,0:T(8,128)(2,1)S(1)}, bf16[64,1024]{1,0:T(8,128)(2,1)S(1)}, u32[]{:S(2)}, u32[]{:S(2)}) %collective-permute-start.8) | collective-permute-done | bytes 131104 | tf_op jit(solution)/shard_map/ppermute | solution.py:36
  65.3 5.3 %collective-permute-done.10 = bf16[128,384]{1,0:T(8,128)(2,1)S(1)} collective-permute-done((bf16[128,384]{1,0:T(8,128)(2,1)}, bf16[128,384]{1,0:T(8,128)(2,1)S(1)}, u32[]{:S(2)}, u32[]{:S(2)}) %collective-permute-start.10) | collective-permute-done | bytes 98336 | tf_op jit(solution)/shard_map/ppermute | solution.py:89
  79.3 3.6 %collective-permute-done.12.refs_9_ = bf16[256,384]{1,0:T(8,128)(2,1)S(1)} collective-permute-done((bf16[256,384]{1,0:T(8,128)(2,1)S(1)}, bf16[256,384]{1,0:T(8,128)(2,1)S(1)}, u32[]{:S(2)}, u32[]{:S(2)}) %collective-permute-start.12) | collective-permute-done | bytes 196640 | tf_op jit(solution)/shard_map/ppermute | solution.py:93
  91.3 2.0 %shard_map.83 = (bf16[512,128]{1,0:T(8,128)(2,1)S(1)}, bf16[256,256]{1,0:T(8,128)(2,1)}, bf16[256,256]{1,0:T(8,128)(2,1)}, bf16[1024,384]{1,0:T(8,128)(2,1)S(1)}) custom-call(s32[5]{0:T(128)S(1)} %stack.23.refs_0_, bf16[64,1024]{1,0:T(8,128)(2,1)S(1)} %get-tuple-element.43.refs_1_, bf16[64,1024]{1,0:T(8,128)(2,1)S(1)} %collective-permute-done.5.refs_2_, ...), custom_call_target="tpu_custom_call" | custom-call | tf_op jit(solution)/shard_map/pallas_call | solution.py:156
  95.7 2.0 %collective-permute-start.21 = (bf16[256,256]{1,0:T(8,128)(2,1)}, bf16[256,256]{1,0:T(8,128)(2,1)S(1)}, u32[]{:S(2)}, u32[]{:S(2)}) collective-permute-start(bf16[256,256]{1,0:T(8,128)(2,1)} %get-tuple-element.26.refs_4_), channel_id=1, source_target_pairs={{0,2},{1,3},{2,0},{3,1},{4,6},{5,7},{6,4},{7,5},{8,10},{9,11},{10,... | collective-permute-start | bytes 393224 | tf_op jit(solution)/shard_map/ppermute | solution.py:36
  99.2 3.5 %collective-permute-done.23.refs_8_ = bf16[256,256]{1,0:T(8,128)(2,1)S(1)} collective-permute-done((bf16[256,256]{1,0:T(8,128)(2,1)}, bf16[256,256]{1,0:T(8,128)(2,1)S(1)}, u32[]{:S(2)}, u32[]{:S(2)}) %collective-permute-start.23) | collective-permute-done | bytes 131104 | tf_op jit(solution)/shard_map/ppermute | solution.py:36
  105.3 2.0 %collective-permute-start.25 = (bf16[256,256]{1,0:T(8,128)(2,1)S(1)}, bf16[256,256]{1,0:T(8,128)(2,1)S(1)}, u32[]{:S(2)}, u32[]{:S(2)}) collective-permute-start(bf16[256,256]{1,0:T(8,128)(2,1)S(1)} %collective-permute-done.23.refs_8_), channel_id=1, source_target_pairs={{0,2},{1,3},{2,0},{3,1},{4,6},{5,7},{6,4},{7,5},{8,10},{9,11},{10,... | collective-permute-start | bytes 393224 | tf_op jit(solution)/shard_map/ppermute | solution.py:36
  108.6 2.8 %collective-permute-done.22.refs_7_ = bf16[256,256]{1,0:T(8,128)(2,1)S(1)} collective-permute-done((bf16[256,256]{1,0:T(8,128)(2,1)}, bf16[256,256]{1,0:T(8,128)(2,1)S(1)}, u32[]{:S(2)}, u32[]{:S(2)}) %collective-permute-start.22) | collective-permute-done | bytes 131104 | tf_op jit(solution)/shard_map/ppermute | solution.py:36
  112.8 6.8 %shard_map.85 = (bf16[512,128]{1,0:T(8,128)(2,1)S(1)}, bf16[256,256]{1,0:T(8,128)(2,1)S(1)}, bf16[256,256]{1,0:T(8,128)(2,1)S(1)}, bf16[256,256]{1,0:T(8,128)(2,...) custom-call(s32[5]{0:T(128)S(1)} %stack.23.refs_0_, ...), custom_call_target="tpu_custom_call" | custom-call | flops 1610612736 | bytes 2490368 | tf_op jit(solution)/shard_map/pallas_call | solution.py:255
  121.4 3.7 %collective-permute-start.26 = (bf16[256,256]{1,0:T(8,128)(2,1)S(1)}, bf16[256,256]{1,0:T(8,128)(2,1)S(1)}, u32[]{:S(2)}, u32[]{:S(2)}) collective-permute-start(bf16[256,256]{1,0:T(8,128)(2,1)S(1)} %get-tuple-element.31), channel_id=1, source_target_pairs={{16,0},{17,1},{18,2},{19,3},{20,4},{21,5},{22,6},{23,7},{24,8},{25... | collective-permute-start | bytes 393224 | tf_op jit(solution)/shard_map/ppermute | solution.py:36
  130.8 2.6 %collective-permute-done.27.refs_2_ = bf16[256,256]{1,0:T(8,128)(2,1)S(1)} collective-permute-done((bf16[256,256]{1,0:T(8,128)(2,1)S(1)}, bf16[256,256]{1,0:T(8,128)(2,1)S(1)}, u32[]{:S(2)}, u32[]{:S(2)}) %collective-permute-start.27) | collective-permute-done | bytes 131104 | tf_op jit(solution)/shard_map/ppermute | solution.py:36
  137.7 4.4 %collective-permute-done.33 = bf16[64,1024]{1,0:T(8,128)(2,1)S(1)} collective-permute-done((bf16[64,1024]{1,0:T(8,128)(2,1)S(1)}, bf16[64,1024]{1,0:T(8,128)(2,1)S(1)}, u32[]{:S(2)}, u32[]{:S(2)}) %collective-permute-start.33) | collective-permute-done | bytes 131104 | tf_op jit(solution)/shard_map/ppermute | solution.py:36
  142.3 3.5 %collective-permute-start.34 = (bf16[128,1024]{1,0:T(8,128)(2,1)S(1)}, bf16[128,1024]{1,0:T(8,128)(2,1)S(1)}, u32[]{:S(2)}, u32[]{:S(2)}) collective-permute-start(bf16[128,1024]{1,0:T(8,128)(2,1)S(1)} %fusion.6), channel_id=1, source_target_pairs={{0,12},{1,5},{2,14},{3,7},{4,0},{5,9},{6,2},{7,11},{8,4},{9,13},{1... | collective-permute-start | bytes 786440 | tf_op jit(solution)/shard_map/ppermute | solution.py:36
  145.7 6.7 %collective-permute-done.34 = bf16[128,1024]{1,0:T(8,128)(2,1)S(1)} collective-permute-done((bf16[128,1024]{1,0:T(8,128)(2,1)S(1)}, bf16[128,1024]{1,0:T(8,128)(2,1)S(1)}, u32[]{:S(2)}, u32[]{:S(2)}) %collective-permute-start.34) | collective-permute-done | bytes 262176 | tf_op jit(solution)/shard_map/ppermute | solution.py:36
  154.7 2.3 %collective-permute-start.36 = (bf16[64,1024]{1,0:T(8,128)(2,1)S(1)}, bf16[64,1024]{1,0:T(8,128)(2,1)S(1)}, u32[]{:S(2)}, u32[]{:S(2)}) collective-permute-start(bf16[64,1024]{1,0:T(8,128)(2,1)S(1)} %divide_convert_fusion), channel_id=1, source_target_pairs={{0,1},{1,2},{2,3},{3,4},{4,5},{5,6},{6,7},{7,8},{8,9},{9,10},{10,1... | collective-permute-start | bytes 393224 | tf_op jit(solution)/shard_map/ppermute | solution.py:41
  156.9 6.9 %collective-permute-start.37 = (bf16[64,1024]{1,0:T(8,128)(2,1)S(1)}, bf16[64,1024]{1,0:T(8,128)(2,1)S(1)}, u32[]{:S(2)}, u32[]{:S(2)}) collective-permute-start(bf16[64,1024]{1,0:T(8,128)(2,1)S(1)} %divide_convert_fusion), channel_id=1, source_target_pairs={{1,0},{2,1},{3,2},{4,3},{5,4},{6,5},{7,6},{8,7},{9,8},{10,9},{11,1... | collective-permute-start | bytes 393224 | tf_op jit(solution)/shard_map/ppermute | solution.py:41
  (145 shorter events, 56.1 us)
Async XLA Ops:
  6.5 91.2 %all-gather.3.cloned.1.call-start = ((), (), s32[]{:S(2)}) async-start(), calls=%async_computation | async-start | bytes 1179648 | tf_op jit(solution)/shard_map/all_gather | solution.py:101
  6.5 11.7 %collective-permute-start.1 = (s32[64]{0:T(128)}, s32[64]{0:T(128)S(1)}, u32[]{:S(2)}, u32[]{:S(2)}) collective-permute-start(s32[64]{0:T(128)} %bitcast.28), channel_id=1, source_target_pairs={{1,0},{2,1},{3,2},{4,3},{5,4},{6,5},{7,6},{8,7},{9,8},{10,9},{11,1... | collective-permute-start | bytes 776 | tf_op jit(solution)/shard_map/ppermute | solution.py:41
  14.7 8.6 %collective-permute-start = (s32[64]{0:T(128)}, s32[64]{0:T(128)S(1)}, u32[]{:S(2)}, u32[]{:S(2)}) collective-permute-start(s32[64]{0:T(128)} %bitcast.29), channel_id=1, source_target_pairs={{0,1},{1,2},{2,3},{3,4},{4,5},{5,6},{6,7},{7,8},{8,9},{9,10},{10,1... | collective-permute-start | bytes 776 | tf_op jit(solution)/shard_map/ppermute | solution.py:41
  26.7 9.9 %collective-permute-start.2 = (bf16[64,2048]{1,0:T(8,128)(2,1)S(1)}, bf16[64,2048]{1,0:T(8,128)(2,1)S(1)}, u32[]{:S(2)}, u32[]{:S(2)}) collective-permute-start(bf16[64,2048]{1,0:T(8,128)(2,1)S(1)} %pad_maximum_fusion), channel_id=1, source_target_pairs={{1,0},{2,1},{3,2},{4,3},{5,4},{6,5},{7,6},{8,7},{9,8},{10,9},{11,1... | collective-permute-start | bytes 786440 | tf_op jit(solution)/shard_map/ppermute | solution.py:41
  29.0 11.4 %collective-permute-start.3 = (bf16[64,2048]{1,0:T(8,128)(2,1)S(1)}, bf16[64,2048]{1,0:T(8,128)(2,1)S(1)}, u32[]{:S(2)}, u32[]{:S(2)}) collective-permute-start(bf16[64,2048]{1,0:T(8,128)(2,1)S(1)} %fusion.13), channel_id=1, source_target_pairs={{0,1},{1,2},{2,3},{3,4},{4,5},{5,6},{6,7},{7,8},{8,9},{9,10},{10,1... | collective-permute-start | bytes 786440 | tf_op jit(solution)/shard_map/ppermute | solution.py:41
  43.6 10.0 %collective-permute-start.6 = (bf16[128,1024]{1,0:T(8,128)(2,1)S(1)}, bf16[128,1024]{1,0:T(8,128)(2,1)S(1)}, u32[]{:S(2)}, u32[]{:S(2)}) collective-permute-start(bf16[128,1024]{1,0:T(8,128)(2,1)S(1)} %pad_maximum_fusion.1), channel_id=1, source_target_pairs={{0,4},{1,13},{2,6},{3,15},{4,8},{5,1},{6,10},{7,3},{8,12},{9,5},{1... | collective-permute-start | bytes 786440 | tf_op jit(solution)/shard_map/ppermute | solution.py:36
  53.6 10.1 %collective-permute-start.8 = (bf16[64,1024]{1,0:T(8,128)(2,1)S(1)}, bf16[64,1024]{1,0:T(8,128)(2,1)S(1)}, u32[]{:S(2)}, u32[]{:S(2)}) collective-permute-start(bf16[64,1024]{1,0:T(8,128)(2,1)S(1)} %slice.93), channel_id=1, source_target_pairs={{0,4},{1,13},{2,6},{3,15},{4,8},{5,1},{6,10},{7,3},{8,12},{9,5},{1... | collective-permute-start | bytes 393224 | tf_op jit(solution)/shard_map/ppermute | solution.py:36
  65.2 11.5 %collective-permute-start.15 = (bf16[128,1024]{1,0:T(8,128)(2,1)S(1)}, bf16[128,1024]{1,0:T(8,128)(2,1)S(1)}, u32[]{:S(2)}, u32[]{:S(2)}) collective-permute-start(bf16[128,1024]{1,0:T(8,128)(2,1)S(1)} %pad_maximum_fusion.2), channel_id=1, source_target_pairs={{0,4},{1,13},{2,6},{3,15},{4,8},{5,1},{6,10},{7,3},{8,12},{9,5},{1... | collective-permute-start | bytes 786440 | tf_op jit(solution)/shard_map/ppermute | solution.py:36
  71.5 7.8 %collective-permute-start.11 = (bf16[256,384]{1,0:T(8,128)(2,1)S(1)}, bf16[256,384]{1,0:T(8,128)(2,1)S(1)}, u32[]{:S(2)}, u32[]{:S(2)}) collective-permute-start(bf16[256,384]{1,0:T(8,128)(2,1)S(1)} %pad_maximum_fusion.3.refs_7_), channel_id=1, source_target_pairs={{0,32},{32,64},{64,96},{96,0},{128,160},{160,192},{192,224},{224,1... | collective-permute-start | bytes 589832 | tf_op jit(solution)/shard_map/ppermute | solution.py:93
  73.0 9.9 %collective-permute-start.12 = (bf16[256,384]{1,0:T(8,128)(2,1)S(1)}, bf16[256,384]{1,0:T(8,128)(2,1)S(1)}, u32[]{:S(2)}, u32[]{:S(2)}) collective-permute-start(bf16[256,384]{1,0:T(8,128)(2,1)S(1)} %pad_maximum_fusion.3.refs_7_), channel_id=1, source_target_pairs={{0,96},{32,0},{64,32},{96,64},{128,224},{160,128},{192,160},{224,1... | collective-permute-start | bytes 589832 | tf_op jit(solution)/shard_map/ppermute | solution.py:93
  74.8 11.2 %collective-permute-start.7 = (bf16[128,1024]{1,0:T(8,128)(2,1)S(1)}, bf16[128,1024]{1,0:T(8,128)(2,1)S(1)}, u32[]{:S(2)}, u32[]{:S(2)}) collective-permute-start(bf16[128,1024]{1,0:T(8,128)(2,1)S(1)} %collective-permute-done.6.refs_3_), channel_id=1, source_target_pairs={{0,1},{1,0},{2,3},{3,2},{4,5},{5,4},{6,7},{7,6},{8,9},{9,8},{10,11... | collective-permute-start | bytes 786440 | tf_op jit(solution)/shard_map/ppermute | solution.py:36
  74.8 9.9 %collective-permute-start.13 = (bf16[256,384]{1,0:T(8,128)(2,1)S(1)}, bf16[256,384]{1,0:T(8,128)(2,1)S(1)}, u32[]{:S(2)}, u32[]{:S(2)}) collective-permute-start(bf16[256,384]{1,0:T(8,128)(2,1)S(1)} %pad_maximum_fusion.3.refs_7_), channel_id=1, source_target_pairs={{0,64},{32,96},{64,0},{96,32},{128,192},{160,224},{192,128},{224,1... | collective-permute-start | bytes 589832 | tf_op jit(solution)/shard_map/ppermute | solution.py:93
  76.7 8.7 %collective-permute-start.9 = (bf16[64,1024]{1,0:T(8,128)(2,1)S(1)}, bf16[64,1024]{1,0:T(8,128)(2,1)S(1)}, u32[]{:S(2)}, u32[]{:S(2)}) collective-permute-start(bf16[64,1024]{1,0:T(8,128)(2,1)S(1)} %collective-permute-done.8.refs_5_), channel_id=1, source_target_pairs={{0,1},{1,0},{2,3},{3,2},{4,5},{5,4},{6,7},{7,6},{8,9},{9,8},{10,11... | collective-permute-start | bytes 393224 | tf_op jit(solution)/shard_map/ppermute | solution.py:36
  79.3 16.1 %collective-permute-start.17 = (bf16[64,1024]{1,0:T(8,128)(2,1)}, bf16[64,1024]{1,0:T(8,128)(2,1)}, u32[]{:S(2)}, u32[]{:S(2)}) collective-permute-start(bf16[64,1024]{1,0:T(8,128)(2,1)} %slice.94), channel_id=1, source_target_pairs={{0,4},{1,13},{2,6},{3,15},{4,8},{5,1},{6,10},{7,3},{8,12},{9,5},{1... | collective-permute-start | bytes 393224 | tf_op jit(solution)/shard_map/ppermute | solution.py:36
  83.6 21.7 %collective-permute-start.16 = (bf16[128,1024]{1,0:T(8,128)(2,1)S(1)}, bf16[128,1024]{1,0:T(8,128)(2,1)S(1)}, u32[]{:S(2)}, u32[]{:S(2)}) collective-permute-start(bf16[128,1024]{1,0:T(8,128)(2,1)S(1)} %collective-permute-done.15.refs_3_), channel_id=1, source_target_pairs={{0,1},{1,0},{2,3},{3,2},{4,5},{5,4},{6,7},{7,6},{8,9},{9,8},{10,11... | collective-permute-start | bytes 786440 | tf_op jit(solution)/shard_map/ppermute | solution.py:36
  94.0 8.7 %collective-permute-start.23 = (bf16[256,256]{1,0:T(8,128)(2,1)}, bf16[256,256]{1,0:T(8,128)(2,1)S(1)}, u32[]{:S(2)}, u32[]{:S(2)}) collective-permute-start(bf16[256,256]{1,0:T(8,128)(2,1)} %get-tuple-element.26.refs_4_), channel_id=1, source_target_pairs={{0,16},{1,17},{2,18},{3,19},{4,20},{5,21},{6,22},{7,23},{8,24},{9,... | collective-permute-start | bytes 393224 | tf_op jit(solution)/shard_map/ppermute | solution.py:36
  95.4 8.6 %collective-permute-start.18 = (bf16[64,1024]{1,0:T(8,128)(2,1)}, bf16[64,1024]{1,0:T(8,128)(2,1)S(1)}, u32[]{:S(2)}, u32[]{:S(2)}) collective-permute-start(bf16[64,1024]{1,0:T(8,128)(2,1)} %collective-permute-done.17.refs_5_), channel_id=1, source_target_pairs={{0,1},{1,0},{2,3},{3,2},{4,5},{5,4},{6,7},{7,6},{8,9},{9,8},{10,11... | collective-permute-start | bytes 393224 | tf_op jit(solution)/shard_map/ppermute | solution.py:36
  95.7 12.9 %collective-permute-start.21 = (bf16[256,256]{1,0:T(8,128)(2,1)}, bf16[256,256]{1,0:T(8,128)(2,1)S(1)}, u32[]{:S(2)}, u32[]{:S(2)}) collective-permute-start(bf16[256,256]{1,0:T(8,128)(2,1)} %get-tuple-element.26.refs_4_), channel_id=1, source_target_pairs={{0,2},{1,3},{2,0},{3,1},{4,6},{5,7},{6,4},{7,5},{8,10},{9,11},{10,... | collective-permute-start | bytes 393224 | tf_op jit(solution)/shard_map/ppermute | solution.py:36
  99.1 8.1 %collective-permute-start.19 = (bf16[64,1024]{1,0:T(8,128)(2,1)S(1)}, bf16[64,1024]{1,0:T(8,128)(2,1)S(1)}, u32[]{:S(2)}, u32[]{:S(2)}) collective-permute-start(bf16[64,1024]{1,0:T(8,128)(2,1)S(1)} %get-tuple-element.45), channel_id=1, source_target_pairs={{0,1},{1,0},{2,3},{3,2},{4,5},{5,4},{6,7},{7,6},{8,9},{9,8},{10,11... | collective-permute-start | bytes 393224 | tf_op jit(solution)/shard_map/ppermute | solution.py:36
  102.7 8.7 %collective-permute-start.22 = (bf16[256,256]{1,0:T(8,128)(2,1)}, bf16[256,256]{1,0:T(8,128)(2,1)S(1)}, u32[]{:S(2)}, u32[]{:S(2)}) collective-permute-start(bf16[256,256]{1,0:T(8,128)(2,1)} %get-tuple-element.25.refs_3_), channel_id=1, source_target_pairs={{0,16},{1,17},{2,18},{3,19},{4,20},{5,21},{6,22},{7,23},{8,24},{9,... | collective-permute-start | bytes 393224 | tf_op jit(solution)/shard_map/ppermute | solution.py:36
  104.0 8.8 %collective-permute-start.24 = (bf16[256,256]{1,0:T(8,128)(2,1)S(1)}, bf16[256,256]{1,0:T(8,128)(2,1)S(1)}, u32[]{:S(2)}, u32[]{:S(2)}) collective-permute-start(bf16[256,256]{1,0:T(8,128)(2,1)S(1)} %collective-permute-done.20.refs_5_), channel_id=1, source_target_pairs={{0,16},{1,17},{2,18},{3,19},{4,20},{5,21},{6,22},{7,23},{8,24},{9,... | collective-permute-start | bytes 393224 | tf_op jit(solution)/shard_map/ppermute | solution.py:36
  142.3 10.2 %collective-permute-start.34 = (bf16[128,1024]{1,0:T(8,128)(2,1)S(1)}, bf16[128,1024]{1,0:T(8,128)(2,1)S(1)}, u32[]{:S(2)}, u32[]{:S(2)}) collective-permute-start(bf16[128,1024]{1,0:T(8,128)(2,1)S(1)} %fusion.6), channel_id=1, source_target_pairs={{0,12},{1,5},{2,14},{3,7},{4,0},{5,9},{6,2},{7,11},{8,4},{9,13},{1... | collective-permute-start | bytes 786440 | tf_op jit(solution)/shard_map/ppermute | solution.py:36
  154.7 9.9 %collective-permute-start.36 = (bf16[64,1024]{1,0:T(8,128)(2,1)S(1)}, bf16[64,1024]{1,0:T(8,128)(2,1)S(1)}, u32[]{:S(2)}, u32[]{:S(2)}) collective-permute-start(bf16[64,1024]{1,0:T(8,128)(2,1)S(1)} %divide_convert_fusion), channel_id=1, source_target_pairs={{0,1},{1,2},{2,3},{3,4},{4,5},{5,6},{6,7},{7,8},{8,9},{9,10},{10,1... | collective-permute-start | bytes 393224 | tf_op jit(solution)/shard_map/ppermute | solution.py:41
  156.9 9.4 %collective-permute-start.37 = (bf16[64,1024]{1,0:T(8,128)(2,1)S(1)}, bf16[64,1024]{1,0:T(8,128)(2,1)S(1)}, u32[]{:S(2)}, u32[]{:S(2)}) collective-permute-start(bf16[64,1024]{1,0:T(8,128)(2,1)S(1)} %divide_convert_fusion), channel_id=1, source_target_pairs={{1,0},{2,1},{3,2},{4,3},{5,4},{6,5},{7,6},{8,7},{9,8},{10,9},{11,1... | collective-permute-start | bytes 393224 | tf_op jit(solution)/shard_map/ppermute | solution.py:41
  (37 other events, 189.2 us)
Sparse Core Ops, SparseCore 0:
  18.4 39.7 all-gather.2

commit v3 on v2

--- a/solution.py
+++ b/solution.py
@@ -17,6 +17,7 @@
 F32 = jnp.float32
 VMEM = pl.BlockSpec(memory_space=pltpu.VMEM)
 SMEM = pl.BlockSpec(memory_space=pltpu.SMEM)
+ANY = pl.BlockSpec(memory_space=pl.ANY)
 PARAMS = pltpu.CompilerParams(vmem_limit_bytes=48 * 1024 * 1024)
 
 
@@ -36,9 +37,13 @@
     return lax.ppermute(value, "ctx", pairs)
 
 
-def along(value, steps):
-    pairs = [(i, i + steps) for i in range(CTX) if 0 <= i + steps < CTX]
+def other_chip(value):
+    pairs = [(i, i + 1 if i % CORES else i - 1) for i in range(1, CTX - 1)]
     return lax.ppermute(value, "ctx", pairs)
+
+
+def two_back(value):
+    return lax.ppermute(value, "ctx", [(i, i - CORES) for i in range(CORES, CTX)])
 
 
 def other_core(value):
@@ -74,7 +79,7 @@
 def columns_in(w_query, w_key, w_value, head):
     rows = w_query.shape[0]
     block = pl.BlockSpec((rows, HEAD), lambda i, h: (0, h[0]))
-    mine = pl.pallas_call(
+    return pl.pallas_call(
         cut_kernel,
         grid_spec=pltpu.PrefetchScalarGridSpec(
             num_scalar_prefetch=1,
@@ -84,15 +89,16 @@
         ),
         out_shape=jax.ShapeDtypeStruct((rows, 3 * HEAD), w_query.dtype),
     )(head[None], w_query, w_key, w_value)
+
+
+def other_x(value):
     count = ROWS_X * ROWS_Y
-    swap = [(d, (d + ROWS_Y) % count) for d in range(count)]
-    both = jnp.concatenate([mine, lax.ppermute(mine, "dp", swap)], axis=0)
-
-    def shifted(step):
-        pairs = [(d, d // ROWS_Y * ROWS_Y + (d + step) % ROWS_Y) for d in range(count)]
-        return lax.ppermute(both, "dp", pairs)
-
-    return [both, shifted(1), shifted(-1), shifted(2)]
+    return lax.ppermute(value, "dp", [(d, (d + ROWS_Y) % count) for d in range(count)])
+
+
+def shifted_y(value, step):
+    pairs = [(d, d // ROWS_Y * ROWS_Y + (d + step) % ROWS_Y) for d in range(ROWS_X * ROWS_Y)]
+    return lax.ppermute(value, "dp", pairs)
 
 
 def rows_out(w_out, turn, core):
@@ -106,9 +112,19 @@
 
 def gathered_rows(shard):
     swapped = other_core(shard)
-    near = turned(jnp.concatenate([shard, swapped], axis=0), 1)
-    far = turned(near[: shard.shape[0]], 1)
-    return [shard, swapped, near, other_core(near), far, other_core(far)]
+    near = turned(shard, 1)
+    far = turned(near, 1)
+    next_to = turned(swapped, 1)
+    return [
+        shard,
+        swapped,
+        near,
+        next_to,
+        other_core(near),
+        other_core(next_to),
+        far,
+        other_core(far),
+    ]
 
 
 def rows_at(row, half, turn, pair, core, seg):
@@ -122,17 +138,127 @@
     return place(half, its_turn, pair, its_core) * seg + row % seg
 
 
-def fill(out_ref, pieces):
-    at = 0
+def fetched(copies, sems):
+    started = []
+    for i, (source, target) in enumerate(copies):
+        started.append(pltpu.make_async_copy(source, target, sems.at[i]))
+        started[-1].start()
+    for copy in started:
+        copy.wait()
+
+
+def stacked(pieces, out_ref):
+    copies, at = [], 0
     for piece in pieces:
-        out_ref[at : at + piece.shape[0], :] = piece[...]
+        copies.append((piece, out_ref.at[at : at + piece.shape[0], :]))
         at += piece.shape[0]
+    return copies
+
+
+def window_kernel(place_ref, edge_ref, token_ref, grad_ref, mine_ref, theirs_ref, *outs):
+    core_ref, chip_ref, mid_token, mid_grad, first_ref, both_ref = outs
+    rows, width = token_ref.shape
+    seg = mid_token.shape[0]
+    ctx, core = place_ref[5], place_ref[3]
+    at = lax.broadcasted_iota(jnp.int32, (1, rows), 1) + ctx * rows
+    opens, ends, nexts = edge_ref[0], edge_ref[1], edge_ref[2]
+    member = ((opens <= at) & (at < ends)).astype(jnp.bfloat16)
+    earlier = ((ends <= at) & (at < nexts)).astype(jnp.bfloat16)
+    token = jnp.dot(member, token_ref[...], preferred_element_type=F32)
+    grad = jnp.dot(earlier, grad_ref[...], preferred_element_type=F32)
+    first = jnp.dot(member[:16], grad_ref[...], preferred_element_type=F32)
+    first_ref[...] = first[:1]
+    mid_token[...] = token[seg : 2 * seg]
+    mid_grad[...] = grad[seg : 2 * seg]
+    both_ref[: mine_ref.shape[0], :] = mine_ref[...]
+    both_ref[mine_ref.shape[0] :, :] = theirs_ref[...]
+
+    def send(lower_ref, upper_ref):
+        lower_ref[:, :width] = token[:seg].astype(WIRE)
+        lower_ref[:, width:] = grad[:seg].astype(WIRE)
+        upper_ref[:, :width] = token[2 * seg :].astype(WIRE)
+        upper_ref[:, width:] = grad[2 * seg :].astype(WIRE)
+
+    @pl.when(core == 0)
+    def _():
+        send(chip_ref, core_ref)
+
+    @pl.when(core == 1)
+    def _():
+        send(core_ref, chip_ref)
+
+
+def window_sums(where, edges, tokens, grads, mine, theirs, seg):
+    width = tokens.shape[1]
+    shape = jax.ShapeDtypeStruct
+    return pl.pallas_call(
+        window_kernel,
+        out_shape=(
+            shape((seg, 2 * width), WIRE),
+            shape((seg, 2 * width), WIRE),
+            shape((seg, width), F32),
+            shape((seg, width), F32),
+            shape((1, width), F32),
+            shape((2 * mine.shape[0], mine.shape[1]), mine.dtype),
+        ),
+        in_specs=[SMEM] + [VMEM] * 5,
+        out_specs=(VMEM,) * 6,
+        compiler_params=PARAMS,
+    )(where, edges, tokens, grads, mine, theirs)
+
+
+def norm_kernel(core_ref, chip_ref, mid_token, mid_grad, count_ref, gain_ref, *refs):
+    normin_ref, normed_ref, rms_ref, dout_ref = refs[-4:]
+    width = mid_token.shape[1]
+    got = core_ref[...].astype(F32) + chip_ref[...].astype(F32)
+    pooled = (mid_token[...] + got[:, :width]) / count_ref[...]
+    rms = jnp.sqrt(jnp.mean(pooled * pooled, axis=1, keepdims=True) + 1e-06)
+    normed = pooled / rms
+    normed_ref[...] = normed
+    rms_ref[...] = rms
+    normin_ref[...] = (normed * gain_ref[...]).astype(jnp.bfloat16)
+    dout_ref[...] = mid_grad[...] + got[:, width:]
+
+
+def norm(from_core, from_chip, mid_token, mid_grad, count, gain, ready):
+    seg, width = mid_token.shape
+    shape = jax.ShapeDtypeStruct
+    return pl.pallas_call(
+        norm_kernel,
+        out_shape=(
+            shape((seg, width), jnp.bfloat16),
+            shape((seg, width), F32),
+            shape((seg, 1), F32),
+            shape((seg, width), F32),
+        ),
+        in_specs=[VMEM] * 6 + [ANY] * len(ready),
+        out_specs=(VMEM,) * 4,
+        compiler_params=PARAMS,
+    )(from_core, from_chip, mid_token, mid_grad, count, gain, *ready)
+
+
+def dout_kernel(dout_ref, second_ref, ready_ref, full_ref, half_ref):
+    seg = dout_ref.shape[0]
+    last = lax.broadcasted_iota(jnp.int32, (seg, 1), 0) == seg - 1
+    dout = dout_ref[...] + jnp.where(last, second_ref[...].astype(F32), 0.0)
+    full_ref[...] = dout
+    half_ref[...] = dout.astype(jnp.bfloat16)
+
+
+def whole_dout(dout, second, ready):
+    shape = jax.ShapeDtypeStruct
+    return pl.pallas_call(
+        dout_kernel,
+        out_shape=(shape(dout.shape, F32), shape(dout.shape, jnp.bfloat16)),
+        in_specs=[VMEM, VMEM, ANY],
+        out_specs=(VMEM, VMEM),
+    )(dout, second, ready)
 
 
 def project_kernel(*refs):
-    place_ref, pieces, weights = refs[0], refs[1:7], refs[7:11]
-    q_ref, top_ref, bottom_ref, w_ref, rows = refs[11:]
-    fill(rows, pieces)
+    place_ref, pieces, weights = refs[0], refs[1:9], refs[9:13]
+    q_ref, top_ref, bottom_ref, w_ref, rows, sems = refs[13:]
+    copies = stacked(pieces, rows)
     dp = place_ref[4]
     x, y = dp // ROWS_Y, dp % ROWS_Y
     depth = weights[0].shape[0] // ROWS_X
@@ -141,7 +267,8 @@
         for i in range(ROWS_X):
             its_x = x if i == 0 else 1 - x
             at = pl.multiple_of((its_x * ROWS_Y + its_y) * depth, depth)
-            w_ref[pl.ds(at, depth), :] = weight[i * depth : (i + 1) * depth, :]
+            copies.append((weight.at[i * depth : (i + 1) * depth, :], w_ref.at[pl.ds(at, depth), :]))
+    fetched(copies, sems)
     out = jnp.dot(rows[...], w_ref[...], preferred_element_type=F32).astype(jnp.bfloat16)
     cut = out.shape[0] // 2
     q_ref[...] = out[:, :HEAD]
@@ -161,28 +288,27 @@
             bf16(rows // 2, 2 * HEAD),
             bf16(width, 3 * HEAD),
         ),
-        in_specs=[SMEM] + [VMEM] * 10,
+        in_specs=[SMEM] + [ANY] * 12,
         out_specs=(VMEM,) * 4,
-        scratch_shapes=[pltpu.VMEM((rows, width), jnp.bfloat16)],
+        scratch_shapes=[
+            pltpu.VMEM((rows, width), jnp.bfloat16),
+            pltpu.SemaphoreType.DMA((16,)),
+        ],
         compiler_params=PARAMS,
     )(where, *pieces, *weights)
 
 
 def dattended_kernel(*refs):
-    place_ref, pieces, mine, theirs, da_ref, rows, weight = (
-        refs[0],
-        refs[1:7],
-        refs[7],
-        refs[8],
-        refs[9],
-        refs[10],
-        refs[11],
-    )
+    place_ref, pieces, mine, theirs = refs[0], refs[1:9], refs[9], refs[10]
+    da_ref, rows, weight, sems = refs[11:]
     core = place_ref[3]
     half = mine.shape[0]
-    fill(rows, pieces)
-    weight[pl.ds(pl.multiple_of(core * half, half), half), :] = mine[...]
-    weight[pl.ds(pl.multiple_of((1 - core) * half, half), half), :] = theirs[...]
+    spot = pl.multiple_of(core * half, half)
+    other = pl.multiple_of((1 - core) * half, half)
+    copies = stacked(pieces, rows)
+    copies.append((mine, weight.at[pl.ds(spot, half), :]))
+    copies.append((theirs, weight.at[pl.ds(other, half), :]))
+    fetched(copies, sems)
     da_ref[...] = contract_last(rows[...], weight[...]).astype(jnp.bfloat16)
 
 
@@ -192,11 +318,12 @@
     return pl.pallas_call(
         dattended_kernel,
         out_shape=jax.ShapeDtypeStruct((rows, HEAD), jnp.bfloat16),
-        in_specs=[SMEM] + [VMEM] * 8,
+        in_specs=[SMEM] + [ANY] * 10,
         out_specs=VMEM,
         scratch_shapes=[
             pltpu.VMEM((rows, width), jnp.bfloat16),
             pltpu.VMEM((HEAD, width), jnp.bfloat16),
+            pltpu.SemaphoreType.DMA((10,)),
         ],
         compiler_params=PARAMS,
     )(where, *pieces, mine, theirs)
@@ -204,10 +331,10 @@
 
 def attention_kernel(tile, seg, *refs):
     place_ref, q_ref, da_ref, blocks = refs[0], refs[1], refs[2], refs[3:11]
-    dq_ref, outs, kv, dkt, dvt = refs[11], refs[12:20], refs[20], refs[21], refs[22]
+    dq_ref, outs, (kv, dkt, dvt, sems) = refs[11], refs[12:20], refs[20:]
     half, turn, pair, core = place_ref[0], place_ref[1], place_ref[2], place_ref[3]
     queries, keys = q_ref.shape[0], kv.shape[0]
-    fill(kv, blocks)
+    fetched(stacked(blocks, kv), sems)
     spot = lax.broadcasted_iota(jnp.int32, (1, keys), 1)
     block = spot // queries
     key_half = jnp.where(block < 2, half, 1 - half)
@@ -255,12 +382,13 @@
     return pl.pallas_call(
         functools.partial(attention_kernel, 128, seg),
         out_shape=(jax.ShapeDtypeStruct((queries, HEAD), jnp.bfloat16),) + (part,) * 8,
-        in_specs=[SMEM] + [VMEM] * 10,
+        in_specs=[SMEM] + [VMEM] * 2 + [ANY] * 8,
         out_specs=(VMEM,) * 9,
         scratch_shapes=[
             pltpu.VMEM((keys, 2 * HEAD), jnp.bfloat16),
             pltpu.VMEM((HEAD, keys), F32),
             pltpu.VMEM((HEAD, keys), F32),
+            pltpu.SemaphoreType.DMA((8,)),
         ],
         compiler_params=PARAMS,
         cost_estimate=pl.CostEstimate(
@@ -272,42 +400,37 @@
 
 
 def unproject_kernel(seg, dq_ref, *refs):
-    dkv_parts, w_ref = refs[:6], refs[6]
-    swap_ref, far_ref, near_ref, own_ref = refs[7:11]
+    dkv_parts, w_ref, swap_ref, outs = refs[:6], refs[6], refs[7], refs[8:]
     top = sum(ref[...].astype(F32) for ref in dkv_parts[0::2])
     bottom = sum(ref[...].astype(F32) for ref in dkv_parts[1::2])
     dkv = jnp.concatenate([top, bottom], axis=0).astype(jnp.bfloat16)
     left = jnp.concatenate([dq_ref[...], dkv], axis=1)
     out = contract_last(left, w_ref[...])
-    own_ref[...] = out[: 2 * seg]
-    near_ref[...] = out[2 * seg : 4 * seg]
     swap_ref[: 2 * seg, :] = out[4 * seg : 6 * seg].astype(WIRE)
-    far_ref[...] = out[6 * seg : 7 * seg]
     swap_ref[2 * seg :, :] = out[7 * seg :].astype(WIRE)
+    for ref, slot in zip(outs, (0, 1, 2, 3, 6)):
+        ref[...] = out[slot * seg : (slot + 1) * seg]
 
 
 def unproject(dq, dkv_parts, w_full, seg):
     width = w_full.shape[0]
     return pl.pallas_call(
         functools.partial(unproject_kernel, seg),
-        out_shape=(
-            jax.ShapeDtypeStruct((3 * seg, width), WIRE),
-            jax.ShapeDtypeStruct((seg, width), F32),
-            jax.ShapeDtypeStruct((2 * seg, width), F32),
-            jax.ShapeDtypeStruct((2 * seg, width), F32),
-        ),
+        out_shape=(jax.ShapeDtypeStruct((3 * seg, width), WIRE),)
+        + (jax.ShapeDtypeStruct((seg, width), F32),) * 5,
         in_specs=[VMEM] * 8,
-        out_specs=(VMEM,) * 4,
+        out_specs=(VMEM,) * 6,
         compiler_params=PARAMS,
     )(dq, *dkv_parts, w_full)
 
 
-def summed_rows(swap, far, near, own, seg):
+def summed_rows(swap, own, beside, near, next_to, far, seg):
     swapped = other_core(swap).astype(F32)
-    back = turned((far + swapped[2 * seg :]).astype(WIRE), -1).astype(F32)
-    near = near + swapped[: 2 * seg] + jnp.pad(back, ((0, seg), (0, 0)))
-    own = own + turned(near.astype(WIRE), -1).astype(F32)
-    return own[:seg] + other_core(own[seg:].astype(WIRE)).astype(F32)
+    far = turned((far + swapped[2 * seg :]).astype(WIRE), -1).astype(F32)
+    next_to = turned((next_to + swapped[seg : 2 * seg]).astype(WIRE), -1).astype(F32)
+    near = turned((near + swapped[:seg] + far).astype(WIRE), -1).astype(F32)
+    beside = other_core((beside + next_to).astype(WIRE)).astype(F32)
+    return own + near + beside
 
 
 def per_device(tokens, starts, gain, w_query, w_key, w_value, w_out, cotangent):
@@ -320,39 +443,39 @@
     ctx = lax.axis_index("ctx")
     core, pair = ctx % CORES, ctx // CORES % PAIR
     turn, half = ctx // (CORES * PAIR) % TURNS, ctx // (CORES * PAIR * TURNS)
-    where = jnp.stack([half, turn, pair, core, lax.axis_index("dp")])
-
-    before = jnp.where(ctx == 0, -1, along(own_starts, 1))
-    after = jnp.where(ctx == CTX - 1, length, along(own_starts, -1))
-    weights = columns_in(w_query, w_key, w_value, turn * CORES + core)
-    out_mine, out_theirs = rows_out(w_out, turn, core)
-    window = jnp.concatenate([before, own_starts, after])
-    positions = ctx * rows + lax.iota(jnp.int32, rows)
-    ends = jnp.concatenate([window[1:], jnp.full((1,), length, jnp.int32)])
-    member = (
-        (window[None, :] <= positions[:, None]) & (positions[:, None] < ends[None, :])
-    ).astype(jnp.bfloat16)
-    token_sum = contract_first(member, token_rows)
-    grad_sum = contract_first(member, grad_out)
-    lower = jnp.concatenate([token_sum[:seg], grad_sum[1 : seg + 1]], axis=1).astype(WIRE)
-    tail = jnp.concatenate([grad_sum[2 * seg + 1 :], jnp.zeros((1, width), F32)], axis=0)
-    upper = jnp.concatenate([token_sum[2 * seg :], tail], axis=1).astype(WIRE)
-    from_after = along(lower, -1).astype(F32)
-    from_before = along(upper, 1).astype(F32)
-    from_second = along(grad_sum[:1].astype(WIRE), -2).astype(F32)
-    count = (ends - window)[seg : 2 * seg].astype(F32)
-    pooled = token_sum[seg : 2 * seg] + from_after[:, :width] + from_before[:, :width]
-    pooled = pooled / count[:, None]
-    last = lax.broadcasted_iota(jnp.int32, (seg, 1), 0) == seg - 1
-    dout = grad_sum[seg + 1 : 2 * seg + 1] + from_after[:, width:] + from_before[:, width:]
-    dout = dout + jnp.where(last, from_second, 0.0)
-    rms = jnp.sqrt(jnp.mean(pooled * pooled, axis=-1, keepdims=True) + 1e-06)
-    normed = pooled / rms
-    normin = (normed * gain).astype(jnp.bfloat16)
-
+    where = jnp.stack([half, turn, pair, core, lax.axis_index("dp"), ctx])
+
+    mine = columns_in(w_query, w_key, w_value, turn * CORES + core)
+    theirs = other_x(mine)
+    beside, facing = other_core(own_starts), other_chip(own_starts)
+    before = jnp.where(core == 0, facing, beside)
+    after = jnp.where(core == 0, beside, facing)
+    before = jnp.where(ctx == 0, -1, before)
+    after = jnp.where(ctx == CTX - 1, length, after)
+    stop = jnp.full((2,), length, jnp.int32)
+    window = jnp.concatenate([before, own_starts, after, stop])
+    slots = 3 * seg
+    opens, ends = window[:slots], window[1 : slots + 1]
+    edges = jnp.stack([opens, ends, window[2:]])[:, :, None]
+    count = (ends - opens)[seg : 2 * seg, None].astype(F32)
+    to_core, to_chip, mid_token, mid_grad, first, both = window_sums(
+        where, edges, token_rows, grad_out, mine, theirs, seg
+    )
+    weights = [both, shifted_y(both, 1), shifted_y(both, -1), shifted_y(both, 2)]
+    second = two_back(first)
+    normin, normed, rms, dout = norm(
+        other_core(to_core),
+        other_chip(to_chip),
+        mid_token,
+        mid_grad,
+        count,
+        gain[None],
+        weights[1:],
+    )
     pieces = gathered_rows(normin)
     q, own_top, own_bottom, w_full = project(where, pieces, weights)
-    dout_b, _ = lax.optimization_barrier((dout.astype(jnp.bfloat16), pieces[4]))
+    dout, dout_b = whole_dout(dout, second, pieces[6])
+    out_mine, out_theirs = rows_out(w_out, turn, core)
     da = dattended(where, gathered_rows(dout_b), out_mine, out_theirs)
     pair_top, far_bottom = other_pair(own_top), across(own_bottom, 0)
     pair_bottom, far_top = other_pair(own_bottom), across(own_top, 0)
@@ -379,9 +502,14 @@
 
     scaled = dnormin * gain
     dpooled = dout + (scaled - normed * jnp.mean(scaled * normed, axis=-1, keepdims=True)) / rms
-    per_seg = (dpooled / count[:, None]).astype(WIRE)
-    per_window = jnp.concatenate([along(per_seg, 1), per_seg, along(per_seg, -1)], axis=0)
-    spread = jnp.dot(member, per_window, preferred_element_type=F32)
+    per_seg = (dpooled / count).astype(WIRE)
+    beside, facing = other_core(per_seg), other_chip(per_seg)
+    before = jnp.where(core == 0, facing, beside)
+    after = jnp.where(core == 0, beside, facing)
+    per_window = jnp.concatenate([before, per_seg, after], axis=0)
+    positions = (ctx * rows + lax.iota(jnp.int32, rows))[:, None]
+    member = (opens[None] <= positions) & (positions < ends[None])
+    spread = jnp.dot(member.astype(WIRE), per_window, preferred_element_type=F32)
     return (grad_out.astype(F32) + spread).astype(jnp.bfloat16)[None]
 
 

time: 177 us -> 168 us (0.949)
  waiting for transfers between devices: 72.6 us -> 55.5 us
  starting transfers between devices: 56.2 us -> 66.1 us
  Pallas kernels: 12.4 us -> 20.3 us
  local copies, waits for them, and re-layouts: 11.5 us -> 7.94 us
  other arithmetic: 4.25 us -> 0.95 us
  matrix products: 3.81 us -> 1.45 us
    ppermute x27 -> x35, waiting for transfers between devices: 46.4 us -> 36.7 us  [moved(): return lax.ppermute(value, 'ctx', pairs)]
    ppermute x27 -> x35, starting transfers between devices: 25.3 us -> 34.7 us  [moved(): return lax.ppermute(value, 'ctx', pairs)]
    ppermute x11 -> x8, waiting for transfers between devices: 26.2 us -> 18.8 us  [the longest x3 11.2 us: shifted_y(): return lax.ppermute(value, 'dp', pairs)]
    pallas_call x0 -> x3, Pallas kernels: none -> 3.3 us  [the longest x1 1.73 us: whole_dout(): pl.pallas_call(dout_kernel, out_shape=(shape(dout.shape, F32), shape(dout...]
    pallas_call x1, Pallas kernels: 1.98 us -> 4.61 us  [project(): pl.pallas_call(project_kernel, out_shape=(bf16(rows, HEAD), bf16(rows //...]
    dot_general x3 -> x1, matrix products: 3.81 us -> 1.45 us  [per_device(): jnp.dot(member.astype(WIRE), per_window, preferred_element_type=F32)]
    unnamed x44 -> x30, local copies, waits for them, and re-layouts: 8 us -> 5.95 us
    ppermute x11 -> x8, starting transfers between devices: 30.9 us -> 31.5 us  [the longest x3 21.1 us: other_chip(): return lax.ppermute(value, 'ctx', pairs)]
  transfers between devices with their start and end apart: 39 -> 44, of which waited for: 22 -> 20; matrix products, arithmetic and copies ran while one was open for 5% -> 1% of each run, Pallas kernels for 3% -> 7%
where the time goes in v3:
time: 168 us; the launch traced here: 166 us
  starting transfers between devices  66.1 us (39%)
  waiting for transfers between devices  55.5 us (33%)
  Pallas kernels  20.3 us (12%)
  between operations  13.9 us (8%)
  local copies, waits for them, and re-layouts  7.94 us (5%)
    ppermute x35, waiting for transfers between devices, moved(): return lax.ppermute(value, 'ctx', pairs)  36.7 us
    ppermute x35, starting transfers between devices, moved(): return lax.ppermute(value, 'ctx', pairs)  34.7 us
    ppermute x3, starting transfers between devices, other_chip(): return lax.ppermute(value, 'ctx', pairs)  21.1 us
    ppermute x3, waiting for transfers between devices, shifted_y(): return lax.ppermute(value, 'dp', pairs)  11.2 us
    pallas_call x1, Pallas kernels, attention(): pl.pallas_call(functools.partial(attention_kernel, 128, seg), out_shape=(...  7.4 us
    unnamed x30, local copies, waits for them, and re-layouts  5.95 us
    ppermute x3, starting transfers between devices, shifted_y(): return lax.ppermute(value, 'dp', pairs)  5.29 us
    ppermute x1, starting transfers between devices, two_back(): lax.ppermute(value, 'ctx', [(i, i - CORES) for i in range(CORES, CTX)])  5.08 us
  transfers between devices with their start and end apart: 44, of which 20 were waited for; matrix products, arithmetic and copies ran while one was open for 1% of the time, Pallas kernels for 7%

profile of v3, /device:TPU:6, one launch (start us, length us, event | category | flops | bytes accessed | tf_op | source)
XLA Modules:
  0.0 166.2 jit_solution(11745548971025765089)
XLA Ops:
  8.3 8.7 %collective-permute-start = (s32[64]{0:T(128)}, s32[64]{0:T(128)S(1)}, u32[]{:S(2)}, u32[]{:S(2)}) collective-permute-start(s32[64]{0:T(128)} %bitcast.34), channel_id=1, source_target_pairs={{1,2},{2,1},{3,4},{4,3},{5,6},{6,5},{7,8},{8,7},{9,10},{10,9},{11,... | collective-permute-start | bytes 776 | tf_op jit(solution)/shard_map/ppermute | solution.py:42
  18.9 4.4 %collective-permute-done.2.theirs_ref = bf16[128,384]{1,0:T(8,128)(2,1)S(1)} collective-permute-done((bf16[128,384]{1,0:T(8,128)(2,1)}, bf16[128,384]{1,0:T(8,128)(2,1)S(1)}, u32[]{:S(2)}, u32[]{:S(2)}) %collective-permute-start.2) | collective-permute-done | bytes 98336 | tf_op jit(solution)/shard_map/ppermute | solution.py:96
  26.9 3.0 %collective-permute-start.4 = (bf16[64,2048]{1,0:T(8,128)(2,1)S(1)}, bf16[64,2048]{1,0:T(8,128)(2,1)S(1)}, u32[]{:S(2)}, u32[]{:S(2)}) collective-permute-start(bf16[64,2048]{1,0:T(8,128)(2,1)S(1)} %get-tuple-element.37), channel_id=1, source_target_pairs={{1,2},{2,1},{3,4},{4,3},{5,6},{6,5},{7,8},{8,7},{9,10},{10,9},{11,... | collective-permute-start | bytes 786440 | tf_op jit(solution)/shard_map/ppermute | solution.py:42
  29.9 3.3 %collective-permute-start.7 = (bf16[256,384]{1,0:T(8,128)(2,1)S(1)}, bf16[256,384]{1,0:T(8,128)(2,1)S(1)}, u32[]{:S(2)}, u32[]{:S(2)}) collective-permute-start(bf16[256,384]{1,0:T(8,128)(2,1)S(1)} %get-tuple-element.40.refs_9_), channel_id=1, source_target_pairs={{0,64},{32,96},{64,0},{96,32},{128,192},{160,224},{192,128},{224,1... | collective-permute-start | bytes 589832 | tf_op jit(solution)/shard_map/ppermute | solution.py:101
  35.3 6.4 %collective-permute-done.7.refs_2_.refs_12_ = bf16[256,384]{1,0:T(8,128)(2,1)S(1)} collective-permute-done((bf16[256,384]{1,0:T(8,128)(2,1)S(1)}, bf16[256,384]{1,0:T(8,128)(2,1)S(1)}, u32[]{:S(2)}, u32[]{:S(2)}) %collective-permute-start.7) | collective-permute-done | bytes 196640 | tf_op jit(solution)/shard_map/ppermute | solution.py:101
  41.7 4.3 %collective-permute-done.6.refs_1_.refs_11_ = bf16[256,384]{1,0:T(8,128)(2,1)S(1)} collective-permute-done((bf16[256,384]{1,0:T(8,128)(2,1)S(1)}, bf16[256,384]{1,0:T(8,128)(2,1)S(1)}, u32[]{:S(2)}, u32[]{:S(2)}) %collective-permute-start.6) | collective-permute-done | bytes 196640 | tf_op jit(solution)/shard_map/ppermute | solution.py:101
  47.9 6.6 %collective-permute-done.9.refs_3_ = bf16[64,1024]{1,0:T(8,128)(2,1)S(1)} collective-permute-done((bf16[64,1024]{1,0:T(8,128)(2,1)S(1)}, bf16[64,1024]{1,0:T(8,128)(2,1)S(1)}, u32[]{:S(2)}, u32[]{:S(2)}) %collective-permute-start.9) | collective-permute-done | bytes 131104 | tf_op jit(solution)/shard_map/ppermute | solution.py:37
  54.8 5.1 %collective-permute-start.8 = (f32[1,1024]{1,0:T(1,128)S(1)}, f32[1,1024]{1,0:T(1,128)S(1)}, u32[]{:S(2)}, u32[]{:S(2)}) collective-permute-start(f32[1,1024]{1,0:T(1,128)S(1)} %get-tuple-element.42), channel_id=1, source_target_pairs={{2,0},{3,1},{4,2},{5,3},{6,4},{7,5},{8,6},{9,7},{10,8},{11,9},{12,... | collective-permute-start | bytes 12296 | tf_op jit(solution)/shard_map/ppermute | solution.py:46
  64.0 2.5 %collective-permute-start.17 = (bf16[64,1024]{1,0:T(8,128)(2,1)}, bf16[64,1024]{1,0:T(8,128)(2,1)S(1)}, u32[]{:S(2)}, u32[]{:S(2)}) collective-permute-start(bf16[64,1024]{1,0:T(8,128)(2,1)} %get-tuple-element.46.refs_1_), channel_id=1, source_target_pairs={{0,4},{1,13},{2,6},{3,15},{4,8},{5,1},{6,10},{7,3},{8,12},{9,5},{1... | collective-permute-start | bytes 393224 | tf_op jit(solution)/shard_map/ppermute | solution.py:37
  68.9 3.1 %collective-permute-done.17.refs_3_ = bf16[64,1024]{1,0:T(8,128)(2,1)S(1)} collective-permute-done((bf16[64,1024]{1,0:T(8,128)(2,1)}, bf16[64,1024]{1,0:T(8,128)(2,1)S(1)}, u32[]{:S(2)}, u32[]{:S(2)}) %collective-permute-start.17) | collective-permute-done | bytes 131104 | tf_op jit(solution)/shard_map/ppermute | solution.py:37
  76.3 4.6 %shard_map.86 = (bf16[512,128]{1,0:T(8,128)(2,1)S(1)}, bf16[256,256]{1,0:T(8,128)(2,1)}, bf16[256,256]{1,0:T(8,128)(2,1)}, bf16[1024,384]{1,0:T(8,128)(2,1)S(1)}) custom-call(s32[6]{0:T(128)S(1)} %stack.35.place_ref.refs_0_, bf16[64,1024]{1,0:T(8,128)(2,1)S(1)} %get-tuple-element.43.refs_1_, bf16[64,1024]{1,0:T(8,128)(2,1)S(1)} %collective-permute-done.11.refs_2_, ...), custom_call_target="tpu_custom_call" | custom-call | tf_op jit(solution)/shard_map/pallas_call | solution.py:283
  81.6 2.7 %collective-permute-start.24 = (bf16[256,256]{1,0:T(8,128)(2,1)}, bf16[256,256]{1,0:T(8,128)(2,1)S(1)}, u32[]{:S(2)}, u32[]{:S(2)}) collective-permute-start(bf16[256,256]{1,0:T(8,128)(2,1)} %get-tuple-element.47.refs_3_), channel_id=1, source_target_pairs={{0,2},{1,3},{2,0},{3,1},{4,6},{5,7},{6,4},{7,5},{8,10},{9,11},{10,... | collective-permute-start | bytes 393224 | tf_op jit(solution)/shard_map/ppermute | solution.py:37
  88.8 4.7 %collective-permute-done.27.refs_8_ = bf16[256,256]{1,0:T(8,128)(2,1)S(1)} collective-permute-done((bf16[256,256]{1,0:T(8,128)(2,1)}, bf16[256,256]{1,0:T(8,128)(2,1)S(1)}, u32[]{:S(2)}, u32[]{:S(2)}) %collective-permute-start.27) | collective-permute-done | bytes 131104 | tf_op jit(solution)/shard_map/ppermute | solution.py:37
  96.9 2.8 %shard_map.87.refs_2_ = bf16[512,128]{1,0:T(8,128)(2,1)S(1)} custom-call(s32[6]{0:T(128)S(1)} %stack.35.place_ref.refs_0_, bf16[64,1024]{1,0:T(8,128)(2,1)S(1)} %copy-done.8, bf16[64,1024]{1,0:T(8,128)(2,1)S(1)} %collective-permute-done.16.refs_2_, bf16[64,1024]{1,0:T(8,128)(2,1)S(1)} %collective-permute-done.17.refs_3_, ...), custom_call_target="tpu_custom_call" | custom-call | tf_op jit(solution)/shard_map/pallas_call | solution.py:318
  100.0 2.3 %collective-permute-done.28.refs_9_ = bf16[256,256]{1,0:T(8,128)(2,1)S(1)} collective-permute-done((bf16[256,256]{1,0:T(8,128)(2,1)S(1)}, bf16[256,256]{1,0:T(8,128)(2,1)S(1)}, u32[]{:S(2)}, u32[]{:S(2)}) %collective-permute-start.28) | collective-permute-done | bytes 131104 | tf_op jit(solution)/shard_map/ppermute | solution.py:37
  102.2 7.4 %shard_map.88 = (bf16[512,128]{1,0:T(8,128)(2,1)S(1)}, bf16[256,256]{1,0:T(8,128)(2,1)S(1)}, bf16[256,256]{1,0:T(8,128)(2,1)S(1)}, bf16[256,256]{1,0:T(8,128)(2,...) custom-call(s32[6]{0:T(128)S(1)} %stack.35.place_ref.refs_0_, ...), custom_call_target="tpu_custom_call" | custom-call | flops 1610612736 | bytes 2490368 | tf_op jit(solution)/shard_map/pallas_call | solution.py:382
  109.7 4.0 %collective-permute-start.30 = (bf16[256,256]{1,0:T(8,128)(2,1)S(1)}, bf16[256,256]{1,0:T(8,128)(2,1)S(1)}, u32[]{:S(2)}, u32[]{:S(2)}) collective-permute-start(bf16[256,256]{1,0:T(8,128)(2,1)S(1)} %get-tuple-element.53), channel_id=1, source_target_pairs={{16,0},{17,1},{18,2},{19,3},{20,4},{21,5},{22,6},{23,7},{24,8},{25... | collective-permute-start | bytes 393224 | tf_op jit(solution)/shard_map/ppermute | solution.py:37
  119.2 3.0 %collective-permute-done.34 = bf16[256,256]{1,0:T(8,128)(2,1)S(1)} collective-permute-done((bf16[256,256]{1,0:T(8,128)(2,1)S(1)}, bf16[256,256]{1,0:T(8,128)(2,1)S(1)}, u32[]{:S(2)}, u32[]{:S(2)}) %collective-permute-start.34) | collective-permute-done | bytes 131104 | tf_op jit(solution)/shard_map/ppermute | solution.py:37
  124.3 2.5 %collective-permute-done.35.refs_5_ = bf16[256,256]{1,0:T(8,128)(2,1)S(1)} collective-permute-done((bf16[256,256]{1,0:T(8,128)(2,1)S(1)}, bf16[256,256]{1,0:T(8,128)(2,1)S(1)}, u32[]{:S(2)}, u32[]{:S(2)}) %collective-permute-start.35) | collective-permute-done | bytes 131104 | tf_op jit(solution)/shard_map/ppermute | solution.py:37
  131.0 4.9 %collective-permute-done.37 = bf16[64,1024]{1,0:T(8,128)(2,1)S(1)} collective-permute-done((bf16[64,1024]{1,0:T(8,128)(2,1)S(1)}, bf16[64,1024]{1,0:T(8,128)(2,1)S(1)}, u32[]{:S(2)}, u32[]{:S(2)}) %collective-permute-start.37) | collective-permute-done | bytes 131104 | tf_op jit(solution)/shard_map/ppermute | solution.py:37
  136.0 2.8 %collective-permute-start.39 = (bf16[64,1024]{1,0:T(8,128)(2,1)S(1)}, bf16[64,1024]{1,0:T(8,128)(2,1)S(1)}, u32[]{:S(2)}, u32[]{:S(2)}) collective-permute-start(bf16[64,1024]{1,0:T(8,128)(2,1)S(1)} %get-tuple-element.72), channel_id=1, source_target_pairs={{0,12},{1,5},{2,14},{3,7},{4,0},{5,9},{6,2},{7,11},{8,4},{9,13},{1... | collective-permute-start | bytes 393224 | tf_op jit(solution)/shard_map/ppermute | solution.py:37
  139.6 3.9 %collective-permute-done.39 = bf16[64,1024]{1,0:T(8,128)(2,1)S(1)} collective-permute-done((bf16[64,1024]{1,0:T(8,128)(2,1)S(1)}, bf16[64,1024]{1,0:T(8,128)(2,1)S(1)}, u32[]{:S(2)}, u32[]{:S(2)}) %collective-permute-start.39) | collective-permute-done | bytes 131104 | tf_op jit(solution)/shard_map/ppermute | solution.py:37
  145.8 9.4 %collective-permute-start.41 = (bf16[64,1024]{1,0:T(8,128)(2,1)S(1)}, bf16[64,1024]{1,0:T(8,128)(2,1)S(1)}, u32[]{:S(2)}, u32[]{:S(2)}) collective-permute-start(bf16[64,1024]{1,0:T(8,128)(2,1)S(1)} %divide_convert_fusion), channel_id=1, source_target_pairs={{1,2},{2,1},{3,4},{4,3},{5,6},{6,5},{7,8},{8,7},{9,10},{10,9},{11,... | collective-permute-start | bytes 393224 | tf_op jit(solution)/shard_map/ppermute | solution.py:42
  155.2 2.6 %collective-permute-done.41 = bf16[64,1024]{1,0:T(8,128)(2,1)S(1)} collective-permute-done((bf16[64,1024]{1,0:T(8,128)(2,1)S(1)}, bf16[64,1024]{1,0:T(8,128)(2,1)S(1)}, u32[]{:S(2)}, u32[]{:S(2)}) %collective-permute-start.41) | collective-permute-done | bytes 131104 | tf_op jit(solution)/shard_map/ppermute | solution.py:42
  (127 shorter events, 47.5 us)
Async XLA Ops:
  6.5 79.6 %all-gather.3.cloned.1.call-start = ((), (), s32[]{:S(2)}) async-start(), calls=%async_computation | async-start | bytes 1179648 | tf_op jit(solution)/shard_map/all_gather | solution.py:107
  8.2 10.4 %collective-permute-start.1 = (s32[64]{0:T(128)}, s32[64]{0:T(128)S(1)}, u32[]{:S(2)}, u32[]{:S(2)}) collective-permute-start(s32[64]{0:T(128)} %bitcast.33), channel_id=1, source_target_pairs={{0,1},{1,0},{2,3},{3,2},{4,5},{5,4},{6,7},{7,6},{8,9},{9,8},{10,11... | collective-permute-start | bytes 776 | tf_op jit(solution)/shard_map/ppermute | solution.py:37
  8.3 10.3 %collective-permute-start = (s32[64]{0:T(128)}, s32[64]{0:T(128)S(1)}, u32[]{:S(2)}, u32[]{:S(2)}) collective-permute-start(s32[64]{0:T(128)} %bitcast.34), channel_id=1, source_target_pairs={{1,2},{2,1},{3,4},{4,3},{5,6},{6,5},{7,8},{8,7},{9,10},{10,9},{11,... | collective-permute-start | bytes 776 | tf_op jit(solution)/shard_map/ppermute | solution.py:42
  26.8 19.8 %collective-permute-start.3 = (bf16[64,2048]{1,0:T(8,128)(2,1)S(1)}, bf16[64,2048]{1,0:T(8,128)(2,1)S(1)}, u32[]{:S(2)}, u32[]{:S(2)}) collective-permute-start(bf16[64,2048]{1,0:T(8,128)(2,1)S(1)} %get-tuple-element.36), channel_id=1, source_target_pairs={{0,1},{1,0},{2,3},{3,2},{4,5},{5,4},{6,7},{7,6},{8,9},{9,8},{10,11... | collective-permute-start | bytes 786440 | tf_op jit(solution)/shard_map/ppermute | solution.py:37
  26.9 19.7 %collective-permute-start.4 = (bf16[64,2048]{1,0:T(8,128)(2,1)S(1)}, bf16[64,2048]{1,0:T(8,128)(2,1)S(1)}, u32[]{:S(2)}, u32[]{:S(2)}) collective-permute-start(bf16[64,2048]{1,0:T(8,128)(2,1)S(1)} %get-tuple-element.37), channel_id=1, source_target_pairs={{1,2},{2,1},{3,4},{4,3},{5,6},{6,5},{7,8},{8,7},{9,10},{10,9},{11,... | collective-permute-start | bytes 786440 | tf_op jit(solution)/shard_map/ppermute | solution.py:42
  29.9 11.9 %collective-permute-start.7 = (bf16[256,384]{1,0:T(8,128)(2,1)S(1)}, bf16[256,384]{1,0:T(8,128)(2,1)S(1)}, u32[]{:S(2)}, u32[]{:S(2)}) collective-permute-start(bf16[256,384]{1,0:T(8,128)(2,1)S(1)} %get-tuple-element.40.refs_9_), channel_id=1, source_target_pairs={{0,64},{32,96},{64,0},{96,32},{128,192},{160,224},{192,128},{224,1... | collective-permute-start | bytes 589832 | tf_op jit(solution)/shard_map/ppermute | solution.py:101
  33.1 12.9 %collective-permute-start.6 = (bf16[256,384]{1,0:T(8,128)(2,1)S(1)}, bf16[256,384]{1,0:T(8,128)(2,1)S(1)}, u32[]{:S(2)}, u32[]{:S(2)}) collective-permute-start(bf16[256,384]{1,0:T(8,128)(2,1)S(1)} %get-tuple-element.40.refs_9_), channel_id=1, source_target_pairs={{0,96},{32,0},{64,32},{96,64},{128,224},{160,128},{192,160},{224,1... | collective-permute-start | bytes 589832 | tf_op jit(solution)/shard_map/ppermute | solution.py:101
  34.2 12.3 %collective-permute-start.5 = (bf16[256,384]{1,0:T(8,128)(2,1)S(1)}, bf16[256,384]{1,0:T(8,128)(2,1)S(1)}, u32[]{:S(2)}, u32[]{:S(2)}) collective-permute-start(bf16[256,384]{1,0:T(8,128)(2,1)S(1)} %get-tuple-element.40.refs_9_), channel_id=1, source_target_pairs={{0,32},{32,64},{64,96},{96,0},{128,160},{160,192},{192,224},{224,1... | collective-permute-start | bytes 589832 | tf_op jit(solution)/shard_map/ppermute | solution.py:101
  47.5 12.4 %collective-permute-start.11 = (bf16[64,1024]{1,0:T(8,128)(2,1)S(1)}, bf16[64,1024]{1,0:T(8,128)(2,1)S(1)}, u32[]{:S(2)}, u32[]{:S(2)}) collective-permute-start(bf16[64,1024]{1,0:T(8,128)(2,1)S(1)} %get-tuple-element.43.refs_1_), channel_id=1, source_target_pairs={{0,1},{1,0},{2,3},{3,2},{4,5},{5,4},{6,7},{7,6},{8,9},{9,8},{10,11... | collective-permute-start | bytes 393224 | tf_op jit(solution)/shard_map/ppermute | solution.py:37
  59.9 8.5 %collective-permute-start.12 = (bf16[64,1024]{1,0:T(8,128)(2,1)S(1)}, bf16[64,1024]{1,0:T(8,128)(2,1)S(1)}, u32[]{:S(2)}, u32[]{:S(2)}) collective-permute-start(bf16[64,1024]{1,0:T(8,128)(2,1)S(1)} %collective-permute-done.11.refs_2_), channel_id=1, source_target_pairs={{0,4},{1,13},{2,6},{3,15},{4,8},{5,1},{6,10},{7,3},{8,12},{9,5},{1... | collective-permute-start | bytes 393224 | tf_op jit(solution)/shard_map/ppermute | solution.py:37
  66.5 8.9 %collective-permute-start.13 = (bf16[64,1024]{1,0:T(8,128)(2,1)S(1)}, bf16[64,1024]{1,0:T(8,128)(2,1)S(1)}, u32[]{:S(2)}, u32[]{:S(2)}) collective-permute-start(bf16[64,1024]{1,0:T(8,128)(2,1)S(1)} %collective-permute-done.9.refs_3_), channel_id=1, source_target_pairs={{0,1},{1,0},{2,3},{3,2},{4,5},{5,4},{6,7},{7,6},{8,9},{9,8},{10,11... | collective-permute-start | bytes 393224 | tf_op jit(solution)/shard_map/ppermute | solution.py:37
  72.0 13.6 %collective-permute-start.21 = (bf16[64,1024]{1,0:T(8,128)(2,1)S(1)}, bf16[64,1024]{1,0:T(8,128)(2,1)S(1)}, u32[]{:S(2)}, u32[]{:S(2)}) collective-permute-start(bf16[64,1024]{1,0:T(8,128)(2,1)S(1)} %collective-permute-done.17.refs_3_), channel_id=1, source_target_pairs={{0,4},{1,13},{2,6},{3,15},{4,8},{5,1},{6,10},{7,3},{8,12},{9,5},{1... | collective-permute-start | bytes 393224 | tf_op jit(solution)/shard_map/ppermute | solution.py:37
  73.9 12.0 %collective-permute-start.18 = (bf16[64,1024]{1,0:T(8,128)(2,1)S(1)}, bf16[64,1024]{1,0:T(8,128)(2,1)S(1)}, u32[]{:S(2)}, u32[]{:S(2)}) collective-permute-start(bf16[64,1024]{1,0:T(8,128)(2,1)S(1)} %collective-permute-done.16.refs_2_), channel_id=1, source_target_pairs={{0,4},{1,13},{2,6},{3,15},{4,8},{5,1},{6,10},{7,3},{8,12},{9,5},{1... | collective-permute-start | bytes 393224 | tf_op jit(solution)/shard_map/ppermute | solution.py:37
  75.4 11.8 %collective-permute-start.19 = (bf16[64,1024]{1,0:T(8,128)(2,1)S(1)}, bf16[64,1024]{1,0:T(8,128)(2,1)S(1)}, u32[]{:S(2)}, u32[]{:S(2)}) collective-permute-start(bf16[64,1024]{1,0:T(8,128)(2,1)S(1)} %collective-permute-done.17.refs_3_), channel_id=1, source_target_pairs={{0,1},{1,0},{2,3},{3,2},{4,5},{5,4},{6,7},{7,6},{8,9},{9,8},{10,11... | collective-permute-start | bytes 393224 | tf_op jit(solution)/shard_map/ppermute | solution.py:37
  84.2 9.2 %collective-permute-start.27 = (bf16[256,256]{1,0:T(8,128)(2,1)}, bf16[256,256]{1,0:T(8,128)(2,1)S(1)}, u32[]{:S(2)}, u32[]{:S(2)}) collective-permute-start(bf16[256,256]{1,0:T(8,128)(2,1)} %get-tuple-element.48.refs_4_), channel_id=1, source_target_pairs={{0,16},{1,17},{2,18},{3,19},{4,20},{5,21},{6,22},{7,23},{8,24},{9,... | collective-permute-start | bytes 393224 | tf_op jit(solution)/shard_map/ppermute | solution.py:37
  85.5 8.3 %collective-permute-start.22 = (bf16[64,1024]{1,0:T(8,128)(2,1)S(1)}, bf16[64,1024]{1,0:T(8,128)(2,1)S(1)}, u32[]{:S(2)}, u32[]{:S(2)}) collective-permute-start(bf16[64,1024]{1,0:T(8,128)(2,1)S(1)} %collective-permute-done.21.refs_7_), channel_id=1, source_target_pairs={{0,1},{1,0},{2,3},{3,2},{4,5},{5,4},{6,7},{7,6},{8,9},{9,8},{10,11... | collective-permute-start | bytes 393224 | tf_op jit(solution)/shard_map/ppermute | solution.py:37
  85.9 9.3 %collective-permute-start.20 = (bf16[64,1024]{1,0:T(8,128)(2,1)S(1)}, bf16[64,1024]{1,0:T(8,128)(2,1)S(1)}, u32[]{:S(2)}, u32[]{:S(2)}) collective-permute-start(bf16[64,1024]{1,0:T(8,128)(2,1)S(1)} %collective-permute-done.18.refs_4_), channel_id=1, source_target_pairs={{0,1},{1,0},{2,3},{3,2},{4,5},{5,4},{6,7},{7,6},{8,9},{9,8},{10,11... | collective-permute-start | bytes 393224 | tf_op jit(solution)/shard_map/ppermute | solution.py:37
  87.2 12.5 %collective-permute-start.26 = (bf16[256,256]{1,0:T(8,128)(2,1)}, bf16[256,256]{1,0:T(8,128)(2,1)S(1)}, u32[]{:S(2)}, u32[]{:S(2)}) collective-permute-start(bf16[256,256]{1,0:T(8,128)(2,1)} %get-tuple-element.47.refs_3_), channel_id=1, source_target_pairs={{0,16},{1,17},{2,18},{3,19},{4,20},{5,21},{6,22},{7,23},{8,24},{9,... | collective-permute-start | bytes 393224 | tf_op jit(solution)/shard_map/ppermute | solution.py:37
  88.6 8.3 %collective-permute-start.23 = (bf16[64,1024]{1,0:T(8,128)(2,1)S(1)}, bf16[64,1024]{1,0:T(8,128)(2,1)S(1)}, u32[]{:S(2)}, u32[]{:S(2)}) collective-permute-start(bf16[64,1024]{1,0:T(8,128)(2,1)S(1)} %get-tuple-element.69), channel_id=1, source_target_pairs={{0,1},{1,0},{2,3},{3,2},{4,5},{5,4},{6,7},{7,6},{8,9},{9,8},{10,11... | collective-permute-start | bytes 393224 | tf_op jit(solution)/shard_map/ppermute | solution.py:37
  93.9 8.4 %collective-permute-start.28 = (bf16[256,256]{1,0:T(8,128)(2,1)S(1)}, bf16[256,256]{1,0:T(8,128)(2,1)S(1)}, u32[]{:S(2)}, u32[]{:S(2)}) collective-permute-start(bf16[256,256]{1,0:T(8,128)(2,1)S(1)} %collective-permute-done.24.refs_5_), channel_id=1, source_target_pairs={{0,16},{1,17},{2,18},{3,19},{4,20},{5,21},{6,22},{7,23},{8,24},{9,... | collective-permute-start | bytes 393224 | tf_op jit(solution)/shard_map/ppermute | solution.py:37
  113.7 10.5 %collective-permute-start.32 = (bf16[256,256]{1,0:T(8,128)(2,1)S(1)}, bf16[256,256]{1,0:T(8,128)(2,1)S(1)}, u32[]{:S(2)}, u32[]{:S(2)}) collective-permute-start(bf16[256,256]{1,0:T(8,128)(2,1)S(1)} %get-tuple-element.54), channel_id=1, source_target_pairs={{0,2},{1,3},{2,0},{3,1},{4,6},{5,7},{6,4},{7,5},{8,10},{9,11},{10,... | collective-permute-start | bytes 393224 | tf_op jit(solution)/shard_map/ppermute | solution.py:37
  115.4 8.8 %collective-permute-start.33 = (bf16[256,256]{1,0:T(8,128)(2,1)S(1)}, bf16[256,256]{1,0:T(8,128)(2,1)S(1)}, u32[]{:S(2)}, u32[]{:S(2)}) collective-permute-start(bf16[256,256]{1,0:T(8,128)(2,1)S(1)} %get-tuple-element.55), channel_id=1, source_target_pairs={{16,0},{17,1},{18,2},{19,3},{20,4},{21,5},{22,6},{23,7},{24,8},{25... | collective-permute-start | bytes 393224 | tf_op jit(solution)/shard_map/ppermute | solution.py:37
  145.7 9.5 %collective-permute-start.42 = (bf16[64,1024]{1,0:T(8,128)(2,1)S(1)}, bf16[64,1024]{1,0:T(8,128)(2,1)S(1)}, u32[]{:S(2)}, u32[]{:S(2)}) collective-permute-start(bf16[64,1024]{1,0:T(8,128)(2,1)S(1)} %divide_convert_fusion), channel_id=1, source_target_pairs={{0,1},{1,0},{2,3},{3,2},{4,5},{5,4},{6,7},{7,6},{8,9},{9,8},{10,11... | collective-permute-start | bytes 393224 | tf_op jit(solution)/shard_map/ppermute | solution.py:37
  145.8 12.0 %collective-permute-start.41 = (bf16[64,1024]{1,0:T(8,128)(2,1)S(1)}, bf16[64,1024]{1,0:T(8,128)(2,1)S(1)}, u32[]{:S(2)}, u32[]{:S(2)}) collective-permute-start(bf16[64,1024]{1,0:T(8,128)(2,1)S(1)} %divide_convert_fusion), channel_id=1, source_target_pairs={{1,2},{2,1},{3,4},{4,3},{5,6},{6,5},{7,8},{8,7},{9,10},{10,9},{11,... | collective-permute-start | bytes 393224 | tf_op jit(solution)/shard_map/ppermute | solution.py:42
  (35 other events, 243.8 us)
Sparse Core Ops, SparseCore 0:
  9.2 44.9 all-gather.2

commit v4 on v3

--- a/solution.py
+++ b/solution.py
@@ -54,14 +54,21 @@
     return moved(value, lambda h, t, p, k: (h, t, 1 - p, k))
 
 
-def across(value, source):
-    return moved(value, lambda h, t, p, k: (1 - h, t, p, k) if h == source else None)
+def across(value, source, cross):
+    return moved(
+        value,
+        lambda h, t, p, k: (1 - h, t, 1 - p if cross else p, k) if h == source else None,
+    )
 
 
 def turned(value, way):
     return moved(value, lambda h, t, p, k: (h, t + way * (1 - 2 * k), p, k))
 
 
+def turned_over(value):
+    return moved(value, lambda h, t, p, k: (h, t - (1 - 2 * k), p, 1 - k))
+
+
 def contract_last(left, right):
     return lax.dot_general(left, right, (((1,), (1,)), ((), ())), preferred_element_type=F32)
 
@@ -70,25 +77,31 @@
     return lax.dot_general(left, right, (((0,), (0,)), ((), ())), preferred_element_type=F32)
 
 
-def cut_kernel(head_ref, q_ref, k_ref, v_ref, out_ref):
+def cut_kernel(head_ref, q_ref, k_ref, v_ref, start_ref, out_ref, start_out):
     out_ref[:, :HEAD] = q_ref[...]
     out_ref[:, HEAD : 2 * HEAD] = k_ref[...]
     out_ref[:, 2 * HEAD :] = v_ref[...]
-
-
-def columns_in(w_query, w_key, w_value, head):
+    start_out[...] = start_ref[...]
+
+
+def columns_in(w_query, w_key, w_value, starts, head):
     rows = w_query.shape[0]
     block = pl.BlockSpec((rows, HEAD), lambda i, h: (0, h[0]))
+    whole = pl.BlockSpec(starts.shape, lambda i, h: (0, 0))
     return pl.pallas_call(
         cut_kernel,
         grid_spec=pltpu.PrefetchScalarGridSpec(
             num_scalar_prefetch=1,
             grid=(1,),
-            in_specs=[block] * 3,
-            out_specs=pl.BlockSpec((rows, 3 * HEAD), lambda i, h: (0, 0)),
-        ),
-        out_shape=jax.ShapeDtypeStruct((rows, 3 * HEAD), w_query.dtype),
-    )(head[None], w_query, w_key, w_value)
+            in_specs=[block] * 3 + [whole],
+            out_specs=(pl.BlockSpec((rows, 3 * HEAD), lambda i, h: (0, 0)), whole),
+        ),
+        out_shape=(
+            jax.ShapeDtypeStruct((rows, 3 * HEAD), w_query.dtype),
+            jax.ShapeDtypeStruct(starts.shape, starts.dtype),
+        ),
+        compiler_params=PARAMS,
+    )(head[None], w_query, w_key, w_value, starts)
 
 
 def other_x(value):
@@ -101,23 +114,34 @@
     return lax.ppermute(value, "dp", pairs)
 
 
-def rows_out(w_out, turn, core):
-    rows = w_out.shape[0] // CORES
-    half = lax.dynamic_slice(w_out, (core * rows, 0), (rows, w_out.shape[1]))
+def rows_out(half, turn, core):
     gathered = lax.all_gather(half, "dp", axis=0, tiled=False)
     mine = lax.dynamic_index_in_dim(gathered, turn * CORES + core, 0, keepdims=False)
     theirs = lax.dynamic_index_in_dim(gathered, turn * CORES + 1 - core, 0, keepdims=False)
     return mine, other_core(theirs)
 
 
-def gathered_rows(shard):
-    swapped = other_core(shard)
+def pass_kernel(value_ref, ready_ref, out_ref):
+    out_ref[...] = value_ref[...]
+
+
+def passed_on(value, ready):
+    return pl.pallas_call(
+        pass_kernel,
+        out_shape=jax.ShapeDtypeStruct(value.shape, value.dtype),
+        in_specs=[VMEM, ANY],
+        out_specs=VMEM,
+        compiler_params=PARAMS,
+    )(value, ready)
+
+
+def gathered_rows(shard, ready):
     near = turned(shard, 1)
-    far = turned(near, 1)
-    next_to = turned(swapped, 1)
+    next_to = turned_over(shard)
+    far = turned(passed_on(near, ready), 1)
     return [
         shard,
-        swapped,
+        other_core(shard),
         near,
         next_to,
         other_core(near),
@@ -155,10 +179,21 @@
     return copies
 
 
-def window_kernel(place_ref, edge_ref, token_ref, grad_ref, mine_ref, theirs_ref, *outs):
-    core_ref, chip_ref, mid_token, mid_grad, first_ref, both_ref = outs
+def window_kernel(place_ref, edge_ref, token_hbm, grad_hbm, mine_hbm, theirs_hbm, *refs):
+    core_ref, chip_ref, mid_token, mid_grad, first_ref, both_ref = refs[:6]
+    token_ref, grad_ref, sems = refs[6:]
     rows, width = token_ref.shape
     seg = mid_token.shape[0]
+    half = mine_hbm.shape[0]
+    fetched(
+        [
+            (token_hbm, token_ref),
+            (grad_hbm, grad_ref),
+            (mine_hbm, both_ref.at[:half, :]),
+            (theirs_hbm, both_ref.at[half:, :]),
+        ],
+        sems,
+    )
     ctx, core = place_ref[5], place_ref[3]
     at = lax.broadcasted_iota(jnp.int32, (1, rows), 1) + ctx * rows
     opens, ends, nexts = edge_ref[0], edge_ref[1], edge_ref[2]
@@ -170,8 +205,6 @@
     first_ref[...] = first[:1]
     mid_token[...] = token[seg : 2 * seg]
     mid_grad[...] = grad[seg : 2 * seg]
-    both_ref[: mine_ref.shape[0], :] = mine_ref[...]
-    both_ref[mine_ref.shape[0] :, :] = theirs_ref[...]
 
     def send(lower_ref, upper_ref):
         lower_ref[:, :width] = token[:seg].astype(WIRE)
@@ -189,7 +222,7 @@
 
 
 def window_sums(where, edges, tokens, grads, mine, theirs, seg):
-    width = tokens.shape[1]
+    rows, width = tokens.shape
     shape = jax.ShapeDtypeStruct
     return pl.pallas_call(
         window_kernel,
@@ -201,64 +234,63 @@
             shape((1, width), F32),
             shape((2 * mine.shape[0], mine.shape[1]), mine.dtype),
         ),
-        in_specs=[SMEM] + [VMEM] * 5,
+        in_specs=[SMEM, VMEM] + [ANY] * 4,
         out_specs=(VMEM,) * 6,
+        scratch_shapes=[
+            pltpu.VMEM((rows, width), tokens.dtype),
+            pltpu.VMEM((rows, width), grads.dtype),
+            pltpu.SemaphoreType.DMA((4,)),
+        ],
         compiler_params=PARAMS,
     )(where, edges, tokens, grads, mine, theirs)
 
 
-def norm_kernel(core_ref, chip_ref, mid_token, mid_grad, count_ref, gain_ref, *refs):
-    normin_ref, normed_ref, rms_ref, dout_ref = refs[-4:]
-    width = mid_token.shape[1]
+def norm_kernel(place_ref, core_ref, chip_ref, mid_token, mid_grad, second_ref, count_ref, *refs):
+    gain_ref, w_ref = refs[:2]
+    both_ref, normed_ref, rms_ref, dout_ref, half_ref, sem = refs[-6:]
+    seg, width = mid_token.shape
+    rows = half_ref.shape[0]
+    core = place_ref[3]
+    at = pl.multiple_of(core * rows, rows)
+    copy = pltpu.make_async_copy(w_ref.at[pl.ds(at, rows), :], half_ref, sem)
+    copy.start()
     got = core_ref[...].astype(F32) + chip_ref[...].astype(F32)
     pooled = (mid_token[...] + got[:, :width]) / count_ref[...]
     rms = jnp.sqrt(jnp.mean(pooled * pooled, axis=1, keepdims=True) + 1e-06)
     normed = pooled / rms
     normed_ref[...] = normed
     rms_ref[...] = rms
-    normin_ref[...] = (normed * gain_ref[...]).astype(jnp.bfloat16)
-    dout_ref[...] = mid_grad[...] + got[:, width:]
-
-
-def norm(from_core, from_chip, mid_token, mid_grad, count, gain, ready):
+    last = lax.broadcasted_iota(jnp.int32, (seg, 1), 0) == seg - 1
+    dout = mid_grad[...] + got[:, width:] + jnp.where(last, second_ref[...], 0.0)
+    dout_ref[...] = dout
+    both_ref[:, :width] = (normed * gain_ref[...]).astype(jnp.bfloat16)
+    both_ref[:, width:] = dout.astype(jnp.bfloat16)
+    copy.wait()
+
+
+def norm(where, from_core, from_chip, mid_token, mid_grad, second, count, gain, w_out, ready):
     seg, width = mid_token.shape
     shape = jax.ShapeDtypeStruct
     return pl.pallas_call(
         norm_kernel,
         out_shape=(
-            shape((seg, width), jnp.bfloat16),
+            shape((seg, 2 * width), jnp.bfloat16),
             shape((seg, width), F32),
             shape((seg, 1), F32),
             shape((seg, width), F32),
-        ),
-        in_specs=[VMEM] * 6 + [ANY] * len(ready),
-        out_specs=(VMEM,) * 4,
-        compiler_params=PARAMS,
-    )(from_core, from_chip, mid_token, mid_grad, count, gain, *ready)
-
-
-def dout_kernel(dout_ref, second_ref, ready_ref, full_ref, half_ref):
-    seg = dout_ref.shape[0]
-    last = lax.broadcasted_iota(jnp.int32, (seg, 1), 0) == seg - 1
-    dout = dout_ref[...] + jnp.where(last, second_ref[...].astype(F32), 0.0)
-    full_ref[...] = dout
-    half_ref[...] = dout.astype(jnp.bfloat16)
-
-
-def whole_dout(dout, second, ready):
-    shape = jax.ShapeDtypeStruct
-    return pl.pallas_call(
-        dout_kernel,
-        out_shape=(shape(dout.shape, F32), shape(dout.shape, jnp.bfloat16)),
-        in_specs=[VMEM, VMEM, ANY],
-        out_specs=(VMEM, VMEM),
-    )(dout, second, ready)
+            shape((w_out.shape[0] // CORES, w_out.shape[1]), w_out.dtype),
+        ),
+        in_specs=[SMEM] + [VMEM] * 7 + [ANY] * (1 + len(ready)),
+        out_specs=(VMEM,) * 5,
+        scratch_shapes=[pltpu.SemaphoreType.DMA],
+        compiler_params=PARAMS,
+    )(where, from_core, from_chip, mid_token, mid_grad, second, count, gain, w_out, *ready)
 
 
 def project_kernel(*refs):
     place_ref, pieces, weights = refs[0], refs[1:9], refs[9:13]
-    q_ref, top_ref, bottom_ref, w_ref, rows, sems = refs[13:]
-    copies = stacked(pieces, rows)
+    q_ref, kv_ref, w_ref, rows, sems = refs[13:]
+    copies = stacked([piece.at[:, : rows.shape[1]] for piece in pieces], rows)
     dp = place_ref[4]
     x, y = dp // ROWS_Y, dp % ROWS_Y
     depth = weights[0].shape[0] // ROWS_X
@@ -270,26 +302,23 @@
             copies.append((weight.at[i * depth : (i + 1) * depth, :], w_ref.at[pl.ds(at, depth), :]))
     fetched(copies, sems)
     out = jnp.dot(rows[...], w_ref[...], preferred_element_type=F32).astype(jnp.bfloat16)
-    cut = out.shape[0] // 2
     q_ref[...] = out[:, :HEAD]
-    top_ref[...] = out[:cut, HEAD:]
-    bottom_ref[...] = out[cut:, HEAD:]
+    kv_ref[...] = out[:, HEAD:]
 
 
 def project(where, pieces, weights):
     rows = sum(piece.shape[0] for piece in pieces)
-    width = pieces[0].shape[1]
+    width = pieces[0].shape[1] // 2
     bf16 = lambda *shape: jax.ShapeDtypeStruct(shape, jnp.bfloat16)
     return pl.pallas_call(
         project_kernel,
         out_shape=(
             bf16(rows, HEAD),
-            bf16(rows // 2, 2 * HEAD),
-            bf16(rows // 2, 2 * HEAD),
+            bf16(rows, 2 * HEAD),
             bf16(width, 3 * HEAD),
         ),
         in_specs=[SMEM] + [ANY] * 12,
-        out_specs=(VMEM,) * 4,
+        out_specs=(VMEM,) * 3,
         scratch_shapes=[
             pltpu.VMEM((rows, width), jnp.bfloat16),
             pltpu.SemaphoreType.DMA((16,)),
@@ -305,7 +334,7 @@
     half = mine.shape[0]
     spot = pl.multiple_of(core * half, half)
     other = pl.multiple_of((1 - core) * half, half)
-    copies = stacked(pieces, rows)
+    copies = stacked([piece.at[:, rows.shape[1] :] for piece in pieces], rows)
     copies.append((mine, weight.at[pl.ds(spot, half), :]))
     copies.append((theirs, weight.at[pl.ds(other, half), :]))
     fetched(copies, sems)
@@ -314,7 +343,7 @@
 
 def dattended(where, pieces, mine, theirs):
     rows = sum(piece.shape[0] for piece in pieces)
-    width = pieces[0].shape[1]
+    width = pieces[0].shape[1] // 2
     return pl.pallas_call(
         dattended_kernel,
         out_shape=jax.ShapeDtypeStruct((rows, HEAD), jnp.bfloat16),
@@ -330,8 +359,8 @@
 
 
 def attention_kernel(tile, seg, *refs):
-    place_ref, q_ref, da_ref, blocks = refs[0], refs[1], refs[2], refs[3:11]
-    dq_ref, outs, (kv, dkt, dvt, sems) = refs[11], refs[12:20], refs[20:]
+    place_ref, q_ref, da_ref, blocks = refs[0], refs[1], refs[2], refs[3:7]
+    dq_ref, outs, (kv, dkt, dvt, sems) = refs[7], refs[8:12], refs[12:]
     half, turn, pair, core = place_ref[0], place_ref[1], place_ref[2], place_ref[3]
     queries, keys = q_ref.shape[0], kv.shape[0]
     fetched(stacked(blocks, kv), sems)
@@ -381,14 +410,14 @@
     part = jax.ShapeDtypeStruct(blocks[0].shape, jnp.bfloat16)
     return pl.pallas_call(
         functools.partial(attention_kernel, 128, seg),
-        out_shape=(jax.ShapeDtypeStruct((queries, HEAD), jnp.bfloat16),) + (part,) * 8,
-        in_specs=[SMEM] + [VMEM] * 2 + [ANY] * 8,
-        out_specs=(VMEM,) * 9,
+        out_shape=(jax.ShapeDtypeStruct((queries, HEAD), jnp.bfloat16),) + (part,) * 4,
+        in_specs=[SMEM] + [VMEM] * 2 + [ANY] * 4,
+        out_specs=(VMEM,) * 5,
         scratch_shapes=[
             pltpu.VMEM((keys, 2 * HEAD), jnp.bfloat16),
             pltpu.VMEM((HEAD, keys), F32),
             pltpu.VMEM((HEAD, keys), F32),
-            pltpu.SemaphoreType.DMA((8,)),
+            pltpu.SemaphoreType.DMA((4,)),
         ],
         compiler_params=PARAMS,
         cost_estimate=pl.CostEstimate(
@@ -400,52 +429,69 @@
 
 
 def unproject_kernel(seg, dq_ref, *refs):
-    dkv_parts, w_ref, swap_ref, outs = refs[:6], refs[6], refs[7], refs[8:]
-    top = sum(ref[...].astype(F32) for ref in dkv_parts[0::2])
-    bottom = sum(ref[...].astype(F32) for ref in dkv_parts[1::2])
-    dkv = jnp.concatenate([top, bottom], axis=0).astype(jnp.bfloat16)
+    parts, w_ref, swap_ref, outs = refs[:4], refs[4], refs[5], refs[6:]
+    dkv = sum(ref[...].astype(F32) for ref in parts).astype(jnp.bfloat16)
     left = jnp.concatenate([dq_ref[...], dkv], axis=1)
     out = contract_last(left, w_ref[...])
-    swap_ref[: 2 * seg, :] = out[4 * seg : 6 * seg].astype(WIRE)
-    swap_ref[2 * seg :, :] = out[7 * seg :].astype(WIRE)
-    for ref, slot in zip(outs, (0, 1, 2, 3, 6)):
+    for i, slot in enumerate((1, 4, 5, 7)):
+        swap_ref[i * seg : (i + 1) * seg, :] = out[slot * seg : (slot + 1) * seg].astype(WIRE)
+    for ref, slot in zip(outs, (0, 2, 3, 6)):
         ref[...] = out[slot * seg : (slot + 1) * seg]
 
 
-def unproject(dq, dkv_parts, w_full, seg):
+def unproject(dq, parts, w_full, seg):
     width = w_full.shape[0]
     return pl.pallas_call(
         functools.partial(unproject_kernel, seg),
-        out_shape=(jax.ShapeDtypeStruct((3 * seg, width), WIRE),)
-        + (jax.ShapeDtypeStruct((seg, width), F32),) * 5,
-        in_specs=[VMEM] * 8,
-        out_specs=(VMEM,) * 6,
-        compiler_params=PARAMS,
-    )(dq, *dkv_parts, w_full)
-
-
-def summed_rows(swap, own, beside, near, next_to, far, seg):
-    swapped = other_core(swap).astype(F32)
-    far = turned((far + swapped[2 * seg :]).astype(WIRE), -1).astype(F32)
-    next_to = turned((next_to + swapped[seg : 2 * seg]).astype(WIRE), -1).astype(F32)
-    near = turned((near + swapped[:seg] + far).astype(WIRE), -1).astype(F32)
-    beside = other_core((beside + next_to).astype(WIRE)).astype(F32)
-    return own + near + beside
+        out_shape=(jax.ShapeDtypeStruct((4 * seg, width), WIRE),)
+        + (jax.ShapeDtypeStruct((seg, width), F32),) * 4,
+        in_specs=[VMEM] * 6,
+        out_specs=(VMEM,) * 5,
+        compiler_params=PARAMS,
+    )(dq, *parts, w_full)
+
+
+def join_kernel(swapped, own, near, next_to, far, own_out, near_out, next_out, far_out):
+    seg = own.shape[0]
+    own_out[...] = own[...] + swapped[:seg, :].astype(F32)
+    near_out[...] = near[...] + swapped[seg : 2 * seg, :].astype(F32)
+    next_out[...] = (next_to[...] + swapped[2 * seg : 3 * seg, :].astype(F32)).astype(WIRE)
+    far_out[...] = (far[...] + swapped[3 * seg :, :].astype(F32)).astype(WIRE)
+
+
+def joined(swapped, own, near, next_to, far):
+    wide = jax.ShapeDtypeStruct(own.shape, F32)
+    thin = jax.ShapeDtypeStruct(own.shape, WIRE)
+    return pl.pallas_call(
+        join_kernel,
+        out_shape=(wide, wide, thin, thin),
+        in_specs=[VMEM] * 5,
+        out_specs=(VMEM,) * 4,
+        compiler_params=PARAMS,
+    )(swapped, own, near, next_to, far)
+
+
+def summed_rows(swap, own, near, next_to, far):
+    own, near, next_to, far = joined(other_core(swap), own, near, next_to, far)
+    far = turned(far, -1).astype(F32)
+    next_to = turned_over(next_to).astype(F32)
+    near = turned((near + far).astype(WIRE), -1).astype(F32)
+    return own + next_to + near
 
 
 def per_device(tokens, starts, gain, w_query, w_key, w_value, w_out, cotangent):
     token_rows = tokens[0]
     grad_out = cotangent[0]
-    own_starts = starts[0]
     rows, width = token_rows.shape
-    seg = own_starts.shape[0]
+    seg = starts.shape[1]
     length = rows * CTX
     ctx = lax.axis_index("ctx")
     core, pair = ctx % CORES, ctx // CORES % PAIR
     turn, half = ctx // (CORES * PAIR) % TURNS, ctx // (CORES * PAIR * TURNS)
     where = jnp.stack([half, turn, pair, core, lax.axis_index("dp"), ctx])
 
-    mine = columns_in(w_query, w_key, w_value, turn * CORES + core)
+    mine, own_starts = columns_in(w_query, w_key, w_value, starts, turn * CORES + core)
+    own_starts = own_starts[0]
     theirs = other_x(mine)
     beside, facing = other_core(own_starts), other_chip(own_starts)
     before = jnp.where(core == 0, facing, beside)
@@ -463,42 +509,26 @@
     )
     weights = [both, shifted_y(both, 1), shifted_y(both, -1), shifted_y(both, 2)]
     second = two_back(first)
-    normin, normed, rms, dout = norm(
+    both, normed, rms, dout, out_half = norm(
+        where,
         other_core(to_core),
         other_chip(to_chip),
         mid_token,
         mid_grad,
+        second,
         count,
         gain[None],
-        weights[1:],
+        w_out,
+        weights[1:3],
     )
-    pieces = gathered_rows(normin)
-    q, own_top, own_bottom, w_full = project(where, pieces, weights)
-    dout, dout_b = whole_dout(dout, second, pieces[6])
-    out_mine, out_theirs = rows_out(w_out, turn, core)
-    da = dattended(where, gathered_rows(dout_b), out_mine, out_theirs)
-    pair_top, far_bottom = other_pair(own_top), across(own_bottom, 0)
-    pair_bottom, far_top = other_pair(own_bottom), across(own_top, 0)
-    cross_top, cross_bottom = across(pair_top, 0), other_pair(far_bottom)
-    blocks = (
-        own_top,
-        own_bottom,
-        pair_top,
-        pair_bottom,
-        far_top,
-        far_bottom,
-        cross_top,
-        cross_bottom,
-    )
-    dq, *grads = attention(where, q, da, blocks, seg)
-    own_top, own_bottom, pair_top, pair_bottom, far_top, far_bottom, cross_top, cross_bottom = grads
-    add = lambda a, b: (a.astype(F32) + b.astype(F32)).astype(WIRE)
-    back_top, back_bottom = across(cross_top, 1), other_pair(cross_bottom)
-    got_bottom, got_far_top = other_pair(pair_bottom), across(far_top, 1)
-    got_top = other_pair(add(pair_top, back_top))
-    got_far_bottom = across(add(far_bottom, back_bottom), 1)
-    parts = (own_top, own_bottom, got_top, got_bottom, got_far_top, got_far_bottom)
-    dnormin = summed_rows(*unproject(dq, parts, w_full, seg), seg)
+    pieces = gathered_rows(both, weights[3])
+    q, own, w_full = project(where, pieces, weights)
+    cross, far, beside = across(own, 0, True), across(own, 0, False), other_pair(own)
+    out_mine, out_theirs = rows_out(out_half, turn, core)
+    da = dattended(where, pieces, out_mine, out_theirs)
+    dq, own, beside, far, cross = attention(where, q, da, (own, beside, far, cross), seg)
+    parts = (own, other_pair(beside), across(far, 1, False), across(cross, 1, True))
+    dnormin = summed_rows(*unproject(dq, parts, w_full, seg))
 
     scaled = dnormin * gain
     dpooled = dout + (scaled - normed * jnp.mean(scaled * normed, axis=-1, keepdims=True)) / rms

time: 168 us -> 154 us (0.917)
  starting transfers between devices: 66.1 us -> 42 us
  waiting for transfers between devices: 55.5 us -> 69.6 us
  Pallas kernels: 20.3 us -> 16.8 us
    ppermute x35 -> x21, starting transfers between devices: 34.7 us -> 14.2 us  [moved(): return lax.ppermute(value, 'ctx', pairs)]
    ppermute x35 -> x21, waiting for transfers between devices: 36.7 us -> 50.5 us  [moved(): return lax.ppermute(value, 'ctx', pairs)]
    ppermute x3, waiting for transfers between devices: 11.2 us -> 7.72 us  [shifted_y(): return lax.ppermute(value, 'dp', pairs)]
    ppermute x1, starting transfers between devices: 5.08 us -> 2.28 us  [two_back(): lax.ppermute(value, 'ctx', [(i, i - CORES) for i in range(CORES, CTX)])]
    all_gather x1, waiting for transfers between devices: 0.01 us -> 2.2 us  [rows_out(): gathered = lax.all_gather(half, 'dp', axis=0, tiled=False)]
    ppermute x1, waiting for transfers between devices: 0.64 us -> 2.46 us  [two_back(): lax.ppermute(value, 'ctx', [(i, i - CORES) for i in range(CORES, CTX)])]
    pallas_call x3 -> x4, Pallas kernels: 6.57 us -> 5.24 us  [the longest x1 3.51 us: project(): pl.pallas_call(project_kernel, out_shape=(bf16(rows, HEAD), bf16(rows, 2...]
    unnamed x30 -> x36, local copies, waits for them, and re-layouts: 5.95 us -> 7.12 us
  transfers between devices with their start and end apart: 44 -> 30, of which waited for: 20 -> 19; matrix products, arithmetic and copies ran while one was open for 1% -> 1% of each run, Pallas kernels for 7% -> 3%
where the time goes in v4:
time: 154 us; the launch traced here: 153 us
  waiting for transfers between devices  69.6 us (45%)
  starting transfers between devices  42 us (27%)
  Pallas kernels  16.8 us (11%)
  between operations  13.8 us (9%)
  local copies, waits for them, and re-layouts  8.46 us (5%)
    ppermute x21, waiting for transfers between devices, moved(): return lax.ppermute(value, 'ctx', pairs)  50.5 us
    ppermute x3, starting transfers between devices, other_chip(): return lax.ppermute(value, 'ctx', pairs)  21.4 us
    ppermute x21, starting transfers between devices, moved(): return lax.ppermute(value, 'ctx', pairs)  14.2 us
    ppermute x3, waiting for transfers between devices, shifted_y(): return lax.ppermute(value, 'dp', pairs)  7.72 us
    pallas_call x1, Pallas kernels, attention(): pl.pallas_call(functools.partial(attention_kernel, 128, seg), out_shape=(...  7.39 us
    unnamed x36, local copies, waits for them, and re-layouts  7.12 us
    ppermute x3, starting transfers between devices, shifted_y(): return lax.ppermute(value, 'dp', pairs)  4.02 us
    ppermute x3, waiting for transfers between devices, other_chip(): return lax.ppermute(value, 'ctx', pairs)  3.65 us
  transfers between devices with their start and end apart: 30, of which 19 were waited for; matrix products, arithmetic and copies ran while one was open for 1% of the time, Pallas kernels for 3%

profile of v4, /device:TPU:6, one launch (start us, length us, event | category | flops | bytes accessed | tf_op | source)
XLA Modules:
  0.0 153.4 jit_solution(2332360010275437633)
XLA Ops:
  10.3 8.7 %collective-permute-start = (s32[64]{0:T(128)S(1)}, s32[64]{0:T(128)S(1)}, u32[]{:S(2)}, u32[]{:S(2)}) collective-permute-start(s32[64]{0:T(128)S(1)} %bitcast.30), channel_id=1, source_target_pairs={{1,2},{2,1},{3,4},{4,3},{5,6},{6,5},{7,8},{8,7},{9,10},{10,9},{11,... | collective-permute-start | bytes 776 | tf_op jit(solution)/shard_map/ppermute | solution.py:42
  20.6 3.1 %collective-permute-done.2.theirs_hbm = bf16[128,384]{1,0:T(8,128)(2,1)S(1)} collective-permute-done((bf16[128,384]{1,0:T(8,128)(2,1)S(1)}, bf16[128,384]{1,0:T(8,128)(2,1)S(1)}, u32[]{:S(2)}, u32[]{:S(2)}) %collective-permute-start.2) | collective-permute-done | bytes 98336 | tf_op jit(solution)/shard_map/ppermute | solution.py:109
  26.8 4.1 %collective-permute-start.4 = (bf16[64,2048]{1,0:T(8,128)(2,1)S(1)}, bf16[64,2048]{1,0:T(8,128)(2,1)S(1)}, u32[]{:S(2)}, u32[]{:S(2)}) collective-permute-start(bf16[64,2048]{1,0:T(8,128)(2,1)S(1)} %get-tuple-element.38), channel_id=1, source_target_pairs={{1,2},{2,1},{3,4},{4,3},{5,6},{6,5},{7,8},{8,7},{9,10},{10,9},{11,... | collective-permute-start | bytes 786440 | tf_op jit(solution)/shard_map/ppermute | solution.py:42
  31.0 3.1 %collective-permute-start.7 = (bf16[256,384]{1,0:T(8,128)(2,1)S(1)}, bf16[256,384]{1,0:T(8,128)(2,1)S(1)}, u32[]{:S(2)}, u32[]{:S(2)}) collective-permute-start(bf16[256,384]{1,0:T(8,128)(2,1)S(1)} %get-tuple-element.42.refs_9_), channel_id=1, source_target_pairs={{0,96},{32,0},{64,32},{96,64},{128,224},{160,128},{192,160},{224,1... | collective-permute-start | bytes 589832 | tf_op jit(solution)/shard_map/ppermute | solution.py:114
  34.0 2.3 %collective-permute-start.5 = (f32[1,1024]{1,0:T(1,128)S(1)}, f32[1,1024]{1,0:T(1,128)S(1)}, u32[]{:S(2)}, u32[]{:S(2)}) collective-permute-start(f32[1,1024]{1,0:T(1,128)S(1)} %get-tuple-element.41), channel_id=1, source_target_pairs={{2,0},{3,1},{4,2},{5,3},{6,4},{7,5},{8,6},{9,7},{10,8},{11,9},{12,... | collective-permute-start | bytes 12296 | tf_op jit(solution)/shard_map/ppermute | solution.py:46
  37.1 2.5 %collective-permute-done.5.second_ref = f32[1,1024]{1,0:T(1,128)S(1)} collective-permute-done((f32[1,1024]{1,0:T(1,128)S(1)}, f32[1,1024]{1,0:T(1,128)S(1)}, u32[]{:S(2)}, u32[]{:S(2)}) %collective-permute-start.5) | collective-permute-done | bytes 4128 | tf_op jit(solution)/shard_map/ppermute | solution.py:46
  44.3 6.3 %collective-permute-done.13.ready_ref.refs_12_ = bf16[256,384]{1,0:T(8,128)(2,1)S(1)} collective-permute-done((bf16[256,384]{1,0:T(8,128)(2,1)S(1)}, bf16[256,384]{1,0:T(8,128)(2,1)S(1)}, u32[]{:S(2)}, u32[]{:S(2)}) %collective-permute-start.13) | collective-permute-done | bytes 196640 | tf_op jit(solution)/shard_map/ppermute | solution.py:114
  50.7 8.0 %collective-permute-done.9.value_ref.refs_3_ = bf16[64,2048]{1,0:T(8,128)(2,1)S(1)} collective-permute-done((bf16[64,2048]{1,0:T(8,128)(2,1)S(1)}, bf16[64,2048]{1,0:T(8,128)(2,1)S(1)}, u32[]{:S(2)}, u32[]{:S(2)}) %collective-permute-start.9) | collective-permute-done | bytes 262176 | tf_op jit(solution)/shard_map/ppermute | solution.py:37
  59.5 10.5 %collective-permute-done.14.refs_7_ = bf16[64,2048]{1,0:T(8,128)(2,1)S(1)} collective-permute-done((bf16[64,2048]{1,0:T(8,128)(2,1)S(1)}, bf16[64,2048]{1,0:T(8,128)(2,1)S(1)}, u32[]{:S(2)}, u32[]{:S(2)}) %collective-permute-start.14) | collective-permute-done | bytes 262176 | tf_op jit(solution)/shard_map/ppermute | solution.py:37
  72.5 3.5 %shard_map.86 = (bf16[512,128]{1,0:T(8,128)(2,1)S(1)}, bf16[512,256]{1,0:T(8,128)(2,1)}, bf16[1024,384]{1,0:T(8,128)(2,1)S(1)}) custom-call(s32[6]{0:T(128)S(1)} %stack.35.place_ref.refs_0_, bf16[64,2048]{1,0:T(8,128)(2,1)S(1)} %get-tuple-element.44.refs_1_, bf16[64,2048]{1,0:T(8,128)(2,1)S(1)} %collective-permute-done.8.refs_2_, ...), custom_call_target="tpu_custom_call" | custom-call | tf_op jit(solution)/shard_map/pallas_call | solution.py:313
  79.3 2.2 %all-gather.3.cloned.1.call-done = bf16[512,1024]{1,0:T(8,128)(2,1)} async-done(((bf16[64,1024]{1,0:T(8,128)(2,1)}), bf16[512,1024]{1,0:T(8,128)(2,1)}) %all-gather.3.cloned.1.call-update) | async-done | bytes 1048592 | tf_op jit(solution)/shard_map/all_gather | solution.py:118
  85.8 4.7 %collective-permute-done.19.refs_6_ = bf16[512,256]{1,0:T(8,128)(2,1)} collective-permute-done((bf16[512,256]{1,0:T(8,128)(2,1)}, bf16[512,256]{1,0:T(8,128)(2,1)}, u32[]{:S(2)}, u32[]{:S(2)}) %collective-permute-start.19) | collective-permute-done | bytes 262176 | tf_op jit(solution)/shard_map/ppermute | solution.py:37
  90.4 4.8 %collective-permute-done.18.refs_5_ = bf16[512,256]{1,0:T(8,128)(2,1)} collective-permute-done((bf16[512,256]{1,0:T(8,128)(2,1)}, bf16[512,256]{1,0:T(8,128)(2,1)}, u32[]{:S(2)}, u32[]{:S(2)}) %collective-permute-start.18) | collective-permute-done | bytes 262176 | tf_op jit(solution)/shard_map/ppermute | solution.py:37
  95.2 7.4 %shard_map.88 = (bf16[512,128]{1,0:T(8,128)(2,1)S(1)}, bf16[512,256]{1,0:T(8,128)(2,1)S(1)}, bf16[512,256]{1,0:T(8,128)(2,1)S(1)}, bf16[512,256]{1,0:T(8,128)(2,1)S(1)}, bf16[512,256]{1,0:T(8,128)(2,1)S(1)}) custom-call(s32[6]{0:T(128)S(1)} %stack.35.place_ref.refs_0_, bf16[512,128]{1,0:T(8,128)(2,1)S(1)} %copy-done.16, ...), custom_call_target="tpu_custom_call" | custom-call | flops 1610612736 | bytes 2490368 | tf_op jit(solution)/shard_map/pallas_call | solution.py:411
  102.7 2.5 %collective-permute-start.21 = (bf16[512,256]{1,0:T(8,128)(2,1)S(1)}, bf16[512,256]{1,0:T(8,128)(2,1)S(1)}, u32[]{:S(2)}, u32[]{:S(2)}) collective-permute-start(bf16[512,256]{1,0:T(8,128)(2,1)S(1)} %get-tuple-element.51), channel_id=1, source_target_pairs={{16,0},{17,1},{18,2},{19,3},{20,4},{21,5},{22,6},{23,7},{24,8},{25... | collective-permute-start | bytes 786440 | tf_op jit(solution)/shard_map/ppermute | solution.py:37
  105.2 2.7 %collective-permute-start.22 = (bf16[512,256]{1,0:T(8,128)(2,1)S(1)}, bf16[512,256]{1,0:T(8,128)(2,1)S(1)}, u32[]{:S(2)}, u32[]{:S(2)}) collective-permute-start(bf16[512,256]{1,0:T(8,128)(2,1)S(1)} %get-tuple-element.52), channel_id=1, source_target_pairs={{16,2},{17,3},{18,0},{19,1},{20,6},{21,7},{22,4},{23,5},{24,10},{2... | collective-permute-start | bytes 786440 | tf_op jit(solution)/shard_map/ppermute | solution.py:37
  108.0 3.9 %collective-permute-done.20.refs_1_ = bf16[512,256]{1,0:T(8,128)(2,1)S(1)} collective-permute-done((bf16[512,256]{1,0:T(8,128)(2,1)S(1)}, bf16[512,256]{1,0:T(8,128)(2,1)S(1)}, u32[]{:S(2)}, u32[]{:S(2)}) %collective-permute-start.20) | collective-permute-done | bytes 262176 | tf_op jit(solution)/shard_map/ppermute | solution.py:37
  111.9 4.0 %collective-permute-done.21.refs_2_ = bf16[512,256]{1,0:T(8,128)(2,1)S(1)} collective-permute-done((bf16[512,256]{1,0:T(8,128)(2,1)S(1)}, bf16[512,256]{1,0:T(8,128)(2,1)S(1)}, u32[]{:S(2)}, u32[]{:S(2)}) %collective-permute-start.21) | collective-permute-done | bytes 262176 | tf_op jit(solution)/shard_map/ppermute | solution.py:37
  116.8 1.9 %collective-permute-done.23.swapped = bf16[256,1024]{1,0:T(8,128)(2,1)S(1)} collective-permute-done((bf16[256,1024]{1,0:T(8,128)(2,1)S(1)}, bf16[256,1024]{1,0:T(8,128)(2,1)S(1)}, u32[]{:S(2)}, u32[]{:S(2)}) %collective-permute-start.23) | collective-permute-done | bytes 524320 | tf_op jit(solution)/shard_map/ppermute | solution.py:37
  119.3 3.1 %collective-permute-start.24 = (bf16[64,1024]{1,0:T(8,128)(2,1)S(1)}, bf16[64,1024]{1,0:T(8,128)(2,1)S(1)}, u32[]{:S(2)}, u32[]{:S(2)}) collective-permute-start(bf16[64,1024]{1,0:T(8,128)(2,1)S(1)} %get-tuple-element.60), channel_id=1, source_target_pairs={{0,13},{1,4},{2,15},{3,6},{4,1},{5,8},{6,3},{7,10},{8,5},{9,12},{1... | collective-permute-start | bytes 393224 | tf_op jit(solution)/shard_map/ppermute | solution.py:37
  122.4 4.0 %collective-permute-done.25 = bf16[64,1024]{1,0:T(8,128)(2,1)S(1)} collective-permute-done((bf16[64,1024]{1,0:T(8,128)(2,1)S(1)}, bf16[64,1024]{1,0:T(8,128)(2,1)S(1)}, u32[]{:S(2)}, u32[]{:S(2)}) %collective-permute-start.25) | collective-permute-done | bytes 131104 | tf_op jit(solution)/shard_map/ppermute | solution.py:37
  128.9 4.5 %collective-permute-done.26 = bf16[64,1024]{1,0:T(8,128)(2,1)S(1)} collective-permute-done((bf16[64,1024]{1,0:T(8,128)(2,1)S(1)}, bf16[64,1024]{1,0:T(8,128)(2,1)S(1)}, u32[]{:S(2)}, u32[]{:S(2)}) %collective-permute-start.26) | collective-permute-done | bytes 131104 | tf_op jit(solution)/shard_map/ppermute | solution.py:37
  133.9 8.5 %collective-permute-start.27 = (bf16[64,1024]{1,0:T(8,128)(2,1)S(1)}, bf16[64,1024]{1,0:T(8,128)(2,1)S(1)}, u32[]{:S(2)}, u32[]{:S(2)}) collective-permute-start(bf16[64,1024]{1,0:T(8,128)(2,1)S(1)} %divide_convert_fusion), channel_id=1, source_target_pairs={{1,2},{2,1},{3,4},{4,3},{5,6},{6,5},{7,8},{8,7},{9,10},{10,9},{11,... | collective-permute-start | bytes 393224 | tf_op jit(solution)/shard_map/ppermute | solution.py:42
  142.4 2.6 %collective-permute-done.27 = bf16[64,1024]{1,0:T(8,128)(2,1)S(1)} collective-permute-done((bf16[64,1024]{1,0:T(8,128)(2,1)S(1)}, bf16[64,1024]{1,0:T(8,128)(2,1)S(1)}, u32[]{:S(2)}, u32[]{:S(2)}) %collective-permute-start.27) | collective-permute-done | bytes 131104 | tf_op jit(solution)/shard_map/ppermute | solution.py:42
  (100 shorter events, 30.6 us)
Async XLA Ops:
  6.5 75.0 %all-gather.3.cloned.1.call-start = ((), (), s32[]{:S(2)}) async-start(), calls=%async_computation | async-start | bytes 1179648 | tf_op jit(solution)/shard_map/all_gather | solution.py:118
  10.2 9.0 %collective-permute-start.1 = (s32[64]{0:T(128)S(1)}, s32[64]{0:T(128)S(1)}, u32[]{:S(2)}, u32[]{:S(2)}) collective-permute-start(s32[64]{0:T(128)S(1)} %bitcast.29), channel_id=1, source_target_pairs={{0,1},{1,0},{2,3},{3,2},{4,5},{5,4},{6,7},{7,6},{8,9},{9,8},{10,11... | collective-permute-start | bytes 776 | tf_op jit(solution)/shard_map/ppermute | solution.py:37
  10.3 10.0 %collective-permute-start = (s32[64]{0:T(128)S(1)}, s32[64]{0:T(128)S(1)}, u32[]{:S(2)}, u32[]{:S(2)}) collective-permute-start(s32[64]{0:T(128)S(1)} %bitcast.30), channel_id=1, source_target_pairs={{1,2},{2,1},{3,4},{4,3},{5,6},{6,5},{7,8},{8,7},{9,10},{10,9},{11,... | collective-permute-start | bytes 776 | tf_op jit(solution)/shard_map/ppermute | solution.py:42
  26.7 14.2 %collective-permute-start.3 = (bf16[64,2048]{1,0:T(8,128)(2,1)S(1)}, bf16[64,2048]{1,0:T(8,128)(2,1)S(1)}, u32[]{:S(2)}, u32[]{:S(2)}) collective-permute-start(bf16[64,2048]{1,0:T(8,128)(2,1)S(1)} %get-tuple-element.37), channel_id=1, source_target_pairs={{0,1},{1,0},{2,3},{3,2},{4,5},{5,4},{6,7},{7,6},{8,9},{9,8},{10,11... | collective-permute-start | bytes 786440 | tf_op jit(solution)/shard_map/ppermute | solution.py:37
  26.8 14.1 %collective-permute-start.4 = (bf16[64,2048]{1,0:T(8,128)(2,1)S(1)}, bf16[64,2048]{1,0:T(8,128)(2,1)S(1)}, u32[]{:S(2)}, u32[]{:S(2)}) collective-permute-start(bf16[64,2048]{1,0:T(8,128)(2,1)S(1)} %get-tuple-element.38), channel_id=1, source_target_pairs={{1,2},{2,1},{3,4},{4,3},{5,6},{6,5},{7,8},{8,7},{9,10},{10,9},{11,... | collective-permute-start | bytes 786440 | tf_op jit(solution)/shard_map/ppermute | solution.py:42
  31.0 8.6 %collective-permute-start.7 = (bf16[256,384]{1,0:T(8,128)(2,1)S(1)}, bf16[256,384]{1,0:T(8,128)(2,1)S(1)}, u32[]{:S(2)}, u32[]{:S(2)}) collective-permute-start(bf16[256,384]{1,0:T(8,128)(2,1)S(1)} %get-tuple-element.42.refs_9_), channel_id=1, source_target_pairs={{0,96},{32,0},{64,32},{96,64},{128,224},{160,128},{192,160},{224,1... | collective-permute-start | bytes 589832 | tf_op jit(solution)/shard_map/ppermute | solution.py:114
  43.3 15.4 %collective-permute-start.9 = (bf16[64,2048]{1,0:T(8,128)(2,1)S(1)}, bf16[64,2048]{1,0:T(8,128)(2,1)S(1)}, u32[]{:S(2)}, u32[]{:S(2)}) collective-permute-start(bf16[64,2048]{1,0:T(8,128)(2,1)S(1)} %get-tuple-element.44.refs_1_), channel_id=1, source_target_pairs={{0,4},{1,13},{2,6},{3,15},{4,8},{5,1},{6,10},{7,3},{8,12},{9,5},{1... | collective-permute-start | bytes 786440 | tf_op jit(solution)/shard_map/ppermute | solution.py:37
  43.4 7.3 %collective-permute-start.13 = (bf16[256,384]{1,0:T(8,128)(2,1)S(1)}, bf16[256,384]{1,0:T(8,128)(2,1)S(1)}, u32[]{:S(2)}, u32[]{:S(2)}) collective-permute-start(bf16[256,384]{1,0:T(8,128)(2,1)S(1)} %get-tuple-element.42.refs_9_), channel_id=1, source_target_pairs={{0,64},{32,96},{64,0},{96,32},{128,192},{160,224},{192,128},{224,1... | collective-permute-start | bytes 589832 | tf_op jit(solution)/shard_map/ppermute | solution.py:114
  44.3 15.1 %collective-permute-start.10 = (bf16[64,2048]{1,0:T(8,128)(2,1)S(1)}, bf16[64,2048]{1,0:T(8,128)(2,1)S(1)}, u32[]{:S(2)}, u32[]{:S(2)}) collective-permute-start(bf16[64,2048]{1,0:T(8,128)(2,1)S(1)} %get-tuple-element.44.refs_1_), channel_id=1, source_target_pairs={{0,13},{1,4},{2,15},{3,6},{4,1},{5,8},{6,3},{7,10},{8,5},{9,12},{1... | collective-permute-start | bytes 786440 | tf_op jit(solution)/shard_map/ppermute | solution.py:37
  58.7 11.3 %collective-permute-start.14 = (bf16[64,2048]{1,0:T(8,128)(2,1)S(1)}, bf16[64,2048]{1,0:T(8,128)(2,1)S(1)}, u32[]{:S(2)}, u32[]{:S(2)}) collective-permute-start(bf16[64,2048]{1,0:T(8,128)(2,1)S(1)} %shard_map.85), channel_id=1, source_target_pairs={{0,4},{1,13},{2,6},{3,15},{4,8},{5,1},{6,10},{7,3},{8,12},{9,5},{1... | collective-permute-start | bytes 786440 | tf_op jit(solution)/shard_map/ppermute | solution.py:37
  58.8 11.2 %collective-permute-start.8 = (bf16[64,2048]{1,0:T(8,128)(2,1)S(1)}, bf16[64,2048]{1,0:T(8,128)(2,1)S(1)}, u32[]{:S(2)}, u32[]{:S(2)}) collective-permute-start(bf16[64,2048]{1,0:T(8,128)(2,1)S(1)} %get-tuple-element.44.refs_1_), channel_id=1, source_target_pairs={{0,1},{1,0},{2,3},{3,2},{4,5},{5,4},{6,7},{7,6},{8,9},{9,8},{10,11... | collective-permute-start | bytes 786440 | tf_op jit(solution)/shard_map/ppermute | solution.py:37
  58.9 11.1 %collective-permute-start.11 = (bf16[64,2048]{1,0:T(8,128)(2,1)S(1)}, bf16[64,2048]{1,0:T(8,128)(2,1)S(1)}, u32[]{:S(2)}, u32[]{:S(2)}) collective-permute-start(bf16[64,2048]{1,0:T(8,128)(2,1)S(1)} %collective-permute-done.9.value_ref.refs_3_), channel_id=1, source_target_pairs={{0,1},{1,0},{2,3},{3,2},{4,5},{5,4},{6,7},{7,6},{8,9},{9,8},{10,11... | collective-permute-start | bytes 786440 | tf_op jit(solution)/shard_map/ppermute | solution.py:37
  59.4 10.6 %collective-permute-start.12 = (bf16[64,2048]{1,0:T(8,128)(2,1)S(1)}, bf16[64,2048]{1,0:T(8,128)(2,1)S(1)}, u32[]{:S(2)}, u32[]{:S(2)}) collective-permute-start(bf16[64,2048]{1,0:T(8,128)(2,1)S(1)} %collective-permute-done.10.refs_4_), channel_id=1, source_target_pairs={{0,1},{1,0},{2,3},{3,2},{4,5},{5,4},{6,7},{7,6},{8,9},{9,8},{10,11... | collective-permute-start | bytes 786440 | tf_op jit(solution)/shard_map/ppermute | solution.py:37
  76.6 13.8 %collective-permute-start.19 = (bf16[512,256]{1,0:T(8,128)(2,1)}, bf16[512,256]{1,0:T(8,128)(2,1)}, u32[]{:S(2)}, u32[]{:S(2)}) collective-permute-start(bf16[512,256]{1,0:T(8,128)(2,1)} %get-tuple-element.47.refs_3_), channel_id=1, source_target_pairs={{0,18},{1,19},{2,16},{3,17},{4,22},{5,23},{6,20},{7,21},{8,26},{9,... | collective-permute-start | bytes 786440 | tf_op jit(solution)/shard_map/ppermute | solution.py:37
  77.9 17.3 %collective-permute-start.18 = (bf16[512,256]{1,0:T(8,128)(2,1)}, bf16[512,256]{1,0:T(8,128)(2,1)}, u32[]{:S(2)}, u32[]{:S(2)}) collective-permute-start(bf16[512,256]{1,0:T(8,128)(2,1)} %get-tuple-element.47.refs_3_), channel_id=1, source_target_pairs={{0,16},{1,17},{2,18},{3,19},{4,20},{5,21},{6,22},{7,23},{8,24},{9,... | collective-permute-start | bytes 786440 | tf_op jit(solution)/shard_map/ppermute | solution.py:37
  79.2 16.0 %collective-permute-start.17 = (bf16[512,256]{1,0:T(8,128)(2,1)}, bf16[512,256]{1,0:T(8,128)(2,1)}, u32[]{:S(2)}, u32[]{:S(2)}) collective-permute-start(bf16[512,256]{1,0:T(8,128)(2,1)} %get-tuple-element.47.refs_3_), channel_id=1, source_target_pairs={{0,2},{1,3},{2,0},{3,1},{4,6},{5,7},{6,4},{7,5},{8,10},{9,11},{10,... | collective-permute-start | bytes 786440 | tf_op jit(solution)/shard_map/ppermute | solution.py:37
  102.6 9.3 %collective-permute-start.20 = (bf16[512,256]{1,0:T(8,128)(2,1)S(1)}, bf16[512,256]{1,0:T(8,128)(2,1)S(1)}, u32[]{:S(2)}, u32[]{:S(2)}) collective-permute-start(bf16[512,256]{1,0:T(8,128)(2,1)S(1)} %get-tuple-element.50), channel_id=1, source_target_pairs={{0,2},{1,3},{2,0},{3,1},{4,6},{5,7},{6,4},{7,5},{8,10},{9,11},{10,... | collective-permute-start | bytes 786440 | tf_op jit(solution)/shard_map/ppermute | solution.py:37
  102.7 13.2 %collective-permute-start.21 = (bf16[512,256]{1,0:T(8,128)(2,1)S(1)}, bf16[512,256]{1,0:T(8,128)(2,1)S(1)}, u32[]{:S(2)}, u32[]{:S(2)}) collective-permute-start(bf16[512,256]{1,0:T(8,128)(2,1)S(1)} %get-tuple-element.51), channel_id=1, source_target_pairs={{16,0},{17,1},{18,2},{19,3},{20,4},{21,5},{22,6},{23,7},{24,8},{25... | collective-permute-start | bytes 786440 | tf_op jit(solution)/shard_map/ppermute | solution.py:37
  105.2 10.7 %collective-permute-start.22 = (bf16[512,256]{1,0:T(8,128)(2,1)S(1)}, bf16[512,256]{1,0:T(8,128)(2,1)S(1)}, u32[]{:S(2)}, u32[]{:S(2)}) collective-permute-start(bf16[512,256]{1,0:T(8,128)(2,1)S(1)} %get-tuple-element.52), channel_id=1, source_target_pairs={{16,2},{17,3},{18,0},{19,1},{20,6},{21,7},{22,4},{23,5},{24,10},{2... | collective-permute-start | bytes 786440 | tf_op jit(solution)/shard_map/ppermute | solution.py:37
  118.8 7.6 %collective-permute-start.25 = (bf16[64,1024]{1,0:T(8,128)(2,1)S(1)}, bf16[64,1024]{1,0:T(8,128)(2,1)S(1)}, u32[]{:S(2)}, u32[]{:S(2)}) collective-permute-start(bf16[64,1024]{1,0:T(8,128)(2,1)S(1)} %get-tuple-element.62), channel_id=1, source_target_pairs={{0,12},{1,5},{2,14},{3,7},{4,0},{5,9},{6,2},{7,11},{8,4},{9,13},{1... | collective-permute-start | bytes 393224 | tf_op jit(solution)/shard_map/ppermute | solution.py:37
  119.3 9.6 %collective-permute-start.24 = (bf16[64,1024]{1,0:T(8,128)(2,1)S(1)}, bf16[64,1024]{1,0:T(8,128)(2,1)S(1)}, u32[]{:S(2)}, u32[]{:S(2)}) collective-permute-start(bf16[64,1024]{1,0:T(8,128)(2,1)S(1)} %get-tuple-element.60), channel_id=1, source_target_pairs={{0,13},{1,4},{2,15},{3,6},{4,1},{5,8},{6,3},{7,10},{8,5},{9,12},{1... | collective-permute-start | bytes 393224 | tf_op jit(solution)/shard_map/ppermute | solution.py:37
  126.4 7.0 %collective-permute-start.26 = (bf16[64,1024]{1,0:T(8,128)(2,1)S(1)}, bf16[64,1024]{1,0:T(8,128)(2,1)S(1)}, u32[]{:S(2)}, u32[]{:S(2)}) collective-permute-start(bf16[64,1024]{1,0:T(8,128)(2,1)S(1)} %add_convert_fusion.1), channel_id=1, source_target_pairs={{0,12},{1,5},{2,14},{3,7},{4,0},{5,9},{6,2},{7,11},{8,4},{9,13},{1... | collective-permute-start | bytes 393224 | tf_op jit(solution)/shard_map/ppermute | solution.py:37
  133.8 8.7 %collective-permute-start.28 = (bf16[64,1024]{1,0:T(8,128)(2,1)S(1)}, bf16[64,1024]{1,0:T(8,128)(2,1)S(1)}, u32[]{:S(2)}, u32[]{:S(2)}) collective-permute-start(bf16[64,1024]{1,0:T(8,128)(2,1)S(1)} %divide_convert_fusion), channel_id=1, source_target_pairs={{0,1},{1,0},{2,3},{3,2},{4,5},{5,4},{6,7},{7,6},{8,9},{9,8},{10,11... | collective-permute-start | bytes 393224 | tf_op jit(solution)/shard_map/ppermute | solution.py:37
  133.9 11.2 %collective-permute-start.27 = (bf16[64,1024]{1,0:T(8,128)(2,1)S(1)}, bf16[64,1024]{1,0:T(8,128)(2,1)S(1)}, u32[]{:S(2)}, u32[]{:S(2)}) collective-permute-start(bf16[64,1024]{1,0:T(8,128)(2,1)S(1)} %divide_convert_fusion), channel_id=1, source_target_pairs={{1,2},{2,1},{3,4},{4,3},{5,6},{6,5},{7,8},{8,7},{9,10},{10,9},{11,... | collective-permute-start | bytes 393224 | tf_op jit(solution)/shard_map/ppermute | solution.py:42
  (24 other events, 170.9 us)
Sparse Core Ops, SparseCore 0:
  43.4 38.0 all-gather.2

commit v5 on v4

--- a/solution.py
+++ b/solution.py
@@ -11,7 +11,6 @@
 HEAD = 128
 HALVES, TURNS, PAIR, CORES = 2, 4, 2, 2
 CTX = HALVES * TURNS * PAIR * CORES
-ROWS_X, ROWS_Y = 2, 4
 NEG = -1e30
 WIRE = jnp.bfloat16
 F32 = jnp.float32
@@ -77,68 +76,55 @@
     return lax.dot_general(left, right, (((0,), (0,)), ((), ())), preferred_element_type=F32)
 
 
-def cut_kernel(head_ref, q_ref, k_ref, v_ref, start_ref, out_ref, start_out):
-    out_ref[:, :HEAD] = q_ref[...]
-    out_ref[:, HEAD : 2 * HEAD] = k_ref[...]
-    out_ref[:, 2 * HEAD :] = v_ref[...]
-    start_out[...] = start_ref[...]
-
-
-def columns_in(w_query, w_key, w_value, starts, head):
-    rows = w_query.shape[0]
-    block = pl.BlockSpec((rows, HEAD), lambda i, h: (0, h[0]))
-    whole = pl.BlockSpec(starts.shape, lambda i, h: (0, 0))
+def cut_kernel(place_ref, q_ref, k_ref, v_ref, o_ref, start_ref, out_ref, start_out, sems):
+    rows = out_ref.shape[0]
+    half, width = rows // CORES, o_ref.shape[1]
+    core = place_ref[3]
+    lane = pl.multiple_of((place_ref[1] * CORES + core) * HEAD, HEAD)
+    copies = [
+        (w.at[:, pl.ds(lane, HEAD)], out_ref.at[:, i * HEAD : (i + 1) * HEAD])
+        for i, w in enumerate((q_ref, k_ref, v_ref))
+    ]
+    at = pl.multiple_of(core * half, half)
+    for i in range(2):
+        lanes = slice(i * width // 2, (i + 1) * width // 2)
+        copies.append(
+            (o_ref.at[pl.ds(at, half), lanes], out_ref.at[i * half : (i + 1) * half, 3 * HEAD :])
+        )
+    copies.append((start_ref, start_out))
+    fetched(copies, sems)
+
+
+def cut_weights(where, w_query, w_key, w_value, w_out, starts):
+    rows, width = w_out.shape
     return pl.pallas_call(
         cut_kernel,
-        grid_spec=pltpu.PrefetchScalarGridSpec(
-            num_scalar_prefetch=1,
-            grid=(1,),
-            in_specs=[block] * 3 + [whole],
-            out_specs=(pl.BlockSpec((rows, 3 * HEAD), lambda i, h: (0, 0)), whole),
-        ),
         out_shape=(
-            jax.ShapeDtypeStruct((rows, 3 * HEAD), w_query.dtype),
+            jax.ShapeDtypeStruct((rows, 3 * HEAD + width // 2), w_query.dtype),
             jax.ShapeDtypeStruct(starts.shape, starts.dtype),
         ),
-        compiler_params=PARAMS,
-    )(head[None], w_query, w_key, w_value, starts)
-
-
-def other_x(value):
-    count = ROWS_X * ROWS_Y
-    return lax.ppermute(value, "dp", [(d, (d + ROWS_Y) % count) for d in range(count)])
-
-
-def shifted_y(value, step):
-    pairs = [(d, d // ROWS_Y * ROWS_Y + (d + step) % ROWS_Y) for d in range(ROWS_X * ROWS_Y)]
-    return lax.ppermute(value, "dp", pairs)
-
-
-def rows_out(half, turn, core):
-    gathered = lax.all_gather(half, "dp", axis=0, tiled=False)
-    mine = lax.dynamic_index_in_dim(gathered, turn * CORES + core, 0, keepdims=False)
-    theirs = lax.dynamic_index_in_dim(gathered, turn * CORES + 1 - core, 0, keepdims=False)
+        in_specs=[SMEM] + [ANY] * 5,
+        out_specs=(VMEM, VMEM),
+        scratch_shapes=[pltpu.SemaphoreType.DMA((6,))],
+        compiler_params=PARAMS,
+    )(where, w_query, w_key, w_value, w_out, starts)
+
+
+def gathered_weights(mine):
+    return lax.all_gather(mine, "dp", axis=0, tiled=False)
+
+
+def rows_out(weights, turn, core):
+    rows = weights[:, :, 3 * HEAD :]
+    mine = lax.dynamic_index_in_dim(rows, turn * CORES + core, 0, keepdims=False)
+    theirs = lax.dynamic_index_in_dim(rows, turn * CORES + 1 - core, 0, keepdims=False)
     return mine, other_core(theirs)
 
 
-def pass_kernel(value_ref, ready_ref, out_ref):
-    out_ref[...] = value_ref[...]
-
-
-def passed_on(value, ready):
-    return pl.pallas_call(
-        pass_kernel,
-        out_shape=jax.ShapeDtypeStruct(value.shape, value.dtype),
-        in_specs=[VMEM, ANY],
-        out_specs=VMEM,
-        compiler_params=PARAMS,
-    )(value, ready)
-
-
-def gathered_rows(shard, ready):
+def gathered_rows(shard):
     near = turned(shard, 1)
     next_to = turned_over(shard)
-    far = turned(passed_on(near, ready), 1)
+    far = turned(near, 1)
     return [
         shard,
         other_core(shard),
@@ -179,21 +165,12 @@
     return copies
 
 
-def window_kernel(place_ref, edge_ref, token_hbm, grad_hbm, mine_hbm, theirs_hbm, *refs):
-    core_ref, chip_ref, mid_token, mid_grad, first_ref, both_ref = refs[:6]
-    token_ref, grad_ref, sems = refs[6:]
+def window_kernel(place_ref, edge_ref, token_hbm, grad_hbm, *refs):
+    core_ref, chip_ref, mid_token, mid_grad, first_ref = refs[:5]
+    token_ref, grad_ref, sems = refs[5:]
     rows, width = token_ref.shape
     seg = mid_token.shape[0]
-    half = mine_hbm.shape[0]
-    fetched(
-        [
-            (token_hbm, token_ref),
-            (grad_hbm, grad_ref),
-            (mine_hbm, both_ref.at[:half, :]),
-            (theirs_hbm, both_ref.at[half:, :]),
-        ],
-        sems,
-    )
+    fetched([(token_hbm, token_ref), (grad_hbm, grad_ref)], sems)
     ctx, core = place_ref[5], place_ref[3]
     at = lax.broadcasted_iota(jnp.int32, (1, rows), 1) + ctx * rows
     opens, ends, nexts = edge_ref[0], edge_ref[1], edge_ref[2]
@@ -221,7 +198,7 @@
         send(core_ref, chip_ref)
 
 
-def window_sums(where, edges, tokens, grads, mine, theirs, seg):
+def window_sums(where, edges, tokens, grads, seg):
     rows, width = tokens.shape
     shape = jax.ShapeDtypeStruct
     return pl.pallas_call(
@@ -232,83 +209,83 @@
             shape((seg, width), F32),
             shape((seg, width), F32),
             shape((1, width), F32),
-            shape((2 * mine.shape[0], mine.shape[1]), mine.dtype),
         ),
-        in_specs=[SMEM, VMEM] + [ANY] * 4,
-        out_specs=(VMEM,) * 6,
+        in_specs=[SMEM, VMEM] + [ANY] * 2,
+        out_specs=(VMEM,) * 5,
         scratch_shapes=[
             pltpu.VMEM((rows, width), tokens.dtype),
             pltpu.VMEM((rows, width), grads.dtype),
-            pltpu.SemaphoreType.DMA((4,)),
+            pltpu.SemaphoreType.DMA((2,)),
         ],
         compiler_params=PARAMS,
-    )(where, edges, tokens, grads, mine, theirs)
-
-
-def norm_kernel(place_ref, core_ref, chip_ref, mid_token, mid_grad, second_ref, count_ref, *refs):
-    gain_ref, w_ref = refs[:2]
-    both_ref, normed_ref, rms_ref, dout_ref, half_ref, sem = refs[-6:]
-    seg, width = mid_token.shape
-    rows = half_ref.shape[0]
-    core = place_ref[3]
-    at = pl.multiple_of(core * rows, rows)
-    copy = pltpu.make_async_copy(w_ref.at[pl.ds(at, rows), :], half_ref, sem)
-    copy.start()
+    )(where, edges, tokens, grads)
+
+
+def norm_kernel(core_ref, chip_ref, mid_token, mid_grad, count_ref, gain_ref, *outs):
+    normin_ref, normed_ref, rms_ref, dout_ref = outs
+    width = mid_token.shape[1]
     got = core_ref[...].astype(F32) + chip_ref[...].astype(F32)
     pooled = (mid_token[...] + got[:, :width]) / count_ref[...]
     rms = jnp.sqrt(jnp.mean(pooled * pooled, axis=1, keepdims=True) + 1e-06)
     normed = pooled / rms
     normed_ref[...] = normed
     rms_ref[...] = rms
-    last = lax.broadcasted_iota(jnp.int32, (seg, 1), 0) == seg - 1
-    dout = mid_grad[...] + got[:, width:] + jnp.where(last, second_ref[...], 0.0)
-    dout_ref[...] = dout
-    both_ref[:, :width] = (normed * gain_ref[...]).astype(jnp.bfloat16)
-    both_ref[:, width:] = dout.astype(jnp.bfloat16)
-    copy.wait()
-
-
-def norm(where, from_core, from_chip, mid_token, mid_grad, second, count, gain, w_out, ready):
+    normin_ref[...] = (normed * gain_ref[...]).astype(jnp.bfloat16)
+    dout_ref[...] = mid_grad[...] + got[:, width:]
+
+
+def norm(from_core, from_chip, mid_token, mid_grad, count, gain):
     seg, width = mid_token.shape
     shape = jax.ShapeDtypeStruct
     return pl.pallas_call(
         norm_kernel,
         out_shape=(
-            shape((seg, 2 * width), jnp.bfloat16),
+            shape((seg, width), jnp.bfloat16),
             shape((seg, width), F32),
             shape((seg, 1), F32),
             shape((seg, width), F32),
-            shape((w_out.shape[0] // CORES, w_out.shape[1]), w_out.dtype),
         ),
-        in_specs=[SMEM] + [VMEM] * 7 + [ANY] * (1 + len(ready)),
-        out_specs=(VMEM,) * 5,
-        scratch_shapes=[pltpu.SemaphoreType.DMA],
-        compiler_params=PARAMS,
-    )(where, from_core, from_chip, mid_token, mid_grad, second, count, gain, w_out, *ready)
+        in_specs=[VMEM] * 6,
+        out_specs=(VMEM,) * 4,
+        compiler_params=PARAMS,
+    )(from_core, from_chip, mid_token, mid_grad, count, gain)
+
+
+def dout_kernel(dout_ref, second_ref, ready_ref, full_ref, half_ref):
+    seg = dout_ref.shape[0]
+    last = lax.broadcasted_iota(jnp.int32, (seg, 1), 0) == seg - 1
+    dout = dout_ref[...] + jnp.where(last, second_ref[...], 0.0)
+    full_ref[...] = dout
+    half_ref[...] = dout.astype(jnp.bfloat16)
+
+
+def whole_dout(dout, second, ready):
+    shape = jax.ShapeDtypeStruct
+    return pl.pallas_call(
+        dout_kernel,
+        out_shape=(shape(dout.shape, F32), shape(dout.shape, jnp.bfloat16)),
+        in_specs=[VMEM, VMEM, ANY],
+        out_specs=(VMEM, VMEM),
+        compiler_params=PARAMS,
+    )(dout, second, ready)
 
 
 def project_kernel(*refs):
-    place_ref, pieces, weights = refs[0], refs[1:9], refs[9:13]
-    q_ref, kv_ref, w_ref, rows, sems = refs[13:]
-    copies = stacked([piece.at[:, : rows.shape[1]] for piece in pieces], rows)
-    dp = place_ref[4]
-    x, y = dp // ROWS_Y, dp % ROWS_Y
-    depth = weights[0].shape[0] // ROWS_X
-    for weight, step in zip(weights, (0, 1, -1, 2)):
-        its_y = (y - step + ROWS_Y) % ROWS_Y
-        for i in range(ROWS_X):
-            its_x = x if i == 0 else 1 - x
-            at = pl.multiple_of((its_x * ROWS_Y + its_y) * depth, depth)
-            copies.append((weight.at[i * depth : (i + 1) * depth, :], w_ref.at[pl.ds(at, depth), :]))
+    pieces, weight = refs[:8], refs[8]
+    q_ref, kv_ref, w_ref, rows, sems = refs[9:]
+    copies = stacked(pieces, rows)
+    depth = weight.shape[1]
+    for i in range(weight.shape[0]):
+        copies.append((weight.at[i, :, : 3 * HEAD], w_ref.at[i * depth : (i + 1) * depth, :]))
     fetched(copies, sems)
     out = jnp.dot(rows[...], w_ref[...], preferred_element_type=F32).astype(jnp.bfloat16)
     q_ref[...] = out[:, :HEAD]
     kv_ref[...] = out[:, HEAD:]
 
 
-def project(where, pieces, weights):
+def project(pieces, weights):
     rows = sum(piece.shape[0] for piece in pieces)
-    width = pieces[0].shape[1] // 2
+    width = pieces[0].shape[1]
     bf16 = lambda *shape: jax.ShapeDtypeStruct(shape, jnp.bfloat16)
     return pl.pallas_call(
         project_kernel,
@@ -317,33 +294,35 @@
             bf16(rows, 2 * HEAD),
             bf16(width, 3 * HEAD),
         ),
-        in_specs=[SMEM] + [ANY] * 12,
+        in_specs=[ANY] * 9,
         out_specs=(VMEM,) * 3,
         scratch_shapes=[
             pltpu.VMEM((rows, width), jnp.bfloat16),
             pltpu.SemaphoreType.DMA((16,)),
         ],
         compiler_params=PARAMS,
-    )(where, *pieces, *weights)
+    )(*pieces, weights)
 
 
 def dattended_kernel(*refs):
     place_ref, pieces, mine, theirs = refs[0], refs[1:9], refs[9], refs[10]
     da_ref, rows, weight, sems = refs[11:]
     core = place_ref[3]
-    half = mine.shape[0]
+    half, wide = mine.shape[0] // 2, mine.shape[1]
     spot = pl.multiple_of(core * half, half)
     other = pl.multiple_of((1 - core) * half, half)
-    copies = stacked([piece.at[:, rows.shape[1] :] for piece in pieces], rows)
-    copies.append((mine, weight.at[pl.ds(spot, half), :]))
-    copies.append((theirs, weight.at[pl.ds(other, half), :]))
+    copies = stacked(pieces, rows)
+    for i in range(2):
+        part, lanes = slice(i * half, (i + 1) * half), slice(i * wide, (i + 1) * wide)
+        copies.append((mine.at[part, :], weight.at[pl.ds(spot, half), lanes]))
+        copies.append((theirs.at[part, :], weight.at[pl.ds(other, half), lanes]))
     fetched(copies, sems)
     da_ref[...] = contract_last(rows[...], weight[...]).astype(jnp.bfloat16)
 
 
 def dattended(where, pieces, mine, theirs):
     rows = sum(piece.shape[0] for piece in pieces)
-    width = pieces[0].shape[1] // 2
+    width = pieces[0].shape[1]
     return pl.pallas_call(
         dattended_kernel,
         out_shape=jax.ShapeDtypeStruct((rows, HEAD), jnp.bfloat16),
@@ -352,7 +331,7 @@
         scratch_shapes=[
             pltpu.VMEM((rows, width), jnp.bfloat16),
             pltpu.VMEM((HEAD, width), jnp.bfloat16),
-            pltpu.SemaphoreType.DMA((10,)),
+            pltpu.SemaphoreType.DMA((12,)),
         ],
         compiler_params=PARAMS,
     )(where, *pieces, mine, theirs)
@@ -490,9 +469,9 @@
     turn, half = ctx // (CORES * PAIR) % TURNS, ctx // (CORES * PAIR * TURNS)
     where = jnp.stack([half, turn, pair, core, lax.axis_index("dp"), ctx])
 
-    mine, own_starts = columns_in(w_query, w_key, w_value, starts, turn * CORES + core)
+    mine, own_starts = cut_weights(where, w_query, w_key, w_value, w_out, starts)
     own_starts = own_starts[0]
-    theirs = other_x(mine)
+    weights = gathered_weights(mine)
     beside, facing = other_core(own_starts), other_chip(own_starts)
     before = jnp.where(core == 0, facing, beside)
     after = jnp.where(core == 0, beside, facing)
@@ -504,28 +483,19 @@
     opens, ends = window[:slots], window[1 : slots + 1]
     edges = jnp.stack([opens, ends, window[2:]])[:, :, None]
     count = (ends - opens)[seg : 2 * seg, None].astype(F32)
-    to_core, to_chip, mid_token, mid_grad, first, both = window_sums(
-        where, edges, token_rows, grad_out, mine, theirs, seg
+    to_core, to_chip, mid_token, mid_grad, first = window_sums(
+        where, edges, token_rows, grad_out, seg
     )
-    weights = [both, shifted_y(both, 1), shifted_y(both, -1), shifted_y(both, 2)]
     second = two_back(first)
-    both, normed, rms, dout, out_half = norm(
-        where,
-        other_core(to_core),
-        other_chip(to_chip),
-        mid_token,
-        mid_grad,
-        second,
-        count,
-        gain[None],
-        w_out,
-        weights[1:3],
+    normin, normed, rms, dout = norm(
+        other_core(to_core), other_chip(to_chip), mid_token, mid_grad, count, gain[None]
     )
-    pieces = gathered_rows(both, weights[3])
-    q, own, w_full = project(where, pieces, weights)
+    pieces = gathered_rows(normin)
+    q, own, w_full = project(pieces, weights)
+    dout, dout_b = whole_dout(dout, second, pieces[2])
     cross, far, beside = across(own, 0, True), across(own, 0, False), other_pair(own)
-    out_mine, out_theirs = rows_out(out_half, turn, core)
-    da = dattended(where, pieces, out_mine, out_theirs)
+    out_mine, out_theirs = rows_out(weights, turn, core)
+    da = dattended(where, gathered_rows(dout_b), out_mine, out_theirs)
     dq, own, beside, far, cross = attention(where, q, da, (own, beside, far, cross), seg)
     parts = (own, other_pair(beside), across(far, 1, False), across(cross, 1, True))
     dnormin = summed_rows(*unproject(dq, parts, w_full, seg))

time: 154 us -> 150 us (0.974)
  waiting for transfers between devices: 69.6 us -> 44.7 us
  starting transfers between devices: 42 us -> 53.8 us
  local copies, waits for them, and re-layouts: 8.46 us -> 16.8 us
    ppermute x21 -> x28, starting transfers between devices: 14.2 us -> 31 us  [moved(): return lax.ppermute(value, 'ctx', pairs)]
    ppermute x21 -> x28, waiting for transfers between devices: 50.5 us -> 34 us  [moved(): return lax.ppermute(value, 'ctx', pairs)]
    ppermute x4 -> x0, waiting for transfers between devices: 10.8 us -> none  [the longest x3 7.72 us: shifted_y(): return lax.ppermute(value, 'dp', pairs)]
    unnamed x36 -> x52, local copies, waits for them, and re-layouts: 7.12 us -> 16.3 us
    ppermute x3, waiting for transfers between devices: 3.65 us -> 10.7 us  [other_chip(): return lax.ppermute(value, 'ctx', pairs)]
    ppermute x4 -> x0, starting transfers between devices: 4.11 us -> none  [the longest x3 4.02 us: shifted_y(): return lax.ppermute(value, 'dp', pairs)]
    ppermute x1, waiting for transfers between devices: 2.46 us -> 0.01 us  [two_back(): lax.ppermute(value, 'ctx', [(i, i - CORES) for i in range(CORES, CTX)])]
    all_gather x1, waiting for transfers between devices: 2.2 us -> 0.01 us  [gathered_weights(): return lax.all_gather(mine, 'dp', axis=0, tiled=False)]
  transfers between devices with their start and end apart: 30 -> 33, of which waited for: 19 -> 13; matrix products, arithmetic and copies ran while one was open for 1% -> 1% of each run, Pallas kernels for 3% -> 5%
where the time goes in v5:
time: 150 us; the launch traced here: 149 us
  starting transfers between devices  53.8 us (36%)
  waiting for transfers between devices  44.7 us (30%)
  Pallas kernels  17.3 us (12%)
  local copies, waits for them, and re-layouts  16.8 us (11%)
  between operations  13.8 us (9%)
    ppermute x28, waiting for transfers between devices, moved(): return lax.ppermute(value, 'ctx', pairs)  34 us
    ppermute x28, starting transfers between devices, moved(): return lax.ppermute(value, 'ctx', pairs)  31 us
    ppermute x3, starting transfers between devices, other_chip(): return lax.ppermute(value, 'ctx', pairs)  19.3 us
    unnamed x52, local copies, waits for them, and re-layouts  16.3 us
    ppermute x3, waiting for transfers between devices, other_chip(): return lax.ppermute(value, 'ctx', pairs)  10.7 us
    pallas_call x1, Pallas kernels, attention(): pl.pallas_call(functools.partial(attention_kernel, 128, seg), out_shape=(...  7.33 us
    ppermute x1, starting transfers between devices, two_back(): lax.ppermute(value, 'ctx', [(i, i - CORES) for i in range(CORES, CTX)])  3.48 us
  transfers between devices with their start and end apart: 33, of which 13 were waited for; matrix products, arithmetic and copies ran while one was open for 1% of the time, Pallas kernels for 5%

profile of v5, /device:TPU:6, one launch (start us, length us, event | category | flops | bytes accessed | tf_op | source)
XLA Modules:
  0.0 148.9 jit_solution(14309879846130436250)
XLA Ops:
  12.5 8.0 %collective-permute-start = (s32[64]{0:T(128)S(1)}, s32[64]{0:T(128)S(1)}, u32[]{:S(2)}, u32[]{:S(2)}) collective-permute-start(s32[64]{0:T(128)S(1)} %bitcast.30), channel_id=1, source_target_pairs={{1,2},{2,1},{3,4},{4,3},{5,6},{6,5},{7,8},{8,7},{9,10},{10,9},{11,... | collective-permute-start | bytes 776 | tf_op jit(solution)/shard_map/ppermute | solution.py:41
  25.2 7.1 %collective-permute-start.3 = (bf16[64,2048]{1,0:T(8,128)(2,1)S(1)}, bf16[64,2048]{1,0:T(8,128)(2,1)S(1)}, u32[]{:S(2)}, u32[]{:S(2)}) collective-permute-start(bf16[64,2048]{1,0:T(8,128)(2,1)S(1)} %get-tuple-element.37), channel_id=1, source_target_pairs={{1,2},{2,1},{3,4},{4,3},{5,6},{6,5},{7,8},{8,7},{9,10},{10,9},{11,... | collective-permute-start | bytes 786440 | tf_op jit(solution)/shard_map/ppermute | solution.py:41
  32.9 3.9 %collective-permute-done.3.chip_ref = bf16[64,2048]{1,0:T(8,128)(2,1)S(1)} collective-permute-done((bf16[64,2048]{1,0:T(8,128)(2,1)S(1)}, bf16[64,2048]{1,0:T(8,128)(2,1)S(1)}, u32[]{:S(2)}, u32[]{:S(2)}) %collective-permute-start.3) | collective-permute-done | bytes 262176 | tf_op jit(solution)/shard_map/ppermute | solution.py:41
  37.7 3.5 %collective-permute-start.4 = (f32[1,1024]{1,0:T(1,128)S(1)}, f32[1,1024]{1,0:T(1,128)S(1)}, u32[]{:S(2)}, u32[]{:S(2)}) collective-permute-start(f32[1,1024]{1,0:T(1,128)S(1)} %get-tuple-element.41), channel_id=1, source_target_pairs={{2,0},{3,1},{4,2},{5,3},{6,4},{7,5},{8,6},{9,7},{10,8},{11,9},{12,... | collective-permute-start | bytes 12296 | tf_op jit(solution)/shard_map/ppermute | solution.py:45
  41.3 4.1 %collective-permute-start.6 = (bf16[64,1024]{1,0:T(8,128)(2,1)S(1)}, bf16[64,1024]{1,0:T(8,128)(2,1)S(1)}, u32[]{:S(2)}, u32[]{:S(2)}) collective-permute-start(bf16[64,1024]{1,0:T(8,128)(2,1)S(1)} %get-tuple-element.42.refs_0_), channel_id=1, source_target_pairs={{0,1},{1,0},{2,3},{3,2},{4,5},{5,4},{6,7},{7,6},{8,9},{9,8},{10,11... | collective-permute-start | bytes 393224 | tf_op jit(solution)/shard_map/ppermute | solution.py:36
  45.4 2.4 %collective-permute-start.10 = (bf16[64,1024]{1,0:T(8,128)(2,1)S(1)}, bf16[64,1024]{1,0:T(8,128)(2,1)S(1)}, u32[]{:S(2)}, u32[]{:S(2)}) collective-permute-start(bf16[64,1024]{1,0:T(8,128)(2,1)S(1)} %collective-permute-done.5.ready_ref.refs_2_), channel_id=1, source_target_pairs={{0,4},{1,13},{2,6},{3,15},{4,8},{5,1},{6,10},{7,3},{8,12},{9,5},{1... | collective-permute-start | bytes 393224 | tf_op jit(solution)/shard_map/ppermute | solution.py:36
  48.5 3.7 %collective-permute-start.14 = (bf16[64,1024]{1,0:T(8,128)(2,1)}, bf16[64,1024]{1,0:T(8,128)(2,1)}, u32[]{:S(2)}, u32[]{:S(2)}) collective-permute-start(bf16[64,1024]{1,0:T(8,128)(2,1)} %get-tuple-element.46.refs_1_), channel_id=1, source_target_pairs={{0,13},{1,4},{2,15},{3,6},{4,1},{5,8},{6,3},{7,10},{8,5},{9,12},{1... | collective-permute-start | bytes 393224 | tf_op jit(solution)/shard_map/ppermute | solution.py:36
  52.2 3.0 %collective-permute-start.8 = (bf16[64,1024]{1,0:T(8,128)(2,1)S(1)}, bf16[64,1024]{1,0:T(8,128)(2,1)S(1)}, u32[]{:S(2)}, u32[]{:S(2)}) collective-permute-start(bf16[64,1024]{1,0:T(8,128)(2,1)S(1)} %collective-permute-done.5.ready_ref.refs_2_), channel_id=1, source_target_pairs={{0,1},{1,0},{2,3},{3,2},{4,5},{5,4},{6,7},{7,6},{8,9},{9,8},{10,11... | collective-permute-start | bytes 393224 | tf_op jit(solution)/shard_map/ppermute | solution.py:36
  55.9 2.4 %collective-permute-done.10.refs_6_ = bf16[64,1024]{1,0:T(8,128)(2,1)S(1)} collective-permute-done((bf16[64,1024]{1,0:T(8,128)(2,1)S(1)}, bf16[64,1024]{1,0:T(8,128)(2,1)S(1)}, u32[]{:S(2)}, u32[]{:S(2)}) %collective-permute-start.10) | collective-permute-done | bytes 131104 | tf_op jit(solution)/shard_map/ppermute | solution.py:36
  62.7 1.5 %copy-done = bf16[1024,896]{1,0:T(8,128)(2,1)S(1)} copy-done((bf16[1024,896]{1,0:T(8,128)(2,1)S(1)}, bf16[1024,896]{1,0:T(8,128)(2,1)}, u32[]{:S(2)}) %copy-start) | copy-done | bytes 1835032
  68.7 3.0 %shard_map.86 = (bf16[512,128]{1,0:T(8,128)(2,1)S(1)}, bf16[512,256]{1,0:T(8,128)(2,1)}, bf16[1024,384]{1,0:T(8,128)(2,1)S(1)}) custom-call(bf16[64,1024]{1,0:T(8,128)(2,1)S(1)} %get-tuple-element.42.refs_0_, bf16[64,1024]{1,0:T(8,128)(2,1)S(1)} %copy-done.10, bf16[64,1024]{1,0:T(8,128)(2,1)S(1)} %collective-permute-done.5.ready_ref.refs_2_, ...), custom_call_target="tpu_custom_call" | custom-call | tf_op jit(solution)/shard_map/pallas_call | solution.py:290
  77.9 2.3 %shard_map.87.refs_2_ = bf16[512,128]{1,0:T(8,128)(2,1)S(1)} custom-call(s32[6]{0:T(128)S(1)} %stack.35.place_ref.refs_0_, bf16[64,1024]{1,0:T(8,128)(2,1)} %get-tuple-element.46.refs_1_, bf16[64,1024]{1,0:T(8,128)(2,1)} %collective-permute-done.12.refs_2_, bf16[64,1024]{1,0:T(8,128)(2,1)} %collective-permute-done.13.refs_3_, ...), custom_call_target="tpu_custom_call" | custom-call | tf_op jit(solution)/shard_map/pallas_call | solution.py:326
  81.3 9.2 %collective-permute-done.21.refs_5_ = bf16[512,256]{1,0:T(8,128)(2,1)} collective-permute-done((bf16[512,256]{1,0:T(8,128)(2,1)}, bf16[512,256]{1,0:T(8,128)(2,1)}, u32[]{:S(2)}, u32[]{:S(2)}) %collective-permute-start.21) | collective-permute-done | bytes 262176 | tf_op jit(solution)/shard_map/ppermute | solution.py:36
  90.6 7.3 %shard_map.88 = (bf16[512,128]{1,0:T(8,128)(2,1)S(1)}, bf16[512,256]{1,0:T(8,128)(2,1)S(1)}, bf16[512,256]{1,0:T(8,128)(2,1)S(1)}, bf16[512,256]{1,0:T(8,128)(2,1)S(1)}, bf16[512,256]{1,0:T(8,128)(2,1)S(1)}) custom-call(s32[6]{0:T(128)S(1)} %stack.35.place_ref.refs_0_, bf16[512,128]{1,0:T(8,128)(2,1)S(1)} %copy-done.24, ...), custom_call_target="tpu_custom_call" | custom-call | flops 1610612736 | bytes 2490368 | tf_op jit(solution)/shard_map/pallas_call | solution.py:390
  97.9 1.7 %collective-permute-start.23 = (bf16[512,256]{1,0:T(8,128)(2,1)S(1)}, bf16[512,256]{1,0:T(8,128)(2,1)S(1)}, u32[]{:S(2)}, u32[]{:S(2)}) collective-permute-start(bf16[512,256]{1,0:T(8,128)(2,1)S(1)} %get-tuple-element.50), channel_id=1, source_target_pairs={{0,2},{1,3},{2,0},{3,1},{4,6},{5,7},{6,4},{7,5},{8,10},{9,11},{10,... | collective-permute-start | bytes 786440 | tf_op jit(solution)/shard_map/ppermute | solution.py:36
  102.4 4.9 %collective-permute-done.23.refs_1_ = bf16[512,256]{1,0:T(8,128)(2,1)S(1)} collective-permute-done((bf16[512,256]{1,0:T(8,128)(2,1)S(1)}, bf16[512,256]{1,0:T(8,128)(2,1)S(1)}, u32[]{:S(2)}, u32[]{:S(2)}) %collective-permute-start.23) | collective-permute-done | bytes 262176 | tf_op jit(solution)/shard_map/ppermute | solution.py:36
  107.2 4.4 %collective-permute-done.24.refs_2_ = bf16[512,256]{1,0:T(8,128)(2,1)S(1)} collective-permute-done((bf16[512,256]{1,0:T(8,128)(2,1)S(1)}, bf16[512,256]{1,0:T(8,128)(2,1)S(1)}, u32[]{:S(2)}, u32[]{:S(2)}) %collective-permute-start.24) | collective-permute-done | bytes 262176 | tf_op jit(solution)/shard_map/ppermute | solution.py:36
  112.5 1.9 %collective-permute-done.26.swapped = bf16[256,1024]{1,0:T(8,128)(2,1)S(1)} collective-permute-done((bf16[256,1024]{1,0:T(8,128)(2,1)S(1)}, bf16[256,1024]{1,0:T(8,128)(2,1)S(1)}, u32[]{:S(2)}, u32[]{:S(2)}) %collective-permute-start.26) | collective-permute-done | bytes 524320 | tf_op jit(solution)/shard_map/ppermute | solution.py:36
  114.5 2.9 %collective-permute-start.28 = (bf16[64,1024]{1,0:T(8,128)(2,1)S(1)}, bf16[64,1024]{1,0:T(8,128)(2,1)S(1)}, u32[]{:S(2)}, u32[]{:S(2)}) collective-permute-start(bf16[64,1024]{1,0:T(8,128)(2,1)S(1)} %get-tuple-element.62), channel_id=1, source_target_pairs={{0,12},{1,5},{2,14},{3,7},{4,0},{5,9},{6,2},{7,11},{8,4},{9,13},{1... | collective-permute-start | bytes 393224 | tf_op jit(solution)/shard_map/ppermute | solution.py:36
  118.2 3.8 %collective-permute-done.28 = bf16[64,1024]{1,0:T(8,128)(2,1)S(1)} collective-permute-done((bf16[64,1024]{1,0:T(8,128)(2,1)S(1)}, bf16[64,1024]{1,0:T(8,128)(2,1)S(1)}, u32[]{:S(2)}, u32[]{:S(2)}) %collective-permute-start.28) | collective-permute-done | bytes 131104 | tf_op jit(solution)/shard_map/ppermute | solution.py:36
  122.0 4.0 %collective-permute-start.29 = (bf16[64,1024]{1,0:T(8,128)(2,1)S(1)}, bf16[64,1024]{1,0:T(8,128)(2,1)S(1)}, u32[]{:S(2)}, u32[]{:S(2)}) collective-permute-start(bf16[64,1024]{1,0:T(8,128)(2,1)S(1)} %add_convert_fusion.1), channel_id=1, source_target_pairs={{0,12},{1,5},{2,14},{3,7},{4,0},{5,9},{6,2},{7,11},{8,4},{9,13},{1... | collective-permute-start | bytes 393224 | tf_op jit(solution)/shard_map/ppermute | solution.py:36
  126.1 4.3 %collective-permute-done.29 = bf16[64,1024]{1,0:T(8,128)(2,1)S(1)} collective-permute-done((bf16[64,1024]{1,0:T(8,128)(2,1)S(1)}, bf16[64,1024]{1,0:T(8,128)(2,1)S(1)}, u32[]{:S(2)}, u32[]{:S(2)}) %collective-permute-start.29) | collective-permute-done | bytes 131104 | tf_op jit(solution)/shard_map/ppermute | solution.py:36
  130.7 4.2 %collective-permute-start.30 = (bf16[64,1024]{1,0:T(8,128)(2,1)S(1)}, bf16[64,1024]{1,0:T(8,128)(2,1)S(1)}, u32[]{:S(2)}, u32[]{:S(2)}) collective-permute-start(bf16[64,1024]{1,0:T(8,128)(2,1)S(1)} %divide_convert_fusion), channel_id=1, source_target_pairs={{1,2},{2,1},{3,4},{4,3},{5,6},{6,5},{7,8},{8,7},{9,10},{10,9},{11,... | collective-permute-start | bytes 393224 | tf_op jit(solution)/shard_map/ppermute | solution.py:41
  135.0 5.6 %collective-permute-done.30 = bf16[64,1024]{1,0:T(8,128)(2,1)S(1)} collective-permute-done((bf16[64,1024]{1,0:T(8,128)(2,1)S(1)}, bf16[64,1024]{1,0:T(8,128)(2,1)S(1)}, u32[]{:S(2)}, u32[]{:S(2)}) %collective-permute-start.30) | collective-permute-done | bytes 131104 | tf_op jit(solution)/shard_map/ppermute | solution.py:41
  (123 shorter events, 36.0 us)
Async XLA Ops:
  6.5 56.2 %all-gather.3.cloned.1.call-start = ((), (), s32[]{:S(2)}) async-start(), calls=%async_computation | async-start | bytes 2064384 | tf_op jit(solution)/shard_map/all_gather | solution.py:114
  12.5 9.3 %collective-permute-start = (s32[64]{0:T(128)S(1)}, s32[64]{0:T(128)S(1)}, u32[]{:S(2)}, u32[]{:S(2)}) collective-permute-start(s32[64]{0:T(128)S(1)} %bitcast.30), channel_id=1, source_target_pairs={{1,2},{2,1},{3,4},{4,3},{5,6},{6,5},{7,8},{8,7},{9,10},{10,9},{11,... | collective-permute-start | bytes 776 | tf_op jit(solution)/shard_map/ppermute | solution.py:41
  25.0 8.0 %collective-permute-start.2 = (bf16[64,2048]{1,0:T(8,128)(2,1)S(1)}, bf16[64,2048]{1,0:T(8,128)(2,1)S(1)}, u32[]{:S(2)}, u32[]{:S(2)}) collective-permute-start(bf16[64,2048]{1,0:T(8,128)(2,1)S(1)} %get-tuple-element.36), channel_id=1, source_target_pairs={{0,1},{1,0},{2,3},{3,2},{4,5},{5,4},{6,7},{7,6},{8,9},{9,8},{10,11... | collective-permute-start | bytes 786440 | tf_op jit(solution)/shard_map/ppermute | solution.py:36
  25.2 11.6 %collective-permute-start.3 = (bf16[64,2048]{1,0:T(8,128)(2,1)S(1)}, bf16[64,2048]{1,0:T(8,128)(2,1)S(1)}, u32[]{:S(2)}, u32[]{:S(2)}) collective-permute-start(bf16[64,2048]{1,0:T(8,128)(2,1)S(1)} %get-tuple-element.37), channel_id=1, source_target_pairs={{1,2},{2,1},{3,4},{4,3},{5,6},{6,5},{7,8},{8,7},{9,10},{10,9},{11,... | collective-permute-start | bytes 786440 | tf_op jit(solution)/shard_map/ppermute | solution.py:41
  37.7 10.2 %collective-permute-start.4 = (f32[1,1024]{1,0:T(1,128)S(1)}, f32[1,1024]{1,0:T(1,128)S(1)}, u32[]{:S(2)}, u32[]{:S(2)}) collective-permute-start(f32[1,1024]{1,0:T(1,128)S(1)} %get-tuple-element.41), channel_id=1, source_target_pairs={{2,0},{3,1},{4,2},{5,3},{6,4},{7,5},{8,6},{9,7},{10,8},{11,9},{12,... | collective-permute-start | bytes 12296 | tf_op jit(solution)/shard_map/ppermute | solution.py:45
  41.2 11.0 %collective-permute-start.7 = (bf16[64,1024]{1,0:T(8,128)(2,1)S(1)}, bf16[64,1024]{1,0:T(8,128)(2,1)S(1)}, u32[]{:S(2)}, u32[]{:S(2)}) collective-permute-start(bf16[64,1024]{1,0:T(8,128)(2,1)S(1)} %get-tuple-element.42.refs_0_), channel_id=1, source_target_pairs={{0,13},{1,4},{2,15},{3,6},{4,1},{5,8},{6,3},{7,10},{8,5},{9,12},{1... | collective-permute-start | bytes 393224 | tf_op jit(solution)/shard_map/ppermute | solution.py:36
  41.3 13.9 %collective-permute-start.6 = (bf16[64,1024]{1,0:T(8,128)(2,1)S(1)}, bf16[64,1024]{1,0:T(8,128)(2,1)S(1)}, u32[]{:S(2)}, u32[]{:S(2)}) collective-permute-start(bf16[64,1024]{1,0:T(8,128)(2,1)S(1)} %get-tuple-element.42.refs_0_), channel_id=1, source_target_pairs={{0,1},{1,0},{2,3},{3,2},{4,5},{5,4},{6,7},{7,6},{8,9},{9,8},{10,11... | collective-permute-start | bytes 393224 | tf_op jit(solution)/shard_map/ppermute | solution.py:36
  45.4 13.0 %collective-permute-start.10 = (bf16[64,1024]{1,0:T(8,128)(2,1)S(1)}, bf16[64,1024]{1,0:T(8,128)(2,1)S(1)}, u32[]{:S(2)}, u32[]{:S(2)}) collective-permute-start(bf16[64,1024]{1,0:T(8,128)(2,1)S(1)} %collective-permute-done.5.ready_ref.refs_2_), channel_id=1, source_target_pairs={{0,4},{1,13},{2,6},{3,15},{4,8},{5,1},{6,10},{7,3},{8,12},{9,5},{1... | collective-permute-start | bytes 393224 | tf_op jit(solution)/shard_map/ppermute | solution.py:36
  48.5 11.4 %collective-permute-start.13 = (bf16[64,1024]{1,0:T(8,128)(2,1)}, bf16[64,1024]{1,0:T(8,128)(2,1)}, u32[]{:S(2)}, u32[]{:S(2)}) collective-permute-start(bf16[64,1024]{1,0:T(8,128)(2,1)} %get-tuple-element.46.refs_1_), channel_id=1, source_target_pairs={{0,4},{1,13},{2,6},{3,15},{4,8},{5,1},{6,10},{7,3},{8,12},{9,5},{1... | collective-permute-start | bytes 393224 | tf_op jit(solution)/shard_map/ppermute | solution.py:36
  48.5 11.4 %collective-permute-start.14 = (bf16[64,1024]{1,0:T(8,128)(2,1)}, bf16[64,1024]{1,0:T(8,128)(2,1)}, u32[]{:S(2)}, u32[]{:S(2)}) collective-permute-start(bf16[64,1024]{1,0:T(8,128)(2,1)} %get-tuple-element.46.refs_1_), channel_id=1, source_target_pairs={{0,13},{1,4},{2,15},{3,6},{4,1},{5,8},{6,3},{7,10},{8,5},{9,12},{1... | collective-permute-start | bytes 393224 | tf_op jit(solution)/shard_map/ppermute | solution.py:36
  52.2 7.8 %collective-permute-start.8 = (bf16[64,1024]{1,0:T(8,128)(2,1)S(1)}, bf16[64,1024]{1,0:T(8,128)(2,1)S(1)}, u32[]{:S(2)}, u32[]{:S(2)}) collective-permute-start(bf16[64,1024]{1,0:T(8,128)(2,1)S(1)} %collective-permute-done.5.ready_ref.refs_2_), channel_id=1, source_target_pairs={{0,1},{1,0},{2,3},{3,2},{4,5},{5,4},{6,7},{7,6},{8,9},{9,8},{10,11... | collective-permute-start | bytes 393224 | tf_op jit(solution)/shard_map/ppermute | solution.py:36
  60.0 13.3 %collective-permute-start.12 = (bf16[64,1024]{1,0:T(8,128)(2,1)}, bf16[64,1024]{1,0:T(8,128)(2,1)}, u32[]{:S(2)}, u32[]{:S(2)}) collective-permute-start(bf16[64,1024]{1,0:T(8,128)(2,1)} %get-tuple-element.46.refs_1_), channel_id=1, source_target_pairs={{0,1},{1,0},{2,3},{3,2},{4,5},{5,4},{6,7},{7,6},{8,9},{9,8},{10,11... | collective-permute-start | bytes 393224 | tf_op jit(solution)/shard_map/ppermute | solution.py:36
  60.0 14.8 %collective-permute-start.17 = (bf16[64,1024]{1,0:T(8,128)(2,1)}, bf16[64,1024]{1,0:T(8,128)(2,1)}, u32[]{:S(2)}, u32[]{:S(2)}) collective-permute-start(bf16[64,1024]{1,0:T(8,128)(2,1)} %collective-permute-done.13.refs_3_), channel_id=1, source_target_pairs={{0,4},{1,13},{2,6},{3,15},{4,8},{5,1},{6,10},{7,3},{8,12},{9,5},{1... | collective-permute-start | bytes 393224 | tf_op jit(solution)/shard_map/ppermute | solution.py:36
  60.7 15.6 %collective-permute-start.15 = (bf16[64,1024]{1,0:T(8,128)(2,1)}, bf16[64,1024]{1,0:T(8,128)(2,1)}, u32[]{:S(2)}, u32[]{:S(2)}) collective-permute-start(bf16[64,1024]{1,0:T(8,128)(2,1)} %collective-permute-done.13.refs_3_), channel_id=1, source_target_pairs={{0,1},{1,0},{2,3},{3,2},{4,5},{5,4},{6,7},{7,6},{8,9},{9,8},{10,11... | collective-permute-start | bytes 393224 | tf_op jit(solution)/shard_map/ppermute | solution.py:36
  62.0 14.3 %collective-permute-start.16 = (bf16[64,1024]{1,0:T(8,128)(2,1)}, bf16[64,1024]{1,0:T(8,128)(2,1)}, u32[]{:S(2)}, u32[]{:S(2)}) collective-permute-start(bf16[64,1024]{1,0:T(8,128)(2,1)} %collective-permute-done.14.refs_4_), channel_id=1, source_target_pairs={{0,1},{1,0},{2,3},{3,2},{4,5},{5,4},{6,7},{7,6},{8,9},{9,8},{10,11... | collective-permute-start | bytes 393224 | tf_op jit(solution)/shard_map/ppermute | solution.py:36
  72.4 8.9 %collective-permute-start.20 = (bf16[512,256]{1,0:T(8,128)(2,1)}, bf16[512,256]{1,0:T(8,128)(2,1)S(1)}, u32[]{:S(2)}, u32[]{:S(2)}) collective-permute-start(bf16[512,256]{1,0:T(8,128)(2,1)} %get-tuple-element.47.refs_3_), channel_id=1, source_target_pairs={{0,2},{1,3},{2,0},{3,1},{4,6},{5,7},{6,4},{7,5},{8,10},{9,11},{10,... | collective-permute-start | bytes 786440 | tf_op jit(solution)/shard_map/ppermute | solution.py:36
  73.3 17.3 %collective-permute-start.21 = (bf16[512,256]{1,0:T(8,128)(2,1)}, bf16[512,256]{1,0:T(8,128)(2,1)}, u32[]{:S(2)}, u32[]{:S(2)}) collective-permute-start(bf16[512,256]{1,0:T(8,128)(2,1)} %get-tuple-element.47.refs_3_), channel_id=1, source_target_pairs={{0,16},{1,17},{2,18},{3,19},{4,20},{5,21},{6,22},{7,23},{8,24},{9,... | collective-permute-start | bytes 786440 | tf_op jit(solution)/shard_map/ppermute | solution.py:36
  74.8 15.8 %collective-permute-start.22 = (bf16[512,256]{1,0:T(8,128)(2,1)}, bf16[512,256]{1,0:T(8,128)(2,1)}, u32[]{:S(2)}, u32[]{:S(2)}) collective-permute-start(bf16[512,256]{1,0:T(8,128)(2,1)} %get-tuple-element.47.refs_3_), channel_id=1, source_target_pairs={{0,18},{1,19},{2,16},{3,17},{4,22},{5,23},{6,20},{7,21},{8,26},{9,... | collective-permute-start | bytes 786440 | tf_op jit(solution)/shard_map/ppermute | solution.py:36
  97.9 9.3 %collective-permute-start.23 = (bf16[512,256]{1,0:T(8,128)(2,1)S(1)}, bf16[512,256]{1,0:T(8,128)(2,1)S(1)}, u32[]{:S(2)}, u32[]{:S(2)}) collective-permute-start(bf16[512,256]{1,0:T(8,128)(2,1)S(1)} %get-tuple-element.50), channel_id=1, source_target_pairs={{0,2},{1,3},{2,0},{3,1},{4,6},{5,7},{6,4},{7,5},{8,10},{9,11},{10,... | collective-permute-start | bytes 786440 | tf_op jit(solution)/shard_map/ppermute | solution.py:36
  99.6 12.0 %collective-permute-start.24 = (bf16[512,256]{1,0:T(8,128)(2,1)S(1)}, bf16[512,256]{1,0:T(8,128)(2,1)S(1)}, u32[]{:S(2)}, u32[]{:S(2)}) collective-permute-start(bf16[512,256]{1,0:T(8,128)(2,1)S(1)} %get-tuple-element.51), channel_id=1, source_target_pairs={{16,0},{17,1},{18,2},{19,3},{20,4},{21,5},{22,6},{23,7},{24,8},{25... | collective-permute-start | bytes 786440 | tf_op jit(solution)/shard_map/ppermute | solution.py:36
  101.1 10.6 %collective-permute-start.25 = (bf16[512,256]{1,0:T(8,128)(2,1)S(1)}, bf16[512,256]{1,0:T(8,128)(2,1)S(1)}, u32[]{:S(2)}, u32[]{:S(2)}) collective-permute-start(bf16[512,256]{1,0:T(8,128)(2,1)S(1)} %get-tuple-element.52), channel_id=1, source_target_pairs={{16,2},{17,3},{18,0},{19,1},{20,6},{21,7},{22,4},{23,5},{24,10},{2... | collective-permute-start | bytes 786440 | tf_op jit(solution)/shard_map/ppermute | solution.py:36
  117.4 8.7 %collective-permute-start.27 = (bf16[64,1024]{1,0:T(8,128)(2,1)S(1)}, bf16[64,1024]{1,0:T(8,128)(2,1)S(1)}, u32[]{:S(2)}, u32[]{:S(2)}) collective-permute-start(bf16[64,1024]{1,0:T(8,128)(2,1)S(1)} %get-tuple-element.60), channel_id=1, source_target_pairs={{0,13},{1,4},{2,15},{3,6},{4,1},{5,8},{6,3},{7,10},{8,5},{9,12},{1... | collective-permute-start | bytes 393224 | tf_op jit(solution)/shard_map/ppermute | solution.py:36
  122.0 8.4 %collective-permute-start.29 = (bf16[64,1024]{1,0:T(8,128)(2,1)S(1)}, bf16[64,1024]{1,0:T(8,128)(2,1)S(1)}, u32[]{:S(2)}, u32[]{:S(2)}) collective-permute-start(bf16[64,1024]{1,0:T(8,128)(2,1)S(1)} %add_convert_fusion.1), channel_id=1, source_target_pairs={{0,12},{1,5},{2,14},{3,7},{4,0},{5,9},{6,2},{7,11},{8,4},{9,13},{1... | collective-permute-start | bytes 393224 | tf_op jit(solution)/shard_map/ppermute | solution.py:36
  130.7 9.9 %collective-permute-start.30 = (bf16[64,1024]{1,0:T(8,128)(2,1)S(1)}, bf16[64,1024]{1,0:T(8,128)(2,1)S(1)}, u32[]{:S(2)}, u32[]{:S(2)}) collective-permute-start(bf16[64,1024]{1,0:T(8,128)(2,1)S(1)} %divide_convert_fusion), channel_id=1, source_target_pairs={{1,2},{2,1},{3,4},{4,3},{5,6},{6,5},{7,8},{8,7},{9,10},{10,9},{11,... | collective-permute-start | bytes 393224 | tf_op jit(solution)/shard_map/ppermute | solution.py:41
  (35 other events, 174.7 us)
Sparse Core Ops, SparseCore 0:
  12.7 45.7 all-gather.2

commit v6 on v5

--- a/solution.py
+++ b/solution.py
@@ -17,7 +17,11 @@
 VMEM = pl.BlockSpec(memory_space=pltpu.VMEM)
 SMEM = pl.BlockSpec(memory_space=pltpu.SMEM)
 ANY = pl.BlockSpec(memory_space=pl.ANY)
-PARAMS = pltpu.CompilerParams(vmem_limit_bytes=48 * 1024 * 1024)
+HBM = pl.BlockSpec(memory_space=pltpu.HBM)
+
+
+def room(mib):
+    return pltpu.CompilerParams(vmem_limit_bytes=mib * 1024 * 1024)
 
 
 def place(half, turn, pair, core):
@@ -103,10 +107,10 @@
             jax.ShapeDtypeStruct((rows, 3 * HEAD + width // 2), w_query.dtype),
             jax.ShapeDtypeStruct(starts.shape, starts.dtype),
         ),
-        in_specs=[SMEM] + [ANY] * 5,
+        in_specs=[SMEM] + [HBM] * 4 + [ANY],
         out_specs=(VMEM, VMEM),
         scratch_shapes=[pltpu.SemaphoreType.DMA((6,))],
-        compiler_params=PARAMS,
+        compiler_params=room(60),
     )(where, w_query, w_key, w_value, w_out, starts)
 
 
@@ -166,17 +170,23 @@
 
 
 def window_kernel(place_ref, edge_ref, token_hbm, grad_hbm, *refs):
-    core_ref, chip_ref, mid_token, mid_grad, first_ref = refs[:5]
-    token_ref, grad_ref, sems = refs[5:]
+    core_ref, chip_ref, mid_token, mid_grad, first_ref, count_ref = refs[:6]
+    token_ref, grad_ref, sems = refs[6:]
     rows, width = token_ref.shape
     seg = mid_token.shape[0]
-    fetched([(token_hbm, token_ref), (grad_hbm, grad_ref)], sems)
+    token_copy = pltpu.make_async_copy(token_hbm, token_ref, sems.at[0])
+    grad_copy = pltpu.make_async_copy(grad_hbm, grad_ref, sems.at[1])
+    token_copy.start()
+    grad_copy.start()
     ctx, core = place_ref[5], place_ref[3]
     at = lax.broadcasted_iota(jnp.int32, (1, rows), 1) + ctx * rows
     opens, ends, nexts = edge_ref[0], edge_ref[1], edge_ref[2]
+    count_ref[...] = (ends - opens)[seg : 2 * seg].astype(F32)
     member = ((opens <= at) & (at < ends)).astype(jnp.bfloat16)
     earlier = ((ends <= at) & (at < nexts)).astype(jnp.bfloat16)
+    token_copy.wait()
     token = jnp.dot(member, token_ref[...], preferred_element_type=F32)
+    grad_copy.wait()
     grad = jnp.dot(earlier, grad_ref[...], preferred_element_type=F32)
     first = jnp.dot(member[:16], grad_ref[...], preferred_element_type=F32)
     first_ref[...] = first[:1]
@@ -209,15 +219,16 @@
             shape((seg, width), F32),
             shape((seg, width), F32),
             shape((1, width), F32),
+            shape((seg, 1), F32),
         ),
-        in_specs=[SMEM, VMEM] + [ANY] * 2,
-        out_specs=(VMEM,) * 5,
+        in_specs=[SMEM, VMEM] + [HBM] * 2,
+        out_specs=(VMEM,) * 6,
         scratch_shapes=[
             pltpu.VMEM((rows, width), tokens.dtype),
             pltpu.VMEM((rows, width), grads.dtype),
             pltpu.SemaphoreType.DMA((2,)),
         ],
-        compiler_params=PARAMS,
+        compiler_params=room(60),
     )(where, edges, tokens, grads)
 
 
@@ -247,7 +258,7 @@
         ),
         in_specs=[VMEM] * 6,
         out_specs=(VMEM,) * 4,
-        compiler_params=PARAMS,
+        compiler_params=room(6),
     )(from_core, from_chip, mid_token, mid_grad, count, gain)
 
 
@@ -266,7 +277,7 @@
         out_shape=(shape(dout.shape, F32), shape(dout.shape, jnp.bfloat16)),
         in_specs=[VMEM, VMEM, ANY],
         out_specs=(VMEM, VMEM),
-        compiler_params=PARAMS,
+        compiler_params=room(4),
     )(dout, second, ready)
 
 
@@ -300,7 +311,7 @@
             pltpu.VMEM((rows, width), jnp.bfloat16),
             pltpu.SemaphoreType.DMA((16,)),
         ],
-        compiler_params=PARAMS,
+        compiler_params=room(12),
     )(*pieces, weights)
 
 
@@ -333,7 +344,7 @@
             pltpu.VMEM((HEAD, width), jnp.bfloat16),
             pltpu.SemaphoreType.DMA((12,)),
         ],
-        compiler_params=PARAMS,
+        compiler_params=room(10),
     )(where, *pieces, mine, theirs)
 
 
@@ -398,7 +409,7 @@
             pltpu.VMEM((HEAD, keys), F32),
             pltpu.SemaphoreType.DMA((4,)),
         ],
-        compiler_params=PARAMS,
+        compiler_params=room(28),
         cost_estimate=pl.CostEstimate(
             flops=12 * queries * keys * HEAD,
             bytes_accessed=2 * HEAD * (3 * queries + 4 * keys),
@@ -426,7 +437,7 @@
         + (jax.ShapeDtypeStruct((seg, width), F32),) * 4,
         in_specs=[VMEM] * 6,
         out_specs=(VMEM,) * 5,
-        compiler_params=PARAMS,
+        compiler_params=room(16),
     )(dq, *parts, w_full)
 
 
@@ -446,7 +457,7 @@
         out_shape=(wide, wide, thin, thin),
         in_specs=[VMEM] * 5,
         out_specs=(VMEM,) * 4,
-        compiler_params=PARAMS,
+        compiler_params=room(6),
     )(swapped, own, near, next_to, far)
 
 
@@ -482,8 +493,7 @@
     slots = 3 * seg
     opens, ends = window[:slots], window[1 : slots + 1]
     edges = jnp.stack([opens, ends, window[2:]])[:, :, None]
-    count = (ends - opens)[seg : 2 * seg, None].astype(F32)
-    to_core, to_chip, mid_token, mid_grad, first = window_sums(
+    to_core, to_chip, mid_token, mid_grad, first, count = window_sums(
         where, edges, token_rows, grad_out, seg
     )
     second = two_back(first)

time: 150 us -> 154 us (1.027)
  Pallas kernels: 17.3 us -> 21.1 us
  local copies, waits for them, and re-layouts: 16.8 us -> 14.2 us
    unnamed x52 -> x46, local copies, waits for them, and re-layouts: 16.3 us -> 12.6 us
    pallas_call x1, Pallas kernels: 1.49 us -> 4.15 us  [window_sums(): pl.pallas_call(window_kernel, out_shape=(shape((seg, 2 * width), WIRE), s...]
  transfers between devices with their start and end apart: 33 -> 33, of which waited for: 13 -> 12; matrix products, arithmetic and copies ran while one was open for 1% -> 2% of each run, Pallas kernels for 5% -> 7%
where the time goes in v6:
time: 154 us; the launch traced here: 153 us
  starting transfers between devices  54.2 us (35%)
  waiting for transfers between devices  46 us (30%)
  Pallas kernels  21.1 us (14%)
  local copies, waits for them, and re-layouts  14.2 us (9%)
  between operations  13.8 us (9%)
  other arithmetic  2.05 us (1%)
    ppermute x28, waiting for transfers between devices, moved(): return lax.ppermute(value, 'ctx', pairs)  34.2 us
    ppermute x28, starting transfers between devices, moved(): return lax.ppermute(value, 'ctx', pairs)  31.5 us
    ppermute x3, starting transfers between devices, other_chip(): return lax.ppermute(value, 'ctx', pairs)  20 us
    unnamed x46, local copies, waits for them, and re-layouts  12.6 us
    ppermute x3, waiting for transfers between devices, other_chip(): return lax.ppermute(value, 'ctx', pairs)  11.8 us
    pallas_call x1, Pallas kernels, attention(): pl.pallas_call(functools.partial(attention_kernel, 128, seg), out_shape=(...  7.39 us
    pallas_call x1, Pallas kernels, window_sums(): pl.pallas_call(window_kernel, out_shape=(shape((seg, 2 * width), WIRE), s...  4.15 us
  transfers between devices with their start and end apart: 33, of which 12 were waited for; matrix products, arithmetic and copies ran while one was open for 2% of the time, Pallas kernels for 7%

profile of v6, /device:TPU:6, one launch (start us, length us, event | category | flops | bytes accessed | tf_op | source)
XLA Modules:
  0.0 152.7 jit_solution(4396599658067820615)
XLA Ops:
  7.1 2.5 %shard_map.82 = (bf16[128,896]{1,0:T(8,128)(2,1)}, s32[1,64]{1,0:T(1,128)}) custom-call(s32[6]{0:T(128)} %stack.35.place_ref.refs_0_, bf16[128,1024]{1,0:T(8,128)(2,1)} %q_ref.1, bf16[128,1024]{1,0:T(8,128)(2,1)} %k_ref.1, bf16[128,1024]{1,0:T(8,128)(2,1)} %v_ref.1, bf16[128,1024]{1,0:T(8,128)(2,1)} %o_ref.1, s32[1,64]{1,0:T(1,128)} %start_ref.1), custom_call_target="tpu_custom_call" | custom-call | tf_op jit(solution)/shard_map/pallas_call | solution.py:104
  9.6 8.0 %collective-permute-start = (s32[64]{0:T(128)}, s32[64]{0:T(128)S(1)}, u32[]{:S(2)}, u32[]{:S(2)}) collective-permute-start(s32[64]{0:T(128)} %bitcast.31), channel_id=1, source_target_pairs={{1,2},{2,1},{3,4},{4,3},{5,6},{6,5},{7,8},{8,7},{9,10},{10,9},{11,... | collective-permute-start | bytes 776 | tf_op jit(solution)/shard_map/ppermute | solution.py:45
  21.5 4.1 %shard_map.83 = (bf16[64,2048]{1,0:T(8,128)(2,1)}, bf16[64,2048]{1,0:T(8,128)(2,1)}, f32[64,1024]{1,0:T(8,128)}, f32[64,1024]{1,0:T(8,128)}, f32[1,1024]{1,0:T(1,128)}, /*index=5*/f32[64,1]{1,0:T(8,128)}) custom-call(s32[6]{0:T(128)} %stack.35.place_ref.refs_0_, s32[3,192,1]{2,1,0:T(8,128)} %copy.9.edge_ref, bf16[512,1024]{1,0:T(8,128)(2,1)} %bitcast.26, ...), custom_call_target="tpu_custom_call" | custom-call | tf_op jit(solution)/shard_map/pallas_call | solution.py:214
  25.9 7.1 %collective-permute-start.3 = (bf16[64,2048]{1,0:T(8,128)(2,1)}, bf16[64,2048]{1,0:T(8,128)(2,1)S(1)}, u32[]{:S(2)}, u32[]{:S(2)}) collective-permute-start(bf16[64,2048]{1,0:T(8,128)(2,1)} %get-tuple-element.38), channel_id=1, source_target_pairs={{1,2},{2,1},{3,4},{4,3},{5,6},{6,5},{7,8},{8,7},{9,10},{10,9},{11,... | collective-permute-start | bytes 786440 | tf_op jit(solution)/shard_map/ppermute | solution.py:45
  32.9 5.6 %collective-permute-done.3.chip_ref = bf16[64,2048]{1,0:T(8,128)(2,1)S(1)} collective-permute-done((bf16[64,2048]{1,0:T(8,128)(2,1)}, bf16[64,2048]{1,0:T(8,128)(2,1)S(1)}, u32[]{:S(2)}, u32[]{:S(2)}) %collective-permute-start.3) | collective-permute-done | bytes 262176 | tf_op jit(solution)/shard_map/ppermute | solution.py:45
  41.5 2.7 %collective-permute-start.4 = (f32[1,1024]{1,0:T(1,128)}, f32[1,1024]{1,0:T(1,128)S(1)}, u32[]{:S(2)}, u32[]{:S(2)}) collective-permute-start(f32[1,1024]{1,0:T(1,128)} %get-tuple-element.43), channel_id=1, source_target_pairs={{2,0},{3,1},{4,2},{5,3},{6,4},{7,5},{8,6},{9,7},{10,8},{11,9},{12,... | collective-permute-start | bytes 12296 | tf_op jit(solution)/shard_map/ppermute | solution.py:49
  44.3 4.9 %collective-permute-start.6 = (bf16[64,1024]{1,0:T(8,128)(2,1)S(1)}, bf16[64,1024]{1,0:T(8,128)(2,1)S(1)}, u32[]{:S(2)}, u32[]{:S(2)}) collective-permute-start(bf16[64,1024]{1,0:T(8,128)(2,1)S(1)} %get-tuple-element.44.refs_0_), channel_id=1, source_target_pairs={{0,1},{1,0},{2,3},{3,2},{4,5},{5,4},{6,7},{7,6},{8,9},{9,8},{10,11... | collective-permute-start | bytes 393224 | tf_op jit(solution)/shard_map/ppermute | solution.py:40
  49.3 2.4 %collective-permute-start.10 = (bf16[64,1024]{1,0:T(8,128)(2,1)S(1)}, bf16[64,1024]{1,0:T(8,128)(2,1)S(1)}, u32[]{:S(2)}, u32[]{:S(2)}) collective-permute-start(bf16[64,1024]{1,0:T(8,128)(2,1)S(1)} %collective-permute-done.5.ready_ref.refs_2_), channel_id=1, source_target_pairs={{0,4},{1,13},{2,6},{3,15},{4,8},{5,1},{6,10},{7,3},{8,12},{9,5},{1... | collective-permute-start | bytes 393224 | tf_op jit(solution)/shard_map/ppermute | solution.py:40
  52.4 3.7 %collective-permute-start.14 = (bf16[64,1024]{1,0:T(8,128)(2,1)}, bf16[64,1024]{1,0:T(8,128)(2,1)}, u32[]{:S(2)}, u32[]{:S(2)}) collective-permute-start(bf16[64,1024]{1,0:T(8,128)(2,1)} %get-tuple-element.48.refs_1_), channel_id=1, source_target_pairs={{0,13},{1,4},{2,15},{3,6},{4,1},{5,8},{6,3},{7,10},{8,5},{9,12},{1... | collective-permute-start | bytes 393224 | tf_op jit(solution)/shard_map/ppermute | solution.py:40
  58.4 3.8 %collective-permute-done.10.refs_6_ = bf16[64,1024]{1,0:T(8,128)(2,1)S(1)} collective-permute-done((bf16[64,1024]{1,0:T(8,128)(2,1)S(1)}, bf16[64,1024]{1,0:T(8,128)(2,1)S(1)}, u32[]{:S(2)}, u32[]{:S(2)}) %collective-permute-start.10) | collective-permute-done | bytes 131104 | tf_op jit(solution)/shard_map/ppermute | solution.py:40
  72.5 3.0 %shard_map.86 = (bf16[512,128]{1,0:T(8,128)(2,1)S(1)}, bf16[512,256]{1,0:T(8,128)(2,1)}, bf16[1024,384]{1,0:T(8,128)(2,1)S(1)}) custom-call(bf16[64,1024]{1,0:T(8,128)(2,1)S(1)} %get-tuple-element.44.refs_0_, bf16[64,1024]{1,0:T(8,128)(2,1)S(1)} %copy-done.5, bf16[64,1024]{1,0:T(8,128)(2,1)S(1)} %collective-permute-done.5.ready_ref.refs_2_, ...), custom_call_target="tpu_custom_call" | custom-call | tf_op jit(solution)/shard_map/pallas_call | solution.py:301
  82.6 2.3 %shard_map.87.refs_2_ = bf16[512,128]{1,0:T(8,128)(2,1)S(1)} custom-call(s32[6]{0:T(128)S(1)} %copy-done.19, bf16[64,1024]{1,0:T(8,128)(2,1)} %get-tuple-element.48.refs_1_, bf16[64,1024]{1,0:T(8,128)(2,1)} %collective-permute-done.12.refs_2_, bf16[64,1024]{1,0:T(8,128)(2,1)} %collective-permute-done.13.refs_3_, ...), custom_call_target="tpu_custom_call" | custom-call | tf_op jit(solution)/shard_map/pallas_call | solution.py:337
  85.0 10.2 %collective-permute-done.21.refs_5_ = bf16[512,256]{1,0:T(8,128)(2,1)} collective-permute-done((bf16[512,256]{1,0:T(8,128)(2,1)}, bf16[512,256]{1,0:T(8,128)(2,1)}, u32[]{:S(2)}, u32[]{:S(2)}) %collective-permute-start.21) | collective-permute-done | bytes 262176 | tf_op jit(solution)/shard_map/ppermute | solution.py:40
  95.2 7.4 %shard_map.88 = (bf16[512,128]{1,0:T(8,128)(2,1)S(1)}, bf16[512,256]{1,0:T(8,128)(2,1)S(1)}, bf16[512,256]{1,0:T(8,128)(2,1)S(1)}, bf16[512,256]{1,0:T(8,128)(2,1)S(1)}, bf16[512,256]{1,0:T(8,128)(2,1)S(1)}) custom-call(s32[6]{0:T(128)S(1)} %copy-done.19, bf16[512,128]{1,0:T(8,128)(2,1)S(1)} %copy-done.21, bf16[512,128]{1,0:T(8,128)(2,1)S(1)} %shard_map.87.refs_2_, ...), custom_call_target="tpu_custom_call" | custom-call | flops 1610612736 | bytes 2490368 | tf_op jit(solution)/shard_map/pallas_call | solution.py:401
  104.7 2.2 %collective-permute-start.25 = (bf16[512,256]{1,0:T(8,128)(2,1)S(1)}, bf16[512,256]{1,0:T(8,128)(2,1)S(1)}, u32[]{:S(2)}, u32[]{:S(2)}) collective-permute-start(bf16[512,256]{1,0:T(8,128)(2,1)S(1)} %get-tuple-element.54), channel_id=1, source_target_pairs={{16,2},{17,3},{18,0},{19,1},{20,6},{21,7},{22,4},{23,5},{24,10},{2... | collective-permute-start | bytes 786440 | tf_op jit(solution)/shard_map/ppermute | solution.py:40
  106.9 5.0 %collective-permute-done.23.refs_1_ = bf16[512,256]{1,0:T(8,128)(2,1)S(1)} collective-permute-done((bf16[512,256]{1,0:T(8,128)(2,1)S(1)}, bf16[512,256]{1,0:T(8,128)(2,1)S(1)}, u32[]{:S(2)}, u32[]{:S(2)}) %collective-permute-start.23) | collective-permute-done | bytes 262176 | tf_op jit(solution)/shard_map/ppermute | solution.py:40
  112.0 3.0 %collective-permute-done.24.refs_2_ = bf16[512,256]{1,0:T(8,128)(2,1)S(1)} collective-permute-done((bf16[512,256]{1,0:T(8,128)(2,1)S(1)}, bf16[512,256]{1,0:T(8,128)(2,1)S(1)}, u32[]{:S(2)}, u32[]{:S(2)}) %collective-permute-start.24) | collective-permute-done | bytes 262176 | tf_op jit(solution)/shard_map/ppermute | solution.py:40
  115.9 1.9 %collective-permute-done.26.swapped = bf16[256,1024]{1,0:T(8,128)(2,1)S(1)} collective-permute-done((bf16[256,1024]{1,0:T(8,128)(2,1)S(1)}, bf16[256,1024]{1,0:T(8,128)(2,1)S(1)}, u32[]{:S(2)}, u32[]{:S(2)}) %collective-permute-start.26) | collective-permute-done | bytes 524320 | tf_op jit(solution)/shard_map/ppermute | solution.py:40
  117.9 3.4 %collective-permute-start.28 = (bf16[64,1024]{1,0:T(8,128)(2,1)S(1)}, bf16[64,1024]{1,0:T(8,128)(2,1)S(1)}, u32[]{:S(2)}, u32[]{:S(2)}) collective-permute-start(bf16[64,1024]{1,0:T(8,128)(2,1)S(1)} %get-tuple-element.64), channel_id=1, source_target_pairs={{0,12},{1,5},{2,14},{3,7},{4,0},{5,9},{6,2},{7,11},{8,4},{9,13},{1... | collective-permute-start | bytes 393224 | tf_op jit(solution)/shard_map/ppermute | solution.py:40
  121.6 5.2 %collective-permute-done.28 = bf16[64,1024]{1,0:T(8,128)(2,1)S(1)} collective-permute-done((bf16[64,1024]{1,0:T(8,128)(2,1)S(1)}, bf16[64,1024]{1,0:T(8,128)(2,1)S(1)}, u32[]{:S(2)}, u32[]{:S(2)}) %collective-permute-start.28) | collective-permute-done | bytes 131104 | tf_op jit(solution)/shard_map/ppermute | solution.py:40
  126.8 4.2 %collective-permute-start.29 = (bf16[64,1024]{1,0:T(8,128)(2,1)S(1)}, bf16[64,1024]{1,0:T(8,128)(2,1)S(1)}, u32[]{:S(2)}, u32[]{:S(2)}) collective-permute-start(bf16[64,1024]{1,0:T(8,128)(2,1)S(1)} %add_convert_fusion.1), channel_id=1, source_target_pairs={{0,12},{1,5},{2,14},{3,7},{4,0},{5,9},{6,2},{7,11},{8,4},{9,13},{1... | collective-permute-start | bytes 393224 | tf_op jit(solution)/shard_map/ppermute | solution.py:40
  131.2 2.9 %collective-permute-done.29 = bf16[64,1024]{1,0:T(8,128)(2,1)S(1)} collective-permute-done((bf16[64,1024]{1,0:T(8,128)(2,1)S(1)}, bf16[64,1024]{1,0:T(8,128)(2,1)S(1)}, u32[]{:S(2)}, u32[]{:S(2)}) %collective-permute-start.29) | collective-permute-done | bytes 131104 | tf_op jit(solution)/shard_map/ppermute | solution.py:40
  134.5 4.9 %collective-permute-start.30 = (bf16[64,1024]{1,0:T(8,128)(2,1)S(1)}, bf16[64,1024]{1,0:T(8,128)(2,1)S(1)}, u32[]{:S(2)}, u32[]{:S(2)}) collective-permute-start(bf16[64,1024]{1,0:T(8,128)(2,1)S(1)} %divide_convert_fusion), channel_id=1, source_target_pairs={{1,2},{2,1},{3,4},{4,3},{5,6},{6,5},{7,8},{8,7},{9,10},{10,9},{11,... | collective-permute-start | bytes 393224 | tf_op jit(solution)/shard_map/ppermute | solution.py:45
  139.5 4.9 %collective-permute-done.30 = bf16[64,1024]{1,0:T(8,128)(2,1)S(1)} collective-permute-done((bf16[64,1024]{1,0:T(8,128)(2,1)S(1)}, bf16[64,1024]{1,0:T(8,128)(2,1)S(1)}, u32[]{:S(2)}, u32[]{:S(2)}) %collective-permute-start.30) | collective-permute-done | bytes 131104 | tf_op jit(solution)/shard_map/ppermute | solution.py:45
  (116 shorter events, 33.4 us)
Async XLA Ops:
  6.5 60.0 %all-gather.3.cloned.1.call-start = ((), (), s32[]{:S(2)}) async-start(), calls=%async_computation | async-start | bytes 2064384 | tf_op jit(solution)/shard_map/all_gather | solution.py:118
  9.6 9.5 %collective-permute-start = (s32[64]{0:T(128)}, s32[64]{0:T(128)S(1)}, u32[]{:S(2)}, u32[]{:S(2)}) collective-permute-start(s32[64]{0:T(128)} %bitcast.31), channel_id=1, source_target_pairs={{1,2},{2,1},{3,4},{4,3},{5,6},{6,5},{7,8},{8,7},{9,10},{10,9},{11,... | collective-permute-start | bytes 776 | tf_op jit(solution)/shard_map/ppermute | solution.py:45
  25.9 12.7 %collective-permute-start.3 = (bf16[64,2048]{1,0:T(8,128)(2,1)}, bf16[64,2048]{1,0:T(8,128)(2,1)S(1)}, u32[]{:S(2)}, u32[]{:S(2)}) collective-permute-start(bf16[64,2048]{1,0:T(8,128)(2,1)} %get-tuple-element.38), channel_id=1, source_target_pairs={{1,2},{2,1},{3,4},{4,3},{5,6},{6,5},{7,8},{8,7},{9,10},{10,9},{11,... | collective-permute-start | bytes 786440 | tf_op jit(solution)/shard_map/ppermute | solution.py:45
  41.4 7.8 %collective-permute-start.5 = (bf16[64,1024]{1,0:T(8,128)(2,1)S(1)}, bf16[64,1024]{1,0:T(8,128)(2,1)S(1)}, u32[]{:S(2)}, u32[]{:S(2)}) collective-permute-start(bf16[64,1024]{1,0:T(8,128)(2,1)S(1)} %get-tuple-element.44.refs_0_), channel_id=1, source_target_pairs={{0,4},{1,13},{2,6},{3,15},{4,8},{5,1},{6,10},{7,3},{8,12},{9,5},{1... | collective-permute-start | bytes 393224 | tf_op jit(solution)/shard_map/ppermute | solution.py:40
  41.5 10.2 %collective-permute-start.4 = (f32[1,1024]{1,0:T(1,128)}, f32[1,1024]{1,0:T(1,128)S(1)}, u32[]{:S(2)}, u32[]{:S(2)}) collective-permute-start(f32[1,1024]{1,0:T(1,128)} %get-tuple-element.43), channel_id=1, source_target_pairs={{2,0},{3,1},{4,2},{5,3},{6,4},{7,5},{8,6},{9,7},{10,8},{11,9},{12,... | collective-permute-start | bytes 12296 | tf_op jit(solution)/shard_map/ppermute | solution.py:49
  44.2 11.8 %collective-permute-start.7 = (bf16[64,1024]{1,0:T(8,128)(2,1)S(1)}, bf16[64,1024]{1,0:T(8,128)(2,1)S(1)}, u32[]{:S(2)}, u32[]{:S(2)}) collective-permute-start(bf16[64,1024]{1,0:T(8,128)(2,1)S(1)} %get-tuple-element.44.refs_0_), channel_id=1, source_target_pairs={{0,13},{1,4},{2,15},{3,6},{4,1},{5,8},{6,3},{7,10},{8,5},{9,12},{1... | collective-permute-start | bytes 393224 | tf_op jit(solution)/shard_map/ppermute | solution.py:40
  44.3 13.4 %collective-permute-start.6 = (bf16[64,1024]{1,0:T(8,128)(2,1)S(1)}, bf16[64,1024]{1,0:T(8,128)(2,1)S(1)}, u32[]{:S(2)}, u32[]{:S(2)}) collective-permute-start(bf16[64,1024]{1,0:T(8,128)(2,1)S(1)} %get-tuple-element.44.refs_0_), channel_id=1, source_target_pairs={{0,1},{1,0},{2,3},{3,2},{4,5},{5,4},{6,7},{7,6},{8,9},{9,8},{10,11... | collective-permute-start | bytes 393224 | tf_op jit(solution)/shard_map/ppermute | solution.py:40
  49.3 12.9 %collective-permute-start.10 = (bf16[64,1024]{1,0:T(8,128)(2,1)S(1)}, bf16[64,1024]{1,0:T(8,128)(2,1)S(1)}, u32[]{:S(2)}, u32[]{:S(2)}) collective-permute-start(bf16[64,1024]{1,0:T(8,128)(2,1)S(1)} %collective-permute-done.5.ready_ref.refs_2_), channel_id=1, source_target_pairs={{0,4},{1,13},{2,6},{3,15},{4,8},{5,1},{6,10},{7,3},{8,12},{9,5},{1... | collective-permute-start | bytes 393224 | tf_op jit(solution)/shard_map/ppermute | solution.py:40
  52.4 11.4 %collective-permute-start.13 = (bf16[64,1024]{1,0:T(8,128)(2,1)}, bf16[64,1024]{1,0:T(8,128)(2,1)}, u32[]{:S(2)}, u32[]{:S(2)}) collective-permute-start(bf16[64,1024]{1,0:T(8,128)(2,1)} %get-tuple-element.48.refs_1_), channel_id=1, source_target_pairs={{0,4},{1,13},{2,6},{3,15},{4,8},{5,1},{6,10},{7,3},{8,12},{9,5},{1... | collective-permute-start | bytes 393224 | tf_op jit(solution)/shard_map/ppermute | solution.py:40
  52.4 11.4 %collective-permute-start.14 = (bf16[64,1024]{1,0:T(8,128)(2,1)}, bf16[64,1024]{1,0:T(8,128)(2,1)}, u32[]{:S(2)}, u32[]{:S(2)}) collective-permute-start(bf16[64,1024]{1,0:T(8,128)(2,1)} %get-tuple-element.48.refs_1_), channel_id=1, source_target_pairs={{0,13},{1,4},{2,15},{3,6},{4,1},{5,8},{6,3},{7,10},{8,5},{9,12},{1... | collective-permute-start | bytes 393224 | tf_op jit(solution)/shard_map/ppermute | solution.py:40
  56.1 8.0 %collective-permute-start.8 = (bf16[64,1024]{1,0:T(8,128)(2,1)S(1)}, bf16[64,1024]{1,0:T(8,128)(2,1)S(1)}, u32[]{:S(2)}, u32[]{:S(2)}) collective-permute-start(bf16[64,1024]{1,0:T(8,128)(2,1)S(1)} %collective-permute-done.5.ready_ref.refs_2_), channel_id=1, source_target_pairs={{0,1},{1,0},{2,3},{3,2},{4,5},{5,4},{6,7},{7,6},{8,9},{9,8},{10,11... | collective-permute-start | bytes 393224 | tf_op jit(solution)/shard_map/ppermute | solution.py:40
  63.8 14.2 %collective-permute-start.12 = (bf16[64,1024]{1,0:T(8,128)(2,1)}, bf16[64,1024]{1,0:T(8,128)(2,1)}, u32[]{:S(2)}, u32[]{:S(2)}) collective-permute-start(bf16[64,1024]{1,0:T(8,128)(2,1)} %get-tuple-element.48.refs_1_), channel_id=1, source_target_pairs={{0,1},{1,0},{2,3},{3,2},{4,5},{5,4},{6,7},{7,6},{8,9},{9,8},{10,11... | collective-permute-start | bytes 393224 | tf_op jit(solution)/shard_map/ppermute | solution.py:40
  63.8 15.7 %collective-permute-start.17 = (bf16[64,1024]{1,0:T(8,128)(2,1)}, bf16[64,1024]{1,0:T(8,128)(2,1)}, u32[]{:S(2)}, u32[]{:S(2)}) collective-permute-start(bf16[64,1024]{1,0:T(8,128)(2,1)} %collective-permute-done.13.refs_3_), channel_id=1, source_target_pairs={{0,4},{1,13},{2,6},{3,15},{4,8},{5,1},{6,10},{7,3},{8,12},{9,5},{1... | collective-permute-start | bytes 393224 | tf_op jit(solution)/shard_map/ppermute | solution.py:40
  64.7 16.2 %collective-permute-start.15 = (bf16[64,1024]{1,0:T(8,128)(2,1)}, bf16[64,1024]{1,0:T(8,128)(2,1)}, u32[]{:S(2)}, u32[]{:S(2)}) collective-permute-start(bf16[64,1024]{1,0:T(8,128)(2,1)} %collective-permute-done.13.refs_3_), channel_id=1, source_target_pairs={{0,1},{1,0},{2,3},{3,2},{4,5},{5,4},{6,7},{7,6},{8,9},{9,8},{10,11... | collective-permute-start | bytes 393224 | tf_op jit(solution)/shard_map/ppermute | solution.py:40
  65.6 15.4 %collective-permute-start.16 = (bf16[64,1024]{1,0:T(8,128)(2,1)}, bf16[64,1024]{1,0:T(8,128)(2,1)}, u32[]{:S(2)}, u32[]{:S(2)}) collective-permute-start(bf16[64,1024]{1,0:T(8,128)(2,1)} %collective-permute-done.14.refs_4_), channel_id=1, source_target_pairs={{0,1},{1,0},{2,3},{3,2},{4,5},{5,4},{6,7},{7,6},{8,9},{9,8},{10,11... | collective-permute-start | bytes 393224 | tf_op jit(solution)/shard_map/ppermute | solution.py:40
  76.2 8.8 %collective-permute-start.20 = (bf16[512,256]{1,0:T(8,128)(2,1)}, bf16[512,256]{1,0:T(8,128)(2,1)}, u32[]{:S(2)}, u32[]{:S(2)}) collective-permute-start(bf16[512,256]{1,0:T(8,128)(2,1)} %get-tuple-element.49.refs_3_), channel_id=1, source_target_pairs={{0,2},{1,3},{2,0},{3,1},{4,6},{5,7},{6,4},{7,5},{8,10},{9,11},{10,... | collective-permute-start | bytes 786440 | tf_op jit(solution)/shard_map/ppermute | solution.py:40
  78.0 17.3 %collective-permute-start.21 = (bf16[512,256]{1,0:T(8,128)(2,1)}, bf16[512,256]{1,0:T(8,128)(2,1)}, u32[]{:S(2)}, u32[]{:S(2)}) collective-permute-start(bf16[512,256]{1,0:T(8,128)(2,1)} %get-tuple-element.49.refs_3_), channel_id=1, source_target_pairs={{0,16},{1,17},{2,18},{3,19},{4,20},{5,21},{6,22},{7,23},{8,24},{9,... | collective-permute-start | bytes 786440 | tf_op jit(solution)/shard_map/ppermute | solution.py:40
  79.4 15.8 %collective-permute-start.22 = (bf16[512,256]{1,0:T(8,128)(2,1)}, bf16[512,256]{1,0:T(8,128)(2,1)}, u32[]{:S(2)}, u32[]{:S(2)}) collective-permute-start(bf16[512,256]{1,0:T(8,128)(2,1)} %get-tuple-element.49.refs_3_), channel_id=1, source_target_pairs={{0,18},{1,19},{2,16},{3,17},{4,22},{5,23},{6,20},{7,21},{8,26},{9,... | collective-permute-start | bytes 786440 | tf_op jit(solution)/shard_map/ppermute | solution.py:40
  102.6 9.3 %collective-permute-start.23 = (bf16[512,256]{1,0:T(8,128)(2,1)S(1)}, bf16[512,256]{1,0:T(8,128)(2,1)S(1)}, u32[]{:S(2)}, u32[]{:S(2)}) collective-permute-start(bf16[512,256]{1,0:T(8,128)(2,1)S(1)} %get-tuple-element.52), channel_id=1, source_target_pairs={{0,2},{1,3},{2,0},{3,1},{4,6},{5,7},{6,4},{7,5},{8,10},{9,11},{10,... | collective-permute-start | bytes 786440 | tf_op jit(solution)/shard_map/ppermute | solution.py:40
  103.2 11.8 %collective-permute-start.24 = (bf16[512,256]{1,0:T(8,128)(2,1)S(1)}, bf16[512,256]{1,0:T(8,128)(2,1)S(1)}, u32[]{:S(2)}, u32[]{:S(2)}) collective-permute-start(bf16[512,256]{1,0:T(8,128)(2,1)S(1)} %get-tuple-element.53), channel_id=1, source_target_pairs={{16,0},{17,1},{18,2},{19,3},{20,4},{21,5},{22,6},{23,7},{24,8},{25... | collective-permute-start | bytes 786440 | tf_op jit(solution)/shard_map/ppermute | solution.py:40
  104.7 10.3 %collective-permute-start.25 = (bf16[512,256]{1,0:T(8,128)(2,1)S(1)}, bf16[512,256]{1,0:T(8,128)(2,1)S(1)}, u32[]{:S(2)}, u32[]{:S(2)}) collective-permute-start(bf16[512,256]{1,0:T(8,128)(2,1)S(1)} %get-tuple-element.54), channel_id=1, source_target_pairs={{16,2},{17,3},{18,0},{19,1},{20,6},{21,7},{22,4},{23,5},{24,10},{2... | collective-permute-start | bytes 786440 | tf_op jit(solution)/shard_map/ppermute | solution.py:40
  117.9 8.9 %collective-permute-start.28 = (bf16[64,1024]{1,0:T(8,128)(2,1)S(1)}, bf16[64,1024]{1,0:T(8,128)(2,1)S(1)}, u32[]{:S(2)}, u32[]{:S(2)}) collective-permute-start(bf16[64,1024]{1,0:T(8,128)(2,1)S(1)} %get-tuple-element.64), channel_id=1, source_target_pairs={{0,12},{1,5},{2,14},{3,7},{4,0},{5,9},{6,2},{7,11},{8,4},{9,13},{1... | collective-permute-start | bytes 393224 | tf_op jit(solution)/shard_map/ppermute | solution.py:40
  121.3 10.0 %collective-permute-start.27 = (bf16[64,1024]{1,0:T(8,128)(2,1)S(1)}, bf16[64,1024]{1,0:T(8,128)(2,1)S(1)}, u32[]{:S(2)}, u32[]{:S(2)}) collective-permute-start(bf16[64,1024]{1,0:T(8,128)(2,1)S(1)} %get-tuple-element.62), channel_id=1, source_target_pairs={{0,13},{1,4},{2,15},{3,6},{4,1},{5,8},{6,3},{7,10},{8,5},{9,12},{1... | collective-permute-start | bytes 393224 | tf_op jit(solution)/shard_map/ppermute | solution.py:40
  134.5 9.9 %collective-permute-start.30 = (bf16[64,1024]{1,0:T(8,128)(2,1)S(1)}, bf16[64,1024]{1,0:T(8,128)(2,1)S(1)}, u32[]{:S(2)}, u32[]{:S(2)}) collective-permute-start(bf16[64,1024]{1,0:T(8,128)(2,1)S(1)} %divide_convert_fusion), channel_id=1, source_target_pairs={{1,2},{2,1},{3,4},{4,3},{5,6},{6,5},{7,8},{8,7},{9,10},{10,9},{11,... | collective-permute-start | bytes 393224 | tf_op jit(solution)/shard_map/ppermute | solution.py:45
  (32 other events, 191.9 us)
Sparse Core Ops, SparseCore 0:
  9.7 45.7 all-gather.2

commit v7 on v6

--- a/solution.py
+++ b/solution.py
@@ -116,13 +116,6 @@
 
 def gathered_weights(mine):
     return lax.all_gather(mine, "dp", axis=0, tiled=False)
-
-
-def rows_out(weights, turn, core):
-    rows = weights[:, :, 3 * HEAD :]
-    mine = lax.dynamic_index_in_dim(rows, turn * CORES + core, 0, keepdims=False)
-    theirs = lax.dynamic_index_in_dim(rows, turn * CORES + 1 - core, 0, keepdims=False)
-    return mine, other_core(theirs)
 
 
 def gathered_rows(shard):
@@ -228,132 +221,106 @@
             pltpu.VMEM((rows, width), grads.dtype),
             pltpu.SemaphoreType.DMA((2,)),
         ],
-        compiler_params=room(60),
+        compiler_params=room(16),
     )(where, edges, tokens, grads)
 
 
-def norm_kernel(core_ref, chip_ref, mid_token, mid_grad, count_ref, gain_ref, *outs):
-    normin_ref, normed_ref, rms_ref, dout_ref = outs
-    width = mid_token.shape[1]
+def norm_kernel(core_ref, chip_ref, mid_token, mid_grad, second_ref, count_ref, gain_ref, *outs):
+    both_ref, normed_ref, rms_ref, dout_ref = outs
+    seg, width = mid_token.shape
     got = core_ref[...].astype(F32) + chip_ref[...].astype(F32)
     pooled = (mid_token[...] + got[:, :width]) / count_ref[...]
     rms = jnp.sqrt(jnp.mean(pooled * pooled, axis=1, keepdims=True) + 1e-06)
     normed = pooled / rms
     normed_ref[...] = normed
     rms_ref[...] = rms
-    normin_ref[...] = (normed * gain_ref[...]).astype(jnp.bfloat16)
-    dout_ref[...] = mid_grad[...] + got[:, width:]
-
-
-def norm(from_core, from_chip, mid_token, mid_grad, count, gain):
+    last = lax.broadcasted_iota(jnp.int32, (seg, 1), 0) == seg - 1
+    dout = mid_grad[...] + got[:, width:] + jnp.where(last, second_ref[...], 0.0)
+    dout_ref[...] = dout
+    both_ref[:, :width] = (normed * gain_ref[...]).astype(jnp.bfloat16)
+    both_ref[:, width:] = dout.astype(jnp.bfloat16)
+
+
+def norm(from_core, from_chip, mid_token, mid_grad, second, count, gain):
     seg, width = mid_token.shape
     shape = jax.ShapeDtypeStruct
     return pl.pallas_call(
         norm_kernel,
         out_shape=(
-            shape((seg, width), jnp.bfloat16),
+            shape((seg, 2 * width), jnp.bfloat16),
             shape((seg, width), F32),
             shape((seg, 1), F32),
             shape((seg, width), F32),
         ),
-        in_specs=[VMEM] * 6,
+        in_specs=[VMEM] * 7,
         out_specs=(VMEM,) * 4,
         compiler_params=room(6),
-    )(from_core, from_chip, mid_token, mid_grad, count, gain)
-
-
-def dout_kernel(dout_ref, second_ref, ready_ref, full_ref, half_ref):
-    seg = dout_ref.shape[0]
-    last = lax.broadcasted_iota(jnp.int32, (seg, 1), 0) == seg - 1
-    dout = dout_ref[...] + jnp.where(last, second_ref[...], 0.0)
-    full_ref[...] = dout
-    half_ref[...] = dout.astype(jnp.bfloat16)
-
-
-def whole_dout(dout, second, ready):
-    shape = jax.ShapeDtypeStruct
-    return pl.pallas_call(
-        dout_kernel,
-        out_shape=(shape(dout.shape, F32), shape(dout.shape, jnp.bfloat16)),
-        in_specs=[VMEM, VMEM, ANY],
-        out_specs=(VMEM, VMEM),
-        compiler_params=room(4),
-    )(dout, second, ready)
-
-
-def project_kernel(*refs):
-    pieces, weight = refs[:8], refs[8]
-    q_ref, kv_ref, w_ref, rows, sems = refs[9:]
+    )(from_core, from_chip, mid_token, mid_grad, second, count, gain)
+
+
+def project_kernel(seg, *refs):
+    place_ref, pieces, weight = refs[0], refs[1:9], refs[9]
+    q_ref, kv_ref, mine_ref, theirs_ref, rows, w_in, w_back, sems = refs[10:]
+    core, head = place_ref[3], place_ref[1] * CORES
+    half, wide = seg, rows.shape[1] // 4
+    depth = weight.shape[1]
     copies = stacked(pieces, rows)
-    depth = weight.shape[1]
     for i in range(weight.shape[0]):
-        copies.append((weight.at[i, :, : 3 * HEAD], w_ref.at[i * depth : (i + 1) * depth, :]))
+        copies.append((weight.at[i, :, : 3 * HEAD], w_in.at[i * depth : (i + 1) * depth, :]))
+    for j, its_head in enumerate((head + core, head + 1 - core)):
+        for i in range(2):
+            source = weight.at[its_head, i * half : (i + 1) * half, 3 * HEAD :]
+            lanes = slice(i * wide, (i + 1) * wide)
+            copies.append((source, w_back.at[j * half : (j + 1) * half, lanes]))
     fetched(copies, sems)
-    out = jnp.dot(rows[...], w_ref[...], preferred_element_type=F32).astype(jnp.bfloat16)
+    width = rows.shape[1] // 2
+    out = jnp.dot(rows[:, :width], w_in[...], preferred_element_type=F32).astype(jnp.bfloat16)
     q_ref[...] = out[:, :HEAD]
     kv_ref[...] = out[:, HEAD:]
-
-
-def project(pieces, weights):
-    rows = sum(piece.shape[0] for piece in pieces)
-    width = pieces[0].shape[1]
+    da = contract_last(rows[:, width:], w_back[...]).astype(jnp.bfloat16)
+    mine_ref[...] = da[:, :half]
+    for slot, its_slot in enumerate((1, 0, 4, 5, 2, 3, 7, 6)):
+        its_rows = slice(its_slot * seg, (its_slot + 1) * seg)
+        theirs_ref[its_rows, :] = da[slot * seg : (slot + 1) * seg, half:]
+
+
+def project(where, pieces, weights):
+    seg, width = pieces[0].shape
+    rows = seg * len(pieces)
+    half = HEAD // CORES
     bf16 = lambda *shape: jax.ShapeDtypeStruct(shape, jnp.bfloat16)
     return pl.pallas_call(
-        project_kernel,
-        out_shape=(
-            bf16(rows, HEAD),
-            bf16(rows, 2 * HEAD),
-            bf16(width, 3 * HEAD),
-        ),
-        in_specs=[ANY] * 9,
-        out_specs=(VMEM,) * 3,
+        functools.partial(project_kernel, half),
+        out_shape=(bf16(rows, HEAD), bf16(rows, 2 * HEAD), bf16(rows, half), bf16(rows, half)),
+        in_specs=[SMEM] + [ANY] * 9,
+        out_specs=(VMEM,) * 4,
         scratch_shapes=[
             pltpu.VMEM((rows, width), jnp.bfloat16),
-            pltpu.SemaphoreType.DMA((16,)),
+            pltpu.VMEM((width // 2, 3 * HEAD), jnp.bfloat16),
+            pltpu.VMEM((HEAD, width // 2), jnp.bfloat16),
+            pltpu.SemaphoreType.DMA((20,)),
         ],
         compiler_params=room(12),
-    )(*pieces, weights)
-
-
-def dattended_kernel(*refs):
-    place_ref, pieces, mine, theirs = refs[0], refs[1:9], refs[9], refs[10]
-    da_ref, rows, weight, sems = refs[11:]
-    core = place_ref[3]
-    half, wide = mine.shape[0] // 2, mine.shape[1]
-    spot = pl.multiple_of(core * half, half)
-    other = pl.multiple_of((1 - core) * half, half)
-    copies = stacked(pieces, rows)
-    for i in range(2):
-        part, lanes = slice(i * half, (i + 1) * half), slice(i * wide, (i + 1) * wide)
-        copies.append((mine.at[part, :], weight.at[pl.ds(spot, half), lanes]))
-        copies.append((theirs.at[part, :], weight.at[pl.ds(other, half), lanes]))
-    fetched(copies, sems)
-    da_ref[...] = contract_last(rows[...], weight[...]).astype(jnp.bfloat16)
-
-
-def dattended(where, pieces, mine, theirs):
-    rows = sum(piece.shape[0] for piece in pieces)
-    width = pieces[0].shape[1]
-    return pl.pallas_call(
-        dattended_kernel,
-        out_shape=jax.ShapeDtypeStruct((rows, HEAD), jnp.bfloat16),
-        in_specs=[SMEM] + [ANY] * 10,
-        out_specs=VMEM,
-        scratch_shapes=[
-            pltpu.VMEM((rows, width), jnp.bfloat16),
-            pltpu.VMEM((HEAD, width), jnp.bfloat16),
-            pltpu.SemaphoreType.DMA((12,)),
-        ],
-        compiler_params=room(10),
-    )(where, *pieces, mine, theirs)
+    )(where, *pieces, weights)
 
 
 def attention_kernel(tile, seg, *refs):
-    place_ref, q_ref, da_ref, blocks = refs[0], refs[1], refs[2], refs[3:7]
-    dq_ref, outs, (kv, dkt, dvt, sems) = refs[7], refs[8:12], refs[12:]
+    place_ref, q_ref, mine_ref, theirs_ref, blocks = *refs[:4], refs[4:8]
+    dq_ref, outs, (kv, da_ref, dkt, dvt, sems) = refs[8], refs[9:13], refs[13:]
     half, turn, pair, core = place_ref[0], place_ref[1], place_ref[2], place_ref[3]
     queries, keys = q_ref.shape[0], kv.shape[0]
     fetched(stacked(blocks, kv), sems)
+
+    @pl.when(core == 0)
+    def _():
+        da_ref[:, : HEAD // 2] = mine_ref[...]
+        da_ref[:, HEAD // 2 :] = theirs_ref[...]
+
+    @pl.when(core == 1)
+    def _():
+        da_ref[:, : HEAD // 2] = theirs_ref[...]
+        da_ref[:, HEAD // 2 :] = mine_ref[...]
+
     spot = lax.broadcasted_iota(jnp.int32, (1, keys), 1)
     block = spot // queries
     key_half = jnp.where(block < 2, half, 1 - half)
@@ -394,17 +361,18 @@
         out[:, HEAD:] = dvt[:, lanes].T.astype(jnp.bfloat16)
 
 
-def attention(where, q, da, blocks, seg):
+def attention(where, q, mine, theirs, blocks, seg):
     queries = q.shape[0]
     keys = sum(block.shape[0] for block in blocks)
     part = jax.ShapeDtypeStruct(blocks[0].shape, jnp.bfloat16)
     return pl.pallas_call(
         functools.partial(attention_kernel, 128, seg),
         out_shape=(jax.ShapeDtypeStruct((queries, HEAD), jnp.bfloat16),) + (part,) * 4,
-        in_specs=[SMEM] + [VMEM] * 2 + [ANY] * 4,
+        in_specs=[SMEM] + [VMEM] * 3 + [ANY] * 4,
         out_specs=(VMEM,) * 5,
         scratch_shapes=[
             pltpu.VMEM((keys, 2 * HEAD), jnp.bfloat16),
+            pltpu.VMEM((queries, HEAD), jnp.bfloat16),
             pltpu.VMEM((HEAD, keys), F32),
             pltpu.VMEM((HEAD, keys), F32),
             pltpu.SemaphoreType.DMA((4,)),
@@ -415,30 +383,42 @@
             bytes_accessed=2 * HEAD * (3 * queries + 4 * keys),
             transcendentals=queries * keys,
         ),
-    )(where, q, da, *blocks)
+    )(where, q, mine, theirs, *blocks)
 
 
 def unproject_kernel(seg, dq_ref, *refs):
-    parts, w_ref, swap_ref, outs = refs[:4], refs[4], refs[5], refs[6:]
+    parts, weight, swap_ref, outs, (w_in, sems) = refs[:4], refs[4], refs[5], refs[6:10], refs[10:]
+    depth = weight.shape[1]
+    fetched(
+        [
+            (weight.at[i, :, : 3 * HEAD], w_in.at[i * depth : (i + 1) * depth, :])
+            for i in range(weight.shape[0])
+        ],
+        sems,
+    )
     dkv = sum(ref[...].astype(F32) for ref in parts).astype(jnp.bfloat16)
     left = jnp.concatenate([dq_ref[...], dkv], axis=1)
-    out = contract_last(left, w_ref[...])
+    out = contract_last(left, w_in[...])
     for i, slot in enumerate((1, 4, 5, 7)):
         swap_ref[i * seg : (i + 1) * seg, :] = out[slot * seg : (slot + 1) * seg].astype(WIRE)
     for ref, slot in zip(outs, (0, 2, 3, 6)):
         ref[...] = out[slot * seg : (slot + 1) * seg]
 
 
-def unproject(dq, parts, w_full, seg):
-    width = w_full.shape[0]
+def unproject(dq, parts, weights, seg):
+    width = weights.shape[0] * weights.shape[1]
     return pl.pallas_call(
         functools.partial(unproject_kernel, seg),
         out_shape=(jax.ShapeDtypeStruct((4 * seg, width), WIRE),)
         + (jax.ShapeDtypeStruct((seg, width), F32),) * 4,
-        in_specs=[VMEM] * 6,
+        in_specs=[VMEM] * 5 + [ANY],
         out_specs=(VMEM,) * 5,
+        scratch_shapes=[
+            pltpu.VMEM((width, 3 * HEAD), jnp.bfloat16),
+            pltpu.SemaphoreType.DMA((weights.shape[0],)),
+        ],
         compiler_params=room(16),
-    )(dq, *parts, w_full)
+    )(dq, *parts, weights)
 
 
 def join_kernel(swapped, own, near, next_to, far, own_out, near_out, next_out, far_out):
@@ -497,18 +477,16 @@
         where, edges, token_rows, grad_out, seg
     )
     second = two_back(first)
-    normin, normed, rms, dout = norm(
-        other_core(to_core), other_chip(to_chip), mid_token, mid_grad, count, gain[None]
+    both, normed, rms, dout = norm(
+        other_core(to_core), other_chip(to_chip), mid_token, mid_grad, second, count, gain[None]
     )
-    pieces = gathered_rows(normin)
-    q, own, w_full = project(pieces, weights)
-    dout, dout_b = whole_dout(dout, second, pieces[2])
+    q, own, mine, theirs = project(where, gathered_rows(both), weights)
     cross, far, beside = across(own, 0, True), across(own, 0, False), other_pair(own)
-    out_mine, out_theirs = rows_out(weights, turn, core)
-    da = dattended(where, gathered_rows(dout_b), out_mine, out_theirs)
-    dq, own, beside, far, cross = attention(where, q, da, (own, beside, far, cross), seg)
+    theirs = other_core(theirs)
+    blocks = (own, beside, far, cross)
+    dq, own, beside, far, cross = attention(where, q, mine, theirs, blocks, seg)
     parts = (own, other_pair(beside), across(far, 1, False), across(cross, 1, True))
-    dnormin = summed_rows(*unproject(dq, parts, w_full, seg))
+    dnormin = summed_rows(*unproject(dq, parts, weights, seg))
 
     scaled = dnormin * gain
     dpooled = dout + (scaled - normed * jnp.mean(scaled * normed, axis=-1, keepdims=True)) / rms

time: 154 us -> 143 us (0.929)
  waiting for transfers between devices: 46 us -> 74.6 us
  starting transfers between devices: 54.2 us -> 32.5 us
  local copies, waits for them, and re-layouts: 14.2 us -> 4.13 us
  Pallas kernels: 21.1 us -> 14.2 us
    ppermute x28 -> x21, waiting for transfers between devices: 34.2 us -> 59 us  [moved(): return lax.ppermute(value, 'ctx', pairs)]
    ppermute x28 -> x21, starting transfers between devices: 31.5 us -> 12.9 us  [moved(): return lax.ppermute(value, 'ctx', pairs)]
    unnamed x46 -> x16, local copies, waits for them, and re-layouts: 12.6 us -> 3.35 us
    ppermute x1, waiting for transfers between devices: 0.01 us -> 6.6 us  [two_back(): lax.ppermute(value, 'ctx', [(i, i - CORES) for i in range(CORES, CTX)])]
    pallas_call x4 -> x2, Pallas kernels: 6.23 us -> 2.33 us  [the longest x1 2.08 us: project(): pl.pallas_call(functools.partial(project_kernel, half), out_shape=(bf16(r...]
    ppermute x3, waiting for transfers between devices: 11.8 us -> 8.92 us  [other_chip(): return lax.ppermute(value, 'ctx', pairs)]
    ppermute x3, starting transfers between devices: 20 us -> 17.3 us  [other_chip(): return lax.ppermute(value, 'ctx', pairs)]
    pallas_call x1, Pallas kernels: 4.15 us -> 1.77 us  [window_sums(): pl.pallas_call(window_kernel, out_shape=(shape((seg, 2 * width), WIRE), s...]
  transfers between devices with their start and end apart: 33 -> 26, of which waited for: 12 -> 15; matrix products, arithmetic and copies ran while one was open for 2% -> 1% of each run, Pallas kernels for 7% -> 1%
where the time goes in v7:
time: 143 us
  waiting for transfers between devices  74.6 us (52%)
  starting transfers between devices  32.5 us (23%)
  Pallas kernels  14.2 us (10%)
  between operations  13.7 us (10%)
  local copies, waits for them, and re-layouts  4.13 us (3%)
  other arithmetic  2.11 us (1%)
  matrix products  1.46 us (1%)
    ppermute x21, waiting for transfers between devices, moved(): return lax.ppermute(value, 'ctx', pairs)  59 us
    ppermute x3, starting transfers between devices, other_chip(): return lax.ppermute(value, 'ctx', pairs)  17.3 us
    ppermute x21, starting transfers between devices, moved(): return lax.ppermute(value, 'ctx', pairs)  12.9 us
    ppermute x3, waiting for transfers between devices, other_chip(): return lax.ppermute(value, 'ctx', pairs)  8.92 us
    ppermute x1, waiting for transfers between devices, two_back(): lax.ppermute(value, 'ctx', [(i, i - CORES) for i in range(CORES, CTX)])  6.6 us
    pallas_call x1, Pallas kernels, attention(): pl.pallas_call(functools.partial(attention_kernel, 128, seg), out_shape=(...  6.59 us
    unnamed x16, local copies, waits for them, and re-layouts  3.35 us
  transfers between devices with their start and end apart: 26, of which 15 were waited for; matrix products, arithmetic and copies ran while one was open for 1% of the time, Pallas kernels for 1%

profile of v7, /device:TPU:6, one launch (start us, length us, event | category | flops | bytes accessed | tf_op | source)
XLA Modules:
  0.0 142.7 jit_solution(15583175628338090145)
XLA Ops:
  7.2 2.5 %shard_map.82 = (bf16[128,896]{1,0:T(8,128)(2,1)}, s32[1,64]{1,0:T(1,128)}) custom-call(s32[6]{0:T(128)} %stack.35.place_ref.refs_0_, bf16[128,1024]{1,0:T(8,128)(2,1)} %q_ref.1, bf16[128,1024]{1,0:T(8,128)(2,1)} %k_ref.1, bf16[128,1024]{1,0:T(8,128)(2,1)} %v_ref.1, bf16[128,1024]{1,0:T(8,128)(2,1)} %o_ref.1, s32[1,64]{1,0:T(1,128)} %start_ref.1), custom_call_target="tpu_custom_call" | custom-call | tf_op jit(solution)/shard_map/pallas_call | solution.py:104
  9.7 8.0 %collective-permute-start = (s32[64]{0:T(128)}, s32[64]{0:T(128)S(1)}, u32[]{:S(2)}, u32[]{:S(2)}) collective-permute-start(s32[64]{0:T(128)} %bitcast.27), channel_id=1, source_target_pairs={{1,2},{2,1},{3,4},{4,3},{5,6},{6,5},{7,8},{8,7},{9,10},{10,9},{11,... | collective-permute-start | bytes 776 | tf_op jit(solution)/shard_map/ppermute | solution.py:45
  22.7 1.8 %shard_map.83 = (bf16[64,2048]{1,0:T(8,128)(2,1)S(1)}, bf16[64,2048]{1,0:T(8,128)(2,1)S(1)}, f32[64,1024]{1,0:T(8,128)S(1)}, f32[64,1024]{1,0:T(8,128)S(1)}, f32[1,1024]{1,0:T(1,128)S(1)}, /*index=5*/f32[64,1]{1,0:T(8,128)S(1)}) custom-call(s32[6]{0:T(128)S(1)} %copy-done.6, s32[3,192,1]{2,1,0:T(8,128)S(1)} %copy.9.edge_ref, bf16[512,1024]{1,0:T(8,128)(2,1)S(1)} %bitcast.21, ...), custom_call_target="tpu_custom_call" | custom-call | tf_op jit(solution)/shard_map/pallas_call | solution.py:207
  24.6 7.1 %collective-permute-start.3 = (bf16[64,2048]{1,0:T(8,128)(2,1)S(1)}, bf16[64,2048]{1,0:T(8,128)(2,1)S(1)}, u32[]{:S(2)}, u32[]{:S(2)}) collective-permute-start(bf16[64,2048]{1,0:T(8,128)(2,1)S(1)} %get-tuple-element.37), channel_id=1, source_target_pairs={{1,2},{2,1},{3,4},{4,3},{5,6},{6,5},{7,8},{8,7},{9,10},{10,9},{11,... | collective-permute-start | bytes 786440 | tf_op jit(solution)/shard_map/ppermute | solution.py:45
  31.7 2.3 %collective-permute-start.4 = (f32[1,1024]{1,0:T(1,128)S(1)}, f32[1,1024]{1,0:T(1,128)S(1)}, u32[]{:S(2)}, u32[]{:S(2)}) collective-permute-start(f32[1,1024]{1,0:T(1,128)S(1)} %get-tuple-element.40), channel_id=1, source_target_pairs={{2,0},{3,1},{4,2},{5,3},{6,4},{7,5},{8,6},{9,7},{10,8},{11,9},{12,... | collective-permute-start | bytes 12296 | tf_op jit(solution)/shard_map/ppermute | solution.py:49
  34.0 6.6 %collective-permute-done.4.second_ref = f32[1,1024]{1,0:T(1,128)S(1)} collective-permute-done((f32[1,1024]{1,0:T(1,128)S(1)}, f32[1,1024]{1,0:T(1,128)S(1)}, u32[]{:S(2)}, u32[]{:S(2)}) %collective-permute-start.4) | collective-permute-done | bytes 4128 | tf_op jit(solution)/shard_map/ppermute | solution.py:49
  41.1 14.4 %collective-permute-done.6.refs_3_ = bf16[64,2048]{1,0:T(8,128)(2,1)S(1)} collective-permute-done((bf16[64,2048]{1,0:T(8,128)(2,1)S(1)}, bf16[64,2048]{1,0:T(8,128)(2,1)S(1)}, u32[]{:S(2)}, u32[]{:S(2)}) %collective-permute-start.6) | collective-permute-done | bytes 262176 | tf_op jit(solution)/shard_map/ppermute | solution.py:40
  56.0 8.0 %collective-permute-done.10.refs_7_ = bf16[64,2048]{1,0:T(8,128)(2,1)S(1)} collective-permute-done((bf16[64,2048]{1,0:T(8,128)(2,1)S(1)}, bf16[64,2048]{1,0:T(8,128)(2,1)S(1)}, u32[]{:S(2)}, u32[]{:S(2)}) %collective-permute-start.10) | collective-permute-done | bytes 262176 | tf_op jit(solution)/shard_map/ppermute | solution.py:40
  64.0 1.5 %collective-permute-done.11.refs_8_ = bf16[64,2048]{1,0:T(8,128)(2,1)S(1)} collective-permute-done((bf16[64,2048]{1,0:T(8,128)(2,1)S(1)}, bf16[64,2048]{1,0:T(8,128)(2,1)S(1)}, u32[]{:S(2)}, u32[]{:S(2)}) %collective-permute-start.11) | collective-permute-done | bytes 262176 | tf_op jit(solution)/shard_map/ppermute | solution.py:40
  65.5 1.5 %copy-done = bf16[1024,896]{1,0:T(8,128)(2,1)S(1)} copy-done((bf16[1024,896]{1,0:T(8,128)(2,1)S(1)}, bf16[1024,896]{1,0:T(8,128)(2,1)}, u32[]{:S(2)}) %copy-start) | copy-done | bytes 1835032
  67.0 2.1 %shard_map.85 = (bf16[512,128]{1,0:T(8,128)(2,1)S(1)}, bf16[512,256]{1,0:T(8,128)(2,1)S(1)}, bf16[512,64]{1,0:T(8,128)(2,1)S(1)}, bf16[512,64]{1,0:T(8,128)(2,1)S(1)}) custom-call(s32[6]{0:T(128)S(1)} %copy-done.7, bf16[64,2048]{1,0:T(8,128)(2,1)S(1)} %get-tuple-element.43.refs_1_, bf16[64,2048]{1,0:T(8,128)(2,1)S(1)} %collective-permute-done.5.refs_2_, ...), custom_call_target="tpu_custom_call" | custom-call | tf_op jit(solution)/shard_map/pallas_call | solution.py:292
  73.2 4.3 %collective-permute-done.13.refs_5_ = bf16[512,256]{1,0:T(8,128)(2,1)S(1)} collective-permute-done((bf16[512,256]{1,0:T(8,128)(2,1)S(1)}, bf16[512,256]{1,0:T(8,128)(2,1)S(1)}, u32[]{:S(2)}, u32[]{:S(2)}) %collective-permute-start.13) | collective-permute-done | bytes 262176 | tf_op jit(solution)/shard_map/ppermute | solution.py:40
  77.5 9.0 %collective-permute-done.14.refs_6_ = bf16[512,256]{1,0:T(8,128)(2,1)S(1)} collective-permute-done((bf16[512,256]{1,0:T(8,128)(2,1)S(1)}, bf16[512,256]{1,0:T(8,128)(2,1)S(1)}, u32[]{:S(2)}, u32[]{:S(2)}) %collective-permute-start.14) | collective-permute-done | bytes 262176 | tf_op jit(solution)/shard_map/ppermute | solution.py:40
  86.6 6.6 %shard_map.86 = (bf16[512,128]{1,0:T(8,128)(2,1)S(1)}, bf16[512,256]{1,0:T(8,128)(2,1)S(1)}, bf16[512,256]{1,0:T(8,128)(2,1)S(1)}, bf16[512,256]{1,0:T(8,128)(2,1)S(1)}, bf16[512,256]{1,0:T(8,128)(2,1)S(1)}) custom-call(s32[6]{0:T(128)S(1)} %copy-done.7, bf16[512,128]{1,0:T(8,128)(2,1)S(1)} %get-tuple-element.45.refs_1_, ...), custom_call_target="tpu_custom_call" | custom-call | flops 1610612736 | bytes 2490368 | tf_op jit(solution)/shard_map/pallas_call | solution.py:368
  93.2 1.8 %collective-permute-start.16 = (bf16[512,256]{1,0:T(8,128)(2,1)S(1)}, bf16[512,256]{1,0:T(8,128)(2,1)S(1)}, u32[]{:S(2)}, u32[]{:S(2)}) collective-permute-start(bf16[512,256]{1,0:T(8,128)(2,1)S(1)} %get-tuple-element.51), channel_id=1, source_target_pairs={{0,2},{1,3},{2,0},{3,1},{4,6},{5,7},{6,4},{7,5},{8,10},{9,11},{10,... | collective-permute-start | bytes 786440 | tf_op jit(solution)/shard_map/ppermute | solution.py:40
  97.8 4.7 %collective-permute-done.16.refs_1_ = bf16[512,256]{1,0:T(8,128)(2,1)S(1)} collective-permute-done((bf16[512,256]{1,0:T(8,128)(2,1)S(1)}, bf16[512,256]{1,0:T(8,128)(2,1)S(1)}, u32[]{:S(2)}, u32[]{:S(2)}) %collective-permute-start.16) | collective-permute-done | bytes 262176 | tf_op jit(solution)/shard_map/ppermute | solution.py:40
  102.5 4.1 %collective-permute-done.17.refs_2_ = bf16[512,256]{1,0:T(8,128)(2,1)S(1)} collective-permute-done((bf16[512,256]{1,0:T(8,128)(2,1)S(1)}, bf16[512,256]{1,0:T(8,128)(2,1)S(1)}, u32[]{:S(2)}, u32[]{:S(2)}) %collective-permute-start.17) | collective-permute-done | bytes 262176 | tf_op jit(solution)/shard_map/ppermute | solution.py:40
  107.7 1.9 %collective-permute-done.19.swapped = bf16[256,1024]{1,0:T(8,128)(2,1)S(1)} collective-permute-done((bf16[256,1024]{1,0:T(8,128)(2,1)S(1)}, bf16[256,1024]{1,0:T(8,128)(2,1)S(1)}, u32[]{:S(2)}, u32[]{:S(2)}) %collective-permute-start.19) | collective-permute-done | bytes 524320 | tf_op jit(solution)/shard_map/ppermute | solution.py:40
  109.8 3.6 %collective-permute-start.20 = (bf16[64,1024]{1,0:T(8,128)(2,1)S(1)}, bf16[64,1024]{1,0:T(8,128)(2,1)S(1)}, u32[]{:S(2)}, u32[]{:S(2)}) collective-permute-start(bf16[64,1024]{1,0:T(8,128)(2,1)S(1)} %get-tuple-element.60), channel_id=1, source_target_pairs={{0,13},{1,4},{2,15},{3,6},{4,1},{5,8},{6,3},{7,10},{8,5},{9,12},{1... | collective-permute-start | bytes 393224 | tf_op jit(solution)/shard_map/ppermute | solution.py:40
  113.3 4.3 %collective-permute-done.21 = bf16[64,1024]{1,0:T(8,128)(2,1)S(1)} collective-permute-done((bf16[64,1024]{1,0:T(8,128)(2,1)S(1)}, bf16[64,1024]{1,0:T(8,128)(2,1)S(1)}, u32[]{:S(2)}, u32[]{:S(2)}) %collective-permute-start.21) | collective-permute-done | bytes 131104 | tf_op jit(solution)/shard_map/ppermute | solution.py:40
  118.6 2.2 %collective-permute-done.20 = bf16[64,1024]{1,0:T(8,128)(2,1)S(1)} collective-permute-done((bf16[64,1024]{1,0:T(8,128)(2,1)S(1)}, bf16[64,1024]{1,0:T(8,128)(2,1)S(1)}, u32[]{:S(2)}, u32[]{:S(2)}) %collective-permute-start.20) | collective-permute-done | bytes 131104 | tf_op jit(solution)/shard_map/ppermute | solution.py:40
  120.8 3.3 %collective-permute-done.22 = bf16[64,1024]{1,0:T(8,128)(2,1)S(1)} collective-permute-done((bf16[64,1024]{1,0:T(8,128)(2,1)S(1)}, bf16[64,1024]{1,0:T(8,128)(2,1)S(1)}, u32[]{:S(2)}, u32[]{:S(2)}) %collective-permute-start.22) | collective-permute-done | bytes 131104 | tf_op jit(solution)/shard_map/ppermute | solution.py:40
  124.4 2.2 %collective-permute-start.23 = (bf16[64,1024]{1,0:T(8,128)(2,1)S(1)}, bf16[64,1024]{1,0:T(8,128)(2,1)S(1)}, u32[]{:S(2)}, u32[]{:S(2)}) collective-permute-start(bf16[64,1024]{1,0:T(8,128)(2,1)S(1)} %divide_convert_fusion), channel_id=1, source_target_pairs={{1,2},{2,1},{3,4},{4,3},{5,6},{6,5},{7,8},{8,7},{9,10},{10,9},{11,... | collective-permute-start | bytes 393224 | tf_op jit(solution)/shard_map/ppermute | solution.py:45
  126.7 7.6 %collective-permute-done.23 = bf16[64,1024]{1,0:T(8,128)(2,1)S(1)} collective-permute-done((bf16[64,1024]{1,0:T(8,128)(2,1)S(1)}, bf16[64,1024]{1,0:T(8,128)(2,1)S(1)}, u32[]{:S(2)}, u32[]{:S(2)}) %collective-permute-start.23) | collective-permute-done | bytes 131104 | tf_op jit(solution)/shard_map/ppermute | solution.py:45
  (68 shorter events, 17.6 us)
Async XLA Ops:
  6.5 59.0 %all-gather.3.cloned.1.call-start = ((), (), s32[]{:S(2)}) async-start(), calls=%async_computation | async-start | bytes 2064384 | tf_op jit(solution)/shard_map/all_gather | solution.py:118
  9.7 9.5 %collective-permute-start = (s32[64]{0:T(128)}, s32[64]{0:T(128)S(1)}, u32[]{:S(2)}, u32[]{:S(2)}) collective-permute-start(s32[64]{0:T(128)} %bitcast.27), channel_id=1, source_target_pairs={{1,2},{2,1},{3,4},{4,3},{5,6},{6,5},{7,8},{8,7},{9,10},{10,9},{11,... | collective-permute-start | bytes 776 | tf_op jit(solution)/shard_map/ppermute | solution.py:45
  24.5 16.1 %collective-permute-start.2 = (bf16[64,2048]{1,0:T(8,128)(2,1)S(1)}, bf16[64,2048]{1,0:T(8,128)(2,1)S(1)}, u32[]{:S(2)}, u32[]{:S(2)}) collective-permute-start(bf16[64,2048]{1,0:T(8,128)(2,1)S(1)} %get-tuple-element.36), channel_id=1, source_target_pairs={{0,1},{1,0},{2,3},{3,2},{4,5},{5,4},{6,7},{7,6},{8,9},{9,8},{10,11... | collective-permute-start | bytes 786440 | tf_op jit(solution)/shard_map/ppermute | solution.py:40
  24.6 16.0 %collective-permute-start.3 = (bf16[64,2048]{1,0:T(8,128)(2,1)S(1)}, bf16[64,2048]{1,0:T(8,128)(2,1)S(1)}, u32[]{:S(2)}, u32[]{:S(2)}) collective-permute-start(bf16[64,2048]{1,0:T(8,128)(2,1)S(1)} %get-tuple-element.37), channel_id=1, source_target_pairs={{1,2},{2,1},{3,4},{4,3},{5,6},{6,5},{7,8},{8,7},{9,10},{10,9},{11,... | collective-permute-start | bytes 786440 | tf_op jit(solution)/shard_map/ppermute | solution.py:45
  31.7 8.9 %collective-permute-start.4 = (f32[1,1024]{1,0:T(1,128)S(1)}, f32[1,1024]{1,0:T(1,128)S(1)}, u32[]{:S(2)}, u32[]{:S(2)}) collective-permute-start(f32[1,1024]{1,0:T(1,128)S(1)} %get-tuple-element.40), channel_id=1, source_target_pairs={{2,0},{3,1},{4,2},{5,3},{6,4},{7,5},{8,6},{9,7},{10,8},{11,9},{12,... | collective-permute-start | bytes 12296 | tf_op jit(solution)/shard_map/ppermute | solution.py:49
  40.9 14.6 %collective-permute-start.6 = (bf16[64,2048]{1,0:T(8,128)(2,1)S(1)}, bf16[64,2048]{1,0:T(8,128)(2,1)S(1)}, u32[]{:S(2)}, u32[]{:S(2)}) collective-permute-start(bf16[64,2048]{1,0:T(8,128)(2,1)S(1)} %get-tuple-element.43.refs_1_), channel_id=1, source_target_pairs={{0,4},{1,13},{2,6},{3,15},{4,8},{5,1},{6,10},{7,3},{8,12},{9,5},{1... | collective-permute-start | bytes 786440 | tf_op jit(solution)/shard_map/ppermute | solution.py:40
  41.0 15.0 %collective-permute-start.7 = (bf16[64,2048]{1,0:T(8,128)(2,1)S(1)}, bf16[64,2048]{1,0:T(8,128)(2,1)S(1)}, u32[]{:S(2)}, u32[]{:S(2)}) collective-permute-start(bf16[64,2048]{1,0:T(8,128)(2,1)S(1)} %get-tuple-element.43.refs_1_), channel_id=1, source_target_pairs={{0,13},{1,4},{2,15},{3,6},{4,1},{5,8},{6,3},{7,10},{8,5},{9,12},{1... | collective-permute-start | bytes 786440 | tf_op jit(solution)/shard_map/ppermute | solution.py:40
  55.5 8.5 %collective-permute-start.10 = (bf16[64,2048]{1,0:T(8,128)(2,1)S(1)}, bf16[64,2048]{1,0:T(8,128)(2,1)S(1)}, u32[]{:S(2)}, u32[]{:S(2)}) collective-permute-start(bf16[64,2048]{1,0:T(8,128)(2,1)S(1)} %collective-permute-done.6.refs_3_), channel_id=1, source_target_pairs={{0,4},{1,13},{2,6},{3,15},{4,8},{5,1},{6,10},{7,3},{8,12},{9,5},{1... | collective-permute-start | bytes 786440 | tf_op jit(solution)/shard_map/ppermute | solution.py:40
  55.5 8.5 %collective-permute-start.5 = (bf16[64,2048]{1,0:T(8,128)(2,1)S(1)}, bf16[64,2048]{1,0:T(8,128)(2,1)S(1)}, u32[]{:S(2)}, u32[]{:S(2)}) collective-permute-start(bf16[64,2048]{1,0:T(8,128)(2,1)S(1)} %get-tuple-element.43.refs_1_), channel_id=1, source_target_pairs={{0,1},{1,0},{2,3},{3,2},{4,5},{5,4},{6,7},{7,6},{8,9},{9,8},{10,11... | collective-permute-start | bytes 786440 | tf_op jit(solution)/shard_map/ppermute | solution.py:40
  55.5 8.5 %collective-permute-start.8 = (bf16[64,2048]{1,0:T(8,128)(2,1)S(1)}, bf16[64,2048]{1,0:T(8,128)(2,1)S(1)}, u32[]{:S(2)}, u32[]{:S(2)}) collective-permute-start(bf16[64,2048]{1,0:T(8,128)(2,1)S(1)} %collective-permute-done.6.refs_3_), channel_id=1, source_target_pairs={{0,1},{1,0},{2,3},{3,2},{4,5},{5,4},{6,7},{7,6},{8,9},{9,8},{10,11... | collective-permute-start | bytes 786440 | tf_op jit(solution)/shard_map/ppermute | solution.py:40
  56.0 8.0 %collective-permute-start.9 = (bf16[64,2048]{1,0:T(8,128)(2,1)S(1)}, bf16[64,2048]{1,0:T(8,128)(2,1)S(1)}, u32[]{:S(2)}, u32[]{:S(2)}) collective-permute-start(bf16[64,2048]{1,0:T(8,128)(2,1)S(1)} %collective-permute-done.7.refs_4_), channel_id=1, source_target_pairs={{0,1},{1,0},{2,3},{3,2},{4,5},{5,4},{6,7},{7,6},{8,9},{9,8},{10,11... | collective-permute-start | bytes 786440 | tf_op jit(solution)/shard_map/ppermute | solution.py:40
  64.0 1.5 %collective-permute-start.11 = (bf16[64,2048]{1,0:T(8,128)(2,1)S(1)}, bf16[64,2048]{1,0:T(8,128)(2,1)S(1)}, u32[]{:S(2)}, u32[]{:S(2)}) collective-permute-start(bf16[64,2048]{1,0:T(8,128)(2,1)S(1)} %collective-permute-done.10.refs_7_), channel_id=1, source_target_pairs={{0,1},{1,0},{2,3},{3,2},{4,5},{5,4},{6,7},{7,6},{8,9},{9,8},{10,11... | collective-permute-start | bytes 786440 | tf_op jit(solution)/shard_map/ppermute | solution.py:40
  69.1 8.4 %collective-permute-start.13 = (bf16[512,256]{1,0:T(8,128)(2,1)S(1)}, bf16[512,256]{1,0:T(8,128)(2,1)S(1)}, u32[]{:S(2)}, u32[]{:S(2)}) collective-permute-start(bf16[512,256]{1,0:T(8,128)(2,1)S(1)} %get-tuple-element.48.refs_4_), channel_id=1, source_target_pairs={{0,2},{1,3},{2,0},{3,1},{4,6},{5,7},{6,4},{7,5},{8,10},{9,11},{10,... | collective-permute-start | bytes 786440 | tf_op jit(solution)/shard_map/ppermute | solution.py:40
  69.2 17.4 %collective-permute-start.14 = (bf16[512,256]{1,0:T(8,128)(2,1)S(1)}, bf16[512,256]{1,0:T(8,128)(2,1)S(1)}, u32[]{:S(2)}, u32[]{:S(2)}) collective-permute-start(bf16[512,256]{1,0:T(8,128)(2,1)S(1)} %get-tuple-element.48.refs_4_), channel_id=1, source_target_pairs={{0,16},{1,17},{2,18},{3,19},{4,20},{5,21},{6,22},{7,23},{8,24},{9,... | collective-permute-start | bytes 786440 | tf_op jit(solution)/shard_map/ppermute | solution.py:40
  70.5 16.1 %collective-permute-start.15 = (bf16[512,256]{1,0:T(8,128)(2,1)S(1)}, bf16[512,256]{1,0:T(8,128)(2,1)S(1)}, u32[]{:S(2)}, u32[]{:S(2)}) collective-permute-start(bf16[512,256]{1,0:T(8,128)(2,1)S(1)} %get-tuple-element.48.refs_4_), channel_id=1, source_target_pairs={{0,18},{1,19},{2,16},{3,17},{4,22},{5,23},{6,20},{7,21},{8,26},{9,... | collective-permute-start | bytes 786440 | tf_op jit(solution)/shard_map/ppermute | solution.py:40
  93.2 9.3 %collective-permute-start.16 = (bf16[512,256]{1,0:T(8,128)(2,1)S(1)}, bf16[512,256]{1,0:T(8,128)(2,1)S(1)}, u32[]{:S(2)}, u32[]{:S(2)}) collective-permute-start(bf16[512,256]{1,0:T(8,128)(2,1)S(1)} %get-tuple-element.51), channel_id=1, source_target_pairs={{0,2},{1,3},{2,0},{3,1},{4,6},{5,7},{6,4},{7,5},{8,10},{9,11},{10,... | collective-permute-start | bytes 786440 | tf_op jit(solution)/shard_map/ppermute | solution.py:40
  95.0 11.6 %collective-permute-start.17 = (bf16[512,256]{1,0:T(8,128)(2,1)S(1)}, bf16[512,256]{1,0:T(8,128)(2,1)S(1)}, u32[]{:S(2)}, u32[]{:S(2)}) collective-permute-start(bf16[512,256]{1,0:T(8,128)(2,1)S(1)} %get-tuple-element.52), channel_id=1, source_target_pairs={{16,0},{17,1},{18,2},{19,3},{20,4},{21,5},{22,6},{23,7},{24,8},{25... | collective-permute-start | bytes 786440 | tf_op jit(solution)/shard_map/ppermute | solution.py:40
  96.5 10.1 %collective-permute-start.18 = (bf16[512,256]{1,0:T(8,128)(2,1)S(1)}, bf16[512,256]{1,0:T(8,128)(2,1)S(1)}, u32[]{:S(2)}, u32[]{:S(2)}) collective-permute-start(bf16[512,256]{1,0:T(8,128)(2,1)S(1)} %get-tuple-element.53), channel_id=1, source_target_pairs={{16,2},{17,3},{18,0},{19,1},{20,6},{21,7},{22,4},{23,5},{24,10},{2... | collective-permute-start | bytes 786440 | tf_op jit(solution)/shard_map/ppermute | solution.py:40
  107.6 2.0 %collective-permute-start.19 = (bf16[256,1024]{1,0:T(8,128)(2,1)S(1)}, bf16[256,1024]{1,0:T(8,128)(2,1)S(1)}, u32[]{:S(2)}, u32[]{:S(2)}) collective-permute-start(bf16[256,1024]{1,0:T(8,128)(2,1)S(1)} %get-tuple-element.54), channel_id=1, source_target_pairs={{0,1},{1,0},{2,3},{3,2},{4,5},{5,4},{6,7},{7,6},{8,9},{9,8},{10,11... | collective-permute-start | bytes 1572872 | tf_op jit(solution)/shard_map/ppermute | solution.py:40
  109.7 8.0 %collective-permute-start.21 = (bf16[64,1024]{1,0:T(8,128)(2,1)S(1)}, bf16[64,1024]{1,0:T(8,128)(2,1)S(1)}, u32[]{:S(2)}, u32[]{:S(2)}) collective-permute-start(bf16[64,1024]{1,0:T(8,128)(2,1)S(1)} %get-tuple-element.62), channel_id=1, source_target_pairs={{0,12},{1,5},{2,14},{3,7},{4,0},{5,9},{6,2},{7,11},{8,4},{9,13},{1... | collective-permute-start | bytes 393224 | tf_op jit(solution)/shard_map/ppermute | solution.py:40
  109.8 11.0 %collective-permute-start.20 = (bf16[64,1024]{1,0:T(8,128)(2,1)S(1)}, bf16[64,1024]{1,0:T(8,128)(2,1)S(1)}, u32[]{:S(2)}, u32[]{:S(2)}) collective-permute-start(bf16[64,1024]{1,0:T(8,128)(2,1)S(1)} %get-tuple-element.60), channel_id=1, source_target_pairs={{0,13},{1,4},{2,15},{3,6},{4,1},{5,8},{6,3},{7,10},{8,5},{9,12},{1... | collective-permute-start | bytes 393224 | tf_op jit(solution)/shard_map/ppermute | solution.py:40
  117.7 6.4 %collective-permute-start.22 = (bf16[64,1024]{1,0:T(8,128)(2,1)S(1)}, bf16[64,1024]{1,0:T(8,128)(2,1)S(1)}, u32[]{:S(2)}, u32[]{:S(2)}) collective-permute-start(bf16[64,1024]{1,0:T(8,128)(2,1)S(1)} %add_convert_fusion.1), channel_id=1, source_target_pairs={{0,12},{1,5},{2,14},{3,7},{4,0},{5,9},{6,2},{7,11},{8,4},{9,13},{1... | collective-permute-start | bytes 393224 | tf_op jit(solution)/shard_map/ppermute | solution.py:40
  124.4 9.9 %collective-permute-start.23 = (bf16[64,1024]{1,0:T(8,128)(2,1)S(1)}, bf16[64,1024]{1,0:T(8,128)(2,1)S(1)}, u32[]{:S(2)}, u32[]{:S(2)}) collective-permute-start(bf16[64,1024]{1,0:T(8,128)(2,1)S(1)} %divide_convert_fusion), channel_id=1, source_target_pairs={{1,2},{2,1},{3,4},{4,3},{5,6},{6,5},{7,8},{8,7},{9,10},{10,9},{11,... | collective-permute-start | bytes 393224 | tf_op jit(solution)/shard_map/ppermute | solution.py:45
  126.6 7.7 %collective-permute-start.24 = (bf16[64,1024]{1,0:T(8,128)(2,1)S(1)}, bf16[64,1024]{1,0:T(8,128)(2,1)S(1)}, u32[]{:S(2)}, u32[]{:S(2)}) collective-permute-start(bf16[64,1024]{1,0:T(8,128)(2,1)S(1)} %divide_convert_fusion), channel_id=1, source_target_pairs={{0,1},{1,0},{2,3},{3,2},{4,5},{5,4},{6,7},{7,6},{8,9},{9,8},{10,11... | collective-permute-start | bytes 393224 | tf_op jit(solution)/shard_map/ppermute | solution.py:40
  (10 other events, 143.5 us)
Sparse Core Ops, SparseCore 0:
  9.8 45.7 all-gather.2

commit v8 on v7

--- a/solution.py
+++ b/solution.py
@@ -15,7 +15,6 @@
 WIRE = jnp.bfloat16
 F32 = jnp.float32
 VMEM = pl.BlockSpec(memory_space=pltpu.VMEM)
-SMEM = pl.BlockSpec(memory_space=pltpu.SMEM)
 ANY = pl.BlockSpec(memory_space=pl.ANY)
 HBM = pl.BlockSpec(memory_space=pltpu.HBM)
 
@@ -26,6 +25,12 @@
 
 def place(half, turn, pair, core):
     return ((half * TURNS + turn % TURNS) * PAIR + pair) * CORES + core
+
+
+def here():
+    ctx = lax.axis_index("ctx")
+    core, pair = ctx % CORES, ctx // CORES % PAIR
+    return ctx // (CORES * PAIR * TURNS), ctx // (CORES * PAIR) % TURNS, pair, core
 
 
 def moved(value, to):
@@ -80,11 +85,11 @@
     return lax.dot_general(left, right, (((0,), (0,)), ((), ())), preferred_element_type=F32)
 
 
-def cut_kernel(place_ref, q_ref, k_ref, v_ref, o_ref, start_ref, out_ref, start_out, sems):
+def cut_kernel(q_ref, k_ref, v_ref, o_ref, start_ref, out_ref, start_out, sems):
     rows = out_ref.shape[0]
     half, width = rows // CORES, o_ref.shape[1]
-    core = place_ref[3]
-    lane = pl.multiple_of((place_ref[1] * CORES + core) * HEAD, HEAD)
+    _, turn, _, core = here()
+    lane = pl.multiple_of((turn * CORES + core) * HEAD, HEAD)
     copies = [
         (w.at[:, pl.ds(lane, HEAD)], out_ref.at[:, i * HEAD : (i + 1) * HEAD])
         for i, w in enumerate((q_ref, k_ref, v_ref))
@@ -99,7 +104,7 @@
     fetched(copies, sems)
 
 
-def cut_weights(where, w_query, w_key, w_value, w_out, starts):
+def cut_weights(w_query, w_key, w_value, w_out, starts):
     rows, width = w_out.shape
     return pl.pallas_call(
         cut_kernel,
@@ -107,20 +112,34 @@
             jax.ShapeDtypeStruct((rows, 3 * HEAD + width // 2), w_query.dtype),
             jax.ShapeDtypeStruct(starts.shape, starts.dtype),
         ),
-        in_specs=[SMEM] + [HBM] * 4 + [ANY],
+        in_specs=[HBM] * 4 + [ANY],
         out_specs=(VMEM, VMEM),
         scratch_shapes=[pltpu.SemaphoreType.DMA((6,))],
         compiler_params=room(60),
-    )(where, w_query, w_key, w_value, w_out, starts)
+    )(w_query, w_key, w_value, w_out, starts)
 
 
 def gathered_weights(mine):
     return lax.all_gather(mine, "dp", axis=0, tiled=False)
 
 
+def pass_kernel(value_ref, ready_ref, out_ref):
+    out_ref[...] = value_ref[...]
+
+
+def passed_on(value, ready):
+    return pl.pallas_call(
+        pass_kernel,
+        out_shape=jax.ShapeDtypeStruct(value.shape, value.dtype),
+        in_specs=[VMEM, ANY],
+        out_specs=VMEM,
+        compiler_params=room(4),
+    )(value, ready)
+
+
 def gathered_rows(shard):
     near = turned(shard, 1)
-    next_to = turned_over(shard)
+    next_to = turned_over(passed_on(shard, near))
     far = turned(near, 1)
     return [
         shard,
@@ -162,27 +181,32 @@
     return copies
 
 
-def window_kernel(place_ref, edge_ref, token_hbm, grad_hbm, *refs):
-    core_ref, chip_ref, mid_token, mid_grad, first_ref, count_ref = refs[:6]
-    token_ref, grad_ref, sems = refs[6:]
+def window_kernel(own_ref, beside_ref, facing_ref, token_hbm, grad_hbm, *refs):
+    core_ref, chip_ref, mid_token, mid_grad, first_ref = refs[:5]
+    token_ref, grad_ref, sems = refs[5:]
     rows, width = token_ref.shape
     seg = mid_token.shape[0]
     token_copy = pltpu.make_async_copy(token_hbm, token_ref, sems.at[0])
     grad_copy = pltpu.make_async_copy(grad_hbm, grad_ref, sems.at[1])
     token_copy.start()
     grad_copy.start()
-    ctx, core = place_ref[5], place_ref[3]
-    at = lax.broadcasted_iota(jnp.int32, (1, rows), 1) + ctx * rows
-    opens, ends, nexts = edge_ref[0], edge_ref[1], edge_ref[2]
-    count_ref[...] = (ends - opens)[seg : 2 * seg].astype(F32)
-    member = ((opens <= at) & (at < ends)).astype(jnp.bfloat16)
-    earlier = ((ends <= at) & (at < nexts)).astype(jnp.bfloat16)
+    ctx, core = lax.axis_index("ctx"), here()[3]
+    at = lax.broadcasted_iota(jnp.int32, (rows, 1), 0) + ctx * rows
+    before = jnp.where(core == 0, facing_ref[...], beside_ref[...])
+    after = jnp.where(core == 0, beside_ref[...], facing_ref[...])
+    before = jnp.where(ctx == 0, -1, before)
+    after = jnp.where(ctx == CTX - 1, rows * CTX, after)
+    begun = [(part <= at).astype(jnp.int32) for part in (before, own_ref[...], after)]
+    slot = sum(jnp.sum(part, axis=1, keepdims=True) for part in begun) - 1
+    slots = lax.broadcasted_iota(jnp.int32, (1, 3 * seg), 1)
+    member = (slots == slot).astype(jnp.bfloat16)
+    earlier = (slots == slot - 1).astype(jnp.bfloat16)
     token_copy.wait()
-    token = jnp.dot(member, token_ref[...], preferred_element_type=F32)
+    token = contract_first(member, token_ref[...])
     grad_copy.wait()
-    grad = jnp.dot(earlier, grad_ref[...], preferred_element_type=F32)
-    first = jnp.dot(member[:16], grad_ref[...], preferred_element_type=F32)
-    first_ref[...] = first[:1]
+    grad = contract_first(earlier, grad_ref[...])
+    outside = jnp.broadcast_to((slot == 0).astype(jnp.bfloat16), (rows, HEAD))
+    first_ref[...] = contract_first(outside, grad_ref[...])[:1]
     mid_token[...] = token[seg : 2 * seg]
     mid_grad[...] = grad[seg : 2 * seg]
 
@@ -201,8 +225,9 @@
         send(core_ref, chip_ref)
 
 
-def window_sums(where, edges, tokens, grads, seg):
+def window_sums(own, beside, facing, tokens, grads):
     rows, width = tokens.shape
+    seg = own.shape[1]
     shape = jax.ShapeDtypeStruct
     return pl.pallas_call(
         window_kernel,
@@ -212,17 +237,16 @@
             shape((seg, width), F32),
             shape((seg, width), F32),
             shape((1, width), F32),
-            shape((seg, 1), F32),
         ),
-        in_specs=[SMEM, VMEM] + [HBM] * 2,
-        out_specs=(VMEM,) * 6,
+        in_specs=[VMEM] * 3 + [HBM] * 2,
+        out_specs=(VMEM,) * 5,
         scratch_shapes=[
             pltpu.VMEM((rows, width), tokens.dtype),
             pltpu.VMEM((rows, width), grads.dtype),
             pltpu.SemaphoreType.DMA((2,)),
         ],
         compiler_params=room(16),
-    )(where, edges, tokens, grads)
+    )(own, beside, facing, tokens, grads)
 
 
 def norm_kernel(core_ref, chip_ref, mid_token, mid_grad, second_ref, count_ref, gain_ref, *outs):
@@ -259,9 +283,10 @@
 
 
 def project_kernel(seg, *refs):
-    place_ref, pieces, weight = refs[0], refs[1:9], refs[9]
-    q_ref, kv_ref, mine_ref, theirs_ref, rows, w_in, w_back, sems = refs[10:]
-    core, head = place_ref[3], place_ref[1] * CORES
+    pieces, weight = refs[:8], refs[8]
+    q_ref, kv_ref, mine_ref, theirs_ref, rows, w_in, w_back, sems = refs[9:]
+    _, turn, _, core = here()
+    head = turn * CORES
     half, wide = seg, rows.shape[1] // 4
     depth = weight.shape[1]
     copies = stacked(pieces, rows)
@@ -284,7 +309,7 @@
         theirs_ref[its_rows, :] = da[slot * seg : (slot + 1) * seg, half:]
 
 
-def project(where, pieces, weights):
+def project(pieces, weights):
     seg, width = pieces[0].shape
     rows = seg * len(pieces)
     half = HEAD // CORES
@@ -292,7 +317,7 @@
     return pl.pallas_call(
         functools.partial(project_kernel, half),
         out_shape=(bf16(rows, HEAD), bf16(rows, 2 * HEAD), bf16(rows, half), bf16(rows, half)),
-        in_specs=[SMEM] + [ANY] * 9,
+        in_specs=[ANY] * 9,
         out_specs=(VMEM,) * 4,
         scratch_shapes=[
             pltpu.VMEM((rows, width), jnp.bfloat16),
@@ -300,14 +325,14 @@
             pltpu.VMEM((HEAD, width // 2), jnp.bfloat16),
             pltpu.SemaphoreType.DMA((20,)),
         ],
-        compiler_params=room(12),
-    )(where, *pieces, weights)
+        compiler_params=room(40),
+    )(*pieces, weights)
 
 
 def attention_kernel(tile, seg, *refs):
-    place_ref, q_ref, mine_ref, theirs_ref, blocks = *refs[:4], refs[4:8]
-    dq_ref, outs, (kv, da_ref, dkt, dvt, sems) = refs[8], refs[9:13], refs[13:]
-    half, turn, pair, core = place_ref[0], place_ref[1], place_ref[2], place_ref[3]
+    q_ref, mine_ref, theirs_ref, blocks = *refs[:3], refs[3:7]
+    dq_ref, outs, (kv, da_ref, dkt, dvt, sems) = refs[7], refs[8:12], refs[12:]
+    half, turn, pair, core = here()
     queries, keys = q_ref.shape[0], kv.shape[0]
     fetched(stacked(blocks, kv), sems)
 
@@ -361,14 +386,14 @@
         out[:, HEAD:] = dvt[:, lanes].T.astype(jnp.bfloat16)
 
 
-def attention(where, q, mine, theirs, blocks, seg):
+def attention(q, mine, theirs, blocks, seg):
     queries = q.shape[0]
     keys = sum(block.shape[0] for block in blocks)
     part = jax.ShapeDtypeStruct(blocks[0].shape, jnp.bfloat16)
     return pl.pallas_call(
-        functools.partial(attention_kernel, 128, seg),
+        functools.partial(attention_kernel, 256, seg),
         out_shape=(jax.ShapeDtypeStruct((queries, HEAD), jnp.bfloat16),) + (part,) * 4,
-        in_specs=[SMEM] + [VMEM] * 3 + [ANY] * 4,
+        in_specs=[VMEM] * 3 + [ANY] * 4,
         out_specs=(VMEM,) * 5,
         scratch_shapes=[
             pltpu.VMEM((keys, 2 * HEAD), jnp.bfloat16),
@@ -377,13 +402,13 @@
             pltpu.VMEM((HEAD, keys), F32),
             pltpu.SemaphoreType.DMA((4,)),
         ],
-        compiler_params=room(28),
+        compiler_params=room(36),
         cost_estimate=pl.CostEstimate(
             flops=12 * queries * keys * HEAD,
             bytes_accessed=2 * HEAD * (3 * queries + 4 * keys),
             transcendentals=queries * keys,
         ),
-    )(where, q, mine, theirs, *blocks)
+    )(q, mine, theirs, *blocks)
 
 
 def unproject_kernel(seg, dq_ref, *refs):
@@ -455,36 +480,31 @@
     rows, width = token_rows.shape
     seg = starts.shape[1]
     length = rows * CTX
-    ctx = lax.axis_index("ctx")
-    core, pair = ctx % CORES, ctx // CORES % PAIR
-    turn, half = ctx // (CORES * PAIR) % TURNS, ctx // (CORES * PAIR * TURNS)
-    where = jnp.stack([half, turn, pair, core, lax.axis_index("dp"), ctx])
-
-    mine, own_starts = cut_weights(where, w_query, w_key, w_value, w_out, starts)
-    own_starts = own_starts[0]
+    ctx, core = lax.axis_index("ctx"), here()[3]
+
+    mine, own_starts = cut_weights(w_query, w_key, w_value, w_out, starts)
     weights = gathered_weights(mine)
     beside, facing = other_core(own_starts), other_chip(own_starts)
-    before = jnp.where(core == 0, facing, beside)
-    after = jnp.where(core == 0, beside, facing)
+    to_core, to_chip, mid_token, mid_grad, first = window_sums(
+        own_starts, beside, facing, token_rows, grad_out
+    )
+    before = jnp.where(core == 0, facing, beside)[0]
+    after = jnp.where(core == 0, beside, facing)[0]
     before = jnp.where(ctx == 0, -1, before)
     after = jnp.where(ctx == CTX - 1, length, after)
-    stop = jnp.full((2,), length, jnp.int32)
-    window = jnp.concatenate([before, own_starts, after, stop])
-    slots = 3 * seg
-    opens, ends = window[:slots], window[1 : slots + 1]
-    edges = jnp.stack([opens, ends, window[2:]])[:, :, None]
-    to_core, to_chip, mid_token, mid_grad, first, count = window_sums(
-        where, edges, token_rows, grad_out, seg
-    )
+    stop = jnp.full((1,), length, jnp.int32)
+    window = jnp.concatenate([before, own_starts[0], after, stop])
+    opens, ends = window[:-1], window[1:]
+    count = (ends - opens)[seg : 2 * seg, None].astype(F32)
     second = two_back(first)
     both, normed, rms, dout = norm(
         other_core(to_core), other_chip(to_chip), mid_token, mid_grad, second, count, gain[None]
     )
-    q, own, mine, theirs = project(where, gathered_rows(both), weights)
+    q, own, mine, theirs = project(gathered_rows(both), weights)
     cross, far, beside = across(own, 0, True), across(own, 0, False), other_pair(own)
     theirs = other_core(theirs)
     blocks = (own, beside, far, cross)
-    dq, own, beside, far, cross = attention(where, q, mine, theirs, blocks, seg)
+    dq, own, beside, far, cross = attention(q, mine, theirs, blocks, seg)
     parts = (own, other_pair(beside), across(far, 1, False), across(cross, 1, True))
     dnormin = summed_rows(*unproject(dq, parts, weights, seg))
 

time: 143 us -> 141 us (0.986)
  starting transfers between devices: 32.5 us -> 37.3 us
  Pallas kernels: 14.2 us -> 10.9 us
  waiting for transfers between devices: 74.6 us -> 72.7 us
    ppermute x21, starting transfers between devices: 12.9 us -> 15.7 us  [moved(): return lax.ppermute(value, 'ctx', pairs)]
    ppermute x3, starting transfers between devices: 17.3 us -> 19.3 us  [other_chip(): return lax.ppermute(value, 'ctx', pairs)]
    pallas_call x1 -> x2, Pallas kernels: 6.59 us -> 4.68 us  [the longest x1 4.66 us: attention(): pl.pallas_call(functools.partial(attention_kernel, 256, seg), out_shape=(...]
    unnamed x16 -> x12, local copies, waits for them, and re-layouts: 3.35 us -> 3.39 us
  transfers between devices with their start and end apart: 26 -> 26, of which waited for: 15 -> 17; matrix products, arithmetic and copies ran while one was open for 1% -> 0% of each run, Pallas kernels for 1% -> 1%
where the time goes in v8:
time: 141 us; the launch traced here: 140 us
  waiting for transfers between devices  72.7 us (52%)
  starting transfers between devices  37.3 us (26%)
  between operations  13.7 us (10%)
  Pallas kernels  10.9 us (8%)
  local copies, waits for them, and re-layouts  3.49 us (2%)
  matrix products  1.46 us (1%)
    ppermute x21, waiting for transfers between devices, moved(): return lax.ppermute(value, 'ctx', pairs)  58.6 us
    ppermute x3, starting transfers between devices, other_chip(): return lax.ppermute(value, 'ctx', pairs)  19.3 us
    ppermute x21, starting transfers between devices, moved(): return lax.ppermute(value, 'ctx', pairs)  15.7 us
    ppermute x3, waiting for transfers between devices, other_chip(): return lax.ppermute(value, 'ctx', pairs)  7.7 us
    ppermute x1, waiting for transfers between devices, two_back(): lax.ppermute(value, 'ctx', [(i, i - CORES) for i in range(CORES, CTX)])  6.37 us
    pallas_call x1, Pallas kernels, attention(): pl.pallas_call(functools.partial(attention_kernel, 256, seg), out_shape=(...  4.66 us
    unnamed x12, local copies, waits for them, and re-layouts  3.39 us
  transfers between devices with their start and end apart: 26, of which 17 were waited for; matrix products, arithmetic and copies ran while one was open for 0% of the time, Pallas kernels for 1%

profile of v8, /device:TPU:6, one launch (start us, length us, event | category | flops | bytes accessed | tf_op | source)
XLA Modules:
  0.0 140.2 jit_solution(12614001653748290762)
XLA Ops:
  6.5 1.8 %shard_map.82 = (bf16[128,896]{1,0:T(8,128)(2,1)}, s32[1,64]{1,0:T(1,128)}) custom-call(bf16[128,1024]{1,0:T(8,128)(2,1)} %q_ref.1, bf16[128,1024]{1,0:T(8,128)(2,1)} %k_ref.1, bf16[128,1024]{1,0:T(8,128)(2,1)} %v_ref.1, bf16[128,1024]{1,0:T(8,128)(2,1)} %o_ref.1, s32[1,64]{1,0:T(1,128)} %start_ref.1), custom_call_target="tpu_custom_call" | custom-call | tf_op jit(solution)/shard_map/pallas_call | solution.py:109
  8.4 8.7 %collective-permute-start = (s32[1,64]{1,0:T(1,128)}, s32[1,64]{1,0:T(1,128)S(1)}, u32[]{:S(2)}, u32[]{:S(2)}) collective-permute-start(s32[1,64]{1,0:T(1,128)} %get-tuple-element.34.own_ref), channel_id=1, source_target_pairs={{1,2},{2,1},{3,4},{4,3},{5,6},{6,5},{7,8},{8,7},{9,10},{10,9},{11,... | collective-permute-start | bytes 776 | tf_op jit(solution)/shard_map/ppermute | solution.py:50
  20.4 1.7 %shard_map.83 = (bf16[64,2048]{1,0:T(8,128)(2,1)S(1)}, bf16[64,2048]{1,0:T(8,128)(2,1)S(1)}, f32[64,1024]{1,0:T(8,128)S(1)}, f32[64,1024]{1,0:T(8,128)S(1)}, f32[1,1024]{1,0:T(1,128)S(1)}) custom-call(s32[1,64]{1,0:T(1,128)S(1)} %copy-done.5, s32[1,64]{1,0:T(1,128)S(1)} %collective-permute-done.1.beside_ref, s32[1,64]{1,0:T(1,128)S(1)} %collective-permute-done.facing_ref, ...), custom_call_target="tpu_custom_call" | custom-call | tf_op jit(solution)/shard_map/pallas_call | solution.py:232
  22.2 7.1 %collective-permute-start.3 = (bf16[64,2048]{1,0:T(8,128)(2,1)S(1)}, bf16[64,2048]{1,0:T(8,128)(2,1)S(1)}, u32[]{:S(2)}, u32[]{:S(2)}) collective-permute-start(bf16[64,2048]{1,0:T(8,128)(2,1)S(1)} %get-tuple-element.36), channel_id=1, source_target_pairs={{1,2},{2,1},{3,4},{4,3},{5,6},{6,5},{7,8},{8,7},{9,10},{10,9},{11,... | collective-permute-start | bytes 786440 | tf_op jit(solution)/shard_map/ppermute | solution.py:50
  29.3 2.3 %collective-permute-start.4 = (f32[1,1024]{1,0:T(1,128)S(1)}, f32[1,1024]{1,0:T(1,128)S(1)}, u32[]{:S(2)}, u32[]{:S(2)}) collective-permute-start(f32[1,1024]{1,0:T(1,128)S(1)} %get-tuple-element.39), channel_id=1, source_target_pairs={{2,0},{3,1},{4,2},{5,3},{6,4},{7,5},{8,6},{9,7},{10,8},{11,9},{12,... | collective-permute-start | bytes 12296 | tf_op jit(solution)/shard_map/ppermute | solution.py:54
  32.0 6.4 %collective-permute-done.4.second_ref = f32[1,1024]{1,0:T(1,128)S(1)} collective-permute-done((f32[1,1024]{1,0:T(1,128)S(1)}, f32[1,1024]{1,0:T(1,128)S(1)}, u32[]{:S(2)}, u32[]{:S(2)}) %collective-permute-start.4) | collective-permute-done | bytes 4128 | tf_op jit(solution)/shard_map/ppermute | solution.py:54
  38.7 14.2 %collective-permute-done.6.ready_ref.refs_2_ = bf16[64,2048]{1,0:T(8,128)(2,1)S(1)} collective-permute-done((bf16[64,2048]{1,0:T(8,128)(2,1)S(1)}, bf16[64,2048]{1,0:T(8,128)(2,1)S(1)}, u32[]{:S(2)}, u32[]{:S(2)}) %collective-permute-start.6) | collective-permute-done | bytes 262176 | tf_op jit(solution)/shard_map/ppermute | solution.py:45
  53.1 3.9 %collective-permute-start.5 = (bf16[64,2048]{1,0:T(8,128)(2,1)S(1)}, bf16[64,2048]{1,0:T(8,128)(2,1)S(1)}, u32[]{:S(2)}, u32[]{:S(2)}) collective-permute-start(bf16[64,2048]{1,0:T(8,128)(2,1)S(1)} %get-tuple-element.41.value_ref.refs_0_), channel_id=1, source_target_pairs={{0,1},{1,0},{2,3},{3,2},{4,5},{5,4},{6,7},{7,6},{8,9},{9,8},{10,11... | collective-permute-start | bytes 786440 | tf_op jit(solution)/shard_map/ppermute | solution.py:45
  57.0 6.1 %collective-permute-done.7.refs_3_ = bf16[64,2048]{1,0:T(8,128)(2,1)S(1)} collective-permute-done((bf16[64,2048]{1,0:T(8,128)(2,1)S(1)}, bf16[64,2048]{1,0:T(8,128)(2,1)S(1)}, u32[]{:S(2)}, u32[]{:S(2)}) %collective-permute-start.7) | collective-permute-done | bytes 262176 | tf_op jit(solution)/shard_map/ppermute | solution.py:45
  65.2 1.5 %copy-done = bf16[1024,896]{1,0:T(8,128)(2,1)S(1)} copy-done((bf16[1024,896]{1,0:T(8,128)(2,1)S(1)}, bf16[1024,896]{1,0:T(8,128)(2,1)}, u32[]{:S(2)}) %copy-start) | copy-done | bytes 1835032
  66.7 1.5 %shard_map.86 = (bf16[512,128]{1,0:T(8,128)(2,1)S(1)}, bf16[512,256]{1,0:T(8,128)(2,1)S(1)}, bf16[512,64]{1,0:T(8,128)(2,1)S(1)}, bf16[512,64]{1,0:T(8,128)(2,1)S(1)}) custom-call(bf16[64,2048]{1,0:T(8,128)(2,1)S(1)} %get-tuple-element.41.value_ref.refs_0_, bf16[64,2048]{1,0:T(8,128)(2,1)S(1)} %collective-permute-done.5.refs_1_, ...), custom_call_target="tpu_custom_call" | custom-call | tf_op jit(solution)/shard_map/pallas_call | solution.py:317
  72.4 4.3 %collective-permute-done.13.refs_4_ = bf16[512,256]{1,0:T(8,128)(2,1)S(1)} collective-permute-done((bf16[512,256]{1,0:T(8,128)(2,1)S(1)}, bf16[512,256]{1,0:T(8,128)(2,1)S(1)}, u32[]{:S(2)}, u32[]{:S(2)}) %collective-permute-start.13) | collective-permute-done | bytes 262176 | tf_op jit(solution)/shard_map/ppermute | solution.py:45
  76.7 9.0 %collective-permute-done.14.refs_5_ = bf16[512,256]{1,0:T(8,128)(2,1)S(1)} collective-permute-done((bf16[512,256]{1,0:T(8,128)(2,1)S(1)}, bf16[512,256]{1,0:T(8,128)(2,1)S(1)}, u32[]{:S(2)}, u32[]{:S(2)}) %collective-permute-start.14) | collective-permute-done | bytes 262176 | tf_op jit(solution)/shard_map/ppermute | solution.py:45
  85.8 4.7 %shard_map.87 = (bf16[512,128]{1,0:T(8,128)(2,1)S(1)}, bf16[512,256]{1,0:T(8,128)(2,1)S(1)}, bf16[512,256]{1,0:T(8,128)(2,1)S(1)}, bf16[512,256]{1,0:T(8,128)(2,1)S(1)}, bf16[512,256]{1,0:T(8,128)(2,1)S(1)}) custom-call(bf16[512,128]{1,0:T(8,128)(2,1)S(1)} %get-tuple-element.43.refs_0_, bf16[512,64]{1,0:T(8,128)(2,1)S(1)} %get-tuple-element.44.refs_1_, ...), custom_call_target="tpu_custom_call" | custom-call | flops 1610612736 | bytes 2490368 | tf_op jit(solution)/shard_map/pallas_call | solution.py:393
  90.4 1.8 %collective-permute-start.16 = (bf16[512,256]{1,0:T(8,128)(2,1)S(1)}, bf16[512,256]{1,0:T(8,128)(2,1)S(1)}, u32[]{:S(2)}, u32[]{:S(2)}) collective-permute-start(bf16[512,256]{1,0:T(8,128)(2,1)S(1)} %get-tuple-element.49), channel_id=1, source_target_pairs={{0,2},{1,3},{2,0},{3,1},{4,6},{5,7},{6,4},{7,5},{8,10},{9,11},{10,... | collective-permute-start | bytes 786440 | tf_op jit(solution)/shard_map/ppermute | solution.py:45
  95.0 4.8 %collective-permute-done.16.refs_1_ = bf16[512,256]{1,0:T(8,128)(2,1)S(1)} collective-permute-done((bf16[512,256]{1,0:T(8,128)(2,1)S(1)}, bf16[512,256]{1,0:T(8,128)(2,1)S(1)}, u32[]{:S(2)}, u32[]{:S(2)}) %collective-permute-start.16) | collective-permute-done | bytes 262176 | tf_op jit(solution)/shard_map/ppermute | solution.py:45
  99.8 4.1 %collective-permute-done.17.refs_2_ = bf16[512,256]{1,0:T(8,128)(2,1)S(1)} collective-permute-done((bf16[512,256]{1,0:T(8,128)(2,1)S(1)}, bf16[512,256]{1,0:T(8,128)(2,1)S(1)}, u32[]{:S(2)}, u32[]{:S(2)}) %collective-permute-start.17) | collective-permute-done | bytes 262176 | tf_op jit(solution)/shard_map/ppermute | solution.py:45
  104.9 1.9 %collective-permute-done.19.swapped = bf16[256,1024]{1,0:T(8,128)(2,1)S(1)} collective-permute-done((bf16[256,1024]{1,0:T(8,128)(2,1)S(1)}, bf16[256,1024]{1,0:T(8,128)(2,1)S(1)}, u32[]{:S(2)}, u32[]{:S(2)}) %collective-permute-start.19) | collective-permute-done | bytes 524320 | tf_op jit(solution)/shard_map/ppermute | solution.py:45
  107.0 3.6 %collective-permute-start.20 = (bf16[64,1024]{1,0:T(8,128)(2,1)S(1)}, bf16[64,1024]{1,0:T(8,128)(2,1)S(1)}, u32[]{:S(2)}, u32[]{:S(2)}) collective-permute-start(bf16[64,1024]{1,0:T(8,128)(2,1)S(1)} %get-tuple-element.58), channel_id=1, source_target_pairs={{0,13},{1,4},{2,15},{3,6},{4,1},{5,8},{6,3},{7,10},{8,5},{9,12},{1... | collective-permute-start | bytes 393224 | tf_op jit(solution)/shard_map/ppermute | solution.py:45
  110.6 5.1 %collective-permute-done.21 = bf16[64,1024]{1,0:T(8,128)(2,1)S(1)} collective-permute-done((bf16[64,1024]{1,0:T(8,128)(2,1)S(1)}, bf16[64,1024]{1,0:T(8,128)(2,1)S(1)}, u32[]{:S(2)}, u32[]{:S(2)}) %collective-permute-start.21) | collective-permute-done | bytes 131104 | tf_op jit(solution)/shard_map/ppermute | solution.py:45
  115.9 3.0 %collective-permute-done.20 = bf16[64,1024]{1,0:T(8,128)(2,1)S(1)} collective-permute-done((bf16[64,1024]{1,0:T(8,128)(2,1)S(1)}, bf16[64,1024]{1,0:T(8,128)(2,1)S(1)}, u32[]{:S(2)}, u32[]{:S(2)}) %collective-permute-start.20) | collective-permute-done | bytes 131104 | tf_op jit(solution)/shard_map/ppermute | solution.py:45
  118.8 2.8 %collective-permute-done.22 = bf16[64,1024]{1,0:T(8,128)(2,1)S(1)} collective-permute-done((bf16[64,1024]{1,0:T(8,128)(2,1)S(1)}, bf16[64,1024]{1,0:T(8,128)(2,1)S(1)}, u32[]{:S(2)}, u32[]{:S(2)}) %collective-permute-start.22) | collective-permute-done | bytes 131104 | tf_op jit(solution)/shard_map/ppermute | solution.py:45
  121.9 3.5 %collective-permute-start.23 = (bf16[64,1024]{1,0:T(8,128)(2,1)S(1)}, bf16[64,1024]{1,0:T(8,128)(2,1)S(1)}, u32[]{:S(2)}, u32[]{:S(2)}) collective-permute-start(bf16[64,1024]{1,0:T(8,128)(2,1)S(1)} %divide_convert_fusion), channel_id=1, source_target_pairs={{1,2},{2,1},{3,4},{4,3},{5,6},{6,5},{7,8},{8,7},{9,10},{10,9},{11,... | collective-permute-start | bytes 393224 | tf_op jit(solution)/shard_map/ppermute | solution.py:50
  125.5 6.3 %collective-permute-done.23 = bf16[64,1024]{1,0:T(8,128)(2,1)S(1)} collective-permute-done((bf16[64,1024]{1,0:T(8,128)(2,1)S(1)}, bf16[64,1024]{1,0:T(8,128)(2,1)S(1)}, u32[]{:S(2)}, u32[]{:S(2)}) %collective-permute-start.23) | collective-permute-done | bytes 131104 | tf_op jit(solution)/shard_map/ppermute | solution.py:50
  (62 shorter events, 16.7 us)
Async XLA Ops:
  6.5 58.7 %all-gather.3.cloned.1.call-start = ((), (), s32[]{:S(2)}) async-start(), calls=%async_computation | async-start | bytes 2064384 | tf_op jit(solution)/shard_map/all_gather | solution.py:123
  8.3 8.8 %collective-permute-start.1 = (s32[1,64]{1,0:T(1,128)}, s32[1,64]{1,0:T(1,128)S(1)}, u32[]{:S(2)}, u32[]{:S(2)}) collective-permute-start(s32[1,64]{1,0:T(1,128)} %get-tuple-element.34.own_ref), channel_id=1, source_target_pairs={{0,1},{1,0},{2,3},{3,2},{4,5},{5,4},{6,7},{7,6},{8,9},{9,8},{10,11... | collective-permute-start | bytes 776 | tf_op jit(solution)/shard_map/ppermute | solution.py:45
  8.4 10.1 %collective-permute-start = (s32[1,64]{1,0:T(1,128)}, s32[1,64]{1,0:T(1,128)S(1)}, u32[]{:S(2)}, u32[]{:S(2)}) collective-permute-start(s32[1,64]{1,0:T(1,128)} %get-tuple-element.34.own_ref), channel_id=1, source_target_pairs={{1,2},{2,1},{3,4},{4,3},{5,6},{6,5},{7,8},{8,7},{9,10},{10,9},{11,... | collective-permute-start | bytes 776 | tf_op jit(solution)/shard_map/ppermute | solution.py:50
  22.1 16.2 %collective-permute-start.2 = (bf16[64,2048]{1,0:T(8,128)(2,1)S(1)}, bf16[64,2048]{1,0:T(8,128)(2,1)S(1)}, u32[]{:S(2)}, u32[]{:S(2)}) collective-permute-start(bf16[64,2048]{1,0:T(8,128)(2,1)S(1)} %get-tuple-element.35), channel_id=1, source_target_pairs={{0,1},{1,0},{2,3},{3,2},{4,5},{5,4},{6,7},{7,6},{8,9},{9,8},{10,11... | collective-permute-start | bytes 786440 | tf_op jit(solution)/shard_map/ppermute | solution.py:45
  22.2 16.1 %collective-permute-start.3 = (bf16[64,2048]{1,0:T(8,128)(2,1)S(1)}, bf16[64,2048]{1,0:T(8,128)(2,1)S(1)}, u32[]{:S(2)}, u32[]{:S(2)}) collective-permute-start(bf16[64,2048]{1,0:T(8,128)(2,1)S(1)} %get-tuple-element.36), channel_id=1, source_target_pairs={{1,2},{2,1},{3,4},{4,3},{5,6},{6,5},{7,8},{8,7},{9,10},{10,9},{11,... | collective-permute-start | bytes 786440 | tf_op jit(solution)/shard_map/ppermute | solution.py:50
  29.3 9.0 %collective-permute-start.4 = (f32[1,1024]{1,0:T(1,128)S(1)}, f32[1,1024]{1,0:T(1,128)S(1)}, u32[]{:S(2)}, u32[]{:S(2)}) collective-permute-start(f32[1,1024]{1,0:T(1,128)S(1)} %get-tuple-element.39), channel_id=1, source_target_pairs={{2,0},{3,1},{4,2},{5,3},{6,4},{7,5},{8,6},{9,7},{10,8},{11,9},{12,... | collective-permute-start | bytes 12296 | tf_op jit(solution)/shard_map/ppermute | solution.py:54
  38.6 14.3 %collective-permute-start.6 = (bf16[64,2048]{1,0:T(8,128)(2,1)S(1)}, bf16[64,2048]{1,0:T(8,128)(2,1)S(1)}, u32[]{:S(2)}, u32[]{:S(2)}) collective-permute-start(bf16[64,2048]{1,0:T(8,128)(2,1)S(1)} %get-tuple-element.41.value_ref.refs_0_), channel_id=1, source_target_pairs={{0,4},{1,13},{2,6},{3,15},{4,8},{5,1},{6,10},{7,3},{8,12},{9,5},{1... | collective-permute-start | bytes 786440 | tf_op jit(solution)/shard_map/ppermute | solution.py:45
  52.9 10.2 %collective-permute-start.7 = (bf16[64,2048]{1,0:T(8,128)(2,1)S(1)}, bf16[64,2048]{1,0:T(8,128)(2,1)S(1)}, u32[]{:S(2)}, u32[]{:S(2)}) collective-permute-start(bf16[64,2048]{1,0:T(8,128)(2,1)S(1)} %shard_map.85), channel_id=1, source_target_pairs={{0,13},{1,4},{2,15},{3,6},{4,1},{5,8},{6,3},{7,10},{8,5},{9,12},{1... | collective-permute-start | bytes 786440 | tf_op jit(solution)/shard_map/ppermute | solution.py:45
  53.0 10.7 %collective-permute-start.10 = (bf16[64,2048]{1,0:T(8,128)(2,1)S(1)}, bf16[64,2048]{1,0:T(8,128)(2,1)S(1)}, u32[]{:S(2)}, u32[]{:S(2)}) collective-permute-start(bf16[64,2048]{1,0:T(8,128)(2,1)S(1)} %collective-permute-done.6.ready_ref.refs_2_), channel_id=1, source_target_pairs={{0,4},{1,13},{2,6},{3,15},{4,8},{5,1},{6,10},{7,3},{8,12},{9,5},{1... | collective-permute-start | bytes 786440 | tf_op jit(solution)/shard_map/ppermute | solution.py:45
  53.1 10.6 %collective-permute-start.5 = (bf16[64,2048]{1,0:T(8,128)(2,1)S(1)}, bf16[64,2048]{1,0:T(8,128)(2,1)S(1)}, u32[]{:S(2)}, u32[]{:S(2)}) collective-permute-start(bf16[64,2048]{1,0:T(8,128)(2,1)S(1)} %get-tuple-element.41.value_ref.refs_0_), channel_id=1, source_target_pairs={{0,1},{1,0},{2,3},{3,2},{4,5},{5,4},{6,7},{7,6},{8,9},{9,8},{10,11... | collective-permute-start | bytes 786440 | tf_op jit(solution)/shard_map/ppermute | solution.py:45
  57.0 6.8 %collective-permute-start.8 = (bf16[64,2048]{1,0:T(8,128)(2,1)S(1)}, bf16[64,2048]{1,0:T(8,128)(2,1)S(1)}, u32[]{:S(2)}, u32[]{:S(2)}) collective-permute-start(bf16[64,2048]{1,0:T(8,128)(2,1)S(1)} %collective-permute-done.6.ready_ref.refs_2_), channel_id=1, source_target_pairs={{0,1},{1,0},{2,3},{3,2},{4,5},{5,4},{6,7},{7,6},{8,9},{9,8},{10,11... | collective-permute-start | bytes 786440 | tf_op jit(solution)/shard_map/ppermute | solution.py:45
  63.1 1.5 %collective-permute-start.9 = (bf16[64,2048]{1,0:T(8,128)(2,1)S(1)}, bf16[64,2048]{1,0:T(8,128)(2,1)S(1)}, u32[]{:S(2)}, u32[]{:S(2)}) collective-permute-start(bf16[64,2048]{1,0:T(8,128)(2,1)S(1)} %collective-permute-done.7.refs_3_), channel_id=1, source_target_pairs={{0,1},{1,0},{2,3},{3,2},{4,5},{5,4},{6,7},{7,6},{8,9},{9,8},{10,11... | collective-permute-start | bytes 786440 | tf_op jit(solution)/shard_map/ppermute | solution.py:45
  68.3 8.4 %collective-permute-start.13 = (bf16[512,256]{1,0:T(8,128)(2,1)S(1)}, bf16[512,256]{1,0:T(8,128)(2,1)S(1)}, u32[]{:S(2)}, u32[]{:S(2)}) collective-permute-start(bf16[512,256]{1,0:T(8,128)(2,1)S(1)} %get-tuple-element.46.refs_3_), channel_id=1, source_target_pairs={{0,2},{1,3},{2,0},{3,1},{4,6},{5,7},{6,4},{7,5},{8,10},{9,11},{10,... | collective-permute-start | bytes 786440 | tf_op jit(solution)/shard_map/ppermute | solution.py:45
  68.4 17.4 %collective-permute-start.14 = (bf16[512,256]{1,0:T(8,128)(2,1)S(1)}, bf16[512,256]{1,0:T(8,128)(2,1)S(1)}, u32[]{:S(2)}, u32[]{:S(2)}) collective-permute-start(bf16[512,256]{1,0:T(8,128)(2,1)S(1)} %get-tuple-element.46.refs_3_), channel_id=1, source_target_pairs={{0,16},{1,17},{2,18},{3,19},{4,20},{5,21},{6,22},{7,23},{8,24},{9,... | collective-permute-start | bytes 786440 | tf_op jit(solution)/shard_map/ppermute | solution.py:45
  69.7 16.1 %collective-permute-start.15 = (bf16[512,256]{1,0:T(8,128)(2,1)S(1)}, bf16[512,256]{1,0:T(8,128)(2,1)S(1)}, u32[]{:S(2)}, u32[]{:S(2)}) collective-permute-start(bf16[512,256]{1,0:T(8,128)(2,1)S(1)} %get-tuple-element.46.refs_3_), channel_id=1, source_target_pairs={{0,18},{1,19},{2,16},{3,17},{4,22},{5,23},{6,20},{7,21},{8,26},{9,... | collective-permute-start | bytes 786440 | tf_op jit(solution)/shard_map/ppermute | solution.py:45
  90.4 9.3 %collective-permute-start.16 = (bf16[512,256]{1,0:T(8,128)(2,1)S(1)}, bf16[512,256]{1,0:T(8,128)(2,1)S(1)}, u32[]{:S(2)}, u32[]{:S(2)}) collective-permute-start(bf16[512,256]{1,0:T(8,128)(2,1)S(1)} %get-tuple-element.49), channel_id=1, source_target_pairs={{0,2},{1,3},{2,0},{3,1},{4,6},{5,7},{6,4},{7,5},{8,10},{9,11},{10,... | collective-permute-start | bytes 786440 | tf_op jit(solution)/shard_map/ppermute | solution.py:45
  92.2 11.6 %collective-permute-start.17 = (bf16[512,256]{1,0:T(8,128)(2,1)S(1)}, bf16[512,256]{1,0:T(8,128)(2,1)S(1)}, u32[]{:S(2)}, u32[]{:S(2)}) collective-permute-start(bf16[512,256]{1,0:T(8,128)(2,1)S(1)} %get-tuple-element.50), channel_id=1, source_target_pairs={{16,0},{17,1},{18,2},{19,3},{20,4},{21,5},{22,6},{23,7},{24,8},{25... | collective-permute-start | bytes 786440 | tf_op jit(solution)/shard_map/ppermute | solution.py:45
  93.7 10.2 %collective-permute-start.18 = (bf16[512,256]{1,0:T(8,128)(2,1)S(1)}, bf16[512,256]{1,0:T(8,128)(2,1)S(1)}, u32[]{:S(2)}, u32[]{:S(2)}) collective-permute-start(bf16[512,256]{1,0:T(8,128)(2,1)S(1)} %get-tuple-element.51), channel_id=1, source_target_pairs={{16,2},{17,3},{18,0},{19,1},{20,6},{21,7},{22,4},{23,5},{24,10},{2... | collective-permute-start | bytes 786440 | tf_op jit(solution)/shard_map/ppermute | solution.py:45
  104.8 2.0 %collective-permute-start.19 = (bf16[256,1024]{1,0:T(8,128)(2,1)S(1)}, bf16[256,1024]{1,0:T(8,128)(2,1)S(1)}, u32[]{:S(2)}, u32[]{:S(2)}) collective-permute-start(bf16[256,1024]{1,0:T(8,128)(2,1)S(1)} %get-tuple-element.52), channel_id=1, source_target_pairs={{0,1},{1,0},{2,3},{3,2},{4,5},{5,4},{6,7},{7,6},{8,9},{9,8},{10,11... | collective-permute-start | bytes 1572872 | tf_op jit(solution)/shard_map/ppermute | solution.py:45
  106.9 8.8 %collective-permute-start.21 = (bf16[64,1024]{1,0:T(8,128)(2,1)S(1)}, bf16[64,1024]{1,0:T(8,128)(2,1)S(1)}, u32[]{:S(2)}, u32[]{:S(2)}) collective-permute-start(bf16[64,1024]{1,0:T(8,128)(2,1)S(1)} %get-tuple-element.60), channel_id=1, source_target_pairs={{0,12},{1,5},{2,14},{3,7},{4,0},{5,9},{6,2},{7,11},{8,4},{9,13},{1... | collective-permute-start | bytes 393224 | tf_op jit(solution)/shard_map/ppermute | solution.py:45
  107.0 11.9 %collective-permute-start.20 = (bf16[64,1024]{1,0:T(8,128)(2,1)S(1)}, bf16[64,1024]{1,0:T(8,128)(2,1)S(1)}, u32[]{:S(2)}, u32[]{:S(2)}) collective-permute-start(bf16[64,1024]{1,0:T(8,128)(2,1)S(1)} %get-tuple-element.58), channel_id=1, source_target_pairs={{0,13},{1,4},{2,15},{3,6},{4,1},{5,8},{6,3},{7,10},{8,5},{9,12},{1... | collective-permute-start | bytes 393224 | tf_op jit(solution)/shard_map/ppermute | solution.py:45
  115.7 5.9 %collective-permute-start.22 = (bf16[64,1024]{1,0:T(8,128)(2,1)S(1)}, bf16[64,1024]{1,0:T(8,128)(2,1)S(1)}, u32[]{:S(2)}, u32[]{:S(2)}) collective-permute-start(bf16[64,1024]{1,0:T(8,128)(2,1)S(1)} %add_convert_fusion.1), channel_id=1, source_target_pairs={{0,12},{1,5},{2,14},{3,7},{4,0},{5,9},{6,2},{7,11},{8,4},{9,13},{1... | collective-permute-start | bytes 393224 | tf_op jit(solution)/shard_map/ppermute | solution.py:45
  121.9 9.9 %collective-permute-start.23 = (bf16[64,1024]{1,0:T(8,128)(2,1)S(1)}, bf16[64,1024]{1,0:T(8,128)(2,1)S(1)}, u32[]{:S(2)}, u32[]{:S(2)}) collective-permute-start(bf16[64,1024]{1,0:T(8,128)(2,1)S(1)} %divide_convert_fusion), channel_id=1, source_target_pairs={{1,2},{2,1},{3,4},{4,3},{5,6},{6,5},{7,8},{8,7},{9,10},{10,9},{11,... | collective-permute-start | bytes 393224 | tf_op jit(solution)/shard_map/ppermute | solution.py:50
  125.4 6.4 %collective-permute-start.24 = (bf16[64,1024]{1,0:T(8,128)(2,1)S(1)}, bf16[64,1024]{1,0:T(8,128)(2,1)S(1)}, u32[]{:S(2)}, u32[]{:S(2)}) collective-permute-start(bf16[64,1024]{1,0:T(8,128)(2,1)S(1)} %divide_convert_fusion), channel_id=1, source_target_pairs={{0,1},{1,0},{2,3},{3,2},{4,5},{5,4},{6,7},{7,6},{8,9},{9,8},{10,11... | collective-permute-start | bytes 393224 | tf_op jit(solution)/shard_map/ppermute | solution.py:45
  (8 other events, 75.2 us)
Sparse Core Ops, SparseCore 0:
  9.1 45.7 all-gather.2

commit v9 on v8

--- a/solution.py
+++ b/solution.py
@@ -11,6 +11,7 @@
 HEAD = 128
 HALVES, TURNS, PAIR, CORES = 2, 4, 2, 2
 CTX = HALVES * TURNS * PAIR * CORES
+ROWS_X, ROWS_Y = 2, 4
 NEG = -1e30
 WIRE = jnp.bfloat16
 F32 = jnp.float32
@@ -85,21 +86,15 @@
     return lax.dot_general(left, right, (((0,), (0,)), ((), ())), preferred_element_type=F32)
 
 
-def cut_kernel(q_ref, k_ref, v_ref, o_ref, start_ref, out_ref, start_out, sems):
-    rows = out_ref.shape[0]
-    half, width = rows // CORES, o_ref.shape[1]
+def cut_kernel(q_ref, k_ref, v_ref, o_ref, start_ref, out_ref, half_ref, start_out, sems):
     _, turn, _, core = here()
     lane = pl.multiple_of((turn * CORES + core) * HEAD, HEAD)
     copies = [
         (w.at[:, pl.ds(lane, HEAD)], out_ref.at[:, i * HEAD : (i + 1) * HEAD])
         for i, w in enumerate((q_ref, k_ref, v_ref))
     ]
-    at = pl.multiple_of(core * half, half)
-    for i in range(2):
-        lanes = slice(i * width // 2, (i + 1) * width // 2)
-        copies.append(
-            (o_ref.at[pl.ds(at, half), lanes], out_ref.at[i * half : (i + 1) * half, 3 * HEAD :])
-        )
+    half = half_ref.shape[0]
+    copies.append((o_ref.at[pl.ds(pl.multiple_of(core * half, half), half), :], half_ref))
     copies.append((start_ref, start_out))
     fetched(copies, sems)
 
@@ -109,38 +104,49 @@
     return pl.pallas_call(
         cut_kernel,
         out_shape=(
-            jax.ShapeDtypeStruct((rows, 3 * HEAD + width // 2), w_query.dtype),
+            jax.ShapeDtypeStruct((rows, 3 * HEAD), w_query.dtype),
+            jax.ShapeDtypeStruct((rows // CORES, width), w_out.dtype),
             jax.ShapeDtypeStruct(starts.shape, starts.dtype),
         ),
         in_specs=[HBM] * 4 + [ANY],
-        out_specs=(VMEM, VMEM),
-        scratch_shapes=[pltpu.SemaphoreType.DMA((6,))],
+        out_specs=(VMEM, VMEM, VMEM),
+        scratch_shapes=[pltpu.SemaphoreType.DMA((5,))],
         compiler_params=room(60),
     )(w_query, w_key, w_value, w_out, starts)
 
 
-def gathered_weights(mine):
-    return lax.all_gather(mine, "dp", axis=0, tiled=False)
-
-
-def pass_kernel(value_ref, ready_ref, out_ref):
-    out_ref[...] = value_ref[...]
-
-
-def passed_on(value, ready):
+def other_x(value):
+    count = ROWS_X * ROWS_Y
+    return lax.ppermute(value, "dp", [(d, (d + ROWS_Y) % count) for d in range(count)])
+
+
+def shifted_y(value, step):
+    pairs = [(d, d // ROWS_Y * ROWS_Y + (d + step) % ROWS_Y) for d in range(ROWS_X * ROWS_Y)]
+    return lax.ppermute(value, "dp", pairs)
+
+
+def gathered_halves(half):
+    return lax.all_gather(half, "dp", axis=0, tiled=False)
+
+
+def pass_kernel(value_ref, *refs):
+    refs[-1][...] = value_ref[...]
+
+
+def passed_on(value, *ready):
     return pl.pallas_call(
         pass_kernel,
         out_shape=jax.ShapeDtypeStruct(value.shape, value.dtype),
-        in_specs=[VMEM, ANY],
+        in_specs=[VMEM] + [ANY] * len(ready),
         out_specs=VMEM,
         compiler_params=room(4),
-    )(value, ready)
-
-
-def gathered_rows(shard):
+    )(value, *ready)
+
+
+def gathered_rows(shard, first_ready, last_ready):
     near = turned(shard, 1)
     next_to = turned_over(passed_on(shard, near))
-    far = turned(near, 1)
+    far = passed_on(turned(passed_on(near, *first_ready), 1), *last_ready)
     return [
         shard,
         other_core(shard),
@@ -249,102 +255,149 @@
     )(own, beside, facing, tokens, grads)
 
 
-def norm_kernel(core_ref, chip_ref, mid_token, mid_grad, second_ref, count_ref, gain_ref, *outs):
-    both_ref, normed_ref, rms_ref, dout_ref = outs
-    seg, width = mid_token.shape
+def norm_kernel(core_ref, chip_ref, mid_token, mid_grad, count_ref, gain_ref, *refs):
+    mine_ref, theirs_ref, normin_ref, normed_ref, rms_ref, dout_ref, pair_ref = refs
+    width = mid_token.shape[1]
+    rows = mine_ref.shape[0]
+    pair_ref[:rows, :] = mine_ref[...]
+    pair_ref[rows:, :] = theirs_ref[...]
     got = core_ref[...].astype(F32) + chip_ref[...].astype(F32)
     pooled = (mid_token[...] + got[:, :width]) / count_ref[...]
     rms = jnp.sqrt(jnp.mean(pooled * pooled, axis=1, keepdims=True) + 1e-06)
     normed = pooled / rms
     normed_ref[...] = normed
     rms_ref[...] = rms
-    last = lax.broadcasted_iota(jnp.int32, (seg, 1), 0) == seg - 1
-    dout = mid_grad[...] + got[:, width:] + jnp.where(last, second_ref[...], 0.0)
-    dout_ref[...] = dout
-    both_ref[:, :width] = (normed * gain_ref[...]).astype(jnp.bfloat16)
-    both_ref[:, width:] = dout.astype(jnp.bfloat16)
-
-
-def norm(from_core, from_chip, mid_token, mid_grad, second, count, gain):
+    normin_ref[...] = (normed * gain_ref[...]).astype(jnp.bfloat16)
+    dout_ref[...] = mid_grad[...] + got[:, width:]
+
+
+def norm(from_core, from_chip, mid_token, mid_grad, count, gain, mine, theirs):
     seg, width = mid_token.shape
     shape = jax.ShapeDtypeStruct
     return pl.pallas_call(
         norm_kernel,
         out_shape=(
-            shape((seg, 2 * width), jnp.bfloat16),
+            shape((seg, width), jnp.bfloat16),
             shape((seg, width), F32),
             shape((seg, 1), F32),
             shape((seg, width), F32),
+            shape((2 * mine.shape[0], mine.shape[1]), mine.dtype),
         ),
-        in_specs=[VMEM] * 7,
-        out_specs=(VMEM,) * 4,
-        compiler_params=room(6),
-    )(from_core, from_chip, mid_token, mid_grad, second, count, gain)
-
-
-def project_kernel(seg, *refs):
-    pieces, weight = refs[:8], refs[8]
-    q_ref, kv_ref, mine_ref, theirs_ref, rows, w_in, w_back, sems = refs[9:]
-    _, turn, _, core = here()
-    head = turn * CORES
-    half, wide = seg, rows.shape[1] // 4
-    depth = weight.shape[1]
+        in_specs=[VMEM] * 8,
+        out_specs=(VMEM,) * 5,
+        compiler_params=room(8),
+    )(from_core, from_chip, mid_token, mid_grad, count, gain, mine, theirs)
+
+
+def dout_kernel(dout_ref, second_ref, ready_ref, full_ref, half_ref):
+    seg = dout_ref.shape[0]
+    last = lax.broadcasted_iota(jnp.int32, (seg, 1), 0) == seg - 1
+    dout = dout_ref[...] + jnp.where(last, second_ref[...], 0.0)
+    full_ref[...] = dout
+    half_ref[...] = dout.astype(jnp.bfloat16)
+
+
+def whole_dout(dout, second, ready):
+    shape = jax.ShapeDtypeStruct
+    return pl.pallas_call(
+        dout_kernel,
+        out_shape=(shape(dout.shape, F32), shape(dout.shape, jnp.bfloat16)),
+        in_specs=[VMEM, VMEM, ANY],
+        out_specs=(VMEM, VMEM),
+        compiler_params=room(4),
+    )(dout, second, ready)
+
+
+def dattended_kernel(own_ref, other_ref, weight_ref, ready_ref, *refs):
+    outs, rows, weight, sems = refs[:TURNS], *refs[TURNS:]
+    heads, half = weight_ref.shape[:2]
+    copies = stacked([own_ref, other_ref], rows)
+    copies += [(weight_ref.at[i], weight.at[i * half : (i + 1) * half, :]) for i in range(heads)]
+    fetched(copies, sems)
+    turn = here()[1]
+    for step, out in enumerate(outs):
+        at = pl.multiple_of((turn + step) % TURNS * CORES * half, CORES * half)
+        part = weight[pl.ds(at, CORES * half), :]
+        out[...] = contract_last(rows[...], part).astype(jnp.bfloat16)
+
+
+def dattended(own, other, halves, ready):
+    heads, half, width = halves.shape
+    rows = 2 * own.shape[0]
+    return pl.pallas_call(
+        dattended_kernel,
+        out_shape=(jax.ShapeDtypeStruct((rows, CORES * half), jnp.bfloat16),) * TURNS,
+        in_specs=[ANY] * 4,
+        out_specs=(VMEM,) * TURNS,
+        scratch_shapes=[
+            pltpu.VMEM((rows, width), jnp.bfloat16),
+            pltpu.VMEM((heads * half, width), jnp.bfloat16),
+            pltpu.SemaphoreType.DMA((2 + heads,)),
+        ],
+        compiler_params=room(12),
+    )(own, other, halves, ready)
+
+
+def project_kernel(*refs):
+    pieces, weights = refs[:8], refs[8:12]
+    q_ref, kv_ref, w_ref, rows, sems = refs[12:]
     copies = stacked(pieces, rows)
-    for i in range(weight.shape[0]):
-        copies.append((weight.at[i, :, : 3 * HEAD], w_in.at[i * depth : (i + 1) * depth, :]))
-    for j, its_head in enumerate((head + core, head + 1 - core)):
-        for i in range(2):
-            source = weight.at[its_head, i * half : (i + 1) * half, 3 * HEAD :]
-            lanes = slice(i * wide, (i + 1) * wide)
-            copies.append((source, w_back.at[j * half : (j + 1) * half, lanes]))
+    dp = lax.axis_index("dp")
+    x, y = dp // ROWS_Y, dp % ROWS_Y
+    depth = weights[0].shape[0] // ROWS_X
+    for weight, step in zip(weights, (0, 1, -1, 2)):
+        its_y = (y - step + ROWS_Y) % ROWS_Y
+        for i in range(ROWS_X):
+            its_x = x if i == 0 else 1 - x
+            at = pl.multiple_of((its_x * ROWS_Y + its_y) * depth, depth)
+            copies.append((weight.at[i * depth : (i + 1) * depth, :], w_ref.at[pl.ds(at, depth), :]))
     fetched(copies, sems)
-    width = rows.shape[1] // 2
-    out = jnp.dot(rows[:, :width], w_in[...], preferred_element_type=F32).astype(jnp.bfloat16)
+    out = jnp.dot(rows[...], w_ref[...], preferred_element_type=F32).astype(jnp.bfloat16)
     q_ref[...] = out[:, :HEAD]
     kv_ref[...] = out[:, HEAD:]
-    da = contract_last(rows[:, width:], w_back[...]).astype(jnp.bfloat16)
-    mine_ref[...] = da[:, :half]
-    for slot, its_slot in enumerate((1, 0, 4, 5, 2, 3, 7, 6)):
-        its_rows = slice(its_slot * seg, (its_slot + 1) * seg)
-        theirs_ref[its_rows, :] = da[slot * seg : (slot + 1) * seg, half:]
 
 
 def project(pieces, weights):
     seg, width = pieces[0].shape
     rows = seg * len(pieces)
-    half = HEAD // CORES
     bf16 = lambda *shape: jax.ShapeDtypeStruct(shape, jnp.bfloat16)
     return pl.pallas_call(
-        functools.partial(project_kernel, half),
-        out_shape=(bf16(rows, HEAD), bf16(rows, 2 * HEAD), bf16(rows, half), bf16(rows, half)),
-        in_specs=[ANY] * 9,
-        out_specs=(VMEM,) * 4,
+        project_kernel,
+        out_shape=(bf16(rows, HEAD), bf16(rows, 2 * HEAD), bf16(width, 3 * HEAD)),
+        in_specs=[ANY] * 12,
+        out_specs=(VMEM,) * 3,
         scratch_shapes=[
             pltpu.VMEM((rows, width), jnp.bfloat16),
-            pltpu.VMEM((width // 2, 3 * HEAD), jnp.bfloat16),
-            pltpu.VMEM((HEAD, width // 2), jnp.bfloat16),
-            pltpu.SemaphoreType.DMA((20,)),
+            pltpu.SemaphoreType.DMA((16,)),
         ],
-        compiler_params=room(40),
-    )(*pieces, weights)
+        compiler_params=room(12),
+    )(*pieces, *weights)
+
+
+def place_dattended(core, seg, here_refs, there_refs, out_ref):
+    half = out_ref.shape[1] // CORES
+    mine = slice(core * half, (core + 1) * half)
+    other = slice((1 - core) * half, (2 - core) * half)
+    slots = ((0, 1), (2, 3), (6, 7), (5, 4)) if core == 0 else ((0, 1), (5, 4), (6, 7), (2, 3))
+    for refs in zip(here_refs, there_refs, slots):
+        for i, slot in enumerate(refs[2]):
+            rows = slice(slot * seg, (slot + 1) * seg)
+            out_ref[rows, mine] = refs[0][i * seg : (i + 1) * seg, mine]
+            out_ref[rows, other] = refs[1][(1 - i) * seg : (2 - i) * seg, mine]
 
 
 def attention_kernel(tile, seg, *refs):
-    q_ref, mine_ref, theirs_ref, blocks = *refs[:3], refs[3:7]
-    dq_ref, outs, (kv, da_ref, dkt, dvt, sems) = refs[7], refs[8:12], refs[12:]
+    q_ref, here_refs, there_refs, blocks = refs[0], refs[1:5], refs[5:9], refs[9:13]
+    dq_ref, outs, (kv, da_ref, dkt, dvt, sems) = refs[13], refs[14:18], refs[18:]
     half, turn, pair, core = here()
     queries, keys = q_ref.shape[0], kv.shape[0]
     fetched(stacked(blocks, kv), sems)
 
-    @pl.when(core == 0)
-    def _():
-        da_ref[:, : HEAD // 2] = mine_ref[...]
-        da_ref[:, HEAD // 2 :] = theirs_ref[...]
-
-    @pl.when(core == 1)
-    def _():
-        da_ref[:, : HEAD // 2] = theirs_ref[...]
-        da_ref[:, HEAD // 2 :] = mine_ref[...]
+    for which in range(CORES):
+
+        @pl.when(core == which)
+        def _(which=which):
+            place_dattended(which, seg, here_refs, there_refs, da_ref)
 
     spot = lax.broadcasted_iota(jnp.int32, (1, keys), 1)
     block = spot // queries
@@ -386,14 +439,14 @@
         out[:, HEAD:] = dvt[:, lanes].T.astype(jnp.bfloat16)
 
 
-def attention(q, mine, theirs, blocks, seg):
+def attention(q, da_here, da_there, blocks, seg):
     queries = q.shape[0]
     keys = sum(block.shape[0] for block in blocks)
     part = jax.ShapeDtypeStruct(blocks[0].shape, jnp.bfloat16)
     return pl.pallas_call(
         functools.partial(attention_kernel, 256, seg),
         out_shape=(jax.ShapeDtypeStruct((queries, HEAD), jnp.bfloat16),) + (part,) * 4,
-        in_specs=[VMEM] * 3 + [ANY] * 4,
+        in_specs=[VMEM] * 9 + [ANY] * 4,
         out_specs=(VMEM,) * 5,
         scratch_shapes=[
             pltpu.VMEM((keys, 2 * HEAD), jnp.bfloat16),
@@ -408,42 +461,30 @@
             bytes_accessed=2 * HEAD * (3 * queries + 4 * keys),
             transcendentals=queries * keys,
         ),
-    )(q, mine, theirs, *blocks)
+    )(q, *da_here, *da_there, *blocks)
 
 
 def unproject_kernel(seg, dq_ref, *refs):
-    parts, weight, swap_ref, outs, (w_in, sems) = refs[:4], refs[4], refs[5], refs[6:10], refs[10:]
-    depth = weight.shape[1]
-    fetched(
-        [
-            (weight.at[i, :, : 3 * HEAD], w_in.at[i * depth : (i + 1) * depth, :])
-            for i in range(weight.shape[0])
-        ],
-        sems,
-    )
+    parts, w_ref, swap_ref, outs = refs[:4], refs[4], refs[5], refs[6:]
     dkv = sum(ref[...].astype(F32) for ref in parts).astype(jnp.bfloat16)
     left = jnp.concatenate([dq_ref[...], dkv], axis=1)
-    out = contract_last(left, w_in[...])
+    out = contract_last(left, w_ref[...])
     for i, slot in enumerate((1, 4, 5, 7)):
         swap_ref[i * seg : (i + 1) * seg, :] = out[slot * seg : (slot + 1) * seg].astype(WIRE)
     for ref, slot in zip(outs, (0, 2, 3, 6)):
         ref[...] = out[slot * seg : (slot + 1) * seg]
 
 
-def unproject(dq, parts, weights, seg):
-    width = weights.shape[0] * weights.shape[1]
+def unproject(dq, parts, w_full, seg):
+    width = w_full.shape[0]
     return pl.pallas_call(
         functools.partial(unproject_kernel, seg),
         out_shape=(jax.ShapeDtypeStruct((4 * seg, width), WIRE),)
         + (jax.ShapeDtypeStruct((seg, width), F32),) * 4,
-        in_specs=[VMEM] * 5 + [ANY],
+        in_specs=[VMEM] * 6,
         out_specs=(VMEM,) * 5,
-        scratch_shapes=[
-            pltpu.VMEM((width, 3 * HEAD), jnp.bfloat16),
-            pltpu.SemaphoreType.DMA((weights.shape[0],)),
-        ],
         compiler_params=room(16),
-    )(dq, *parts, weights)
+    )(dq, *parts, w_full)
 
 
 def join_kernel(swapped, own, near, next_to, far, own_out, near_out, next_out, far_out):
@@ -482,8 +523,9 @@
     length = rows * CTX
     ctx, core = lax.axis_index("ctx"), here()[3]
 
-    mine, own_starts = cut_weights(w_query, w_key, w_value, w_out, starts)
-    weights = gathered_weights(mine)
+    mine, half, own_starts = cut_weights(w_query, w_key, w_value, w_out, starts)
+    halves = gathered_halves(half)
+    theirs = other_x(mine)
     beside, facing = other_core(own_starts), other_chip(own_starts)
     to_core, to_chip, mid_token, mid_grad, first = window_sums(
         own_starts, beside, facing, token_rows, grad_out
@@ -497,16 +539,23 @@
     opens, ends = window[:-1], window[1:]
     count = (ends - opens)[seg : 2 * seg, None].astype(F32)
     second = two_back(first)
-    both, normed, rms, dout = norm(
-        other_core(to_core), other_chip(to_chip), mid_token, mid_grad, second, count, gain[None]
+    normin, normed, rms, dout, both = norm(
+        other_core(to_core), other_chip(to_chip), mid_token, mid_grad, count, gain[None], mine, theirs
     )
-    q, own, mine, theirs = project(gathered_rows(both), weights)
+    weights = [both, shifted_y(both, 1), shifted_y(both, -1), shifted_y(both, 2)]
+    pieces = gathered_rows(normin, weights[1:3], weights[3:])
+    q, own, w_full = project(pieces, weights)
     cross, far, beside = across(own, 0, True), across(own, 0, False), other_pair(own)
-    theirs = other_core(theirs)
+    dout, dout_b = whole_dout(dout, second, pieces[2])
+    da = dattended(dout_b, other_core(dout_b), halves, beside)
+    da_here = [da[0]] + [
+        moved(da[i], lambda h, t, p, k, i=i: (h, t + i, p, k)) for i in range(1, TURNS)
+    ]
+    da_there = [other_core(piece) for piece in da_here]
     blocks = (own, beside, far, cross)
-    dq, own, beside, far, cross = attention(q, mine, theirs, blocks, seg)
+    dq, own, beside, far, cross = attention(q, da_here, da_there, blocks, seg)
     parts = (own, other_pair(beside), across(far, 1, False), across(cross, 1, True))
-    dnormin = summed_rows(*unproject(dq, parts, weights, seg))
+    dnormin = summed_rows(*unproject(dq, parts, w_full, seg))
 
     scaled = dnormin * gain
     dpooled = dout + (scaled - normed * jnp.mean(scaled * normed, axis=-1, keepdims=True)) / rms

time: 141 us -> 149 us (1.057); the launches traced: 140 us -> 147 us
  starting transfers between devices: 37.3 us -> 62.2 us
  waiting for transfers between devices: 72.7 us -> 50.5 us
  Pallas kernels: 10.9 us -> 14.6 us
    ppermute x21 -> x28, waiting for transfers between devices: 58.6 us -> 38 us  [moved(): return lax.ppermute(value, 'ctx', pairs)]
    ppermute x21 -> x28, starting transfers between devices: 15.7 us -> 27.4 us  [moved(): return lax.ppermute(value, 'ctx', pairs)]
    ppermute x1, waiting for transfers between devices: 6.37 us -> 1.31 us  [two_back(): lax.ppermute(value, 'ctx', [(i, i - CORES) for i in range(CORES, CTX)])]
    ppermute x0 -> x4, starting transfers between devices: none -> 4.54 us  [the longest x3 4.45 us: shifted_y(): return lax.ppermute(value, 'dp', pairs)]
    ppermute x1, starting transfers between devices: 2.29 us -> 6.68 us  [two_back(): lax.ppermute(value, 'ctx', [(i, i - CORES) for i in range(CORES, CTX)])]
    ppermute x3, starting transfers between devices: 19.3 us -> 23.5 us  [other_chip(): return lax.ppermute(value, 'ctx', pairs)]
    pallas_call x2 -> x4, Pallas kernels: 1.78 us -> 5.86 us  [the longest x1 3.37 us: project(): pl.pallas_call(project_kernel, out_shape=(bf16(rows, HEAD), bf16(rows, 2...]
    ppermute x0 -> x4, waiting for transfers between devices: none -> 2.49 us  [the longest x3 2.49 us: shifted_y(): return lax.ppermute(value, 'dp', pairs)]
  transfers between devices with their start and end apart: 26 -> 37, of which waited for: 17 -> 19; matrix products, arithmetic and copies ran while one was open for 0% -> 0% of each run, Pallas kernels for 1% -> 5%
where the time goes in v9:
time: 149 us; the launch traced here: 147 us
  starting transfers between devices  62.2 us (42%)
  waiting for transfers between devices  50.5 us (34%)
  Pallas kernels  14.6 us (10%)
  between operations  13.8 us (9%)
  local copies, waits for them, and re-layouts  3.22 us (2%)
    ppermute x28, waiting for transfers between devices, moved(): return lax.ppermute(value, 'ctx', pairs)  38 us
    ppermute x28, starting transfers between devices, moved(): return lax.ppermute(value, 'ctx', pairs)  27.4 us
    ppermute x3, starting transfers between devices, other_chip(): return lax.ppermute(value, 'ctx', pairs)  23.5 us
    ppermute x3, waiting for transfers between devices, other_chip(): return lax.ppermute(value, 'ctx', pairs)  8.73 us
    ppermute x1, starting transfers between devices, two_back(): lax.ppermute(value, 'ctx', [(i, i - CORES) for i in range(CORES, CTX)])  6.68 us
    pallas_call x1, Pallas kernels, attention(): pl.pallas_call(functools.partial(attention_kernel, 256, seg), out_shape=(...  4.48 us
    ppermute x3, starting transfers between devices, shifted_y(): return lax.ppermute(value, 'dp', pairs)  4.45 us
    pallas_call x1, Pallas kernels, project(): pl.pallas_call(project_kernel, out_shape=(bf16(rows, HEAD), bf16(rows, 2...  3.37 us
  transfers between devices with their start and end apart: 37, of which 19 were waited for; matrix products, arithmetic and copies ran while one was open for 0% of the time, Pallas kernels for 5%

profile of v9, /device:TPU:6, one launch (start us, length us, event | category | flops | bytes accessed | tf_op | source)
XLA Modules:
  0.0 146.5 jit_solution(4429892224847558655)
XLA Ops:
  6.5 1.8 %shard_map.82 = (bf16[128,384]{1,0:T(8,128)(2,1)}, bf16[64,1024]{1,0:T(8,128)(2,1)}, s32[1,64]{1,0:T(1,128)}) custom-call(bf16[128,1024]{1,0:T(8,128)(2,1)} %q_ref.1, bf16[128,1024]{1,0:T(8,128)(2,1)} %k_ref.1, bf16[128,1024]{1,0:T(8,128)(2,1)} %v_ref.1, bf16[128,1024]{1,0:T(8,128)(2,1)} %o_ref.1, s32[1,64]{1,0:T(1,128)} %start_ref.1), custom_call_target="tpu_custom_call" | custom-call | tf_op jit(solution)/shard_map/pallas_call | solution.py:104
  8.4 8.7 %collective-permute-start = (s32[1,64]{1,0:T(1,128)}, s32[1,64]{1,0:T(1,128)S(1)}, u32[]{:S(2)}, u32[]{:S(2)}) collective-permute-start(s32[1,64]{1,0:T(1,128)} %get-tuple-element.41.own_ref), channel_id=1, source_target_pairs={{1,2},{2,1},{3,4},{4,3},{5,6},{6,5},{7,8},{8,7},{9,10},{10,9},{11,... | collective-permute-start | bytes 776 | tf_op jit(solution)/shard_map/ppermute | solution.py:51
  22.2 7.1 %collective-permute-start.3 = (bf16[64,2048]{1,0:T(8,128)(2,1)S(1)}, bf16[64,2048]{1,0:T(8,128)(2,1)S(1)}, u32[]{:S(2)}, u32[]{:S(2)}) collective-permute-start(bf16[64,2048]{1,0:T(8,128)(2,1)S(1)} %get-tuple-element.43), channel_id=1, source_target_pairs={{1,2},{2,1},{3,4},{4,3},{5,6},{6,5},{7,8},{8,7},{9,10},{10,9},{11,... | collective-permute-start | bytes 786440 | tf_op jit(solution)/shard_map/ppermute | solution.py:51
  29.7 4.9 %collective-permute-done.3.chip_ref = bf16[64,2048]{1,0:T(8,128)(2,1)S(1)} collective-permute-done((bf16[64,2048]{1,0:T(8,128)(2,1)S(1)}, bf16[64,2048]{1,0:T(8,128)(2,1)S(1)}, u32[]{:S(2)}, u32[]{:S(2)}) %collective-permute-start.3) | collective-permute-done | bytes 262176 | tf_op jit(solution)/shard_map/ppermute | solution.py:51
  35.8 2.4 %collective-permute-start.12 = (bf16[256,384]{1,0:T(8,128)(2,1)S(1)}, bf16[256,384]{1,0:T(8,128)(2,1)S(1)}, u32[]{:S(2)}, u32[]{:S(2)}) collective-permute-start(bf16[256,384]{1,0:T(8,128)(2,1)S(1)} %get-tuple-element.51.refs_8_), channel_id=1, source_target_pairs={{0,96},{32,0},{64,32},{96,64},{128,224},{160,128},{192,160},{224,1... | collective-permute-start | bytes 589832 | tf_op jit(solution)/shard_map/ppermute | solution.py:125
  39.3 7.2 %collective-permute-done.6.ready_ref.refs_0_.value_ref.refs_2_ = bf16[64,1024]{1,0:T(8,128)(2,1)S(1)} collective-permute-done((bf16[64,1024]{1,0:T(8,128)(2,1)S(1)}, bf16[64,1024]{1,0:T(8,128)(2,1)S(1)}, u32[]{:S(2)}, u32[]{:S(2)}) %collective-permute-start.6) | collective-permute-done | bytes 131104 | tf_op jit(solution)/shard_map/ppermute | solution.py:46
  46.6 2.5 %collective-permute-done.11.refs_0_.refs_9_ = bf16[256,384]{1,0:T(8,128)(2,1)S(1)} collective-permute-done((bf16[256,384]{1,0:T(8,128)(2,1)S(1)}, bf16[256,384]{1,0:T(8,128)(2,1)S(1)}, u32[]{:S(2)}, u32[]{:S(2)}) %collective-permute-start.11) | collective-permute-done | bytes 196640 | tf_op jit(solution)/shard_map/ppermute | solution.py:125
  50.7 3.0 %collective-permute-done.8.refs_3_ = bf16[64,1024]{1,0:T(8,128)(2,1)S(1)} collective-permute-done((bf16[64,1024]{1,0:T(8,128)(2,1)S(1)}, bf16[64,1024]{1,0:T(8,128)(2,1)S(1)}, u32[]{:S(2)}, u32[]{:S(2)}) %collective-permute-start.8) | collective-permute-done | bytes 131104 | tf_op jit(solution)/shard_map/ppermute | solution.py:46
  53.7 2.6 %collective-permute-done.13.value_ref = bf16[64,1024]{1,0:T(8,128)(2,1)S(1)} collective-permute-done((bf16[64,1024]{1,0:T(8,128)(2,1)S(1)}, bf16[64,1024]{1,0:T(8,128)(2,1)S(1)}, u32[]{:S(2)}, u32[]{:S(2)}) %collective-permute-start.13) | collective-permute-done | bytes 131104 | tf_op jit(solution)/shard_map/ppermute | solution.py:46
  57.7 3.4 %shard_map.89 = (bf16[512,128]{1,0:T(8,128)(2,1)S(1)}, bf16[512,256]{1,0:T(8,128)(2,1)S(1)}, bf16[1024,384]{1,0:T(8,128)(2,1)S(1)}) custom-call(bf16[64,1024]{1,0:T(8,128)(2,1)S(1)} %get-tuple-element.49.value_ref.refs_0_, bf16[64,1024]{1,0:T(8,128)(2,1)S(1)} %collective-permute-done.7.refs_1_, ...), custom_call_target="tpu_custom_call" | custom-call | tf_op jit(solution)/shard_map/pallas_call | solution.py:364
  63.8 6.7 %collective-permute-start.5 = (f32[1,1024]{1,0:T(1,128)S(1)}, f32[1,1024]{1,0:T(1,128)S(1)}, u32[]{:S(2)}, u32[]{:S(2)}) collective-permute-start(f32[1,1024]{1,0:T(1,128)S(1)} %get-tuple-element.48), channel_id=1, source_target_pairs={{2,0},{3,1},{4,2},{5,3},{6,4},{7,5},{8,6},{9,7},{10,8},{11,9},{12,... | collective-permute-start | bytes 12296 | tf_op jit(solution)/shard_map/ppermute | solution.py:55
  74.7 2.2 %shard_map.90 = (bf16[128,128]{1,0:T(8,128)(2,1)S(1)}, bf16[128,128]{1,0:T(8,128)(2,1)S(1)}, bf16[128,128]{1,0:T(8,128)(2,1)S(1)}, bf16[128,128]{1,0:T(8,128)(2,1)S(1)}) custom-call(bf16[64,1024]{1,0:T(8,128)(2,1)S(1)} %get-tuple-element.53.own_ref, bf16[64,1024]{1,0:T(8,128)(2,1)S(1)} %collective-permute-done.16.other_ref, ...), custom_call_target="tpu_custom_call" | custom-call | tf_op jit(solution)/shard_map/pallas_call | solution.py:327
  78.0 3.9 %collective-permute-start.20 = (bf16[128,128]{1,0:T(8,128)(2,1)S(1)}, bf16[128,128]{1,0:T(8,128)(2,1)S(1)}, u32[]{:S(2)}, u32[]{:S(2)}) collective-permute-start(bf16[128,128]{1,0:T(8,128)(2,1)S(1)} %get-tuple-element.59), channel_id=1, source_target_pairs={{0,12},{1,13},{2,14},{3,15},{4,0},{5,1},{6,2},{7,3},{8,4},{9,5},{1... | collective-permute-start | bytes 98312 | tf_op jit(solution)/shard_map/ppermute | solution.py:46
  83.1 1.8 %collective-permute-done.19.refs_3_ = bf16[128,128]{1,0:T(8,128)(2,1)S(1)} collective-permute-done((bf16[128,128]{1,0:T(8,128)(2,1)S(1)}, bf16[128,128]{1,0:T(8,128)(2,1)S(1)}, u32[]{:S(2)}, u32[]{:S(2)}) %collective-permute-start.19) | collective-permute-done | bytes 32800 | tf_op jit(solution)/shard_map/ppermute | solution.py:46
  86.8 4.5 %shard_map.91 = (bf16[512,128]{1,0:T(8,128)(2,1)S(1)}, bf16[512,256]{1,0:T(8,128)(2,1)S(1)}, bf16[512,256]{1,0:T(8,128)(2,1)S(1)}, bf16[512,256]{1,0:T(8,128)(2,1)S(1)}, bf16[512,256]{1,0:T(8,128)(2,1)S(1)}) custom-call(bf16[512,128]{1,0:T(8,128)(2,1)S(1)} %get-tuple-element.52.refs_0_, bf16[128,128]{1,0:T(8,128)(2,1)S(1)} %get-tuple-element.56.refs_1_, ...), custom_call_target="tpu_custom_call" | custom-call | flops 1610612736 | bytes 2490368 | tf_op jit(solution)/shard_map/pallas_call | solution.py:446
  91.4 8.4 %collective-permute-start.28 = (bf16[512,256]{1,0:T(8,128)(2,1)S(1)}, bf16[512,256]{1,0:T(8,128)(2,1)S(1)}, u32[]{:S(2)}, u32[]{:S(2)}) collective-permute-start(bf16[512,256]{1,0:T(8,128)(2,1)S(1)} %get-tuple-element.63), channel_id=1, source_target_pairs={{16,0},{17,1},{18,2},{19,3},{20,4},{21,5},{22,6},{23,7},{24,8},{25... | collective-permute-start | bytes 786440 | tf_op jit(solution)/shard_map/ppermute | solution.py:46
  101.4 9.6 %collective-permute-done.28.refs_2_ = bf16[512,256]{1,0:T(8,128)(2,1)S(1)} collective-permute-done((bf16[512,256]{1,0:T(8,128)(2,1)S(1)}, bf16[512,256]{1,0:T(8,128)(2,1)S(1)}, u32[]{:S(2)}, u32[]{:S(2)}) %collective-permute-start.28) | collective-permute-done | bytes 262176 | tf_op jit(solution)/shard_map/ppermute | solution.py:46
  111.8 1.9 %collective-permute-done.30.swapped = bf16[256,1024]{1,0:T(8,128)(2,1)S(1)} collective-permute-done((bf16[256,1024]{1,0:T(8,128)(2,1)S(1)}, bf16[256,1024]{1,0:T(8,128)(2,1)S(1)}, u32[]{:S(2)}, u32[]{:S(2)}) %collective-permute-start.30) | collective-permute-done | bytes 524320 | tf_op jit(solution)/shard_map/ppermute | solution.py:46
  113.8 3.7 %collective-permute-start.32 = (bf16[64,1024]{1,0:T(8,128)(2,1)S(1)}, bf16[64,1024]{1,0:T(8,128)(2,1)S(1)}, u32[]{:S(2)}, u32[]{:S(2)}) collective-permute-start(bf16[64,1024]{1,0:T(8,128)(2,1)S(1)} %get-tuple-element.74), channel_id=1, source_target_pairs={{0,12},{1,5},{2,14},{3,7},{4,0},{5,9},{6,2},{7,11},{8,4},{9,13},{1... | collective-permute-start | bytes 393224 | tf_op jit(solution)/shard_map/ppermute | solution.py:46
  117.5 3.7 %collective-permute-done.32 = bf16[64,1024]{1,0:T(8,128)(2,1)S(1)} collective-permute-done((bf16[64,1024]{1,0:T(8,128)(2,1)S(1)}, bf16[64,1024]{1,0:T(8,128)(2,1)S(1)}, u32[]{:S(2)}, u32[]{:S(2)}) %collective-permute-start.32) | collective-permute-done | bytes 131104 | tf_op jit(solution)/shard_map/ppermute | solution.py:46
  121.2 3.5 %collective-permute-start.33 = (bf16[64,1024]{1,0:T(8,128)(2,1)S(1)}, bf16[64,1024]{1,0:T(8,128)(2,1)S(1)}, u32[]{:S(2)}, u32[]{:S(2)}) collective-permute-start(bf16[64,1024]{1,0:T(8,128)(2,1)S(1)} %add_convert_fusion.1), channel_id=1, source_target_pairs={{0,12},{1,5},{2,14},{3,7},{4,0},{5,9},{6,2},{7,11},{8,4},{9,13},{1... | collective-permute-start | bytes 393224 | tf_op jit(solution)/shard_map/ppermute | solution.py:46
  124.9 2.6 %collective-permute-done.33 = bf16[64,1024]{1,0:T(8,128)(2,1)S(1)} collective-permute-done((bf16[64,1024]{1,0:T(8,128)(2,1)S(1)}, bf16[64,1024]{1,0:T(8,128)(2,1)S(1)}, u32[]{:S(2)}, u32[]{:S(2)}) %collective-permute-start.33) | collective-permute-done | bytes 131104 | tf_op jit(solution)/shard_map/ppermute | solution.py:46
  127.8 7.7 %collective-permute-start.34 = (bf16[64,1024]{1,0:T(8,128)(2,1)S(1)}, bf16[64,1024]{1,0:T(8,128)(2,1)S(1)}, u32[]{:S(2)}, u32[]{:S(2)}) collective-permute-start(bf16[64,1024]{1,0:T(8,128)(2,1)S(1)} %divide_convert_fusion), channel_id=1, source_target_pairs={{1,2},{2,1},{3,4},{4,3},{5,6},{6,5},{7,8},{8,7},{9,10},{10,9},{11,... | collective-permute-start | bytes 393224 | tf_op jit(solution)/shard_map/ppermute | solution.py:51
  135.6 2.5 %collective-permute-done.34 = bf16[64,1024]{1,0:T(8,128)(2,1)S(1)} collective-permute-done((bf16[64,1024]{1,0:T(8,128)(2,1)S(1)}, bf16[64,1024]{1,0:T(8,128)(2,1)S(1)}, u32[]{:S(2)}, u32[]{:S(2)}) %collective-permute-start.34) | collective-permute-done | bytes 131104 | tf_op jit(solution)/shard_map/ppermute | solution.py:51
  (90 shorter events, 26.6 us)
Async XLA Ops:
  6.5 66.9 %all-gather.3.cloned.1.call-start = ((), (), s32[]{:S(2)}) async-start(), calls=%async_computation | async-start | bytes 1179648 | tf_op jit(solution)/shard_map/all_gather | solution.py:129
  8.3 8.9 %collective-permute-start.1 = (s32[1,64]{1,0:T(1,128)}, s32[1,64]{1,0:T(1,128)S(1)}, u32[]{:S(2)}, u32[]{:S(2)}) collective-permute-start(s32[1,64]{1,0:T(1,128)} %get-tuple-element.41.own_ref), channel_id=1, source_target_pairs={{0,1},{1,0},{2,3},{3,2},{4,5},{5,4},{6,7},{7,6},{8,9},{9,8},{10,11... | collective-permute-start | bytes 776 | tf_op jit(solution)/shard_map/ppermute | solution.py:46
  8.4 10.1 %collective-permute-start = (s32[1,64]{1,0:T(1,128)}, s32[1,64]{1,0:T(1,128)S(1)}, u32[]{:S(2)}, u32[]{:S(2)}) collective-permute-start(s32[1,64]{1,0:T(1,128)} %get-tuple-element.41.own_ref), channel_id=1, source_target_pairs={{1,2},{2,1},{3,4},{4,3},{5,6},{6,5},{7,8},{8,7},{9,10},{10,9},{11,... | collective-permute-start | bytes 776 | tf_op jit(solution)/shard_map/ppermute | solution.py:51
  17.1 12.6 %collective-permute-start.4 = (bf16[128,384]{1,0:T(8,128)(2,1)}, bf16[128,384]{1,0:T(8,128)(2,1)S(1)}, u32[]{:S(2)}, u32[]{:S(2)}) collective-permute-start(bf16[128,384]{1,0:T(8,128)(2,1)} %get-tuple-element.46.refs_0_), channel_id=1, source_target_pairs={{0,128},{32,160},{64,192},{96,224},{128,0},{160,32},{192,64},{224,... | collective-permute-start | bytes 294920 | tf_op jit(solution)/shard_map/ppermute | solution.py:120
  22.1 7.6 %collective-permute-start.2 = (bf16[64,2048]{1,0:T(8,128)(2,1)S(1)}, bf16[64,2048]{1,0:T(8,128)(2,1)S(1)}, u32[]{:S(2)}, u32[]{:S(2)}) collective-permute-start(bf16[64,2048]{1,0:T(8,128)(2,1)S(1)} %get-tuple-element.42), channel_id=1, source_target_pairs={{0,1},{1,0},{2,3},{3,2},{4,5},{5,4},{6,7},{7,6},{8,9},{9,8},{10,11... | collective-permute-start | bytes 786440 | tf_op jit(solution)/shard_map/ppermute | solution.py:46
  22.2 12.4 %collective-permute-start.3 = (bf16[64,2048]{1,0:T(8,128)(2,1)S(1)}, bf16[64,2048]{1,0:T(8,128)(2,1)S(1)}, u32[]{:S(2)}, u32[]{:S(2)}) collective-permute-start(bf16[64,2048]{1,0:T(8,128)(2,1)S(1)} %get-tuple-element.43), channel_id=1, source_target_pairs={{1,2},{2,1},{3,4},{4,3},{5,6},{6,5},{7,8},{8,7},{9,10},{10,9},{11,... | collective-permute-start | bytes 786440 | tf_op jit(solution)/shard_map/ppermute | solution.py:51
  34.9 14.2 %collective-permute-start.11 = (bf16[256,384]{1,0:T(8,128)(2,1)S(1)}, bf16[256,384]{1,0:T(8,128)(2,1)S(1)}, u32[]{:S(2)}, u32[]{:S(2)}) collective-permute-start(bf16[256,384]{1,0:T(8,128)(2,1)S(1)} %get-tuple-element.51.refs_8_), channel_id=1, source_target_pairs={{0,32},{32,64},{64,96},{96,0},{128,160},{160,192},{192,224},{224,1... | collective-permute-start | bytes 589832 | tf_op jit(solution)/shard_map/ppermute | solution.py:125
  35.8 13.3 %collective-permute-start.12 = (bf16[256,384]{1,0:T(8,128)(2,1)S(1)}, bf16[256,384]{1,0:T(8,128)(2,1)S(1)}, u32[]{:S(2)}, u32[]{:S(2)}) collective-permute-start(bf16[256,384]{1,0:T(8,128)(2,1)S(1)} %get-tuple-element.51.refs_8_), channel_id=1, source_target_pairs={{0,96},{32,0},{64,32},{96,64},{128,224},{160,128},{192,160},{224,1... | collective-permute-start | bytes 589832 | tf_op jit(solution)/shard_map/ppermute | solution.py:125
  38.2 8.3 %collective-permute-start.6 = (bf16[64,1024]{1,0:T(8,128)(2,1)S(1)}, bf16[64,1024]{1,0:T(8,128)(2,1)S(1)}, u32[]{:S(2)}, u32[]{:S(2)}) collective-permute-start(bf16[64,1024]{1,0:T(8,128)(2,1)S(1)} %get-tuple-element.49.value_ref.refs_0_), channel_id=1, source_target_pairs={{0,4},{1,13},{2,6},{3,15},{4,8},{5,1},{6,10},{7,3},{8,12},{9,5},{1... | collective-permute-start | bytes 393224 | tf_op jit(solution)/shard_map/ppermute | solution.py:46
  38.2 15.5 %collective-permute-start.14 = (bf16[256,384]{1,0:T(8,128)(2,1)S(1)}, bf16[256,384]{1,0:T(8,128)(2,1)S(1)}, u32[]{:S(2)}, u32[]{:S(2)}) collective-permute-start(bf16[256,384]{1,0:T(8,128)(2,1)S(1)} %get-tuple-element.51.refs_8_), channel_id=1, source_target_pairs={{0,64},{32,96},{64,0},{96,32},{128,192},{160,224},{192,128},{224,1... | collective-permute-start | bytes 589832 | tf_op jit(solution)/shard_map/ppermute | solution.py:125
  46.5 7.2 %collective-permute-start.8 = (bf16[64,1024]{1,0:T(8,128)(2,1)S(1)}, bf16[64,1024]{1,0:T(8,128)(2,1)S(1)}, u32[]{:S(2)}, u32[]{:S(2)}) collective-permute-start(bf16[64,1024]{1,0:T(8,128)(2,1)S(1)} %shard_map.86), channel_id=1, source_target_pairs={{0,13},{1,4},{2,15},{3,6},{4,1},{5,8},{6,3},{7,10},{8,5},{9,12},{1... | collective-permute-start | bytes 393224 | tf_op jit(solution)/shard_map/ppermute | solution.py:46
  49.2 7.2 %collective-permute-start.7 = (bf16[64,1024]{1,0:T(8,128)(2,1)S(1)}, bf16[64,1024]{1,0:T(8,128)(2,1)S(1)}, u32[]{:S(2)}, u32[]{:S(2)}) collective-permute-start(bf16[64,1024]{1,0:T(8,128)(2,1)S(1)} %get-tuple-element.49.value_ref.refs_0_), channel_id=1, source_target_pairs={{0,1},{1,0},{2,3},{3,2},{4,5},{5,4},{6,7},{7,6},{8,9},{9,8},{10,11... | collective-permute-start | bytes 393224 | tf_op jit(solution)/shard_map/ppermute | solution.py:46
  61.1 12.3 %collective-permute-start.17 = (bf16[512,256]{1,0:T(8,128)(2,1)S(1)}, bf16[512,256]{1,0:T(8,128)(2,1)S(1)}, u32[]{:S(2)}, u32[]{:S(2)}) collective-permute-start(bf16[512,256]{1,0:T(8,128)(2,1)S(1)} %get-tuple-element.55.refs_9_), channel_id=1, source_target_pairs={{0,2},{1,3},{2,0},{3,1},{4,6},{5,7},{6,4},{7,5},{8,10},{9,11},{10,... | collective-permute-start | bytes 786440 | tf_op jit(solution)/shard_map/ppermute | solution.py:46
  61.2 20.7 %collective-permute-start.25 = (bf16[512,256]{1,0:T(8,128)(2,1)S(1)}, bf16[512,256]{1,0:T(8,128)(2,1)S(1)}, u32[]{:S(2)}, u32[]{:S(2)}) collective-permute-start(bf16[512,256]{1,0:T(8,128)(2,1)S(1)} %get-tuple-element.55.refs_9_), channel_id=1, source_target_pairs={{0,16},{1,17},{2,18},{3,19},{4,20},{5,21},{6,22},{7,23},{8,24},{9,... | collective-permute-start | bytes 786440 | tf_op jit(solution)/shard_map/ppermute | solution.py:46
  62.5 23.1 %collective-permute-start.26 = (bf16[512,256]{1,0:T(8,128)(2,1)S(1)}, bf16[512,256]{1,0:T(8,128)(2,1)S(1)}, u32[]{:S(2)}, u32[]{:S(2)}) collective-permute-start(bf16[512,256]{1,0:T(8,128)(2,1)S(1)} %get-tuple-element.55.refs_9_), channel_id=1, source_target_pairs={{0,18},{1,19},{2,16},{3,17},{4,22},{5,23},{6,20},{7,21},{8,26},{9,... | collective-permute-start | bytes 786440 | tf_op jit(solution)/shard_map/ppermute | solution.py:46
  63.8 8.0 %collective-permute-start.5 = (f32[1,1024]{1,0:T(1,128)S(1)}, f32[1,1024]{1,0:T(1,128)S(1)}, u32[]{:S(2)}, u32[]{:S(2)}) collective-permute-start(f32[1,1024]{1,0:T(1,128)S(1)} %get-tuple-element.48), channel_id=1, source_target_pairs={{2,0},{3,1},{4,2},{5,3},{6,4},{7,5},{8,6},{9,7},{10,8},{11,9},{12,... | collective-permute-start | bytes 12296 | tf_op jit(solution)/shard_map/ppermute | solution.py:55
  77.0 7.9 %collective-permute-start.19 = (bf16[128,128]{1,0:T(8,128)(2,1)S(1)}, bf16[128,128]{1,0:T(8,128)(2,1)S(1)}, u32[]{:S(2)}, u32[]{:S(2)}) collective-permute-start(bf16[128,128]{1,0:T(8,128)(2,1)S(1)} %get-tuple-element.58), channel_id=1, source_target_pairs={{0,8},{1,9},{2,10},{3,11},{4,12},{5,13},{6,14},{7,15},{8,0},{9,1},... | collective-permute-start | bytes 98312 | tf_op jit(solution)/shard_map/ppermute | solution.py:46
  78.0 7.6 %collective-permute-start.20 = (bf16[128,128]{1,0:T(8,128)(2,1)S(1)}, bf16[128,128]{1,0:T(8,128)(2,1)S(1)}, u32[]{:S(2)}, u32[]{:S(2)}) collective-permute-start(bf16[128,128]{1,0:T(8,128)(2,1)S(1)} %get-tuple-element.59), channel_id=1, source_target_pairs={{0,12},{1,13},{2,14},{3,15},{4,0},{5,1},{6,2},{7,3},{8,4},{9,5},{1... | collective-permute-start | bytes 98312 | tf_op jit(solution)/shard_map/ppermute | solution.py:46
  91.3 10.1 %collective-permute-start.27 = (bf16[512,256]{1,0:T(8,128)(2,1)S(1)}, bf16[512,256]{1,0:T(8,128)(2,1)S(1)}, u32[]{:S(2)}, u32[]{:S(2)}) collective-permute-start(bf16[512,256]{1,0:T(8,128)(2,1)S(1)} %get-tuple-element.62), channel_id=1, source_target_pairs={{0,2},{1,3},{2,0},{3,1},{4,6},{5,7},{6,4},{7,5},{8,10},{9,11},{10,... | collective-permute-start | bytes 786440 | tf_op jit(solution)/shard_map/ppermute | solution.py:46
  91.4 19.6 %collective-permute-start.28 = (bf16[512,256]{1,0:T(8,128)(2,1)S(1)}, bf16[512,256]{1,0:T(8,128)(2,1)S(1)}, u32[]{:S(2)}, u32[]{:S(2)}) collective-permute-start(bf16[512,256]{1,0:T(8,128)(2,1)S(1)} %get-tuple-element.63), channel_id=1, source_target_pairs={{16,0},{17,1},{18,2},{19,3},{20,4},{21,5},{22,6},{23,7},{24,8},{25... | collective-permute-start | bytes 786440 | tf_op jit(solution)/shard_map/ppermute | solution.py:46
  99.8 11.2 %collective-permute-start.29 = (bf16[512,256]{1,0:T(8,128)(2,1)S(1)}, bf16[512,256]{1,0:T(8,128)(2,1)S(1)}, u32[]{:S(2)}, u32[]{:S(2)}) collective-permute-start(bf16[512,256]{1,0:T(8,128)(2,1)S(1)} %get-tuple-element.64), channel_id=1, source_target_pairs={{16,2},{17,3},{18,0},{19,1},{20,6},{21,7},{22,4},{23,5},{24,10},{2... | collective-permute-start | bytes 786440 | tf_op jit(solution)/shard_map/ppermute | solution.py:46
  113.8 7.4 %collective-permute-start.32 = (bf16[64,1024]{1,0:T(8,128)(2,1)S(1)}, bf16[64,1024]{1,0:T(8,128)(2,1)S(1)}, u32[]{:S(2)}, u32[]{:S(2)}) collective-permute-start(bf16[64,1024]{1,0:T(8,128)(2,1)S(1)} %get-tuple-element.74), channel_id=1, source_target_pairs={{0,12},{1,5},{2,14},{3,7},{4,0},{5,9},{6,2},{7,11},{8,4},{9,13},{1... | collective-permute-start | bytes 393224 | tf_op jit(solution)/shard_map/ppermute | solution.py:46
  117.5 7.4 %collective-permute-start.31 = (bf16[64,1024]{1,0:T(8,128)(2,1)S(1)}, bf16[64,1024]{1,0:T(8,128)(2,1)S(1)}, u32[]{:S(2)}, u32[]{:S(2)}) collective-permute-start(bf16[64,1024]{1,0:T(8,128)(2,1)S(1)} %get-tuple-element.72), channel_id=1, source_target_pairs={{0,13},{1,4},{2,15},{3,6},{4,1},{5,8},{6,3},{7,10},{8,5},{9,12},{1... | collective-permute-start | bytes 393224 | tf_op jit(solution)/shard_map/ppermute | solution.py:46
  127.8 10.3 %collective-permute-start.34 = (bf16[64,1024]{1,0:T(8,128)(2,1)S(1)}, bf16[64,1024]{1,0:T(8,128)(2,1)S(1)}, u32[]{:S(2)}, u32[]{:S(2)}) collective-permute-start(bf16[64,1024]{1,0:T(8,128)(2,1)S(1)} %divide_convert_fusion), channel_id=1, source_target_pairs={{1,2},{2,1},{3,4},{4,3},{5,6},{6,5},{7,8},{8,7},{9,10},{10,9},{11,... | collective-permute-start | bytes 393224 | tf_op jit(solution)/shard_map/ppermute | solution.py:51
  (20 other events, 98.3 us)
Sparse Core Ops, SparseCore 0:
  9.1 44.4 all-gather.2

commit v10 on v9

--- a/solution.py
+++ b/solution.py
@@ -256,7 +256,8 @@
 
 
 def norm_kernel(core_ref, chip_ref, mid_token, mid_grad, count_ref, gain_ref, *refs):
-    mine_ref, theirs_ref, normin_ref, normed_ref, rms_ref, dout_ref, pair_ref = refs
+    mine_ref, theirs_ref = refs[:2]
+    normin_ref, normed_ref, rms_ref, dout_ref, pair_ref = refs[-5:]
     width = mid_token.shape[1]
     rows = mine_ref.shape[0]
     pair_ref[:rows, :] = mine_ref[...]
@@ -271,7 +272,7 @@
     dout_ref[...] = mid_grad[...] + got[:, width:]
 
 
-def norm(from_core, from_chip, mid_token, mid_grad, count, gain, mine, theirs):
+def norm(from_core, from_chip, mid_token, mid_grad, count, gain, mine, theirs, ready):
     seg, width = mid_token.shape
     shape = jax.ShapeDtypeStruct
     return pl.pallas_call(
@@ -283,13 +284,13 @@
             shape((seg, width), F32),
             shape((2 * mine.shape[0], mine.shape[1]), mine.dtype),
         ),
-        in_specs=[VMEM] * 8,
+        in_specs=[VMEM] * 8 + [ANY],
         out_specs=(VMEM,) * 5,
         compiler_params=room(8),
-    )(from_core, from_chip, mid_token, mid_grad, count, gain, mine, theirs)
-
-
-def dout_kernel(dout_ref, second_ref, ready_ref, full_ref, half_ref):
+    )(from_core, from_chip, mid_token, mid_grad, count, gain, mine, theirs, ready)
+
+
+def dout_kernel(dout_ref, second_ref, full_ref, half_ref):
     seg = dout_ref.shape[0]
     last = lax.broadcasted_iota(jnp.int32, (seg, 1), 0) == seg - 1
     dout = dout_ref[...] + jnp.where(last, second_ref[...], 0.0)
@@ -297,15 +298,15 @@
     half_ref[...] = dout.astype(jnp.bfloat16)
 
 
-def whole_dout(dout, second, ready):
+def whole_dout(dout, second):
     shape = jax.ShapeDtypeStruct
     return pl.pallas_call(
         dout_kernel,
         out_shape=(shape(dout.shape, F32), shape(dout.shape, jnp.bfloat16)),
-        in_specs=[VMEM, VMEM, ANY],
+        in_specs=[VMEM, VMEM],
         out_specs=(VMEM, VMEM),
         compiler_params=room(4),
-    )(dout, second, ready)
+    )(dout, second)
 
 
 def dattended_kernel(own_ref, other_ref, weight_ref, ready_ref, *refs):
@@ -540,14 +541,23 @@
     count = (ends - opens)[seg : 2 * seg, None].astype(F32)
     second = two_back(first)
     normin, normed, rms, dout, both = norm(
-        other_core(to_core), other_chip(to_chip), mid_token, mid_grad, count, gain[None], mine, theirs
+        other_core(to_core),
+        other_chip(to_chip),
+        mid_token,
+        mid_grad,
+        count,
+        gain[None],
+        mine,
+        theirs,
+        second,
     )
     weights = [both, shifted_y(both, 1), shifted_y(both, -1), shifted_y(both, 2)]
-    pieces = gathered_rows(normin, weights[1:3], weights[3:])
+    dout, dout_b = whole_dout(dout, second)
+    dout_there = other_core(dout_b)
+    pieces = gathered_rows(normin, weights[1:3] + [dout_there], weights[3:])
     q, own, w_full = project(pieces, weights)
     cross, far, beside = across(own, 0, True), across(own, 0, False), other_pair(own)
-    dout, dout_b = whole_dout(dout, second, pieces[2])
-    da = dattended(dout_b, other_core(dout_b), halves, beside)
+    da = dattended(dout_b, dout_there, halves, q)
     da_here = [da[0]] + [
         moved(da[i], lambda h, t, p, k, i=i: (h, t + i, p, k)) for i in range(1, TURNS)
     ]

time: 149 us -> 141 us (0.946)
  waiting for transfers between devices: 50.5 us -> 46.7 us
  starting transfers between devices: 62.2 us -> 59.3 us
    ppermute x1, starting transfers between devices: 6.68 us -> 2.28 us  [two_back(): lax.ppermute(value, 'ctx', [(i, i - CORES) for i in range(CORES, CTX)])]
    ppermute x28, starting transfers between devices: 27.4 us -> 31 us  [moved(): return lax.ppermute(value, 'ctx', pairs)]
    ppermute x3, starting transfers between devices: 23.5 us -> 20.5 us  [other_chip(): return lax.ppermute(value, 'ctx', pairs)]
    ppermute x3, waiting for transfers between devices: 2.49 us -> 0.15 us  [shifted_y(): return lax.ppermute(value, 'dp', pairs)]
    ppermute x3, waiting for transfers between devices: 8.73 us -> 6.53 us  [other_chip(): return lax.ppermute(value, 'ctx', pairs)]
    ppermute x1, waiting for transfers between devices: 1.31 us -> 3.07 us  [two_back(): lax.ppermute(value, 'ctx', [(i, i - CORES) for i in range(CORES, CTX)])]
  transfers between devices with their start and end apart: 37 -> 37, of which waited for: 19 -> 20; matrix products, arithmetic and copies ran while one was open for 0% -> 0% of each run, Pallas kernels for 5% -> 5%
where the time goes in v10:
time: 141 us; the launch traced here: 140 us
  starting transfers between devices  59.3 us (42%)
  waiting for transfers between devices  46.7 us (33%)
  Pallas kernels  14.6 us (10%)
  between operations  13.8 us (10%)
  local copies, waits for them, and re-layouts  3.22 us (2%)
  matrix products  1.46 us (1%)
    ppermute x28, waiting for transfers between devices, moved(): return lax.ppermute(value, 'ctx', pairs)  36.9 us
    ppermute x28, starting transfers between devices, moved(): return lax.ppermute(value, 'ctx', pairs)  31 us
    ppermute x3, starting transfers between devices, other_chip(): return lax.ppermute(value, 'ctx', pairs)  20.5 us
    ppermute x3, waiting for transfers between devices, other_chip(): return lax.ppermute(value, 'ctx', pairs)  6.53 us
    ppermute x3, starting transfers between devices, shifted_y(): return lax.ppermute(value, 'dp', pairs)  5.35 us
    pallas_call x1, Pallas kernels, attention(): pl.pallas_call(functools.partial(attention_kernel, 256, seg), out_shape=(...  4.48 us
    pallas_call x1, Pallas kernels, project(): pl.pallas_call(project_kernel, out_shape=(bf16(rows, HEAD), bf16(rows, 2...  3.37 us
    unnamed x14, local copies, waits for them, and re-layouts  3.12 us
  transfers between devices with their start and end apart: 37, of which 20 were waited for; matrix products, arithmetic and copies ran while one was open for 0% of the time, Pallas kernels for 5%

profile of v10, /device:TPU:6, one launch (start us, length us, event | category | flops | bytes accessed | tf_op | source)
XLA Modules:
  0.0 139.8 jit_solution(14028601020949017455)
XLA Ops:
  8.4 8.7 %collective-permute-start = (s32[1,64]{1,0:T(1,128)}, s32[1,64]{1,0:T(1,128)S(1)}, u32[]{:S(2)}, u32[]{:S(2)}) collective-permute-start(s32[1,64]{1,0:T(1,128)} %get-tuple-element.41.own_ref), channel_id=1, source_target_pairs={{1,2},{2,1},{3,4},{4,3},{5,6},{6,5},{7,8},{8,7},{9,10},{10,9},{11,... | collective-permute-start | bytes 776 | tf_op jit(solution)/shard_map/ppermute | solution.py:51
  22.2 7.1 %collective-permute-start.3 = (bf16[64,2048]{1,0:T(8,128)(2,1)S(1)}, bf16[64,2048]{1,0:T(8,128)(2,1)S(1)}, u32[]{:S(2)}, u32[]{:S(2)}) collective-permute-start(bf16[64,2048]{1,0:T(8,128)(2,1)S(1)} %get-tuple-element.43), channel_id=1, source_target_pairs={{1,2},{2,1},{3,4},{4,3},{5,6},{6,5},{7,8},{8,7},{9,10},{10,9},{11,... | collective-permute-start | bytes 786440 | tf_op jit(solution)/shard_map/ppermute | solution.py:51
  29.5 2.3 %collective-permute-start.5 = (f32[1,1024]{1,0:T(1,128)S(1)}, f32[1,1024]{1,0:T(1,128)S(1)}, u32[]{:S(2)}, u32[]{:S(2)}) collective-permute-start(f32[1,1024]{1,0:T(1,128)S(1)} %get-tuple-element.47), channel_id=1, source_target_pairs={{2,0},{3,1},{4,2},{5,3},{6,4},{7,5},{8,6},{9,7},{10,8},{11,9},{12,... | collective-permute-start | bytes 12296 | tf_op jit(solution)/shard_map/ppermute | solution.py:55
  32.0 3.1 %collective-permute-done.5.refs_2_.second_ref = f32[1,1024]{1,0:T(1,128)S(1)} collective-permute-done((f32[1,1024]{1,0:T(1,128)S(1)}, f32[1,1024]{1,0:T(1,128)S(1)}, u32[]{:S(2)}, u32[]{:S(2)}) %collective-permute-start.5) | collective-permute-done | bytes 4128 | tf_op jit(solution)/shard_map/ppermute | solution.py:55
  38.8 2.0 %collective-permute-start.15 = (bf16[256,384]{1,0:T(8,128)(2,1)S(1)}, bf16[256,384]{1,0:T(8,128)(2,1)S(1)}, u32[]{:S(2)}, u32[]{:S(2)}) collective-permute-start(bf16[256,384]{1,0:T(8,128)(2,1)S(1)} %get-tuple-element.51.refs_8_), channel_id=1, source_target_pairs={{0,64},{32,96},{64,0},{96,32},{128,192},{160,224},{192,128},{224,1... | collective-permute-start | bytes 589832 | tf_op jit(solution)/shard_map/ppermute | solution.py:125
  40.8 4.9 %collective-permute-done.7.refs_0_.value_ref.refs_2_ = bf16[64,1024]{1,0:T(8,128)(2,1)S(1)} collective-permute-done((bf16[64,1024]{1,0:T(8,128)(2,1)S(1)}, bf16[64,1024]{1,0:T(8,128)(2,1)S(1)}, u32[]{:S(2)}, u32[]{:S(2)}) %collective-permute-start.7) | collective-permute-done | bytes 131104 | tf_op jit(solution)/shard_map/ppermute | solution.py:46
  46.1 3.8 %collective-permute-start.6 = (bf16[64,1024]{1,0:T(8,128)(2,1)S(1)}, bf16[64,1024]{1,0:T(8,128)(2,1)S(1)}, u32[]{:S(2)}, u32[]{:S(2)}) collective-permute-start(bf16[64,1024]{1,0:T(8,128)(2,1)S(1)} %get-tuple-element.50.value_ref.refs_0_), channel_id=1, source_target_pairs={{0,1},{1,0},{2,3},{3,2},{4,5},{5,4},{6,7},{7,6},{8,9},{9,8},{10,11... | collective-permute-start | bytes 393224 | tf_op jit(solution)/shard_map/ppermute | solution.py:46
  49.9 3.1 %collective-permute-done.8.refs_3_ = bf16[64,1024]{1,0:T(8,128)(2,1)S(1)} collective-permute-done((bf16[64,1024]{1,0:T(8,128)(2,1)S(1)}, bf16[64,1024]{1,0:T(8,128)(2,1)S(1)}, u32[]{:S(2)}, u32[]{:S(2)}) %collective-permute-start.8) | collective-permute-done | bytes 131104 | tf_op jit(solution)/shard_map/ppermute | solution.py:46
  55.2 3.4 %shard_map.89 = (bf16[512,128]{1,0:T(8,128)(2,1)S(1)}, bf16[512,256]{1,0:T(8,128)(2,1)S(1)}, bf16[1024,384]{1,0:T(8,128)(2,1)S(1)}) custom-call(bf16[64,1024]{1,0:T(8,128)(2,1)S(1)} %get-tuple-element.50.value_ref.refs_0_, bf16[64,1024]{1,0:T(8,128)(2,1)S(1)} %collective-permute-done.6.refs_1_, ...), custom_call_target="tpu_custom_call" | custom-call | tf_op jit(solution)/shard_map/pallas_call | solution.py:365
  58.6 3.0 %collective-permute-start.24 = (bf16[512,256]{1,0:T(8,128)(2,1)S(1)}, bf16[512,256]{1,0:T(8,128)(2,1)S(1)}, u32[]{:S(2)}, u32[]{:S(2)}) collective-permute-start(bf16[512,256]{1,0:T(8,128)(2,1)S(1)} %get-tuple-element.59.refs_9_), channel_id=1, source_target_pairs={{0,2},{1,3},{2,0},{3,1},{4,6},{5,7},{6,4},{7,5},{8,10},{9,11},{10,... | collective-permute-start | bytes 786440 | tf_op jit(solution)/shard_map/ppermute | solution.py:46
  65.6 2.2 %shard_map.90 = (bf16[128,128]{1,0:T(8,128)(2,1)S(1)}, bf16[128,128]{1,0:T(8,128)(2,1)S(1)}, bf16[128,128]{1,0:T(8,128)(2,1)S(1)}, bf16[128,128]{1,0:T(8,128)(2,1)S(1)}) custom-call(bf16[64,1024]{1,0:T(8,128)(2,1)S(1)} %get-tuple-element.52.own_ref, bf16[64,1024]{1,0:T(8,128)(2,1)S(1)} %collective-permute-done.13.refs_2_.other_ref, ...), custom_call_target="tpu_custom_call" | custom-call | tf_op jit(solution)/shard_map/pallas_call | solution.py:328
  67.9 2.8 %collective-permute-start.18 = (bf16[128,128]{1,0:T(8,128)(2,1)S(1)}, bf16[128,128]{1,0:T(8,128)(2,1)S(1)}, u32[]{:S(2)}, u32[]{:S(2)}) collective-permute-start(bf16[128,128]{1,0:T(8,128)(2,1)S(1)} %get-tuple-element.57), channel_id=1, source_target_pairs={{0,8},{1,9},{2,10},{3,11},{4,12},{5,13},{6,14},{7,15},{8,0},{9,1},... | collective-permute-start | bytes 98312 | tf_op jit(solution)/shard_map/ppermute | solution.py:46
  70.7 3.5 %collective-permute-start.19 = (bf16[128,128]{1,0:T(8,128)(2,1)S(1)}, bf16[128,128]{1,0:T(8,128)(2,1)S(1)}, u32[]{:S(2)}, u32[]{:S(2)}) collective-permute-start(bf16[128,128]{1,0:T(8,128)(2,1)S(1)} %get-tuple-element.58), channel_id=1, source_target_pairs={{0,12},{1,13},{2,14},{3,15},{4,0},{5,1},{6,2},{7,3},{8,4},{9,5},{1... | collective-permute-start | bytes 98312 | tf_op jit(solution)/shard_map/ppermute | solution.py:46
  74.2 4.5 %collective-permute-done.25.refs_11_ = bf16[512,256]{1,0:T(8,128)(2,1)S(1)} collective-permute-done((bf16[512,256]{1,0:T(8,128)(2,1)S(1)}, bf16[512,256]{1,0:T(8,128)(2,1)S(1)}, u32[]{:S(2)}, u32[]{:S(2)}) %collective-permute-start.25) | collective-permute-done | bytes 262176 | tf_op jit(solution)/shard_map/ppermute | solution.py:46
  80.6 4.5 %shard_map.91 = (bf16[512,128]{1,0:T(8,128)(2,1)S(1)}, bf16[512,256]{1,0:T(8,128)(2,1)S(1)}, bf16[512,256]{1,0:T(8,128)(2,1)S(1)}, bf16[512,256]{1,0:T(8,128)(2,1)S(1)}, bf16[512,256]{1,0:T(8,128)(2,1)S(1)}) custom-call(bf16[512,128]{1,0:T(8,128)(2,1)S(1)} %get-tuple-element.53.ready_ref.refs_0_, bf16[128,128]{1,0:T(8,128)(2,1)S(1)} %get-tuple-element.55.refs_1_, ...), custom_call_target="tpu_custom_call" | custom-call | flops 1610612736 | bytes 2490368 | tf_op jit(solution)/shard_map/pallas_call | solution.py:447
  85.2 4.8 %collective-permute-start.28 = (bf16[512,256]{1,0:T(8,128)(2,1)S(1)}, bf16[512,256]{1,0:T(8,128)(2,1)S(1)}, u32[]{:S(2)}, u32[]{:S(2)}) collective-permute-start(bf16[512,256]{1,0:T(8,128)(2,1)S(1)} %get-tuple-element.63), channel_id=1, source_target_pairs={{16,0},{17,1},{18,2},{19,3},{20,4},{21,5},{22,6},{23,7},{24,8},{25... | collective-permute-start | bytes 786440 | tf_op jit(solution)/shard_map/ppermute | solution.py:46
  90.0 2.4 %collective-permute-start.29 = (bf16[512,256]{1,0:T(8,128)(2,1)S(1)}, bf16[512,256]{1,0:T(8,128)(2,1)S(1)}, u32[]{:S(2)}, u32[]{:S(2)}) collective-permute-start(bf16[512,256]{1,0:T(8,128)(2,1)S(1)} %get-tuple-element.64), channel_id=1, source_target_pairs={{16,2},{17,3},{18,0},{19,1},{20,6},{21,7},{22,4},{23,5},{24,10},{2... | collective-permute-start | bytes 786440 | tf_op jit(solution)/shard_map/ppermute | solution.py:46
  93.9 7.3 %collective-permute-done.28.refs_2_ = bf16[512,256]{1,0:T(8,128)(2,1)S(1)} collective-permute-done((bf16[512,256]{1,0:T(8,128)(2,1)S(1)}, bf16[512,256]{1,0:T(8,128)(2,1)S(1)}, u32[]{:S(2)}, u32[]{:S(2)}) %collective-permute-start.28) | collective-permute-done | bytes 262176 | tf_op jit(solution)/shard_map/ppermute | solution.py:46
  102.0 1.9 %collective-permute-done.30.swapped = bf16[256,1024]{1,0:T(8,128)(2,1)S(1)} collective-permute-done((bf16[256,1024]{1,0:T(8,128)(2,1)S(1)}, bf16[256,1024]{1,0:T(8,128)(2,1)S(1)}, u32[]{:S(2)}, u32[]{:S(2)}) %collective-permute-start.30) | collective-permute-done | bytes 524320 | tf_op jit(solution)/shard_map/ppermute | solution.py:46
  104.0 4.2 %collective-permute-start.32 = (bf16[64,1024]{1,0:T(8,128)(2,1)S(1)}, bf16[64,1024]{1,0:T(8,128)(2,1)S(1)}, u32[]{:S(2)}, u32[]{:S(2)}) collective-permute-start(bf16[64,1024]{1,0:T(8,128)(2,1)S(1)} %get-tuple-element.74), channel_id=1, source_target_pairs={{0,12},{1,5},{2,14},{3,7},{4,0},{5,9},{6,2},{7,11},{8,4},{9,13},{1... | collective-permute-start | bytes 393224 | tf_op jit(solution)/shard_map/ppermute | solution.py:46
  108.3 5.4 %collective-permute-done.32 = bf16[64,1024]{1,0:T(8,128)(2,1)S(1)} collective-permute-done((bf16[64,1024]{1,0:T(8,128)(2,1)S(1)}, bf16[64,1024]{1,0:T(8,128)(2,1)S(1)}, u32[]{:S(2)}, u32[]{:S(2)}) %collective-permute-start.32) | collective-permute-done | bytes 131104 | tf_op jit(solution)/shard_map/ppermute | solution.py:46
  117.5 3.6 %collective-permute-done.33 = bf16[64,1024]{1,0:T(8,128)(2,1)S(1)} collective-permute-done((bf16[64,1024]{1,0:T(8,128)(2,1)S(1)}, bf16[64,1024]{1,0:T(8,128)(2,1)S(1)}, u32[]{:S(2)}, u32[]{:S(2)}) %collective-permute-start.33) | collective-permute-done | bytes 131104 | tf_op jit(solution)/shard_map/ppermute | solution.py:46
  121.4 4.7 %collective-permute-start.34 = (bf16[64,1024]{1,0:T(8,128)(2,1)S(1)}, bf16[64,1024]{1,0:T(8,128)(2,1)S(1)}, u32[]{:S(2)}, u32[]{:S(2)}) collective-permute-start(bf16[64,1024]{1,0:T(8,128)(2,1)S(1)} %divide_convert_fusion), channel_id=1, source_target_pairs={{1,2},{2,1},{3,4},{4,3},{5,6},{6,5},{7,8},{8,7},{9,10},{10,9},{11,... | collective-permute-start | bytes 393224 | tf_op jit(solution)/shard_map/ppermute | solution.py:51
  126.2 5.2 %collective-permute-done.34 = bf16[64,1024]{1,0:T(8,128)(2,1)S(1)} collective-permute-done((bf16[64,1024]{1,0:T(8,128)(2,1)S(1)}, bf16[64,1024]{1,0:T(8,128)(2,1)S(1)}, u32[]{:S(2)}, u32[]{:S(2)}) %collective-permute-start.34) | collective-permute-done | bytes 131104 | tf_op jit(solution)/shard_map/ppermute | solution.py:51
  (90 shorter events, 27.7 us)
Async XLA Ops:
  6.5 57.8 %all-gather.3.cloned.1.call-start = ((), (), s32[]{:S(2)}) async-start(), calls=%async_computation | async-start | bytes 1179648 | tf_op jit(solution)/shard_map/all_gather | solution.py:129
  8.3 8.9 %collective-permute-start.1 = (s32[1,64]{1,0:T(1,128)}, s32[1,64]{1,0:T(1,128)S(1)}, u32[]{:S(2)}, u32[]{:S(2)}) collective-permute-start(s32[1,64]{1,0:T(1,128)} %get-tuple-element.41.own_ref), channel_id=1, source_target_pairs={{0,1},{1,0},{2,3},{3,2},{4,5},{5,4},{6,7},{7,6},{8,9},{9,8},{10,11... | collective-permute-start | bytes 776 | tf_op jit(solution)/shard_map/ppermute | solution.py:46
  8.4 10.1 %collective-permute-start = (s32[1,64]{1,0:T(1,128)}, s32[1,64]{1,0:T(1,128)S(1)}, u32[]{:S(2)}, u32[]{:S(2)}) collective-permute-start(s32[1,64]{1,0:T(1,128)} %get-tuple-element.41.own_ref), channel_id=1, source_target_pairs={{1,2},{2,1},{3,4},{4,3},{5,6},{6,5},{7,8},{8,7},{9,10},{10,9},{11,... | collective-permute-start | bytes 776 | tf_op jit(solution)/shard_map/ppermute | solution.py:51
  17.1 17.9 %collective-permute-start.4 = (bf16[128,384]{1,0:T(8,128)(2,1)}, bf16[128,384]{1,0:T(8,128)(2,1)S(1)}, u32[]{:S(2)}, u32[]{:S(2)}) collective-permute-start(bf16[128,384]{1,0:T(8,128)(2,1)} %get-tuple-element.46.refs_0_), channel_id=1, source_target_pairs={{0,128},{32,160},{64,192},{96,224},{128,0},{160,32},{192,64},{224,... | collective-permute-start | bytes 294920 | tf_op jit(solution)/shard_map/ppermute | solution.py:120
  22.1 12.9 %collective-permute-start.2 = (bf16[64,2048]{1,0:T(8,128)(2,1)S(1)}, bf16[64,2048]{1,0:T(8,128)(2,1)S(1)}, u32[]{:S(2)}, u32[]{:S(2)}) collective-permute-start(bf16[64,2048]{1,0:T(8,128)(2,1)S(1)} %get-tuple-element.42), channel_id=1, source_target_pairs={{0,1},{1,0},{2,3},{3,2},{4,5},{5,4},{6,7},{7,6},{8,9},{9,8},{10,11... | collective-permute-start | bytes 786440 | tf_op jit(solution)/shard_map/ppermute | solution.py:46
  22.2 12.8 %collective-permute-start.3 = (bf16[64,2048]{1,0:T(8,128)(2,1)S(1)}, bf16[64,2048]{1,0:T(8,128)(2,1)S(1)}, u32[]{:S(2)}, u32[]{:S(2)}) collective-permute-start(bf16[64,2048]{1,0:T(8,128)(2,1)S(1)} %get-tuple-element.43), channel_id=1, source_target_pairs={{1,2},{2,1},{3,4},{4,3},{5,6},{6,5},{7,8},{8,7},{9,10},{10,9},{11,... | collective-permute-start | bytes 786440 | tf_op jit(solution)/shard_map/ppermute | solution.py:51
  35.3 10.5 %collective-permute-start.11 = (bf16[256,384]{1,0:T(8,128)(2,1)S(1)}, bf16[256,384]{1,0:T(8,128)(2,1)S(1)}, u32[]{:S(2)}, u32[]{:S(2)}) collective-permute-start(bf16[256,384]{1,0:T(8,128)(2,1)S(1)} %get-tuple-element.51.refs_8_), channel_id=1, source_target_pairs={{0,32},{32,64},{64,96},{96,0},{128,160},{160,192},{192,224},{224,1... | collective-permute-start | bytes 589832 | tf_op jit(solution)/shard_map/ppermute | solution.py:125
  37.0 9.1 %collective-permute-start.12 = (bf16[256,384]{1,0:T(8,128)(2,1)S(1)}, bf16[256,384]{1,0:T(8,128)(2,1)S(1)}, u32[]{:S(2)}, u32[]{:S(2)}) collective-permute-start(bf16[256,384]{1,0:T(8,128)(2,1)S(1)} %get-tuple-element.51.refs_8_), channel_id=1, source_target_pairs={{0,96},{32,0},{64,32},{96,64},{128,224},{160,128},{192,160},{224,1... | collective-permute-start | bytes 589832 | tf_op jit(solution)/shard_map/ppermute | solution.py:125
  38.8 14.2 %collective-permute-start.15 = (bf16[256,384]{1,0:T(8,128)(2,1)S(1)}, bf16[256,384]{1,0:T(8,128)(2,1)S(1)}, u32[]{:S(2)}, u32[]{:S(2)}) collective-permute-start(bf16[256,384]{1,0:T(8,128)(2,1)S(1)} %get-tuple-element.51.refs_8_), channel_id=1, source_target_pairs={{0,64},{32,96},{64,0},{96,32},{128,192},{160,224},{192,128},{224,1... | collective-permute-start | bytes 589832 | tf_op jit(solution)/shard_map/ppermute | solution.py:125
  46.0 7.8 %collective-permute-start.14 = (bf16[64,1024]{1,0:T(8,128)(2,1)S(1)}, bf16[64,1024]{1,0:T(8,128)(2,1)S(1)}, u32[]{:S(2)}, u32[]{:S(2)}) collective-permute-start(bf16[64,1024]{1,0:T(8,128)(2,1)S(1)} %shard_map.87), channel_id=1, source_target_pairs={{0,4},{1,13},{2,6},{3,15},{4,8},{5,1},{6,10},{7,3},{8,12},{9,5},{1... | collective-permute-start | bytes 393224 | tf_op jit(solution)/shard_map/ppermute | solution.py:46
  46.1 7.8 %collective-permute-start.6 = (bf16[64,1024]{1,0:T(8,128)(2,1)S(1)}, bf16[64,1024]{1,0:T(8,128)(2,1)S(1)}, u32[]{:S(2)}, u32[]{:S(2)}) collective-permute-start(bf16[64,1024]{1,0:T(8,128)(2,1)S(1)} %get-tuple-element.50.value_ref.refs_0_), channel_id=1, source_target_pairs={{0,1},{1,0},{2,3},{3,2},{4,5},{5,4},{6,7},{7,6},{8,9},{9,8},{10,11... | collective-permute-start | bytes 393224 | tf_op jit(solution)/shard_map/ppermute | solution.py:46
  58.6 12.1 %collective-permute-start.24 = (bf16[512,256]{1,0:T(8,128)(2,1)S(1)}, bf16[512,256]{1,0:T(8,128)(2,1)S(1)}, u32[]{:S(2)}, u32[]{:S(2)}) collective-permute-start(bf16[512,256]{1,0:T(8,128)(2,1)S(1)} %get-tuple-element.59.refs_9_), channel_id=1, source_target_pairs={{0,2},{1,3},{2,0},{3,1},{4,6},{5,7},{6,4},{7,5},{8,10},{9,11},{10,... | collective-permute-start | bytes 786440 | tf_op jit(solution)/shard_map/ppermute | solution.py:46
  61.6 17.1 %collective-permute-start.25 = (bf16[512,256]{1,0:T(8,128)(2,1)S(1)}, bf16[512,256]{1,0:T(8,128)(2,1)S(1)}, u32[]{:S(2)}, u32[]{:S(2)}) collective-permute-start(bf16[512,256]{1,0:T(8,128)(2,1)S(1)} %get-tuple-element.59.refs_9_), channel_id=1, source_target_pairs={{0,16},{1,17},{2,18},{3,19},{4,20},{5,21},{6,22},{7,23},{8,24},{9,... | collective-permute-start | bytes 786440 | tf_op jit(solution)/shard_map/ppermute | solution.py:46
  62.9 16.8 %collective-permute-start.26 = (bf16[512,256]{1,0:T(8,128)(2,1)S(1)}, bf16[512,256]{1,0:T(8,128)(2,1)S(1)}, u32[]{:S(2)}, u32[]{:S(2)}) collective-permute-start(bf16[512,256]{1,0:T(8,128)(2,1)S(1)} %get-tuple-element.59.refs_9_), channel_id=1, source_target_pairs={{0,18},{1,19},{2,16},{3,17},{4,22},{5,23},{6,20},{7,21},{8,26},{9,... | collective-permute-start | bytes 786440 | tf_op jit(solution)/shard_map/ppermute | solution.py:46
  67.8 10.8 %collective-permute-start.17 = (bf16[128,128]{1,0:T(8,128)(2,1)S(1)}, bf16[128,128]{1,0:T(8,128)(2,1)S(1)}, u32[]{:S(2)}, u32[]{:S(2)}) collective-permute-start(bf16[128,128]{1,0:T(8,128)(2,1)S(1)} %get-tuple-element.56), channel_id=1, source_target_pairs={{0,4},{1,5},{2,6},{3,7},{4,8},{5,9},{6,10},{7,11},{8,12},{9,13},{1... | collective-permute-start | bytes 98312 | tf_op jit(solution)/shard_map/ppermute | solution.py:46
  67.9 11.3 %collective-permute-start.18 = (bf16[128,128]{1,0:T(8,128)(2,1)S(1)}, bf16[128,128]{1,0:T(8,128)(2,1)S(1)}, u32[]{:S(2)}, u32[]{:S(2)}) collective-permute-start(bf16[128,128]{1,0:T(8,128)(2,1)S(1)} %get-tuple-element.57), channel_id=1, source_target_pairs={{0,8},{1,9},{2,10},{3,11},{4,12},{5,13},{6,14},{7,15},{8,0},{9,1},... | collective-permute-start | bytes 98312 | tf_op jit(solution)/shard_map/ppermute | solution.py:46
  70.7 8.6 %collective-permute-start.19 = (bf16[128,128]{1,0:T(8,128)(2,1)S(1)}, bf16[128,128]{1,0:T(8,128)(2,1)S(1)}, u32[]{:S(2)}, u32[]{:S(2)}) collective-permute-start(bf16[128,128]{1,0:T(8,128)(2,1)S(1)} %get-tuple-element.58), channel_id=1, source_target_pairs={{0,12},{1,13},{2,14},{3,15},{4,0},{5,1},{6,2},{7,3},{8,4},{9,5},{1... | collective-permute-start | bytes 98312 | tf_op jit(solution)/shard_map/ppermute | solution.py:46
  85.1 8.9 %collective-permute-start.27 = (bf16[512,256]{1,0:T(8,128)(2,1)S(1)}, bf16[512,256]{1,0:T(8,128)(2,1)S(1)}, u32[]{:S(2)}, u32[]{:S(2)}) collective-permute-start(bf16[512,256]{1,0:T(8,128)(2,1)S(1)} %get-tuple-element.62), channel_id=1, source_target_pairs={{0,2},{1,3},{2,0},{3,1},{4,6},{5,7},{6,4},{7,5},{8,10},{9,11},{10,... | collective-permute-start | bytes 786440 | tf_op jit(solution)/shard_map/ppermute | solution.py:46
  85.2 16.0 %collective-permute-start.28 = (bf16[512,256]{1,0:T(8,128)(2,1)S(1)}, bf16[512,256]{1,0:T(8,128)(2,1)S(1)}, u32[]{:S(2)}, u32[]{:S(2)}) collective-permute-start(bf16[512,256]{1,0:T(8,128)(2,1)S(1)} %get-tuple-element.63), channel_id=1, source_target_pairs={{16,0},{17,1},{18,2},{19,3},{20,4},{21,5},{22,6},{23,7},{24,8},{25... | collective-permute-start | bytes 786440 | tf_op jit(solution)/shard_map/ppermute | solution.py:46
  90.0 11.2 %collective-permute-start.29 = (bf16[512,256]{1,0:T(8,128)(2,1)S(1)}, bf16[512,256]{1,0:T(8,128)(2,1)S(1)}, u32[]{:S(2)}, u32[]{:S(2)}) collective-permute-start(bf16[512,256]{1,0:T(8,128)(2,1)S(1)} %get-tuple-element.64), channel_id=1, source_target_pairs={{16,2},{17,3},{18,0},{19,1},{20,6},{21,7},{22,4},{23,5},{24,10},{2... | collective-permute-start | bytes 786440 | tf_op jit(solution)/shard_map/ppermute | solution.py:46
  104.0 9.6 %collective-permute-start.32 = (bf16[64,1024]{1,0:T(8,128)(2,1)S(1)}, bf16[64,1024]{1,0:T(8,128)(2,1)S(1)}, u32[]{:S(2)}, u32[]{:S(2)}) collective-permute-start(bf16[64,1024]{1,0:T(8,128)(2,1)S(1)} %get-tuple-element.74), channel_id=1, source_target_pairs={{0,12},{1,5},{2,14},{3,7},{4,0},{5,9},{6,2},{7,11},{8,4},{9,13},{1... | collective-permute-start | bytes 393224 | tf_op jit(solution)/shard_map/ppermute | solution.py:46
  108.3 9.2 %collective-permute-start.31 = (bf16[64,1024]{1,0:T(8,128)(2,1)S(1)}, bf16[64,1024]{1,0:T(8,128)(2,1)S(1)}, u32[]{:S(2)}, u32[]{:S(2)}) collective-permute-start(bf16[64,1024]{1,0:T(8,128)(2,1)S(1)} %get-tuple-element.72), channel_id=1, source_target_pairs={{0,13},{1,4},{2,15},{3,6},{4,1},{5,8},{6,3},{7,10},{8,5},{9,12},{1... | collective-permute-start | bytes 393224 | tf_op jit(solution)/shard_map/ppermute | solution.py:46
  113.7 7.4 %collective-permute-start.33 = (bf16[64,1024]{1,0:T(8,128)(2,1)S(1)}, bf16[64,1024]{1,0:T(8,128)(2,1)S(1)}, u32[]{:S(2)}, u32[]{:S(2)}) collective-permute-start(bf16[64,1024]{1,0:T(8,128)(2,1)S(1)} %add_convert_fusion.1), channel_id=1, source_target_pairs={{0,12},{1,5},{2,14},{3,7},{4,0},{5,9},{6,2},{7,11},{8,4},{9,13},{1... | collective-permute-start | bytes 393224 | tf_op jit(solution)/shard_map/ppermute | solution.py:46
  121.4 10.0 %collective-permute-start.34 = (bf16[64,1024]{1,0:T(8,128)(2,1)S(1)}, bf16[64,1024]{1,0:T(8,128)(2,1)S(1)}, u32[]{:S(2)}, u32[]{:S(2)}) collective-permute-start(bf16[64,1024]{1,0:T(8,128)(2,1)S(1)} %divide_convert_fusion), channel_id=1, source_target_pairs={{1,2},{2,1},{3,4},{4,3},{5,6},{6,5},{7,8},{8,7},{9,10},{10,9},{11,... | collective-permute-start | bytes 393224 | tf_op jit(solution)/shard_map/ppermute | solution.py:51
  (20 other events, 100.8 us)
Sparse Core Ops, SparseCore 0:
  9.1 44.2 all-gather.2

commit v11 on v10

--- a/solution.py
+++ b/solution.py
@@ -61,6 +61,10 @@
 
 def other_pair(value):
     return moved(value, lambda h, t, p, k: (h, t, 1 - p, k))
+
+
+def later_pair(value):
+    return moved(value, lambda h, t, p, k: (h, t, 1 - p, k) if h == 1 else None)
 
 
 def across(value, source, cross):
@@ -179,12 +183,11 @@
         copy.wait()
 
 
-def stacked(pieces, out_ref):
-    copies, at = [], 0
+def fill(out_ref, pieces):
+    at = 0
     for piece in pieces:
-        copies.append((piece, out_ref.at[at : at + piece.shape[0], :]))
+        out_ref[at : at + piece.shape[0], :] = piece[...]
         at += piece.shape[0]
-    return copies
 
 
 def window_kernel(own_ref, beside_ref, facing_ref, token_hbm, grad_hbm, *refs):
@@ -312,9 +315,10 @@
 def dattended_kernel(own_ref, other_ref, weight_ref, ready_ref, *refs):
     outs, rows, weight, sems = refs[:TURNS], *refs[TURNS:]
     heads, half = weight_ref.shape[:2]
-    copies = stacked([own_ref, other_ref], rows)
-    copies += [(weight_ref.at[i], weight.at[i * half : (i + 1) * half, :]) for i in range(heads)]
-    fetched(copies, sems)
+    fill(rows, [own_ref, other_ref])
+    fetched(
+        [(weight_ref.at[i], weight.at[i * half : (i + 1) * half, :]) for i in range(heads)], sems
+    )
     turn = here()[1]
     for step, out in enumerate(outs):
         at = pl.multiple_of((turn + step) % TURNS * CORES * half, CORES * half)
@@ -328,12 +332,12 @@
     return pl.pallas_call(
         dattended_kernel,
         out_shape=(jax.ShapeDtypeStruct((rows, CORES * half), jnp.bfloat16),) * TURNS,
-        in_specs=[ANY] * 4,
+        in_specs=[VMEM, VMEM, ANY, ANY],
         out_specs=(VMEM,) * TURNS,
         scratch_shapes=[
             pltpu.VMEM((rows, width), jnp.bfloat16),
             pltpu.VMEM((heads * half, width), jnp.bfloat16),
-            pltpu.SemaphoreType.DMA((2 + heads,)),
+            pltpu.SemaphoreType.DMA((heads,)),
         ],
         compiler_params=room(12),
     )(own, other, halves, ready)
@@ -341,8 +345,8 @@
 
 def project_kernel(*refs):
     pieces, weights = refs[:8], refs[8:12]
-    q_ref, kv_ref, w_ref, rows, sems = refs[12:]
-    copies = stacked(pieces, rows)
+    q_ref, kv_ref, top_ref, bottom_ref, w_ref, rows = refs[12:]
+    fill(rows, pieces)
     dp = lax.axis_index("dp")
     x, y = dp // ROWS_Y, dp % ROWS_Y
     depth = weights[0].shape[0] // ROWS_X
@@ -351,11 +355,13 @@
         for i in range(ROWS_X):
             its_x = x if i == 0 else 1 - x
             at = pl.multiple_of((its_x * ROWS_Y + its_y) * depth, depth)
-            copies.append((weight.at[i * depth : (i + 1) * depth, :], w_ref.at[pl.ds(at, depth), :]))
-    fetched(copies, sems)
+            w_ref[pl.ds(at, depth), :] = weight[i * depth : (i + 1) * depth, :]
     out = jnp.dot(rows[...], w_ref[...], preferred_element_type=F32).astype(jnp.bfloat16)
+    cut = out.shape[0] // 2
     q_ref[...] = out[:, :HEAD]
     kv_ref[...] = out[:, HEAD:]
+    top_ref[...] = out[:cut, HEAD:]
+    bottom_ref[...] = out[cut:, HEAD:]
 
 
 def project(pieces, weights):
@@ -364,13 +370,16 @@
     bf16 = lambda *shape: jax.ShapeDtypeStruct(shape, jnp.bfloat16)
     return pl.pallas_call(
         project_kernel,
-        out_shape=(bf16(rows, HEAD), bf16(rows, 2 * HEAD), bf16(width, 3 * HEAD)),
-        in_specs=[ANY] * 12,
-        out_specs=(VMEM,) * 3,
-        scratch_shapes=[
-            pltpu.VMEM((rows, width), jnp.bfloat16),
-            pltpu.SemaphoreType.DMA((16,)),
-        ],
+        out_shape=(
+            bf16(rows, HEAD),
+            bf16(rows, 2 * HEAD),
+            bf16(rows // 2, 2 * HEAD),
+            bf16(rows // 2, 2 * HEAD),
+            bf16(width, 3 * HEAD),
+        ),
+        in_specs=[VMEM] * 12,
+        out_specs=(VMEM,) * 5,
+        scratch_shapes=[pltpu.VMEM((rows, width), jnp.bfloat16)],
         compiler_params=room(12),
     )(*pieces, *weights)
 
@@ -388,11 +397,11 @@
 
 
 def attention_kernel(tile, seg, *refs):
-    q_ref, here_refs, there_refs, blocks = refs[0], refs[1:5], refs[5:9], refs[9:13]
-    dq_ref, outs, (kv, da_ref, dkt, dvt, sems) = refs[13], refs[14:18], refs[18:]
+    q_ref, here_refs, there_refs, blocks = refs[0], refs[1:5], refs[5:9], refs[9:15]
+    dq_ref, outs, (kv, da_ref, dkt, dvt) = refs[15], refs[16:22], refs[22:]
     half, turn, pair, core = here()
     queries, keys = q_ref.shape[0], kv.shape[0]
-    fetched(stacked(blocks, kv), sems)
+    fill(kv, blocks)
 
     for which in range(CORES):
 
@@ -433,9 +442,10 @@
         else:
             dkt[...] += dk_part
             dvt[...] += dv_part
-    part = keys // len(outs)
-    for i, out in enumerate(outs):
-        lanes = slice(i * part, (i + 1) * part)
+    at = 0
+    for out in outs:
+        lanes = slice(at, at + out.shape[0])
+        at += out.shape[0]
         out[:, :HEAD] = (dkt[:, lanes] * scale).T.astype(jnp.bfloat16)
         out[:, HEAD:] = dvt[:, lanes].T.astype(jnp.bfloat16)
 
@@ -443,18 +453,17 @@
 def attention(q, da_here, da_there, blocks, seg):
     queries = q.shape[0]
     keys = sum(block.shape[0] for block in blocks)
-    part = jax.ShapeDtypeStruct(blocks[0].shape, jnp.bfloat16)
+    parts = tuple(jax.ShapeDtypeStruct(block.shape, jnp.bfloat16) for block in blocks)
     return pl.pallas_call(
         functools.partial(attention_kernel, 256, seg),
-        out_shape=(jax.ShapeDtypeStruct((queries, HEAD), jnp.bfloat16),) + (part,) * 4,
-        in_specs=[VMEM] * 9 + [ANY] * 4,
-        out_specs=(VMEM,) * 5,
+        out_shape=(jax.ShapeDtypeStruct((queries, HEAD), jnp.bfloat16),) + parts,
+        in_specs=[VMEM] * 15,
+        out_specs=(VMEM,) * 7,
         scratch_shapes=[
             pltpu.VMEM((keys, 2 * HEAD), jnp.bfloat16),
             pltpu.VMEM((queries, HEAD), jnp.bfloat16),
             pltpu.VMEM((HEAD, keys), F32),
             pltpu.VMEM((HEAD, keys), F32),
-            pltpu.SemaphoreType.DMA((4,)),
         ],
         compiler_params=room(36),
         cost_estimate=pl.CostEstimate(
@@ -466,8 +475,10 @@
 
 
 def unproject_kernel(seg, dq_ref, *refs):
-    parts, w_ref, swap_ref, outs = refs[:4], refs[4], refs[5], refs[6:]
-    dkv = sum(ref[...].astype(F32) for ref in parts).astype(jnp.bfloat16)
+    parts, w_ref, swap_ref, outs = refs[:5], refs[5], refs[6], refs[7:]
+    own, beside, far_top, cross_top, far_bottom = (ref[...].astype(F32) for ref in parts)
+    far = jnp.concatenate([far_top + cross_top, far_bottom], axis=0)
+    dkv = (own + beside + far).astype(jnp.bfloat16)
     left = jnp.concatenate([dq_ref[...], dkv], axis=1)
     out = contract_last(left, w_ref[...])
     for i, slot in enumerate((1, 4, 5, 7)):
@@ -482,7 +493,7 @@
         functools.partial(unproject_kernel, seg),
         out_shape=(jax.ShapeDtypeStruct((4 * seg, width), WIRE),)
         + (jax.ShapeDtypeStruct((seg, width), F32),) * 4,
-        in_specs=[VMEM] * 6,
+        in_specs=[VMEM] * 7,
         out_specs=(VMEM,) * 5,
         compiler_params=room(16),
     )(dq, *parts, w_full)
@@ -528,6 +539,7 @@
     halves = gathered_halves(half)
     theirs = other_x(mine)
     beside, facing = other_core(own_starts), other_chip(own_starts)
+    own_starts = starts
     to_core, to_chip, mid_token, mid_grad, first = window_sums(
         own_starts, beside, facing, token_rows, grad_out
     )
@@ -555,16 +567,23 @@
     dout, dout_b = whole_dout(dout, second)
     dout_there = other_core(dout_b)
     pieces = gathered_rows(normin, weights[1:3] + [dout_there], weights[3:])
-    q, own, w_full = project(pieces, weights)
-    cross, far, beside = across(own, 0, True), across(own, 0, False), other_pair(own)
+    q, own, top, bottom, w_full = project(pieces, weights)
+    far_bottom, beside = across(bottom, 0, False), other_pair(own)
+    far_top, cross_top = across(top, 0, False), across(top, 0, True)
+    cross_bottom = later_pair(far_bottom)
     da = dattended(dout_b, dout_there, halves, q)
     da_here = [da[0]] + [
         moved(da[i], lambda h, t, p, k, i=i: (h, t + i, p, k)) for i in range(1, TURNS)
     ]
     da_there = [other_core(piece) for piece in da_here]
-    blocks = (own, beside, far, cross)
-    dq, own, beside, far, cross = attention(q, da_here, da_there, blocks, seg)
-    parts = (own, other_pair(beside), across(far, 1, False), across(cross, 1, True))
+    blocks = (own, beside, far_top, far_bottom, cross_top, cross_bottom)
+    dq, *grads = attention(q, da_here, da_there, blocks, seg)
+    own, beside, far_top, far_bottom, cross_top, cross_bottom = grads
+    passed = later_pair(cross_bottom)
+    beside, far_top, cross_top = other_pair(beside), across(far_top, 1, False), across(cross_top, 1, True)
+    far_bottom = (far_bottom.astype(F32) + passed.astype(F32)).astype(WIRE)
+    far_bottom = across(far_bottom, 1, False)
+    parts = (own, beside, far_top, cross_top, far_bottom)
     dnormin = summed_rows(*unproject(dq, parts, w_full, seg))
 
     scaled = dnormin * gain

time: 141 us -> 147 us (1.043)
  waiting for transfers between devices: 46.7 us -> 52.2 us
  starting transfers between devices: 59.3 us -> 62.5 us
  Pallas kernels: 14.6 us -> 11.8 us
    ppermute x28 -> x32, waiting for transfers between devices: 36.9 us -> 41.8 us  [moved(): return lax.ppermute(value, 'ctx', pairs)]
    ppermute x28 -> x32, starting transfers between devices: 31 us -> 34.9 us  [moved(): return lax.ppermute(value, 'ctx', pairs)]
    pallas_call x1, Pallas kernels: 3.37 us -> 0.8 us  [project(): pl.pallas_call(project_kernel, out_shape=(bf16(rows, HEAD), bf16(rows, 2...]
  transfers between devices with their start and end apart: 37 -> 41, of which waited for: 20 -> 17; matrix products, arithmetic and copies ran while one was open for 0% -> 0% of each run, Pallas kernels for 5% -> 3%
where the time goes in v11:
time: 147 us; the launch traced here: 145 us
  starting transfers between devices  62.5 us (43%)
  waiting for transfers between devices  52.2 us (36%)
  between operations  13.8 us (9%)
  Pallas kernels  11.8 us (8%)
  local copies, waits for them, and re-layouts  2.56 us (2%)
    ppermute x32, waiting for transfers between devices, moved(): return lax.ppermute(value, 'ctx', pairs)  41.8 us
    ppermute x32, starting transfers between devices, moved(): return lax.ppermute(value, 'ctx', pairs)  34.9 us
    ppermute x3, starting transfers between devices, other_chip(): return lax.ppermute(value, 'ctx', pairs)  19.8 us
    ppermute x3, waiting for transfers between devices, other_chip(): return lax.ppermute(value, 'ctx', pairs)  7.31 us
    ppermute x3, starting transfers between devices, shifted_y(): return lax.ppermute(value, 'dp', pairs)  5.38 us
    pallas_call x1, Pallas kernels, attention(): pl.pallas_call(functools.partial(attention_kernel, 256, seg), out_shape=(...  4.5 us
    ppermute x1, waiting for transfers between devices, two_back(): lax.ppermute(value, 'ctx', [(i, i - CORES) for i in range(CORES, CTX)])  3.03 us
  transfers between devices with their start and end apart: 41, of which 17 were waited for; matrix products, arithmetic and copies ran while one was open for 0% of the time, Pallas kernels for 3%

profile of v11, /device:TPU:6, one launch (start us, length us, event | category | flops | bytes accessed | tf_op | source)
XLA Modules:
  0.0 145.1 jit_solution(13379704983198563413)
XLA Ops:
  6.5 1.8 %shard_map.82 = (bf16[128,384]{1,0:T(8,128)(2,1)}, bf16[64,1024]{1,0:T(8,128)(2,1)}, s32[1,64]{1,0:T(1,128)}) custom-call(bf16[128,1024]{1,0:T(8,128)(2,1)} %q_ref.1, bf16[128,1024]{1,0:T(8,128)(2,1)} %k_ref.1, bf16[128,1024]{1,0:T(8,128)(2,1)} %v_ref.1, bf16[128,1024]{1,0:T(8,128)(2,1)} %o_ref.1, s32[1,64]{1,0:T(1,128)} %own_ref.1), custom_call_target="tpu_custom_call" | custom-call | tf_op jit(solution)/shard_map/pallas_call | solution.py:108
  8.4 8.7 %collective-permute-start = (s32[1,64]{1,0:T(1,128)}, s32[1,64]{1,0:T(1,128)S(1)}, u32[]{:S(2)}, u32[]{:S(2)}) collective-permute-start(s32[1,64]{1,0:T(1,128)} %get-tuple-element.45), channel_id=1, source_target_pairs={{1,2},{2,1},{3,4},{4,3},{5,6},{6,5},{7,8},{8,7},{9,10},{10,9},{11,... | collective-permute-start | bytes 776 | tf_op jit(solution)/shard_map/ppermute | solution.py:51
  21.6 7.2 %collective-permute-start.3 = (bf16[64,2048]{1,0:T(8,128)(2,1)S(1)}, bf16[64,2048]{1,0:T(8,128)(2,1)S(1)}, u32[]{:S(2)}, u32[]{:S(2)}) collective-permute-start(bf16[64,2048]{1,0:T(8,128)(2,1)S(1)} %get-tuple-element.47), channel_id=1, source_target_pairs={{1,2},{2,1},{3,4},{4,3},{5,6},{6,5},{7,8},{8,7},{9,10},{10,9},{11,... | collective-permute-start | bytes 786440 | tf_op jit(solution)/shard_map/ppermute | solution.py:51
  29.0 2.3 %collective-permute-start.5 = (f32[1,1024]{1,0:T(1,128)S(1)}, f32[1,1024]{1,0:T(1,128)S(1)}, u32[]{:S(2)}, u32[]{:S(2)}) collective-permute-start(f32[1,1024]{1,0:T(1,128)S(1)} %get-tuple-element.51), channel_id=1, source_target_pairs={{2,0},{3,1},{4,2},{5,3},{6,4},{7,5},{8,6},{9,7},{10,8},{11,9},{12,... | collective-permute-start | bytes 12296 | tf_op jit(solution)/shard_map/ppermute | solution.py:55
  31.5 3.0 %collective-permute-done.5.refs_2_.second_ref = f32[1,1024]{1,0:T(1,128)S(1)} collective-permute-done((f32[1,1024]{1,0:T(1,128)S(1)}, f32[1,1024]{1,0:T(1,128)S(1)}, u32[]{:S(2)}, u32[]{:S(2)}) %collective-permute-start.5) | collective-permute-done | bytes 4128 | tf_op jit(solution)/shard_map/ppermute | solution.py:55
  38.3 2.1 %collective-permute-start.15 = (bf16[256,384]{1,0:T(8,128)(2,1)S(1)}, bf16[256,384]{1,0:T(8,128)(2,1)S(1)}, u32[]{:S(2)}, u32[]{:S(2)}) collective-permute-start(bf16[256,384]{1,0:T(8,128)(2,1)S(1)} %get-tuple-element.55.refs_8_), channel_id=1, source_target_pairs={{0,64},{32,96},{64,0},{96,32},{128,192},{160,224},{192,128},{224,1... | collective-permute-start | bytes 589832 | tf_op jit(solution)/shard_map/ppermute | solution.py:129
  40.3 4.9 %collective-permute-done.7.refs_0_.value_ref.refs_2_ = bf16[64,1024]{1,0:T(8,128)(2,1)S(1)} collective-permute-done((bf16[64,1024]{1,0:T(8,128)(2,1)S(1)}, bf16[64,1024]{1,0:T(8,128)(2,1)S(1)}, u32[]{:S(2)}, u32[]{:S(2)}) %collective-permute-start.7) | collective-permute-done | bytes 131104 | tf_op jit(solution)/shard_map/ppermute | solution.py:46
  45.4 3.2 %collective-permute-start.14 = (bf16[64,1024]{1,0:T(8,128)(2,1)S(1)}, bf16[64,1024]{1,0:T(8,128)(2,1)S(1)}, u32[]{:S(2)}, u32[]{:S(2)}) collective-permute-start(bf16[64,1024]{1,0:T(8,128)(2,1)S(1)} %shard_map.87), channel_id=1, source_target_pairs={{0,4},{1,13},{2,6},{3,15},{4,8},{5,1},{6,10},{7,3},{8,12},{9,5},{1... | collective-permute-start | bytes 393224 | tf_op jit(solution)/shard_map/ppermute | solution.py:46
  49.4 3.4 %collective-permute-done.8.refs_3_ = bf16[64,1024]{1,0:T(8,128)(2,1)S(1)} collective-permute-done((bf16[64,1024]{1,0:T(8,128)(2,1)S(1)}, bf16[64,1024]{1,0:T(8,128)(2,1)S(1)}, u32[]{:S(2)}, u32[]{:S(2)}) %collective-permute-start.8) | collective-permute-done | bytes 131104 | tf_op jit(solution)/shard_map/ppermute | solution.py:46
  55.6 3.1 %collective-permute-start.24 = (bf16[512,256]{1,0:T(8,128)(2,1)S(1)}, bf16[512,256]{1,0:T(8,128)(2,1)S(1)}, u32[]{:S(2)}, u32[]{:S(2)}) collective-permute-start(bf16[512,256]{1,0:T(8,128)(2,1)S(1)} %get-tuple-element.63.refs_9_), channel_id=1, source_target_pairs={{0,2},{1,3},{2,0},{3,1},{4,6},{5,7},{6,4},{7,5},{8,10},{9,11},{10,... | collective-permute-start | bytes 786440 | tf_op jit(solution)/shard_map/ppermute | solution.py:46
  62.6 8.7 %collective-permute-done.26.refs_12_ = bf16[256,256]{1,0:T(8,128)(2,1)S(1)} collective-permute-done((bf16[256,256]{1,0:T(8,128)(2,1)S(1)}, bf16[256,256]{1,0:T(8,128)(2,1)S(1)}, u32[]{:S(2)}, u32[]{:S(2)}) %collective-permute-start.26) | collective-permute-done | bytes 131104 | tf_op jit(solution)/shard_map/ppermute | solution.py:46
  71.2 2.1 %collective-permute-start.28 = (bf16[256,256]{1,0:T(8,128)(2,1)S(1)}, bf16[256,256]{1,0:T(8,128)(2,1)S(1)}, u32[]{:S(2)}, u32[]{:S(2)}) collective-permute-start(bf16[256,256]{1,0:T(8,128)(2,1)S(1)} %collective-permute-done.26.refs_12_), channel_id=1, source_target_pairs={{16,18},{17,19},{18,16},{19,17},{20,22},{21,23},{22,20},{23,21},{2... | collective-permute-start | bytes 393224 | tf_op jit(solution)/shard_map/ppermute | solution.py:46
  74.6 1.9 %shard_map.90 = (bf16[128,128]{1,0:T(8,128)(2,1)S(1)}, bf16[128,128]{1,0:T(8,128)(2,1)S(1)}, bf16[128,128]{1,0:T(8,128)(2,1)S(1)}, bf16[128,128]{1,0:T(8,128)(2,1)S(1)}) custom-call(bf16[64,1024]{1,0:T(8,128)(2,1)S(1)} %get-tuple-element.56.own_ref, bf16[64,1024]{1,0:T(8,128)(2,1)S(1)} %collective-permute-done.13.refs_2_.other_ref, ...), custom_call_target="tpu_custom_call" | custom-call | tf_op jit(solution)/shard_map/pallas_call | solution.py:332
  76.8 3.1 %collective-permute-start.18 = (bf16[128,128]{1,0:T(8,128)(2,1)S(1)}, bf16[128,128]{1,0:T(8,128)(2,1)S(1)}, u32[]{:S(2)}, u32[]{:S(2)}) collective-permute-start(bf16[128,128]{1,0:T(8,128)(2,1)S(1)} %get-tuple-element.61), channel_id=1, source_target_pairs={{0,8},{1,9},{2,10},{3,11},{4,12},{5,13},{6,14},{7,15},{8,0},{9,1},... | collective-permute-start | bytes 98312 | tf_op jit(solution)/shard_map/ppermute | solution.py:46
  79.9 4.0 %collective-permute-start.19 = (bf16[128,128]{1,0:T(8,128)(2,1)S(1)}, bf16[128,128]{1,0:T(8,128)(2,1)S(1)}, u32[]{:S(2)}, u32[]{:S(2)}) collective-permute-start(bf16[128,128]{1,0:T(8,128)(2,1)S(1)} %get-tuple-element.62), channel_id=1, source_target_pairs={{0,12},{1,13},{2,14},{3,15},{4,0},{5,1},{6,2},{7,3},{8,4},{9,5},{1... | collective-permute-start | bytes 98312 | tf_op jit(solution)/shard_map/ppermute | solution.py:46
  87.0 4.5 %shard_map.91 = (bf16[512,128]{1,0:T(8,128)(2,1)S(1)}, bf16[512,256]{1,0:T(8,128)(2,1)S(1)}, bf16[512,256]{1,0:T(8,128)(2,1)S(1)}, bf16[256,256]{1,0:T(8,128)(2,...) custom-call(bf16[512,128]{1,0:T(8,128)(2,1)S(1)} %get-tuple-element.57.ready_ref.re, ...), custom_call_target="tpu_custom_call" | custom-call | flops 1610612736 | bytes 2490368 | tf_op jit(solution)/shard_map/pallas_call | solution.py:457
  91.5 3.5 %collective-permute-start.32 = (bf16[256,256]{1,0:T(8,128)(2,1)S(1)}, bf16[256,256]{1,0:T(8,128)(2,1)S(1)}, u32[]{:S(2)}, u32[]{:S(2)}) collective-permute-start(bf16[256,256]{1,0:T(8,128)(2,1)S(1)} %get-tuple-element.72), channel_id=1, source_target_pairs={{16,18},{17,19},{18,16},{19,17},{20,22},{21,23},{22,20},{23,21},{2... | collective-permute-start | bytes 393224 | tf_op jit(solution)/shard_map/ppermute | solution.py:46
  101.1 5.4 %collective-permute-done.31.refs_3_ = bf16[256,256]{1,0:T(8,128)(2,1)S(1)} collective-permute-done((bf16[256,256]{1,0:T(8,128)(2,1)S(1)}, bf16[256,256]{1,0:T(8,128)(2,1)S(1)}, u32[]{:S(2)}, u32[]{:S(2)}) %collective-permute-start.31) | collective-permute-done | bytes 131104 | tf_op jit(solution)/shard_map/ppermute | solution.py:46
  107.3 1.9 %collective-permute-done.34.swapped = bf16[256,1024]{1,0:T(8,128)(2,1)S(1)} collective-permute-done((bf16[256,1024]{1,0:T(8,128)(2,1)S(1)}, bf16[256,1024]{1,0:T(8,128)(2,1)S(1)}, u32[]{:S(2)}, u32[]{:S(2)}) %collective-permute-start.34) | collective-permute-done | bytes 524320 | tf_op jit(solution)/shard_map/ppermute | solution.py:46
  109.3 3.8 %collective-permute-start.36 = (bf16[64,1024]{1,0:T(8,128)(2,1)S(1)}, bf16[64,1024]{1,0:T(8,128)(2,1)S(1)}, u32[]{:S(2)}, u32[]{:S(2)}) collective-permute-start(bf16[64,1024]{1,0:T(8,128)(2,1)S(1)} %get-tuple-element.82), channel_id=1, source_target_pairs={{0,12},{1,5},{2,14},{3,7},{4,0},{5,9},{6,2},{7,11},{8,4},{9,13},{1... | collective-permute-start | bytes 393224 | tf_op jit(solution)/shard_map/ppermute | solution.py:46
  113.1 5.8 %collective-permute-done.36 = bf16[64,1024]{1,0:T(8,128)(2,1)S(1)} collective-permute-done((bf16[64,1024]{1,0:T(8,128)(2,1)S(1)}, bf16[64,1024]{1,0:T(8,128)(2,1)S(1)}, u32[]{:S(2)}, u32[]{:S(2)}) %collective-permute-start.36) | collective-permute-done | bytes 131104 | tf_op jit(solution)/shard_map/ppermute | solution.py:46
  120.6 5.8 %collective-permute-done.37 = bf16[64,1024]{1,0:T(8,128)(2,1)S(1)} collective-permute-done((bf16[64,1024]{1,0:T(8,128)(2,1)S(1)}, bf16[64,1024]{1,0:T(8,128)(2,1)S(1)}, u32[]{:S(2)}, u32[]{:S(2)}) %collective-permute-start.37) | collective-permute-done | bytes 131104 | tf_op jit(solution)/shard_map/ppermute | solution.py:46
  126.7 4.0 %collective-permute-start.38 = (bf16[64,1024]{1,0:T(8,128)(2,1)S(1)}, bf16[64,1024]{1,0:T(8,128)(2,1)S(1)}, u32[]{:S(2)}, u32[]{:S(2)}) collective-permute-start(bf16[64,1024]{1,0:T(8,128)(2,1)S(1)} %divide_convert_fusion), channel_id=1, source_target_pairs={{1,2},{2,1},{3,4},{4,3},{5,6},{6,5},{7,8},{8,7},{9,10},{10,9},{11,... | collective-permute-start | bytes 393224 | tf_op jit(solution)/shard_map/ppermute | solution.py:51
  130.8 6.0 %collective-permute-done.38 = bf16[64,1024]{1,0:T(8,128)(2,1)S(1)} collective-permute-done((bf16[64,1024]{1,0:T(8,128)(2,1)S(1)}, bf16[64,1024]{1,0:T(8,128)(2,1)S(1)}, u32[]{:S(2)}, u32[]{:S(2)}) %collective-permute-start.38) | collective-permute-done | bytes 131104 | tf_op jit(solution)/shard_map/ppermute | solution.py:51
  (99 shorter events, 31.4 us)
Async XLA Ops:
  6.5 66.8 %all-gather.3.cloned.1.call-start = ((), (), s32[]{:S(2)}) async-start(), calls=%async_computation | async-start | bytes 1179648 | tf_op jit(solution)/shard_map/all_gather | solution.py:133
  8.3 8.9 %collective-permute-start.1 = (s32[1,64]{1,0:T(1,128)}, s32[1,64]{1,0:T(1,128)S(1)}, u32[]{:S(2)}, u32[]{:S(2)}) collective-permute-start(s32[1,64]{1,0:T(1,128)} %get-tuple-element.45), channel_id=1, source_target_pairs={{0,1},{1,0},{2,3},{3,2},{4,5},{5,4},{6,7},{7,6},{8,9},{9,8},{10,11... | collective-permute-start | bytes 776 | tf_op jit(solution)/shard_map/ppermute | solution.py:46
  8.4 10.2 %collective-permute-start = (s32[1,64]{1,0:T(1,128)}, s32[1,64]{1,0:T(1,128)S(1)}, u32[]{:S(2)}, u32[]{:S(2)}) collective-permute-start(s32[1,64]{1,0:T(1,128)} %get-tuple-element.45), channel_id=1, source_target_pairs={{1,2},{2,1},{3,4},{4,3},{5,6},{6,5},{7,8},{8,7},{9,10},{10,9},{11,... | collective-permute-start | bytes 776 | tf_op jit(solution)/shard_map/ppermute | solution.py:51
  17.1 17.4 %collective-permute-start.4 = (bf16[128,384]{1,0:T(8,128)(2,1)}, bf16[128,384]{1,0:T(8,128)(2,1)S(1)}, u32[]{:S(2)}, u32[]{:S(2)}) collective-permute-start(bf16[128,384]{1,0:T(8,128)(2,1)} %get-tuple-element.50.refs_0_), channel_id=1, source_target_pairs={{0,128},{32,160},{64,192},{96,224},{128,0},{160,32},{192,64},{224,... | collective-permute-start | bytes 294920 | tf_op jit(solution)/shard_map/ppermute | solution.py:124
  21.5 13.0 %collective-permute-start.2 = (bf16[64,2048]{1,0:T(8,128)(2,1)S(1)}, bf16[64,2048]{1,0:T(8,128)(2,1)S(1)}, u32[]{:S(2)}, u32[]{:S(2)}) collective-permute-start(bf16[64,2048]{1,0:T(8,128)(2,1)S(1)} %get-tuple-element.46), channel_id=1, source_target_pairs={{0,1},{1,0},{2,3},{3,2},{4,5},{5,4},{6,7},{7,6},{8,9},{9,8},{10,11... | collective-permute-start | bytes 786440 | tf_op jit(solution)/shard_map/ppermute | solution.py:46
  21.6 12.9 %collective-permute-start.3 = (bf16[64,2048]{1,0:T(8,128)(2,1)S(1)}, bf16[64,2048]{1,0:T(8,128)(2,1)S(1)}, u32[]{:S(2)}, u32[]{:S(2)}) collective-permute-start(bf16[64,2048]{1,0:T(8,128)(2,1)S(1)} %get-tuple-element.47), channel_id=1, source_target_pairs={{1,2},{2,1},{3,4},{4,3},{5,6},{6,5},{7,8},{8,7},{9,10},{10,9},{11,... | collective-permute-start | bytes 786440 | tf_op jit(solution)/shard_map/ppermute | solution.py:51
  34.8 10.5 %collective-permute-start.11 = (bf16[256,384]{1,0:T(8,128)(2,1)S(1)}, bf16[256,384]{1,0:T(8,128)(2,1)S(1)}, u32[]{:S(2)}, u32[]{:S(2)}) collective-permute-start(bf16[256,384]{1,0:T(8,128)(2,1)S(1)} %get-tuple-element.55.refs_8_), channel_id=1, source_target_pairs={{0,32},{32,64},{64,96},{96,0},{128,160},{160,192},{192,224},{224,1... | collective-permute-start | bytes 589832 | tf_op jit(solution)/shard_map/ppermute | solution.py:129
  36.5 8.9 %collective-permute-start.12 = (bf16[256,384]{1,0:T(8,128)(2,1)S(1)}, bf16[256,384]{1,0:T(8,128)(2,1)S(1)}, u32[]{:S(2)}, u32[]{:S(2)}) collective-permute-start(bf16[256,384]{1,0:T(8,128)(2,1)S(1)} %get-tuple-element.55.refs_8_), channel_id=1, source_target_pairs={{0,96},{32,0},{64,32},{96,64},{128,224},{160,128},{192,160},{224,1... | collective-permute-start | bytes 589832 | tf_op jit(solution)/shard_map/ppermute | solution.py:129
  38.3 14.5 %collective-permute-start.15 = (bf16[256,384]{1,0:T(8,128)(2,1)S(1)}, bf16[256,384]{1,0:T(8,128)(2,1)S(1)}, u32[]{:S(2)}, u32[]{:S(2)}) collective-permute-start(bf16[256,384]{1,0:T(8,128)(2,1)S(1)} %get-tuple-element.55.refs_8_), channel_id=1, source_target_pairs={{0,64},{32,96},{64,0},{96,32},{128,192},{160,224},{192,128},{224,1... | collective-permute-start | bytes 589832 | tf_op jit(solution)/shard_map/ppermute | solution.py:129
  45.2 7.6 %collective-permute-start.8 = (bf16[64,1024]{1,0:T(8,128)(2,1)S(1)}, bf16[64,1024]{1,0:T(8,128)(2,1)S(1)}, u32[]{:S(2)}, u32[]{:S(2)}) collective-permute-start(bf16[64,1024]{1,0:T(8,128)(2,1)S(1)} %shard_map.86), channel_id=1, source_target_pairs={{0,13},{1,4},{2,15},{3,6},{4,1},{5,8},{6,3},{7,10},{8,5},{9,12},{1... | collective-permute-start | bytes 393224 | tf_op jit(solution)/shard_map/ppermute | solution.py:46
  45.4 8.0 %collective-permute-start.14 = (bf16[64,1024]{1,0:T(8,128)(2,1)S(1)}, bf16[64,1024]{1,0:T(8,128)(2,1)S(1)}, u32[]{:S(2)}, u32[]{:S(2)}) collective-permute-start(bf16[64,1024]{1,0:T(8,128)(2,1)S(1)} %shard_map.87), channel_id=1, source_target_pairs={{0,4},{1,13},{2,6},{3,15},{4,8},{5,1},{6,10},{7,3},{8,12},{9,5},{1... | collective-permute-start | bytes 393224 | tf_op jit(solution)/shard_map/ppermute | solution.py:46
  55.6 28.4 %collective-permute-start.24 = (bf16[512,256]{1,0:T(8,128)(2,1)S(1)}, bf16[512,256]{1,0:T(8,128)(2,1)S(1)}, u32[]{:S(2)}, u32[]{:S(2)}) collective-permute-start(bf16[512,256]{1,0:T(8,128)(2,1)S(1)} %get-tuple-element.63.refs_9_), channel_id=1, source_target_pairs={{0,2},{1,3},{2,0},{3,1},{4,6},{5,7},{6,4},{7,5},{8,10},{9,11},{10,... | collective-permute-start | bytes 786440 | tf_op jit(solution)/shard_map/ppermute | solution.py:46
  58.7 12.6 %collective-permute-start.26 = (bf16[256,256]{1,0:T(8,128)(2,1)S(1)}, bf16[256,256]{1,0:T(8,128)(2,1)S(1)}, u32[]{:S(2)}, u32[]{:S(2)}) collective-permute-start(bf16[256,256]{1,0:T(8,128)(2,1)S(1)} %get-tuple-element.65), channel_id=1, source_target_pairs={{0,16},{1,17},{2,18},{3,19},{4,20},{5,21},{6,22},{7,23},{8,24},{9,... | collective-permute-start | bytes 393224 | tf_op jit(solution)/shard_map/ppermute | solution.py:46
  60.0 16.8 %collective-permute-start.25 = (bf16[256,256]{1,0:T(8,128)(2,1)S(1)}, bf16[256,256]{1,0:T(8,128)(2,1)S(1)}, u32[]{:S(2)}, u32[]{:S(2)}) collective-permute-start(bf16[256,256]{1,0:T(8,128)(2,1)S(1)} %get-tuple-element.64), channel_id=1, source_target_pairs={{0,16},{1,17},{2,18},{3,19},{4,20},{5,21},{6,22},{7,23},{8,24},{9,... | collective-permute-start | bytes 393224 | tf_op jit(solution)/shard_map/ppermute | solution.py:46
  61.3 18.7 %collective-permute-start.27 = (bf16[256,256]{1,0:T(8,128)(2,1)S(1)}, bf16[256,256]{1,0:T(8,128)(2,1)S(1)}, u32[]{:S(2)}, u32[]{:S(2)}) collective-permute-start(bf16[256,256]{1,0:T(8,128)(2,1)S(1)} %get-tuple-element.64), channel_id=1, source_target_pairs={{0,18},{1,19},{2,16},{3,17},{4,22},{5,23},{6,20},{7,21},{8,26},{9,... | collective-permute-start | bytes 393224 | tf_op jit(solution)/shard_map/ppermute | solution.py:46
  71.2 14.5 %collective-permute-start.28 = (bf16[256,256]{1,0:T(8,128)(2,1)S(1)}, bf16[256,256]{1,0:T(8,128)(2,1)S(1)}, u32[]{:S(2)}, u32[]{:S(2)}) collective-permute-start(bf16[256,256]{1,0:T(8,128)(2,1)S(1)} %collective-permute-done.26.refs_12_), channel_id=1, source_target_pairs={{16,18},{17,19},{18,16},{19,17},{20,22},{21,23},{22,20},{23,21},{2... | collective-permute-start | bytes 393224 | tf_op jit(solution)/shard_map/ppermute | solution.py:46
  76.8 7.8 %collective-permute-start.18 = (bf16[128,128]{1,0:T(8,128)(2,1)S(1)}, bf16[128,128]{1,0:T(8,128)(2,1)S(1)}, u32[]{:S(2)}, u32[]{:S(2)}) collective-permute-start(bf16[128,128]{1,0:T(8,128)(2,1)S(1)} %get-tuple-element.61), channel_id=1, source_target_pairs={{0,8},{1,9},{2,10},{3,11},{4,12},{5,13},{6,14},{7,15},{8,0},{9,1},... | collective-permute-start | bytes 98312 | tf_op jit(solution)/shard_map/ppermute | solution.py:46
  91.5 8.2 %collective-permute-start.32 = (bf16[256,256]{1,0:T(8,128)(2,1)S(1)}, bf16[256,256]{1,0:T(8,128)(2,1)S(1)}, u32[]{:S(2)}, u32[]{:S(2)}) collective-permute-start(bf16[256,256]{1,0:T(8,128)(2,1)S(1)} %get-tuple-element.72), channel_id=1, source_target_pairs={{16,18},{17,19},{18,16},{19,17},{20,22},{21,23},{22,20},{23,21},{2... | collective-permute-start | bytes 393224 | tf_op jit(solution)/shard_map/ppermute | solution.py:46
  95.0 11.5 %collective-permute-start.29 = (bf16[512,256]{1,0:T(8,128)(2,1)S(1)}, bf16[512,256]{1,0:T(8,128)(2,1)S(1)}, u32[]{:S(2)}, u32[]{:S(2)}) collective-permute-start(bf16[512,256]{1,0:T(8,128)(2,1)S(1)} %get-tuple-element.68), channel_id=1, source_target_pairs={{0,2},{1,3},{2,0},{3,1},{4,6},{5,7},{6,4},{7,5},{8,10},{9,11},{10,... | collective-permute-start | bytes 786440 | tf_op jit(solution)/shard_map/ppermute | solution.py:46
  96.8 9.7 %collective-permute-start.31 = (bf16[256,256]{1,0:T(8,128)(2,1)S(1)}, bf16[256,256]{1,0:T(8,128)(2,1)S(1)}, u32[]{:S(2)}, u32[]{:S(2)}) collective-permute-start(bf16[256,256]{1,0:T(8,128)(2,1)S(1)} %get-tuple-element.70), channel_id=1, source_target_pairs={{16,2},{17,3},{18,0},{19,1},{20,6},{21,7},{22,4},{23,5},{24,10},{2... | collective-permute-start | bytes 393224 | tf_op jit(solution)/shard_map/ppermute | solution.py:46
  109.3 9.6 %collective-permute-start.36 = (bf16[64,1024]{1,0:T(8,128)(2,1)S(1)}, bf16[64,1024]{1,0:T(8,128)(2,1)S(1)}, u32[]{:S(2)}, u32[]{:S(2)}) collective-permute-start(bf16[64,1024]{1,0:T(8,128)(2,1)S(1)} %get-tuple-element.82), channel_id=1, source_target_pairs={{0,12},{1,5},{2,14},{3,7},{4,0},{5,9},{6,2},{7,11},{8,4},{9,13},{1... | collective-permute-start | bytes 393224 | tf_op jit(solution)/shard_map/ppermute | solution.py:46
  113.1 7.6 %collective-permute-start.35 = (bf16[64,1024]{1,0:T(8,128)(2,1)S(1)}, bf16[64,1024]{1,0:T(8,128)(2,1)S(1)}, u32[]{:S(2)}, u32[]{:S(2)}) collective-permute-start(bf16[64,1024]{1,0:T(8,128)(2,1)S(1)} %get-tuple-element.80), channel_id=1, source_target_pairs={{0,13},{1,4},{2,15},{3,6},{4,1},{5,8},{6,3},{7,10},{8,5},{9,12},{1... | collective-permute-start | bytes 393224 | tf_op jit(solution)/shard_map/ppermute | solution.py:46
  118.9 7.4 %collective-permute-start.37 = (bf16[64,1024]{1,0:T(8,128)(2,1)S(1)}, bf16[64,1024]{1,0:T(8,128)(2,1)S(1)}, u32[]{:S(2)}, u32[]{:S(2)}) collective-permute-start(bf16[64,1024]{1,0:T(8,128)(2,1)S(1)} %add_convert_fusion.1), channel_id=1, source_target_pairs={{0,12},{1,5},{2,14},{3,7},{4,0},{5,9},{6,2},{7,11},{8,4},{9,13},{1... | collective-permute-start | bytes 393224 | tf_op jit(solution)/shard_map/ppermute | solution.py:46
  126.7 10.0 %collective-permute-start.38 = (bf16[64,1024]{1,0:T(8,128)(2,1)S(1)}, bf16[64,1024]{1,0:T(8,128)(2,1)S(1)}, u32[]{:S(2)}, u32[]{:S(2)}) collective-permute-start(bf16[64,1024]{1,0:T(8,128)(2,1)S(1)} %divide_convert_fusion), channel_id=1, source_target_pairs={{1,2},{2,1},{3,4},{4,3},{5,6},{6,5},{7,8},{8,7},{9,10},{10,9},{11,... | collective-permute-start | bytes 393224 | tf_op jit(solution)/shard_map/ppermute | solution.py:51
  (24 other events, 137.4 us)
Sparse Core Ops, SparseCore 0:
  9.1 44.3 all-gather.2

commit v12 on v10

--- a/solution.py
+++ b/solution.py
@@ -179,12 +179,11 @@
         copy.wait()
 
 
-def stacked(pieces, out_ref):
-    copies, at = [], 0
+def fill(out_ref, pieces):
+    at = 0
     for piece in pieces:
-        copies.append((piece, out_ref.at[at : at + piece.shape[0], :]))
+        out_ref[at : at + piece.shape[0], :] = piece[...]
         at += piece.shape[0]
-    return copies
 
 
 def window_kernel(own_ref, beside_ref, facing_ref, token_hbm, grad_hbm, *refs):
@@ -256,8 +255,7 @@
 
 
 def norm_kernel(core_ref, chip_ref, mid_token, mid_grad, count_ref, gain_ref, *refs):
-    mine_ref, theirs_ref = refs[:2]
-    normin_ref, normed_ref, rms_ref, dout_ref, pair_ref = refs[-5:]
+    mine_ref, theirs_ref, normin_ref, normed_ref, rms_ref, dout_ref, pair_ref = refs
     width = mid_token.shape[1]
     rows = mine_ref.shape[0]
     pair_ref[:rows, :] = mine_ref[...]
@@ -272,7 +270,7 @@
     dout_ref[...] = mid_grad[...] + got[:, width:]
 
 
-def norm(from_core, from_chip, mid_token, mid_grad, count, gain, mine, theirs, ready):
+def norm(from_core, from_chip, mid_token, mid_grad, count, gain, mine, theirs):
     seg, width = mid_token.shape
     shape = jax.ShapeDtypeStruct
     return pl.pallas_call(
@@ -284,10 +282,10 @@
             shape((seg, width), F32),
             shape((2 * mine.shape[0], mine.shape[1]), mine.dtype),
         ),
-        in_specs=[VMEM] * 8 + [ANY],
+        in_specs=[VMEM] * 8,
         out_specs=(VMEM,) * 5,
         compiler_params=room(8),
-    )(from_core, from_chip, mid_token, mid_grad, count, gain, mine, theirs, ready)
+    )(from_core, from_chip, mid_token, mid_grad, count, gain, mine, theirs)
 
 
 def dout_kernel(dout_ref, second_ref, full_ref, half_ref):
@@ -309,40 +307,18 @@
     )(dout, second)
 
 
-def dattended_kernel(own_ref, other_ref, weight_ref, ready_ref, *refs):
-    outs, rows, weight, sems = refs[:TURNS], *refs[TURNS:]
-    heads, half = weight_ref.shape[:2]
-    copies = stacked([own_ref, other_ref], rows)
-    copies += [(weight_ref.at[i], weight.at[i * half : (i + 1) * half, :]) for i in range(heads)]
-    fetched(copies, sems)
-    turn = here()[1]
-    for step, out in enumerate(outs):
-        at = pl.multiple_of((turn + step) % TURNS * CORES * half, CORES * half)
-        part = weight[pl.ds(at, CORES * half), :]
-        out[...] = contract_last(rows[...], part).astype(jnp.bfloat16)
-
-
-def dattended(own, other, halves, ready):
-    heads, half, width = halves.shape
-    rows = 2 * own.shape[0]
-    return pl.pallas_call(
-        dattended_kernel,
-        out_shape=(jax.ShapeDtypeStruct((rows, CORES * half), jnp.bfloat16),) * TURNS,
-        in_specs=[ANY] * 4,
-        out_specs=(VMEM,) * TURNS,
-        scratch_shapes=[
-            pltpu.VMEM((rows, width), jnp.bfloat16),
-            pltpu.VMEM((heads * half, width), jnp.bfloat16),
-            pltpu.SemaphoreType.DMA((2 + heads,)),
-        ],
-        compiler_params=room(12),
-    )(own, other, halves, ready)
-
-
 def project_kernel(*refs):
-    pieces, weights = refs[:8], refs[8:12]
-    q_ref, kv_ref, w_ref, rows, sems = refs[12:]
-    copies = stacked(pieces, rows)
+    pieces, weights, douts, halves = refs[:8], refs[8:12], refs[12:14], refs[14]
+    q_ref, kv_ref, w_ref, outs = *refs[15:18], refs[18:22]
+    rows, chip_rows, w_back, sems = refs[22:]
+    heads, half = halves.shape[:2]
+    started = []
+    for i in range(heads):
+        target = w_back.at[i * half : (i + 1) * half, :]
+        started.append(pltpu.make_async_copy(halves.at[i], target, sems.at[i]))
+        started[-1].start()
+    fill(rows, pieces)
+    fill(chip_rows, douts)
     dp = lax.axis_index("dp")
     x, y = dp // ROWS_Y, dp % ROWS_Y
     depth = weights[0].shape[0] // ROWS_X
@@ -351,28 +327,38 @@
         for i in range(ROWS_X):
             its_x = x if i == 0 else 1 - x
             at = pl.multiple_of((its_x * ROWS_Y + its_y) * depth, depth)
-            copies.append((weight.at[i * depth : (i + 1) * depth, :], w_ref.at[pl.ds(at, depth), :]))
-    fetched(copies, sems)
+            w_ref[pl.ds(at, depth), :] = weight[i * depth : (i + 1) * depth, :]
     out = jnp.dot(rows[...], w_ref[...], preferred_element_type=F32).astype(jnp.bfloat16)
     q_ref[...] = out[:, :HEAD]
     kv_ref[...] = out[:, HEAD:]
-
-
-def project(pieces, weights):
+    for copy in started:
+        copy.wait()
+    turn = here()[1]
+    for step, ref in enumerate(outs):
+        at = pl.multiple_of((turn + step) % TURNS * CORES * half, CORES * half)
+        part = w_back[pl.ds(at, CORES * half), :]
+        ref[...] = contract_last(chip_rows[...], part).astype(jnp.bfloat16)
+
+
+def project(pieces, weights, douts, halves):
     seg, width = pieces[0].shape
     rows = seg * len(pieces)
+    heads, half = halves.shape[:2]
     bf16 = lambda *shape: jax.ShapeDtypeStruct(shape, jnp.bfloat16)
     return pl.pallas_call(
         project_kernel,
-        out_shape=(bf16(rows, HEAD), bf16(rows, 2 * HEAD), bf16(width, 3 * HEAD)),
-        in_specs=[ANY] * 12,
-        out_specs=(VMEM,) * 3,
+        out_shape=(bf16(rows, HEAD), bf16(rows, 2 * HEAD), bf16(width, 3 * HEAD))
+        + (bf16(2 * seg, CORES * half),) * TURNS,
+        in_specs=[VMEM] * 14 + [ANY],
+        out_specs=(VMEM,) * (3 + TURNS),
         scratch_shapes=[
             pltpu.VMEM((rows, width), jnp.bfloat16),
-            pltpu.SemaphoreType.DMA((16,)),
+            pltpu.VMEM((2 * seg, width), jnp.bfloat16),
+            pltpu.VMEM((heads * half, width), jnp.bfloat16),
+            pltpu.SemaphoreType.DMA((heads,)),
         ],
-        compiler_params=room(12),
-    )(*pieces, *weights)
+        compiler_params=room(50),
+    )(*pieces, *weights, *douts, halves)
 
 
 def place_dattended(core, seg, here_refs, there_refs, out_ref):
@@ -389,10 +375,10 @@
 
 def attention_kernel(tile, seg, *refs):
     q_ref, here_refs, there_refs, blocks = refs[0], refs[1:5], refs[5:9], refs[9:13]
-    dq_ref, outs, (kv, da_ref, dkt, dvt, sems) = refs[13], refs[14:18], refs[18:]
+    dq_ref, outs, (kv, da_ref, dkt, dvt) = refs[13], refs[14:18], refs[18:]
     half, turn, pair, core = here()
     queries, keys = q_ref.shape[0], kv.shape[0]
-    fetched(stacked(blocks, kv), sems)
+    fill(kv, blocks)
 
     for which in range(CORES):
 
@@ -433,9 +419,10 @@
         else:
             dkt[...] += dk_part
             dvt[...] += dv_part
-    part = keys // len(outs)
-    for i, out in enumerate(outs):
-        lanes = slice(i * part, (i + 1) * part)
+    at = 0
+    for out in outs:
+        lanes = slice(at, at + out.shape[0])
+        at += out.shape[0]
         out[:, :HEAD] = (dkt[:, lanes] * scale).T.astype(jnp.bfloat16)
         out[:, HEAD:] = dvt[:, lanes].T.astype(jnp.bfloat16)
 
@@ -443,18 +430,17 @@
 def attention(q, da_here, da_there, blocks, seg):
     queries = q.shape[0]
     keys = sum(block.shape[0] for block in blocks)
-    part = jax.ShapeDtypeStruct(blocks[0].shape, jnp.bfloat16)
+    parts = tuple(jax.ShapeDtypeStruct(block.shape, jnp.bfloat16) for block in blocks)
     return pl.pallas_call(
         functools.partial(attention_kernel, 256, seg),
-        out_shape=(jax.ShapeDtypeStruct((queries, HEAD), jnp.bfloat16),) + (part,) * 4,
-        in_specs=[VMEM] * 9 + [ANY] * 4,
+        out_shape=(jax.ShapeDtypeStruct((queries, HEAD), jnp.bfloat16),) + parts,
+        in_specs=[VMEM] * 13,
         out_specs=(VMEM,) * 5,
         scratch_shapes=[
             pltpu.VMEM((keys, 2 * HEAD), jnp.bfloat16),
             pltpu.VMEM((queries, HEAD), jnp.bfloat16),
             pltpu.VMEM((HEAD, keys), F32),
             pltpu.VMEM((HEAD, keys), F32),
-            pltpu.SemaphoreType.DMA((4,)),
         ],
         compiler_params=room(36),
         cost_estimate=pl.CostEstimate(
@@ -528,6 +514,7 @@
     halves = gathered_halves(half)
     theirs = other_x(mine)
     beside, facing = other_core(own_starts), other_chip(own_starts)
+    own_starts = starts
     to_core, to_chip, mid_token, mid_grad, first = window_sums(
         own_starts, beside, facing, token_rows, grad_out
     )
@@ -549,15 +536,13 @@
         gain[None],
         mine,
         theirs,
-        second,
     )
     weights = [both, shifted_y(both, 1), shifted_y(both, -1), shifted_y(both, 2)]
     dout, dout_b = whole_dout(dout, second)
     dout_there = other_core(dout_b)
-    pieces = gathered_rows(normin, weights[1:3] + [dout_there], weights[3:])
-    q, own, w_full = project(pieces, weights)
+    pieces = gathered_rows(normin, [dout_there], weights[1:])
+    q, own, w_full, *da = project(pieces, weights, (dout_b, dout_there), halves)
     cross, far, beside = across(own, 0, True), across(own, 0, False), other_pair(own)
-    da = dattended(dout_b, dout_there, halves, q)
     da_here = [da[0]] + [
         moved(da[i], lambda h, t, p, k, i=i: (h, t + i, p, k)) for i in range(1, TURNS)
     ]

time: 141 us -> 141 us (level)
  Pallas kernels: 14.6 us -> 11.3 us
  waiting for transfers between devices: 46.7 us -> 49.6 us
  local copies, waits for them, and re-layouts: 3.22 us -> 1.34 us
    ppermute x3, waiting for transfers between devices: 0.15 us -> 6.88 us  [shifted_y(): return lax.ppermute(value, 'dp', pairs)]
    ppermute x28, waiting for transfers between devices: 36.9 us -> 33.8 us  [moved(): return lax.ppermute(value, 'ctx', pairs)]
    ppermute x1, waiting for transfers between devices: 3.07 us -> 0.01 us  [two_back(): lax.ppermute(value, 'ctx', [(i, i - CORES) for i in range(CORES, CTX)])]
    ppermute x3, waiting for transfers between devices: 6.53 us -> 8.86 us  [other_chip(): return lax.ppermute(value, 'ctx', pairs)]
    pallas_call x1 -> x0, Pallas kernels: 2.22 us -> none  [dattended(): pl.pallas_call(dattended_kernel, out_shape=(jax.ShapeDtypeStruct((rows, C...]
    unnamed x14 -> x12, local copies, waits for them, and re-layouts: 3.12 us -> 1.24 us
    ppermute x3, starting transfers between devices: 20.5 us -> 22.2 us  [other_chip(): return lax.ppermute(value, 'ctx', pairs)]
  transfers between devices with their start and end apart: 37 -> 37, of which waited for: 20 -> 19; matrix products, arithmetic and copies ran while one was open for 0% -> 0% of each run, Pallas kernels for 5% -> 1%
where the time goes in v12:
time: 141 us; the launch traced here: 139 us
  starting transfers between devices  60.7 us (43%)
  waiting for transfers between devices  49.6 us (35%)
  between operations  13.7 us (10%)
  Pallas kernels  11.3 us (8%)
  matrix products  1.46 us (1%)
    ppermute x28, waiting for transfers between devices, moved(): return lax.ppermute(value, 'ctx', pairs)  33.8 us
    ppermute x28, starting transfers between devices, moved(): return lax.ppermute(value, 'ctx', pairs)  30.8 us
    ppermute x3, starting transfers between devices, other_chip(): return lax.ppermute(value, 'ctx', pairs)  22.2 us
    ppermute x3, waiting for transfers between devices, other_chip(): return lax.ppermute(value, 'ctx', pairs)  8.86 us
    ppermute x3, waiting for transfers between devices, shifted_y(): return lax.ppermute(value, 'dp', pairs)  6.88 us
    ppermute x3, starting transfers between devices, shifted_y(): return lax.ppermute(value, 'dp', pairs)  5.3 us
    pallas_call x1, Pallas kernels, attention(): pl.pallas_call(functools.partial(attention_kernel, 256, seg), out_shape=(...  4.44 us
  transfers between devices with their start and end apart: 37, of which 19 were waited for; matrix products, arithmetic and copies ran while one was open for 0% of the time, Pallas kernels for 1%

profile of v12, /device:TPU:6, one launch (start us, length us, event | category | flops | bytes accessed | tf_op | source)
XLA Modules:
  0.0 138.9 jit_solution(2319260734699493612)
XLA Ops:
  6.5 1.8 %shard_map.82 = (bf16[128,384]{1,0:T(8,128)(2,1)}, bf16[64,1024]{1,0:T(8,128)(2,1)}, s32[1,64]{1,0:T(1,128)}) custom-call(bf16[128,1024]{1,0:T(8,128)(2,1)} %q_ref.1, bf16[128,1024]{1,0:T(8,128)(2,1)} %k_ref.1, bf16[128,1024]{1,0:T(8,128)(2,1)} %v_ref.1, bf16[128,1024]{1,0:T(8,128)(2,1)} %o_ref.1, s32[1,64]{1,0:T(1,128)} %own_ref.1), custom_call_target="tpu_custom_call" | custom-call | tf_op jit(solution)/shard_map/pallas_call | solution.py:104
  8.4 8.7 %collective-permute-start = (s32[1,64]{1,0:T(1,128)}, s32[1,64]{1,0:T(1,128)S(1)}, u32[]{:S(2)}, u32[]{:S(2)}) collective-permute-start(s32[1,64]{1,0:T(1,128)} %get-tuple-element.41), channel_id=1, source_target_pairs={{1,2},{2,1},{3,4},{4,3},{5,6},{6,5},{7,8},{8,7},{9,10},{10,9},{11,... | collective-permute-start | bytes 776 | tf_op jit(solution)/shard_map/ppermute | solution.py:51
  21.6 7.1 %collective-permute-start.3 = (bf16[64,2048]{1,0:T(8,128)(2,1)S(1)}, bf16[64,2048]{1,0:T(8,128)(2,1)S(1)}, u32[]{:S(2)}, u32[]{:S(2)}) collective-permute-start(bf16[64,2048]{1,0:T(8,128)(2,1)S(1)} %get-tuple-element.43), channel_id=1, source_target_pairs={{1,2},{2,1},{3,4},{4,3},{5,6},{6,5},{7,8},{8,7},{9,10},{10,9},{11,... | collective-permute-start | bytes 786440 | tf_op jit(solution)/shard_map/ppermute | solution.py:51
  28.9 2.3 %collective-permute-start.5 = (f32[1,1024]{1,0:T(1,128)S(1)}, f32[1,1024]{1,0:T(1,128)S(1)}, u32[]{:S(2)}, u32[]{:S(2)}) collective-permute-start(f32[1,1024]{1,0:T(1,128)S(1)} %get-tuple-element.48), channel_id=1, source_target_pairs={{2,0},{3,1},{4,2},{5,3},{6,4},{7,5},{8,6},{9,7},{10,8},{11,9},{12,... | collective-permute-start | bytes 12296 | tf_op jit(solution)/shard_map/ppermute | solution.py:55
  31.3 4.1 %collective-permute-done.3.chip_ref = bf16[64,2048]{1,0:T(8,128)(2,1)S(1)} collective-permute-done((bf16[64,2048]{1,0:T(8,128)(2,1)S(1)}, bf16[64,2048]{1,0:T(8,128)(2,1)S(1)}, u32[]{:S(2)}, u32[]{:S(2)}) %collective-permute-start.3) | collective-permute-done | bytes 262176 | tf_op jit(solution)/shard_map/ppermute | solution.py:51
  39.2 2.0 %collective-permute-start.15 = (bf16[256,384]{1,0:T(8,128)(2,1)S(1)}, bf16[256,384]{1,0:T(8,128)(2,1)S(1)}, u32[]{:S(2)}, u32[]{:S(2)}) collective-permute-start(bf16[256,384]{1,0:T(8,128)(2,1)S(1)} %get-tuple-element.52.refs_8_), channel_id=1, source_target_pairs={{0,64},{32,96},{64,0},{96,32},{128,192},{160,224},{192,128},{224,1... | collective-permute-start | bytes 589832 | tf_op jit(solution)/shard_map/ppermute | solution.py:125
  42.8 1.8 %collective-permute-start.8 = (bf16[64,1024]{1,0:T(8,128)(2,1)S(1)}, bf16[64,1024]{1,0:T(8,128)(2,1)S(1)}, u32[]{:S(2)}, u32[]{:S(2)}) collective-permute-start(bf16[64,1024]{1,0:T(8,128)(2,1)S(1)} %shard_map.86), channel_id=1, source_target_pairs={{0,13},{1,4},{2,15},{3,6},{4,1},{5,8},{6,3},{7,10},{8,5},{9,12},{1... | collective-permute-start | bytes 393224 | tf_op jit(solution)/shard_map/ppermute | solution.py:46
  44.7 2.2 %collective-permute-done.13.refs_0_.refs_9_ = bf16[256,384]{1,0:T(8,128)(2,1)S(1)} collective-permute-done((bf16[256,384]{1,0:T(8,128)(2,1)S(1)}, bf16[256,384]{1,0:T(8,128)(2,1)S(1)}, u32[]{:S(2)}, u32[]{:S(2)}) %collective-permute-start.13) | collective-permute-done | bytes 196640 | tf_op jit(solution)/shard_map/ppermute | solution.py:125
  49.4 3.7 %collective-permute-done.15.refs_2_.refs_11_ = bf16[256,384]{1,0:T(8,128)(2,1)S(1)} collective-permute-done((bf16[256,384]{1,0:T(8,128)(2,1)S(1)}, bf16[256,384]{1,0:T(8,128)(2,1)S(1)}, u32[]{:S(2)}, u32[]{:S(2)}) %collective-permute-start.15) | collective-permute-done | bytes 196640 | tf_op jit(solution)/shard_map/ppermute | solution.py:125
  54.6 2.3 %shard_map.89 = (bf16[512,128]{1,0:T(8,128)(2,1)S(1)}, bf16[512,256]{1,0:T(8,128)(2,1)S(1)}, bf16[1024,384]{1,0:T(8,128)(2,1)S(1)}, bf16[128,128]{1,0:T(8,128)(2...) custom-call(bf16[64,1024]{1,0:T(8,128)(2,1)S(1)} %get-tuple-element.50.value_ref.r, ...), custom_call_target="tpu_custom_call" | custom-call | tf_op jit(solution)/shard_map/pallas_call | solution.py:348
  59.8 3.0 %collective-permute-start.17 = (bf16[128,128]{1,0:T(8,128)(2,1)S(1)}, bf16[128,128]{1,0:T(8,128)(2,1)S(1)}, u32[]{:S(2)}, u32[]{:S(2)}) collective-permute-start(bf16[128,128]{1,0:T(8,128)(2,1)S(1)} %get-tuple-element.56), channel_id=1, source_target_pairs={{0,4},{1,5},{2,6},{3,7},{4,8},{5,9},{6,10},{7,11},{8,12},{9,13},{1... | collective-permute-start | bytes 98312 | tf_op jit(solution)/shard_map/ppermute | solution.py:46
  62.8 3.5 %collective-permute-start.18 = (bf16[128,128]{1,0:T(8,128)(2,1)S(1)}, bf16[128,128]{1,0:T(8,128)(2,1)S(1)}, u32[]{:S(2)}, u32[]{:S(2)}) collective-permute-start(bf16[128,128]{1,0:T(8,128)(2,1)S(1)} %get-tuple-element.57), channel_id=1, source_target_pairs={{0,8},{1,9},{2,10},{3,11},{4,12},{5,13},{6,14},{7,15},{8,0},{9,1},... | collective-permute-start | bytes 98312 | tf_op jit(solution)/shard_map/ppermute | solution.py:46
  66.3 3.7 %collective-permute-done.17.refs_2_ = bf16[128,128]{1,0:T(8,128)(2,1)S(1)} collective-permute-done((bf16[128,128]{1,0:T(8,128)(2,1)S(1)}, bf16[128,128]{1,0:T(8,128)(2,1)S(1)}, u32[]{:S(2)}, u32[]{:S(2)}) %collective-permute-start.17) | collective-permute-done | bytes 32800 | tf_op jit(solution)/shard_map/ppermute | solution.py:46
  71.0 3.7 %collective-permute-done.19.refs_4_ = bf16[128,128]{1,0:T(8,128)(2,1)S(1)} collective-permute-done((bf16[128,128]{1,0:T(8,128)(2,1)S(1)}, bf16[128,128]{1,0:T(8,128)(2,1)S(1)}, u32[]{:S(2)}, u32[]{:S(2)}) %collective-permute-start.19) | collective-permute-done | bytes 32800 | tf_op jit(solution)/shard_map/ppermute | solution.py:46
  77.2 4.4 %shard_map.90 = (bf16[512,128]{1,0:T(8,128)(2,1)S(1)}, bf16[512,256]{1,0:T(8,128)(2,1)S(1)}, bf16[512,256]{1,0:T(8,128)(2,1)S(1)}, bf16[512,256]{1,0:T(8,128)(2,1)S(1)}, bf16[512,256]{1,0:T(8,128)(2,1)S(1)}) custom-call(bf16[512,128]{1,0:T(8,128)(2,1)S(1)} %get-tuple-element.54.refs_0_, bf16[128,128]{1,0:T(8,128)(2,1)S(1)} %get-tuple-element.55.refs_1_, ...), custom_call_target="tpu_custom_call" | custom-call | flops 1610612736 | bytes 2490368 | tf_op jit(solution)/shard_map/pallas_call | solution.py:434
  82.6 9.7 %collective-permute-start.28 = (bf16[512,256]{1,0:T(8,128)(2,1)S(1)}, bf16[512,256]{1,0:T(8,128)(2,1)S(1)}, u32[]{:S(2)}, u32[]{:S(2)}) collective-permute-start(bf16[512,256]{1,0:T(8,128)(2,1)S(1)} %get-tuple-element.63), channel_id=1, source_target_pairs={{16,0},{17,1},{18,2},{19,3},{20,4},{21,5},{22,6},{23,7},{24,8},{25... | collective-permute-start | bytes 786440 | tf_op jit(solution)/shard_map/ppermute | solution.py:46
  92.4 2.7 %collective-permute-start.29 = (bf16[512,256]{1,0:T(8,128)(2,1)S(1)}, bf16[512,256]{1,0:T(8,128)(2,1)S(1)}, u32[]{:S(2)}, u32[]{:S(2)}) collective-permute-start(bf16[512,256]{1,0:T(8,128)(2,1)S(1)} %get-tuple-element.64), channel_id=1, source_target_pairs={{16,2},{17,3},{18,0},{19,1},{20,6},{21,7},{22,4},{23,5},{24,10},{2... | collective-permute-start | bytes 786440 | tf_op jit(solution)/shard_map/ppermute | solution.py:46
  95.1 8.7 %collective-permute-done.28.refs_2_ = bf16[512,256]{1,0:T(8,128)(2,1)S(1)} collective-permute-done((bf16[512,256]{1,0:T(8,128)(2,1)S(1)}, bf16[512,256]{1,0:T(8,128)(2,1)S(1)}, u32[]{:S(2)}, u32[]{:S(2)}) %collective-permute-start.28) | collective-permute-done | bytes 262176 | tf_op jit(solution)/shard_map/ppermute | solution.py:46
  104.7 1.9 %collective-permute-done.30.swapped = bf16[256,1024]{1,0:T(8,128)(2,1)S(1)} collective-permute-done((bf16[256,1024]{1,0:T(8,128)(2,1)S(1)}, bf16[256,1024]{1,0:T(8,128)(2,1)S(1)}, u32[]{:S(2)}, u32[]{:S(2)}) %collective-permute-start.30) | collective-permute-done | bytes 524320 | tf_op jit(solution)/shard_map/ppermute | solution.py:46
  108.0 2.4 %collective-permute-start.31 = (bf16[64,1024]{1,0:T(8,128)(2,1)S(1)}, bf16[64,1024]{1,0:T(8,128)(2,1)S(1)}, u32[]{:S(2)}, u32[]{:S(2)}) collective-permute-start(bf16[64,1024]{1,0:T(8,128)(2,1)S(1)} %get-tuple-element.72), channel_id=1, source_target_pairs={{0,13},{1,4},{2,15},{3,6},{4,1},{5,8},{6,3},{7,10},{8,5},{9,12},{1... | collective-permute-start | bytes 393224 | tf_op jit(solution)/shard_map/ppermute | solution.py:46
  110.4 3.8 %collective-permute-done.32 = bf16[64,1024]{1,0:T(8,128)(2,1)S(1)} collective-permute-done((bf16[64,1024]{1,0:T(8,128)(2,1)S(1)}, bf16[64,1024]{1,0:T(8,128)(2,1)S(1)}, u32[]{:S(2)}, u32[]{:S(2)}) %collective-permute-start.32) | collective-permute-done | bytes 131104 | tf_op jit(solution)/shard_map/ppermute | solution.py:46
  116.8 3.4 %collective-permute-done.33 = bf16[64,1024]{1,0:T(8,128)(2,1)S(1)} collective-permute-done((bf16[64,1024]{1,0:T(8,128)(2,1)S(1)}, bf16[64,1024]{1,0:T(8,128)(2,1)S(1)}, u32[]{:S(2)}, u32[]{:S(2)}) %collective-permute-start.33) | collective-permute-done | bytes 131104 | tf_op jit(solution)/shard_map/ppermute | solution.py:46
  120.5 6.4 %collective-permute-start.34 = (bf16[64,1024]{1,0:T(8,128)(2,1)S(1)}, bf16[64,1024]{1,0:T(8,128)(2,1)S(1)}, u32[]{:S(2)}, u32[]{:S(2)}) collective-permute-start(bf16[64,1024]{1,0:T(8,128)(2,1)S(1)} %divide_convert_fusion), channel_id=1, source_target_pairs={{1,2},{2,1},{3,4},{4,3},{5,6},{6,5},{7,8},{8,7},{9,10},{10,9},{11,... | collective-permute-start | bytes 393224 | tf_op jit(solution)/shard_map/ppermute | solution.py:51
  127.0 3.5 %collective-permute-done.34 = bf16[64,1024]{1,0:T(8,128)(2,1)S(1)} collective-permute-done((bf16[64,1024]{1,0:T(8,128)(2,1)S(1)}, bf16[64,1024]{1,0:T(8,128)(2,1)S(1)}, u32[]{:S(2)}, u32[]{:S(2)}) %collective-permute-start.34) | collective-permute-done | bytes 131104 | tf_op jit(solution)/shard_map/ppermute | solution.py:51
  (87 shorter events, 28.3 us)
Async XLA Ops:
  6.5 48.1 %all-gather.3.cloned.1.call-start = ((), (), s32[]{:S(2)}) async-start(), calls=%async_computation | async-start | bytes 1179648 | tf_op jit(solution)/shard_map/all_gather | solution.py:129
  8.3 8.9 %collective-permute-start.1 = (s32[1,64]{1,0:T(1,128)}, s32[1,64]{1,0:T(1,128)S(1)}, u32[]{:S(2)}, u32[]{:S(2)}) collective-permute-start(s32[1,64]{1,0:T(1,128)} %get-tuple-element.41), channel_id=1, source_target_pairs={{0,1},{1,0},{2,3},{3,2},{4,5},{5,4},{6,7},{7,6},{8,9},{9,8},{10,11... | collective-permute-start | bytes 776 | tf_op jit(solution)/shard_map/ppermute | solution.py:46
  8.4 10.1 %collective-permute-start = (s32[1,64]{1,0:T(1,128)}, s32[1,64]{1,0:T(1,128)S(1)}, u32[]{:S(2)}, u32[]{:S(2)}) collective-permute-start(s32[1,64]{1,0:T(1,128)} %get-tuple-element.41), channel_id=1, source_target_pairs={{1,2},{2,1},{3,4},{4,3},{5,6},{6,5},{7,8},{8,7},{9,10},{10,9},{11,... | collective-permute-start | bytes 776 | tf_op jit(solution)/shard_map/ppermute | solution.py:51
  17.1 14.2 %collective-permute-start.4 = (bf16[128,384]{1,0:T(8,128)(2,1)}, bf16[128,384]{1,0:T(8,128)(2,1)S(1)}, u32[]{:S(2)}, u32[]{:S(2)}) collective-permute-start(bf16[128,384]{1,0:T(8,128)(2,1)} %get-tuple-element.46.refs_0_), channel_id=1, source_target_pairs={{0,128},{32,160},{64,192},{96,224},{128,0},{160,32},{192,64},{224,... | collective-permute-start | bytes 294920 | tf_op jit(solution)/shard_map/ppermute | solution.py:120
  21.5 9.9 %collective-permute-start.2 = (bf16[64,2048]{1,0:T(8,128)(2,1)S(1)}, bf16[64,2048]{1,0:T(8,128)(2,1)S(1)}, u32[]{:S(2)}, u32[]{:S(2)}) collective-permute-start(bf16[64,2048]{1,0:T(8,128)(2,1)S(1)} %get-tuple-element.42), channel_id=1, source_target_pairs={{0,1},{1,0},{2,3},{3,2},{4,5},{5,4},{6,7},{7,6},{8,9},{9,8},{10,11... | collective-permute-start | bytes 786440 | tf_op jit(solution)/shard_map/ppermute | solution.py:46
  21.6 13.8 %collective-permute-start.3 = (bf16[64,2048]{1,0:T(8,128)(2,1)S(1)}, bf16[64,2048]{1,0:T(8,128)(2,1)S(1)}, u32[]{:S(2)}, u32[]{:S(2)}) collective-permute-start(bf16[64,2048]{1,0:T(8,128)(2,1)S(1)} %get-tuple-element.43), channel_id=1, source_target_pairs={{1,2},{2,1},{3,4},{4,3},{5,6},{6,5},{7,8},{8,7},{9,10},{10,9},{11,... | collective-permute-start | bytes 786440 | tf_op jit(solution)/shard_map/ppermute | solution.py:51
  28.9 6.9 %collective-permute-start.5 = (f32[1,1024]{1,0:T(1,128)S(1)}, f32[1,1024]{1,0:T(1,128)S(1)}, u32[]{:S(2)}, u32[]{:S(2)}) collective-permute-start(f32[1,1024]{1,0:T(1,128)S(1)} %get-tuple-element.48), channel_id=1, source_target_pairs={{2,0},{3,1},{4,2},{5,3},{6,4},{7,5},{8,6},{9,7},{10,8},{11,9},{12,... | collective-permute-start | bytes 12296 | tf_op jit(solution)/shard_map/ppermute | solution.py:55
  35.7 7.2 %collective-permute-start.7 = (bf16[64,1024]{1,0:T(8,128)(2,1)S(1)}, bf16[64,1024]{1,0:T(8,128)(2,1)S(1)}, u32[]{:S(2)}, u32[]{:S(2)}) collective-permute-start(bf16[64,1024]{1,0:T(8,128)(2,1)S(1)} %get-tuple-element.50.value_ref.refs_0_), channel_id=1, source_target_pairs={{0,4},{1,13},{2,6},{3,15},{4,8},{5,1},{6,10},{7,3},{8,12},{9,5},{1... | collective-permute-start | bytes 393224 | tf_op jit(solution)/shard_map/ppermute | solution.py:46
  35.8 8.8 %collective-permute-start.11 = (bf16[64,1024]{1,0:T(8,128)(2,1)S(1)}, bf16[64,1024]{1,0:T(8,128)(2,1)S(1)}, u32[]{:S(2)}, u32[]{:S(2)}) collective-permute-start(bf16[64,1024]{1,0:T(8,128)(2,1)S(1)} %get-tuple-element.51.refs_12_), channel_id=1, source_target_pairs={{0,1},{1,0},{2,3},{3,2},{4,5},{5,4},{6,7},{7,6},{8,9},{9,8},{10,11... | collective-permute-start | bytes 393224 | tf_op jit(solution)/shard_map/ppermute | solution.py:46
  35.9 11.0 %collective-permute-start.13 = (bf16[256,384]{1,0:T(8,128)(2,1)S(1)}, bf16[256,384]{1,0:T(8,128)(2,1)S(1)}, u32[]{:S(2)}, u32[]{:S(2)}) collective-permute-start(bf16[256,384]{1,0:T(8,128)(2,1)S(1)} %get-tuple-element.52.refs_8_), channel_id=1, source_target_pairs={{0,32},{32,64},{64,96},{96,0},{128,160},{160,192},{192,224},{224,1... | collective-permute-start | bytes 589832 | tf_op jit(solution)/shard_map/ppermute | solution.py:125
  37.6 10.4 %collective-permute-start.14 = (bf16[256,384]{1,0:T(8,128)(2,1)S(1)}, bf16[256,384]{1,0:T(8,128)(2,1)S(1)}, u32[]{:S(2)}, u32[]{:S(2)}) collective-permute-start(bf16[256,384]{1,0:T(8,128)(2,1)S(1)} %get-tuple-element.52.refs_8_), channel_id=1, source_target_pairs={{0,96},{32,0},{64,32},{96,64},{128,224},{160,128},{192,160},{224,1... | collective-permute-start | bytes 589832 | tf_op jit(solution)/shard_map/ppermute | solution.py:125
  39.2 13.9 %collective-permute-start.15 = (bf16[256,384]{1,0:T(8,128)(2,1)S(1)}, bf16[256,384]{1,0:T(8,128)(2,1)S(1)}, u32[]{:S(2)}, u32[]{:S(2)}) collective-permute-start(bf16[256,384]{1,0:T(8,128)(2,1)S(1)} %get-tuple-element.52.refs_8_), channel_id=1, source_target_pairs={{0,64},{32,96},{64,0},{96,32},{128,192},{160,224},{192,128},{224,1... | collective-permute-start | bytes 589832 | tf_op jit(solution)/shard_map/ppermute | solution.py:125
  44.6 8.5 %collective-permute-start.12 = (bf16[64,1024]{1,0:T(8,128)(2,1)S(1)}, bf16[64,1024]{1,0:T(8,128)(2,1)S(1)}, u32[]{:S(2)}, u32[]{:S(2)}) collective-permute-start(bf16[64,1024]{1,0:T(8,128)(2,1)S(1)} %shard_map.87), channel_id=1, source_target_pairs={{0,4},{1,13},{2,6},{3,15},{4,8},{5,1},{6,10},{7,3},{8,12},{9,5},{1... | collective-permute-start | bytes 393224 | tf_op jit(solution)/shard_map/ppermute | solution.py:46
  57.0 20.2 %collective-permute-start.24 = (bf16[512,256]{1,0:T(8,128)(2,1)S(1)}, bf16[512,256]{1,0:T(8,128)(2,1)S(1)}, u32[]{:S(2)}, u32[]{:S(2)}) collective-permute-start(bf16[512,256]{1,0:T(8,128)(2,1)S(1)} %get-tuple-element.59.refs_9_), channel_id=1, source_target_pairs={{0,2},{1,3},{2,0},{3,1},{4,6},{5,7},{6,4},{7,5},{8,10},{9,11},{10,... | collective-permute-start | bytes 786440 | tf_op jit(solution)/shard_map/ppermute | solution.py:46
  57.2 19.9 %collective-permute-start.25 = (bf16[512,256]{1,0:T(8,128)(2,1)S(1)}, bf16[512,256]{1,0:T(8,128)(2,1)S(1)}, u32[]{:S(2)}, u32[]{:S(2)}) collective-permute-start(bf16[512,256]{1,0:T(8,128)(2,1)S(1)} %get-tuple-element.59.refs_9_), channel_id=1, source_target_pairs={{0,16},{1,17},{2,18},{3,19},{4,20},{5,21},{6,22},{7,23},{8,24},{9,... | collective-permute-start | bytes 786440 | tf_op jit(solution)/shard_map/ppermute | solution.py:46
  58.5 18.7 %collective-permute-start.26 = (bf16[512,256]{1,0:T(8,128)(2,1)S(1)}, bf16[512,256]{1,0:T(8,128)(2,1)S(1)}, u32[]{:S(2)}, u32[]{:S(2)}) collective-permute-start(bf16[512,256]{1,0:T(8,128)(2,1)S(1)} %get-tuple-element.59.refs_9_), channel_id=1, source_target_pairs={{0,18},{1,19},{2,16},{3,17},{4,22},{5,23},{6,20},{7,21},{8,26},{9,... | collective-permute-start | bytes 786440 | tf_op jit(solution)/shard_map/ppermute | solution.py:46
  59.8 10.1 %collective-permute-start.17 = (bf16[128,128]{1,0:T(8,128)(2,1)S(1)}, bf16[128,128]{1,0:T(8,128)(2,1)S(1)}, u32[]{:S(2)}, u32[]{:S(2)}) collective-permute-start(bf16[128,128]{1,0:T(8,128)(2,1)S(1)} %get-tuple-element.56), channel_id=1, source_target_pairs={{0,4},{1,5},{2,6},{3,7},{4,8},{5,9},{6,10},{7,11},{8,12},{9,13},{1... | collective-permute-start | bytes 98312 | tf_op jit(solution)/shard_map/ppermute | solution.py:46
  62.8 8.2 %collective-permute-start.18 = (bf16[128,128]{1,0:T(8,128)(2,1)S(1)}, bf16[128,128]{1,0:T(8,128)(2,1)S(1)}, u32[]{:S(2)}, u32[]{:S(2)}) collective-permute-start(bf16[128,128]{1,0:T(8,128)(2,1)S(1)} %get-tuple-element.57), channel_id=1, source_target_pairs={{0,8},{1,9},{2,10},{3,11},{4,12},{5,13},{6,14},{7,15},{8,0},{9,1},... | collective-permute-start | bytes 98312 | tf_op jit(solution)/shard_map/ppermute | solution.py:46
  81.6 13.5 %collective-permute-start.27 = (bf16[512,256]{1,0:T(8,128)(2,1)S(1)}, bf16[512,256]{1,0:T(8,128)(2,1)S(1)}, u32[]{:S(2)}, u32[]{:S(2)}) collective-permute-start(bf16[512,256]{1,0:T(8,128)(2,1)S(1)} %get-tuple-element.62), channel_id=1, source_target_pairs={{0,2},{1,3},{2,0},{3,1},{4,6},{5,7},{6,4},{7,5},{8,10},{9,11},{10,... | collective-permute-start | bytes 786440 | tf_op jit(solution)/shard_map/ppermute | solution.py:46
  82.6 21.2 %collective-permute-start.28 = (bf16[512,256]{1,0:T(8,128)(2,1)S(1)}, bf16[512,256]{1,0:T(8,128)(2,1)S(1)}, u32[]{:S(2)}, u32[]{:S(2)}) collective-permute-start(bf16[512,256]{1,0:T(8,128)(2,1)S(1)} %get-tuple-element.63), channel_id=1, source_target_pairs={{16,0},{17,1},{18,2},{19,3},{20,4},{21,5},{22,6},{23,7},{24,8},{25... | collective-permute-start | bytes 786440 | tf_op jit(solution)/shard_map/ppermute | solution.py:46
  92.4 11.5 %collective-permute-start.29 = (bf16[512,256]{1,0:T(8,128)(2,1)S(1)}, bf16[512,256]{1,0:T(8,128)(2,1)S(1)}, u32[]{:S(2)}, u32[]{:S(2)}) collective-permute-start(bf16[512,256]{1,0:T(8,128)(2,1)S(1)} %get-tuple-element.64), channel_id=1, source_target_pairs={{16,2},{17,3},{18,0},{19,1},{20,6},{21,7},{22,4},{23,5},{24,10},{2... | collective-permute-start | bytes 786440 | tf_op jit(solution)/shard_map/ppermute | solution.py:46
  106.7 7.4 %collective-permute-start.32 = (bf16[64,1024]{1,0:T(8,128)(2,1)S(1)}, bf16[64,1024]{1,0:T(8,128)(2,1)S(1)}, u32[]{:S(2)}, u32[]{:S(2)}) collective-permute-start(bf16[64,1024]{1,0:T(8,128)(2,1)S(1)} %get-tuple-element.74), channel_id=1, source_target_pairs={{0,12},{1,5},{2,14},{3,7},{4,0},{5,9},{6,2},{7,11},{8,4},{9,13},{1... | collective-permute-start | bytes 393224 | tf_op jit(solution)/shard_map/ppermute | solution.py:46
  108.0 8.8 %collective-permute-start.31 = (bf16[64,1024]{1,0:T(8,128)(2,1)S(1)}, bf16[64,1024]{1,0:T(8,128)(2,1)S(1)}, u32[]{:S(2)}, u32[]{:S(2)}) collective-permute-start(bf16[64,1024]{1,0:T(8,128)(2,1)S(1)} %get-tuple-element.72), channel_id=1, source_target_pairs={{0,13},{1,4},{2,15},{3,6},{4,1},{5,8},{6,3},{7,10},{8,5},{9,12},{1... | collective-permute-start | bytes 393224 | tf_op jit(solution)/shard_map/ppermute | solution.py:46
  120.5 10.0 %collective-permute-start.34 = (bf16[64,1024]{1,0:T(8,128)(2,1)S(1)}, bf16[64,1024]{1,0:T(8,128)(2,1)S(1)}, u32[]{:S(2)}, u32[]{:S(2)}) collective-permute-start(bf16[64,1024]{1,0:T(8,128)(2,1)S(1)} %divide_convert_fusion), channel_id=1, source_target_pairs={{1,2},{2,1},{3,4},{4,3},{5,6},{6,5},{7,8},{8,7},{9,10},{10,9},{11,... | collective-permute-start | bytes 393224 | tf_op jit(solution)/shard_map/ppermute | solution.py:51
  (19 other events, 114.3 us)
Sparse Core Ops, SparseCore 0:
  9.1 44.2 all-gather.2

commit v13 on v12

--- a/solution.py
+++ b/solution.py
@@ -377,54 +377,65 @@
     q_ref, here_refs, there_refs, blocks = refs[0], refs[1:5], refs[5:9], refs[9:13]
     dq_ref, outs, (kv, da_ref, dkt, dvt) = refs[13], refs[14:18], refs[18:]
     half, turn, pair, core = here()
-    queries, keys = q_ref.shape[0], kv.shape[0]
-    fill(kv, blocks)
-
+    queries = q_ref.shape[0]
     for which in range(CORES):
 
         @pl.when(core == which)
         def _(which=which):
             place_dattended(which, seg, here_refs, there_refs, da_ref)
 
-    spot = lax.broadcasted_iota(jnp.int32, (1, keys), 1)
-    block = spot // queries
-    key_half = jnp.where(block < 2, half, 1 - half)
-    key_pair = jnp.where(block % 2 == 0, pair, 1 - pair)
-    key_at = rows_at(spot % queries, key_half, turn, key_pair, core, seg)
     turn_up = math.log2(math.e) / math.sqrt(HEAD)
     scale = 1.0 / math.sqrt(HEAD)
-    k = kv[:, :HEAD]
-    v = kv[:, HEAD:]
-    for step in range(queries // tile):
-        rows = slice(step * tile, (step + 1) * tile)
-        query = lax.broadcasted_iota(jnp.int32, (tile, 1), 0) + step * tile
-        query_at = rows_at(query, half, turn, pair, core, seg)
-        q = q_ref[rows, :]
-        da = da_ref[rows, :]
-        score = jnp.where(key_at <= query_at, contract_last(q, k), NEG)
-        peak = jnp.max(score, axis=1, keepdims=True)
-        expo = jnp.exp2((score - peak) * turn_up)
-        probs = expo * (1.0 / jnp.sum(expo, axis=1, keepdims=True))
-        probs_b = probs.astype(jnp.bfloat16)
-        attended = jnp.dot(probs_b, v, preferred_element_type=F32).astype(jnp.bfloat16)
-        delta = jnp.sum(da.astype(F32) * attended.astype(F32), axis=1, keepdims=True)
-        dscore = (probs * (contract_last(da, v) - delta)).astype(jnp.bfloat16)
-        dq = jnp.dot(dscore, k, preferred_element_type=F32) * scale
-        dq_ref[rows, :] = dq.astype(jnp.bfloat16)
-        dk_part = contract_first(q, dscore)
-        dv_part = contract_first(da, probs_b)
-        if step == 0:
-            dkt[...] = dk_part
-            dvt[...] = dv_part
-        else:
-            dkt[...] += dk_part
-            dvt[...] += dv_part
-    at = 0
-    for out in outs:
-        lanes = slice(at, at + out.shape[0])
-        at += out.shape[0]
-        out[:, :HEAD] = (dkt[:, lanes] * scale).T.astype(jnp.bfloat16)
-        out[:, HEAD:] = dvt[:, lanes].T.astype(jnp.bfloat16)
+
+    def run(used):
+        keys = used * queries
+        fill(kv, blocks[:used])
+        near = 2 * queries
+        spot = lax.broadcasted_iota(jnp.int32, (1, near), 1)
+        key_pair = jnp.where(spot < queries, pair, 1 - pair)
+        key_at = rows_at(spot % queries, half, turn, key_pair, core, seg)
+        k = kv[:keys, :HEAD]
+        v = kv[:keys, HEAD:]
+        for step in range(queries // tile):
+            rows = slice(step * tile, (step + 1) * tile)
+            query = lax.broadcasted_iota(jnp.int32, (tile, 1), 0) + step * tile
+            query_at = rows_at(query, half, turn, pair, core, seg)
+            q = q_ref[rows, :]
+            da = da_ref[rows, :]
+            score = contract_last(q, k)
+            masked = jnp.where(key_at <= query_at, score[:, :near], NEG)
+            score = masked if used == 2 else jnp.concatenate([masked, score[:, near:]], axis=1)
+            peak = jnp.max(score, axis=1, keepdims=True)
+            expo = jnp.exp2((score - peak) * turn_up)
+            probs = expo * (1.0 / jnp.sum(expo, axis=1, keepdims=True))
+            probs_b = probs.astype(jnp.bfloat16)
+            attended = jnp.dot(probs_b, v, preferred_element_type=F32).astype(jnp.bfloat16)
+            delta = jnp.sum(da.astype(F32) * attended.astype(F32), axis=1, keepdims=True)
+            dscore = (probs * (contract_last(da, v) - delta)).astype(jnp.bfloat16)
+            dq = jnp.dot(dscore, k, preferred_element_type=F32) * scale
+            dq_ref[rows, :] = dq.astype(jnp.bfloat16)
+            dk_part = contract_first(q, dscore)
+            dv_part = contract_first(da, probs_b)
+            if step == 0:
+                dkt[:, :keys] = dk_part
+                dvt[:, :keys] = dv_part
+            else:
+                dkt[:, :keys] += dk_part
+                dvt[:, :keys] += dv_part
+        for i, out in enumerate(outs[:used]):
+            lanes = slice(i * queries, (i + 1) * queries)
+            out[:, :HEAD] = (dkt[:, lanes] * scale).T.astype(jnp.bfloat16)
+            out[:, HEAD:] = dvt[:, lanes].T.astype(jnp.bfloat16)
+
+    @pl.when(half == 0)
+    def _():
+        run(2)
+        for out in outs[2:]:
+            out[...] = jnp.zeros_like(out)
+
+    @pl.when(half == 1)
+    def _():
+        run(4)
 
 
 def attention(q, da_here, da_there, blocks, seg):
@@ -542,10 +553,11 @@
     dout_there = other_core(dout_b)
     pieces = gathered_rows(normin, [dout_there], weights[1:])
     q, own, w_full, *da = project(pieces, weights, (dout_b, dout_there), halves)
-    cross, far, beside = across(own, 0, True), across(own, 0, False), other_pair(own)
+    far, beside = across(own, 0, False), other_pair(own)
     da_here = [da[0]] + [
         moved(da[i], lambda h, t, p, k, i=i: (h, t + i, p, k)) for i in range(1, TURNS)
     ]
+    cross = across(passed_on(own, *da_here[1:]), 0, True)
     da_there = [other_core(piece) for piece in da_here]
     blocks = (own, beside, far, cross)
     dq, own, beside, far, cross = attention(q, da_here, da_there, blocks, seg)

time: 141 us -> 135 us (0.957)
  starting transfers between devices: 60.7 us -> 57 us
  waiting for transfers between devices: 49.6 us -> 47.5 us
    ppermute x28, starting transfers between devices: 30.8 us -> 25 us  [moved(): return lax.ppermute(value, 'ctx', pairs)]
    ppermute x3, starting transfers between devices: 22.2 us -> 24.3 us  [other_chip(): return lax.ppermute(value, 'ctx', pairs)]
  transfers between devices with their start and end apart: 37 -> 37, of which waited for: 19 -> 20; matrix products, arithmetic and copies ran while one was open for 0% -> 0% of each run, Pallas kernels for 1% -> 1%
where the time goes in v13:
time: 135 us; the launch traced here: 133 us
  starting transfers between devices  57 us (42%)
  waiting for transfers between devices  47.5 us (35%)
  between operations  13.8 us (10%)
  Pallas kernels  11.2 us (8%)
  matrix products  1.46 us (1%)
    ppermute x28, waiting for transfers between devices, moved(): return lax.ppermute(value, 'ctx', pairs)  32.7 us
    ppermute x28, starting transfers between devices, moved(): return lax.ppermute(value, 'ctx', pairs)  25 us
    ppermute x3, starting transfers between devices, other_chip(): return lax.ppermute(value, 'ctx', pairs)  24.3 us
    ppermute x3, waiting for transfers between devices, other_chip(): return lax.ppermute(value, 'ctx', pairs)  7.89 us
    ppermute x3, waiting for transfers between devices, shifted_y(): return lax.ppermute(value, 'dp', pairs)  6.88 us
    ppermute x3, starting transfers between devices, shifted_y(): return lax.ppermute(value, 'dp', pairs)  5.3 us
    pallas_call x1, Pallas kernels, attention(): pl.pallas_call(functools.partial(attention_kernel, 256, seg), out_shape=(...  4.3 us
  transfers between devices with their start and end apart: 37, of which 20 were waited for; matrix products, arithmetic and copies ran while one was open for 0% of the time, Pallas kernels for 1%

profile of v13, /device:TPU:6, one launch (start us, length us, event | category | flops | bytes accessed | tf_op | source)
XLA Modules:
  0.0 133.0 jit_solution(5019419929254646612)
XLA Ops:
  6.5 1.8 %shard_map.82 = (bf16[128,384]{1,0:T(8,128)(2,1)}, bf16[64,1024]{1,0:T(8,128)(2,1)}, s32[1,64]{1,0:T(1,128)}) custom-call(bf16[128,1024]{1,0:T(8,128)(2,1)} %q_ref.1, bf16[128,1024]{1,0:T(8,128)(2,1)} %k_ref.1, bf16[128,1024]{1,0:T(8,128)(2,1)} %v_ref.1, bf16[128,1024]{1,0:T(8,128)(2,1)} %o_ref.1, s32[1,64]{1,0:T(1,128)} %own_ref.1), custom_call_target="tpu_custom_call" | custom-call | tf_op jit(solution)/shard_map/pallas_call | solution.py:104
  8.4 8.7 %collective-permute-start = (s32[1,64]{1,0:T(1,128)}, s32[1,64]{1,0:T(1,128)S(1)}, u32[]{:S(2)}, u32[]{:S(2)}) collective-permute-start(s32[1,64]{1,0:T(1,128)} %get-tuple-element.41), channel_id=1, source_target_pairs={{1,2},{2,1},{3,4},{4,3},{5,6},{6,5},{7,8},{8,7},{9,10},{10,9},{11,... | collective-permute-start | bytes 776 | tf_op jit(solution)/shard_map/ppermute | solution.py:51
  19.8 1.7 %shard_map.83 = (bf16[64,2048]{1,0:T(8,128)(2,1)S(1)}, bf16[64,2048]{1,0:T(8,128)(2,1)S(1)}, f32[64,1024]{1,0:T(8,128)S(1)}, f32[64,1024]{1,0:T(8,128)S(1)}, f32[1,1024]{1,0:T(1,128)S(1)}) custom-call(s32[1,64]{1,0:T(1,128)S(1)} %copy-done.5, s32[1,64]{1,0:T(1,128)S(1)} %collective-permute-done.1.beside_ref, s32[1,64]{1,0:T(1,128)S(1)} %collective-permute-done.facing_ref, ...), custom_call_target="tpu_custom_call" | custom-call | tf_op jit(solution)/shard_map/pallas_call | solution.py:237
  21.6 7.1 %collective-permute-start.3 = (bf16[64,2048]{1,0:T(8,128)(2,1)S(1)}, bf16[64,2048]{1,0:T(8,128)(2,1)S(1)}, u32[]{:S(2)}, u32[]{:S(2)}) collective-permute-start(bf16[64,2048]{1,0:T(8,128)(2,1)S(1)} %get-tuple-element.43), channel_id=1, source_target_pairs={{1,2},{2,1},{3,4},{4,3},{5,6},{6,5},{7,8},{8,7},{9,10},{10,9},{11,... | collective-permute-start | bytes 786440 | tf_op jit(solution)/shard_map/ppermute | solution.py:51
  28.9 2.3 %collective-permute-start.5 = (f32[1,1024]{1,0:T(1,128)S(1)}, f32[1,1024]{1,0:T(1,128)S(1)}, u32[]{:S(2)}, u32[]{:S(2)}) collective-permute-start(f32[1,1024]{1,0:T(1,128)S(1)} %get-tuple-element.48), channel_id=1, source_target_pairs={{2,0},{3,1},{4,2},{5,3},{6,4},{7,5},{8,6},{9,7},{10,8},{11,9},{12,... | collective-permute-start | bytes 12296 | tf_op jit(solution)/shard_map/ppermute | solution.py:55
  31.3 4.1 %collective-permute-done.3.chip_ref = bf16[64,2048]{1,0:T(8,128)(2,1)S(1)} collective-permute-done((bf16[64,2048]{1,0:T(8,128)(2,1)S(1)}, bf16[64,2048]{1,0:T(8,128)(2,1)S(1)}, u32[]{:S(2)}, u32[]{:S(2)}) %collective-permute-start.3) | collective-permute-done | bytes 262176 | tf_op jit(solution)/shard_map/ppermute | solution.py:51
  39.2 2.0 %collective-permute-start.15 = (bf16[256,384]{1,0:T(8,128)(2,1)S(1)}, bf16[256,384]{1,0:T(8,128)(2,1)S(1)}, u32[]{:S(2)}, u32[]{:S(2)}) collective-permute-start(bf16[256,384]{1,0:T(8,128)(2,1)S(1)} %get-tuple-element.52.refs_8_), channel_id=1, source_target_pairs={{0,64},{32,96},{64,0},{96,32},{128,192},{160,224},{192,128},{224,1... | collective-permute-start | bytes 589832 | tf_op jit(solution)/shard_map/ppermute | solution.py:125
  42.8 1.8 %collective-permute-start.8 = (bf16[64,1024]{1,0:T(8,128)(2,1)S(1)}, bf16[64,1024]{1,0:T(8,128)(2,1)S(1)}, u32[]{:S(2)}, u32[]{:S(2)}) collective-permute-start(bf16[64,1024]{1,0:T(8,128)(2,1)S(1)} %shard_map.86), channel_id=1, source_target_pairs={{0,13},{1,4},{2,15},{3,6},{4,1},{5,8},{6,3},{7,10},{8,5},{9,12},{1... | collective-permute-start | bytes 393224 | tf_op jit(solution)/shard_map/ppermute | solution.py:46
  44.7 2.2 %collective-permute-done.13.refs_0_.refs_9_ = bf16[256,384]{1,0:T(8,128)(2,1)S(1)} collective-permute-done((bf16[256,384]{1,0:T(8,128)(2,1)S(1)}, bf16[256,384]{1,0:T(8,128)(2,1)S(1)}, u32[]{:S(2)}, u32[]{:S(2)}) %collective-permute-start.13) | collective-permute-done | bytes 196640 | tf_op jit(solution)/shard_map/ppermute | solution.py:125
  49.4 3.7 %collective-permute-done.15.refs_2_.refs_11_ = bf16[256,384]{1,0:T(8,128)(2,1)S(1)} collective-permute-done((bf16[256,384]{1,0:T(8,128)(2,1)S(1)}, bf16[256,384]{1,0:T(8,128)(2,1)S(1)}, u32[]{:S(2)}, u32[]{:S(2)}) %collective-permute-start.15) | collective-permute-done | bytes 196640 | tf_op jit(solution)/shard_map/ppermute | solution.py:125
  54.6 2.3 %shard_map.89 = (bf16[512,128]{1,0:T(8,128)(2,1)S(1)}, bf16[512,256]{1,0:T(8,128)(2,1)S(1)}, bf16[1024,384]{1,0:T(8,128)(2,1)S(1)}, bf16[128,128]{1,0:T(8,128)(2...) custom-call(bf16[64,1024]{1,0:T(8,128)(2,1)S(1)} %get-tuple-element.50.value_ref.r, ...), custom_call_target="tpu_custom_call" | custom-call | tf_op jit(solution)/shard_map/pallas_call | solution.py:348
  58.2 5.4 %collective-permute-start.18 = (bf16[128,128]{1,0:T(8,128)(2,1)S(1)}, bf16[128,128]{1,0:T(8,128)(2,1)S(1)}, u32[]{:S(2)}, u32[]{:S(2)}) collective-permute-start(bf16[128,128]{1,0:T(8,128)(2,1)S(1)} %get-tuple-element.57), channel_id=1, source_target_pairs={{0,8},{1,9},{2,10},{3,11},{4,12},{5,13},{6,14},{7,15},{8,0},{9,1},... | collective-permute-start | bytes 98312 | tf_op jit(solution)/shard_map/ppermute | solution.py:46
  63.6 2.3 %collective-permute-start.19 = (bf16[128,128]{1,0:T(8,128)(2,1)S(1)}, bf16[128,128]{1,0:T(8,128)(2,1)S(1)}, u32[]{:S(2)}, u32[]{:S(2)}) collective-permute-start(bf16[128,128]{1,0:T(8,128)(2,1)S(1)} %get-tuple-element.58), channel_id=1, source_target_pairs={{0,12},{1,13},{2,14},{3,15},{4,0},{5,1},{6,2},{7,3},{8,4},{9,5},{1... | collective-permute-start | bytes 98312 | tf_op jit(solution)/shard_map/ppermute | solution.py:46
  72.6 9.3 %collective-permute-done.25.refs_11_ = bf16[512,256]{1,0:T(8,128)(2,1)S(1)} collective-permute-done((bf16[512,256]{1,0:T(8,128)(2,1)S(1)}, bf16[512,256]{1,0:T(8,128)(2,1)S(1)}, u32[]{:S(2)}, u32[]{:S(2)}) %collective-permute-start.25) | collective-permute-done | bytes 262176 | tf_op jit(solution)/shard_map/ppermute | solution.py:46
  81.9 4.3 %shard_map.91 = (bf16[512,128]{1,0:T(8,128)(2,1)S(1)}, bf16[512,256]{1,0:T(8,128)(2,1)S(1)}, bf16[512,256]{1,0:T(8,128)(2,1)S(1)}, bf16[512,256]{1,0:T(8,128)(2,1)S(1)}, bf16[512,256]{1,0:T(8,128)(2,1)S(1)}) custom-call(bf16[512,128]{1,0:T(8,128)(2,1)S(1)} %get-tuple-element.54.refs_0_, bf16[128,128]{1,0:T(8,128)(2,1)S(1)} %get-tuple-element.55.refs_1_, ...), custom_call_target="tpu_custom_call" | custom-call | flops 1610612736 | bytes 2490368 | tf_op jit(solution)/shard_map/pallas_call | solution.py:445
  89.8 4.8 %collective-permute-done.27.refs_1_ = bf16[512,256]{1,0:T(8,128)(2,1)S(1)} collective-permute-done((bf16[512,256]{1,0:T(8,128)(2,1)S(1)}, bf16[512,256]{1,0:T(8,128)(2,1)S(1)}, u32[]{:S(2)}, u32[]{:S(2)}) %collective-permute-start.27) | collective-permute-done | bytes 262176 | tf_op jit(solution)/shard_map/ppermute | solution.py:46
  94.7 2.2 %collective-permute-done.28.refs_2_ = bf16[512,256]{1,0:T(8,128)(2,1)S(1)} collective-permute-done((bf16[512,256]{1,0:T(8,128)(2,1)S(1)}, bf16[512,256]{1,0:T(8,128)(2,1)S(1)}, u32[]{:S(2)}, u32[]{:S(2)}) %collective-permute-start.28) | collective-permute-done | bytes 262176 | tf_op jit(solution)/shard_map/ppermute | solution.py:46
  97.9 1.9 %collective-permute-done.30.swapped = bf16[256,1024]{1,0:T(8,128)(2,1)S(1)} collective-permute-done((bf16[256,1024]{1,0:T(8,128)(2,1)S(1)}, bf16[256,1024]{1,0:T(8,128)(2,1)S(1)}, u32[]{:S(2)}, u32[]{:S(2)}) %collective-permute-start.30) | collective-permute-done | bytes 524320 | tf_op jit(solution)/shard_map/ppermute | solution.py:46
  100.8 2.8 %collective-permute-start.31 = (bf16[64,1024]{1,0:T(8,128)(2,1)S(1)}, bf16[64,1024]{1,0:T(8,128)(2,1)S(1)}, u32[]{:S(2)}, u32[]{:S(2)}) collective-permute-start(bf16[64,1024]{1,0:T(8,128)(2,1)S(1)} %get-tuple-element.72), channel_id=1, source_target_pairs={{0,13},{1,4},{2,15},{3,6},{4,1},{5,8},{6,3},{7,10},{8,5},{9,12},{1... | collective-permute-start | bytes 393224 | tf_op jit(solution)/shard_map/ppermute | solution.py:46
  103.6 3.6 %collective-permute-done.32 = bf16[64,1024]{1,0:T(8,128)(2,1)S(1)} collective-permute-done((bf16[64,1024]{1,0:T(8,128)(2,1)S(1)}, bf16[64,1024]{1,0:T(8,128)(2,1)S(1)}, u32[]{:S(2)}, u32[]{:S(2)}) %collective-permute-start.32) | collective-permute-done | bytes 131104 | tf_op jit(solution)/shard_map/ppermute | solution.py:46
  107.2 1.8 %collective-permute-start.33 = (bf16[64,1024]{1,0:T(8,128)(2,1)S(1)}, bf16[64,1024]{1,0:T(8,128)(2,1)S(1)}, u32[]{:S(2)}, u32[]{:S(2)}) collective-permute-start(bf16[64,1024]{1,0:T(8,128)(2,1)S(1)} %add_convert_fusion.1), channel_id=1, source_target_pairs={{0,12},{1,5},{2,14},{3,7},{4,0},{5,9},{6,2},{7,11},{8,4},{9,13},{1... | collective-permute-start | bytes 393224 | tf_op jit(solution)/shard_map/ppermute | solution.py:46
  109.6 3.7 %collective-permute-done.33 = bf16[64,1024]{1,0:T(8,128)(2,1)S(1)} collective-permute-done((bf16[64,1024]{1,0:T(8,128)(2,1)S(1)}, bf16[64,1024]{1,0:T(8,128)(2,1)S(1)}, u32[]{:S(2)}, u32[]{:S(2)}) %collective-permute-start.33) | collective-permute-done | bytes 131104 | tf_op jit(solution)/shard_map/ppermute | solution.py:46
  113.6 8.5 %collective-permute-start.34 = (bf16[64,1024]{1,0:T(8,128)(2,1)S(1)}, bf16[64,1024]{1,0:T(8,128)(2,1)S(1)}, u32[]{:S(2)}, u32[]{:S(2)}) collective-permute-start(bf16[64,1024]{1,0:T(8,128)(2,1)S(1)} %divide_convert_fusion), channel_id=1, source_target_pairs={{1,2},{2,1},{3,4},{4,3},{5,6},{6,5},{7,8},{8,7},{9,10},{10,9},{11,... | collective-permute-start | bytes 393224 | tf_op jit(solution)/shard_map/ppermute | solution.py:51
  122.1 2.5 %collective-permute-done.34 = bf16[64,1024]{1,0:T(8,128)(2,1)S(1)} collective-permute-done((bf16[64,1024]{1,0:T(8,128)(2,1)S(1)}, bf16[64,1024]{1,0:T(8,128)(2,1)S(1)}, u32[]{:S(2)}, u32[]{:S(2)}) %collective-permute-start.34) | collective-permute-done | bytes 131104 | tf_op jit(solution)/shard_map/ppermute | solution.py:51
  (88 shorter events, 28.7 us)
Async XLA Ops:
  6.5 48.1 %all-gather.3.cloned.1.call-start = ((), (), s32[]{:S(2)}) async-start(), calls=%async_computation | async-start | bytes 1179648 | tf_op jit(solution)/shard_map/all_gather | solution.py:129
  8.3 8.9 %collective-permute-start.1 = (s32[1,64]{1,0:T(1,128)}, s32[1,64]{1,0:T(1,128)S(1)}, u32[]{:S(2)}, u32[]{:S(2)}) collective-permute-start(s32[1,64]{1,0:T(1,128)} %get-tuple-element.41), channel_id=1, source_target_pairs={{0,1},{1,0},{2,3},{3,2},{4,5},{5,4},{6,7},{7,6},{8,9},{9,8},{10,11... | collective-permute-start | bytes 776 | tf_op jit(solution)/shard_map/ppermute | solution.py:46
  8.4 10.1 %collective-permute-start = (s32[1,64]{1,0:T(1,128)}, s32[1,64]{1,0:T(1,128)S(1)}, u32[]{:S(2)}, u32[]{:S(2)}) collective-permute-start(s32[1,64]{1,0:T(1,128)} %get-tuple-element.41), channel_id=1, source_target_pairs={{1,2},{2,1},{3,4},{4,3},{5,6},{6,5},{7,8},{8,7},{9,10},{10,9},{11,... | collective-permute-start | bytes 776 | tf_op jit(solution)/shard_map/ppermute | solution.py:51
  17.1 14.2 %collective-permute-start.4 = (bf16[128,384]{1,0:T(8,128)(2,1)}, bf16[128,384]{1,0:T(8,128)(2,1)S(1)}, u32[]{:S(2)}, u32[]{:S(2)}) collective-permute-start(bf16[128,384]{1,0:T(8,128)(2,1)} %get-tuple-element.46.refs_0_), channel_id=1, source_target_pairs={{0,128},{32,160},{64,192},{96,224},{128,0},{160,32},{192,64},{224,... | collective-permute-start | bytes 294920 | tf_op jit(solution)/shard_map/ppermute | solution.py:120
  21.5 9.9 %collective-permute-start.2 = (bf16[64,2048]{1,0:T(8,128)(2,1)S(1)}, bf16[64,2048]{1,0:T(8,128)(2,1)S(1)}, u32[]{:S(2)}, u32[]{:S(2)}) collective-permute-start(bf16[64,2048]{1,0:T(8,128)(2,1)S(1)} %get-tuple-element.42), channel_id=1, source_target_pairs={{0,1},{1,0},{2,3},{3,2},{4,5},{5,4},{6,7},{7,6},{8,9},{9,8},{10,11... | collective-permute-start | bytes 786440 | tf_op jit(solution)/shard_map/ppermute | solution.py:46
  21.6 13.8 %collective-permute-start.3 = (bf16[64,2048]{1,0:T(8,128)(2,1)S(1)}, bf16[64,2048]{1,0:T(8,128)(2,1)S(1)}, u32[]{:S(2)}, u32[]{:S(2)}) collective-permute-start(bf16[64,2048]{1,0:T(8,128)(2,1)S(1)} %get-tuple-element.43), channel_id=1, source_target_pairs={{1,2},{2,1},{3,4},{4,3},{5,6},{6,5},{7,8},{8,7},{9,10},{10,9},{11,... | collective-permute-start | bytes 786440 | tf_op jit(solution)/shard_map/ppermute | solution.py:51
  28.9 6.9 %collective-permute-start.5 = (f32[1,1024]{1,0:T(1,128)S(1)}, f32[1,1024]{1,0:T(1,128)S(1)}, u32[]{:S(2)}, u32[]{:S(2)}) collective-permute-start(f32[1,1024]{1,0:T(1,128)S(1)} %get-tuple-element.48), channel_id=1, source_target_pairs={{2,0},{3,1},{4,2},{5,3},{6,4},{7,5},{8,6},{9,7},{10,8},{11,9},{12,... | collective-permute-start | bytes 12296 | tf_op jit(solution)/shard_map/ppermute | solution.py:55
  35.7 7.2 %collective-permute-start.7 = (bf16[64,1024]{1,0:T(8,128)(2,1)S(1)}, bf16[64,1024]{1,0:T(8,128)(2,1)S(1)}, u32[]{:S(2)}, u32[]{:S(2)}) collective-permute-start(bf16[64,1024]{1,0:T(8,128)(2,1)S(1)} %get-tuple-element.50.value_ref.refs_0_), channel_id=1, source_target_pairs={{0,4},{1,13},{2,6},{3,15},{4,8},{5,1},{6,10},{7,3},{8,12},{9,5},{1... | collective-permute-start | bytes 393224 | tf_op jit(solution)/shard_map/ppermute | solution.py:46
  35.8 8.8 %collective-permute-start.11 = (bf16[64,1024]{1,0:T(8,128)(2,1)S(1)}, bf16[64,1024]{1,0:T(8,128)(2,1)S(1)}, u32[]{:S(2)}, u32[]{:S(2)}) collective-permute-start(bf16[64,1024]{1,0:T(8,128)(2,1)S(1)} %get-tuple-element.51.refs_12_), channel_id=1, source_target_pairs={{0,1},{1,0},{2,3},{3,2},{4,5},{5,4},{6,7},{7,6},{8,9},{9,8},{10,11... | collective-permute-start | bytes 393224 | tf_op jit(solution)/shard_map/ppermute | solution.py:46
  35.9 11.0 %collective-permute-start.13 = (bf16[256,384]{1,0:T(8,128)(2,1)S(1)}, bf16[256,384]{1,0:T(8,128)(2,1)S(1)}, u32[]{:S(2)}, u32[]{:S(2)}) collective-permute-start(bf16[256,384]{1,0:T(8,128)(2,1)S(1)} %get-tuple-element.52.refs_8_), channel_id=1, source_target_pairs={{0,32},{32,64},{64,96},{96,0},{128,160},{160,192},{192,224},{224,1... | collective-permute-start | bytes 589832 | tf_op jit(solution)/shard_map/ppermute | solution.py:125
  37.6 10.4 %collective-permute-start.14 = (bf16[256,384]{1,0:T(8,128)(2,1)S(1)}, bf16[256,384]{1,0:T(8,128)(2,1)S(1)}, u32[]{:S(2)}, u32[]{:S(2)}) collective-permute-start(bf16[256,384]{1,0:T(8,128)(2,1)S(1)} %get-tuple-element.52.refs_8_), channel_id=1, source_target_pairs={{0,96},{32,0},{64,32},{96,64},{128,224},{160,128},{192,160},{224,1... | collective-permute-start | bytes 589832 | tf_op jit(solution)/shard_map/ppermute | solution.py:125
  39.2 13.9 %collective-permute-start.15 = (bf16[256,384]{1,0:T(8,128)(2,1)S(1)}, bf16[256,384]{1,0:T(8,128)(2,1)S(1)}, u32[]{:S(2)}, u32[]{:S(2)}) collective-permute-start(bf16[256,384]{1,0:T(8,128)(2,1)S(1)} %get-tuple-element.52.refs_8_), channel_id=1, source_target_pairs={{0,64},{32,96},{64,0},{96,32},{128,192},{160,224},{192,128},{224,1... | collective-permute-start | bytes 589832 | tf_op jit(solution)/shard_map/ppermute | solution.py:125
  44.6 8.5 %collective-permute-start.12 = (bf16[64,1024]{1,0:T(8,128)(2,1)S(1)}, bf16[64,1024]{1,0:T(8,128)(2,1)S(1)}, u32[]{:S(2)}, u32[]{:S(2)}) collective-permute-start(bf16[64,1024]{1,0:T(8,128)(2,1)S(1)} %shard_map.87), channel_id=1, source_target_pairs={{0,4},{1,13},{2,6},{3,15},{4,8},{5,1},{6,10},{7,3},{8,12},{9,5},{1... | collective-permute-start | bytes 393224 | tf_op jit(solution)/shard_map/ppermute | solution.py:46
  57.0 10.8 %collective-permute-start.17 = (bf16[128,128]{1,0:T(8,128)(2,1)S(1)}, bf16[128,128]{1,0:T(8,128)(2,1)S(1)}, u32[]{:S(2)}, u32[]{:S(2)}) collective-permute-start(bf16[128,128]{1,0:T(8,128)(2,1)S(1)} %get-tuple-element.56), channel_id=1, source_target_pairs={{0,4},{1,5},{2,6},{3,7},{4,8},{5,9},{6,10},{7,11},{8,12},{9,13},{1... | collective-permute-start | bytes 98312 | tf_op jit(solution)/shard_map/ppermute | solution.py:46
  58.2 9.6 %collective-permute-start.18 = (bf16[128,128]{1,0:T(8,128)(2,1)S(1)}, bf16[128,128]{1,0:T(8,128)(2,1)S(1)}, u32[]{:S(2)}, u32[]{:S(2)}) collective-permute-start(bf16[128,128]{1,0:T(8,128)(2,1)S(1)} %get-tuple-element.57), channel_id=1, source_target_pairs={{0,8},{1,9},{2,10},{3,11},{4,12},{5,13},{6,14},{7,15},{8,0},{9,1},... | collective-permute-start | bytes 98312 | tf_op jit(solution)/shard_map/ppermute | solution.py:46
  65.8 6.7 %collective-permute-start.24 = (bf16[512,256]{1,0:T(8,128)(2,1)S(1)}, bf16[512,256]{1,0:T(8,128)(2,1)S(1)}, u32[]{:S(2)}, u32[]{:S(2)}) collective-permute-start(bf16[512,256]{1,0:T(8,128)(2,1)S(1)} %get-tuple-element.59.value_ref.refs_9_), channel_id=1, source_target_pairs={{0,2},{1,3},{2,0},{3,1},{4,6},{5,7},{6,4},{7,5},{8,10},{9,11},{10,... | collective-permute-start | bytes 786440 | tf_op jit(solution)/shard_map/ppermute | solution.py:46
  66.5 15.4 %collective-permute-start.25 = (bf16[512,256]{1,0:T(8,128)(2,1)S(1)}, bf16[512,256]{1,0:T(8,128)(2,1)S(1)}, u32[]{:S(2)}, u32[]{:S(2)}) collective-permute-start(bf16[512,256]{1,0:T(8,128)(2,1)S(1)} %get-tuple-element.59.value_ref.refs_9_), channel_id=1, source_target_pairs={{0,16},{1,17},{2,18},{3,19},{4,20},{5,21},{6,22},{7,23},{8,24},{9,... | collective-permute-start | bytes 786440 | tf_op jit(solution)/shard_map/ppermute | solution.py:46
  68.6 13.3 %collective-permute-start.26 = (bf16[512,256]{1,0:T(8,128)(2,1)S(1)}, bf16[512,256]{1,0:T(8,128)(2,1)S(1)}, u32[]{:S(2)}, u32[]{:S(2)}) collective-permute-start(bf16[512,256]{1,0:T(8,128)(2,1)S(1)} %shard_map.90), channel_id=1, source_target_pairs={{0,18},{1,19},{2,16},{3,17},{4,22},{5,23},{6,20},{7,21},{8,26},{9,... | collective-permute-start | bytes 786440 | tf_op jit(solution)/shard_map/ppermute | solution.py:46
  86.2 8.5 %collective-permute-start.27 = (bf16[512,256]{1,0:T(8,128)(2,1)S(1)}, bf16[512,256]{1,0:T(8,128)(2,1)S(1)}, u32[]{:S(2)}, u32[]{:S(2)}) collective-permute-start(bf16[512,256]{1,0:T(8,128)(2,1)S(1)} %get-tuple-element.62), channel_id=1, source_target_pairs={{0,2},{1,3},{2,0},{3,1},{4,6},{5,7},{6,4},{7,5},{8,10},{9,11},{10,... | collective-permute-start | bytes 786440 | tf_op jit(solution)/shard_map/ppermute | solution.py:46
  87.2 9.6 %collective-permute-start.28 = (bf16[512,256]{1,0:T(8,128)(2,1)S(1)}, bf16[512,256]{1,0:T(8,128)(2,1)S(1)}, u32[]{:S(2)}, u32[]{:S(2)}) collective-permute-start(bf16[512,256]{1,0:T(8,128)(2,1)S(1)} %get-tuple-element.63), channel_id=1, source_target_pairs={{16,0},{17,1},{18,2},{19,3},{20,4},{21,5},{22,6},{23,7},{24,8},{25... | collective-permute-start | bytes 786440 | tf_op jit(solution)/shard_map/ppermute | solution.py:46
  88.5 8.3 %collective-permute-start.29 = (bf16[512,256]{1,0:T(8,128)(2,1)S(1)}, bf16[512,256]{1,0:T(8,128)(2,1)S(1)}, u32[]{:S(2)}, u32[]{:S(2)}) collective-permute-start(bf16[512,256]{1,0:T(8,128)(2,1)S(1)} %get-tuple-element.64), channel_id=1, source_target_pairs={{16,2},{17,3},{18,0},{19,1},{20,6},{21,7},{22,4},{23,5},{24,10},{2... | collective-permute-start | bytes 786440 | tf_op jit(solution)/shard_map/ppermute | solution.py:46
  99.9 7.3 %collective-permute-start.32 = (bf16[64,1024]{1,0:T(8,128)(2,1)S(1)}, bf16[64,1024]{1,0:T(8,128)(2,1)S(1)}, u32[]{:S(2)}, u32[]{:S(2)}) collective-permute-start(bf16[64,1024]{1,0:T(8,128)(2,1)S(1)} %get-tuple-element.74), channel_id=1, source_target_pairs={{0,12},{1,5},{2,14},{3,7},{4,0},{5,9},{6,2},{7,11},{8,4},{9,13},{1... | collective-permute-start | bytes 393224 | tf_op jit(solution)/shard_map/ppermute | solution.py:46
  100.8 8.8 %collective-permute-start.31 = (bf16[64,1024]{1,0:T(8,128)(2,1)S(1)}, bf16[64,1024]{1,0:T(8,128)(2,1)S(1)}, u32[]{:S(2)}, u32[]{:S(2)}) collective-permute-start(bf16[64,1024]{1,0:T(8,128)(2,1)S(1)} %get-tuple-element.72), channel_id=1, source_target_pairs={{0,13},{1,4},{2,15},{3,6},{4,1},{5,8},{6,3},{7,10},{8,5},{9,12},{1... | collective-permute-start | bytes 393224 | tf_op jit(solution)/shard_map/ppermute | solution.py:46
  113.6 11.1 %collective-permute-start.34 = (bf16[64,1024]{1,0:T(8,128)(2,1)S(1)}, bf16[64,1024]{1,0:T(8,128)(2,1)S(1)}, u32[]{:S(2)}, u32[]{:S(2)}) collective-permute-start(bf16[64,1024]{1,0:T(8,128)(2,1)S(1)} %divide_convert_fusion), channel_id=1, source_target_pairs={{1,2},{2,1},{3,4},{4,3},{5,6},{6,5},{7,8},{8,7},{9,10},{10,9},{11,... | collective-permute-start | bytes 393224 | tf_op jit(solution)/shard_map/ppermute | solution.py:51
  (19 other events, 112.4 us)
Sparse Core Ops, SparseCore 0:
  9.1 44.2 all-gather.2

commit v14 on v13

--- a/solution.py
+++ b/solution.py
@@ -86,33 +86,46 @@
     return lax.dot_general(left, right, (((0,), (0,)), ((), ())), preferred_element_type=F32)
 
 
-def cut_kernel(q_ref, k_ref, v_ref, o_ref, start_ref, out_ref, half_ref, start_out, sems):
+def half_kernel(o_ref, start_ref, half_ref, start_out, sems):
+    half = half_ref.shape[0]
+    at = pl.multiple_of(here()[3] * half, half)
+    fetched([(o_ref.at[pl.ds(at, half), :], half_ref), (start_ref, start_out)], sems)
+
+
+def cut_rows(w_out, starts):
+    rows, width = w_out.shape
+    return pl.pallas_call(
+        half_kernel,
+        out_shape=(
+            jax.ShapeDtypeStruct((rows // CORES, width), w_out.dtype),
+            jax.ShapeDtypeStruct(starts.shape, starts.dtype),
+        ),
+        in_specs=[HBM, ANY],
+        out_specs=(VMEM, VMEM),
+        scratch_shapes=[pltpu.SemaphoreType.DMA((2,))],
+        compiler_params=room(60),
+    )(w_out, starts)
+
+
+def cut_kernel(q_ref, k_ref, v_ref, ready_ref, out_ref, sems):
     _, turn, _, core = here()
     lane = pl.multiple_of((turn * CORES + core) * HEAD, HEAD)
     copies = [
         (w.at[:, pl.ds(lane, HEAD)], out_ref.at[:, i * HEAD : (i + 1) * HEAD])
         for i, w in enumerate((q_ref, k_ref, v_ref))
     ]
-    half = half_ref.shape[0]
-    copies.append((o_ref.at[pl.ds(pl.multiple_of(core * half, half), half), :], half_ref))
-    copies.append((start_ref, start_out))
     fetched(copies, sems)
 
 
-def cut_weights(w_query, w_key, w_value, w_out, starts):
-    rows, width = w_out.shape
+def cut_columns(w_query, w_key, w_value, ready):
     return pl.pallas_call(
         cut_kernel,
-        out_shape=(
-            jax.ShapeDtypeStruct((rows, 3 * HEAD), w_query.dtype),
-            jax.ShapeDtypeStruct((rows // CORES, width), w_out.dtype),
-            jax.ShapeDtypeStruct(starts.shape, starts.dtype),
-        ),
-        in_specs=[HBM] * 4 + [ANY],
-        out_specs=(VMEM, VMEM, VMEM),
-        scratch_shapes=[pltpu.SemaphoreType.DMA((5,))],
+        out_shape=jax.ShapeDtypeStruct((w_query.shape[0], 3 * HEAD), w_query.dtype),
+        in_specs=[HBM] * 3 + [ANY],
+        out_specs=VMEM,
+        scratch_shapes=[pltpu.SemaphoreType.DMA((3,))],
         compiler_params=room(60),
-    )(w_query, w_key, w_value, w_out, starts)
+    )(w_query, w_key, w_value, ready)
 
 
 def other_x(value):
@@ -145,14 +158,15 @@
 
 def gathered_rows(shard, first_ready, last_ready):
     near = turned(shard, 1)
-    next_to = turned_over(passed_on(shard, near))
-    far = passed_on(turned(passed_on(near, *first_ready), 1), *last_ready)
+    near_there = other_core(near)
+    next_to = turned_over(passed_on(shard, near, *first_ready))
+    far = passed_on(turned(near, 1), *last_ready)
     return [
         shard,
         other_core(shard),
         near,
         next_to,
-        other_core(near),
+        near_there,
         other_core(next_to),
         far,
         other_core(far),
@@ -521,7 +535,8 @@
     length = rows * CTX
     ctx, core = lax.axis_index("ctx"), here()[3]
 
-    mine, half, own_starts = cut_weights(w_query, w_key, w_value, w_out, starts)
+    half, own_starts = cut_rows(w_out, starts)
+    mine = cut_columns(w_query, w_key, w_value, own_starts)
     halves = gathered_halves(half)
     theirs = other_x(mine)
     beside, facing = other_core(own_starts), other_chip(own_starts)

time: 135 us -> 135 us (level)
  starting transfers between devices: 57 us -> 54.4 us
  waiting for transfers between devices: 47.5 us -> 49.9 us
  Pallas kernels: 11.2 us -> 12.6 us
    ppermute x3, starting transfers between devices: 24.3 us -> 21.6 us  [other_chip(): return lax.ppermute(value, 'ctx', pairs)]
    ppermute x28, waiting for transfers between devices: 32.7 us -> 34.9 us  [moved(): return lax.ppermute(value, 'ctx', pairs)]
    pallas_call x1 -> x2, Pallas kernels: 1.77 us -> 3.14 us  [the longest x1 1.67 us: cut_rows(): pl.pallas_call(half_kernel, out_shape=(jax.ShapeDtypeStruct((rows // CORE...]
  transfers between devices with their start and end apart: 37 -> 37, of which waited for: 20 -> 18; matrix products, arithmetic and copies ran while one was open for 0% -> 0% of each run, Pallas kernels for 1% -> 3%
where the time goes in v14:
time: 135 us; the launch traced here: 134 us
  starting transfers between devices  54.4 us (40%)
  waiting for transfers between devices  49.9 us (37%)
  between operations  13.8 us (10%)
  Pallas kernels  12.6 us (9%)
  matrix products  1.46 us (1%)
    ppermute x28, waiting for transfers between devices, moved(): return lax.ppermute(value, 'ctx', pairs)  34.9 us
    ppermute x28, starting transfers between devices, moved(): return lax.ppermute(value, 'ctx', pairs)  25.1 us
    ppermute x3, starting transfers between devices, other_chip(): return lax.ppermute(value, 'ctx', pairs)  21.6 us
    ppermute x3, waiting for transfers between devices, other_chip(): return lax.ppermute(value, 'ctx', pairs)  7.95 us
    ppermute x3, waiting for transfers between devices, shifted_y(): return lax.ppermute(value, 'dp', pairs)  7.04 us
    ppermute x3, starting transfers between devices, shifted_y(): return lax.ppermute(value, 'dp', pairs)  5.29 us
    pallas_call x1, Pallas kernels, attention(): pl.pallas_call(functools.partial(attention_kernel, 256, seg), out_shape=(...  4.29 us
  transfers between devices with their start and end apart: 37, of which 18 were waited for; matrix products, arithmetic and copies ran while one was open for 0% of the time, Pallas kernels for 3%

profile of v14, /device:TPU:6, one launch (start us, length us, event | category | flops | bytes accessed | tf_op | source)
XLA Modules:
  0.0 134.2 jit_solution(797895322617337537)
XLA Ops:
  6.5 1.7 %shard_map.82 = (bf16[64,1024]{1,0:T(8,128)(2,1)}, s32[1,64]{1,0:T(1,128)}) custom-call(bf16[128,1024]{1,0:T(8,128)(2,1)} %o_ref.1, s32[1,64]{1,0:T(1,128)} %own_ref.1), custom_call_target="tpu_custom_call" | custom-call | tf_op jit(solution)/shard_map/pallas_call | solution.py:97
  8.3 8.7 %collective-permute-start = (s32[1,64]{1,0:T(1,128)}, s32[1,64]{1,0:T(1,128)S(1)}, u32[]{:S(2)}, u32[]{:S(2)}) collective-permute-start(s32[1,64]{1,0:T(1,128)} %get-tuple-element.40.ready_ref), channel_id=1, source_target_pairs={{1,2},{2,1},{3,4},{4,3},{5,6},{6,5},{7,8},{8,7},{9,10},{10,9},{11,... | collective-permute-start | bytes 776 | tf_op jit(solution)/shard_map/ppermute | solution.py:51
  19.9 1.7 %shard_map.83 = (bf16[64,2048]{1,0:T(8,128)(2,1)S(1)}, bf16[64,2048]{1,0:T(8,128)(2,1)S(1)}, f32[64,1024]{1,0:T(8,128)S(1)}, f32[64,1024]{1,0:T(8,128)S(1)}, f32[1,1024]{1,0:T(1,128)S(1)}) custom-call(s32[1,64]{1,0:T(1,128)S(1)} %copy-done.5, s32[1,64]{1,0:T(1,128)S(1)} %collective-permute-done.1.beside_ref, s32[1,64]{1,0:T(1,128)S(1)} %collective-permute-done.facing_ref, ...), custom_call_target="tpu_custom_call" | custom-call | tf_op jit(solution)/shard_map/pallas_call | solution.py:251
  21.7 6.9 %collective-permute-start.3 = (bf16[64,2048]{1,0:T(8,128)(2,1)S(1)}, bf16[64,2048]{1,0:T(8,128)(2,1)S(1)}, u32[]{:S(2)}, u32[]{:S(2)}) collective-permute-start(bf16[64,2048]{1,0:T(8,128)(2,1)S(1)} %get-tuple-element.42), channel_id=1, source_target_pairs={{1,2},{2,1},{3,4},{4,3},{5,6},{6,5},{7,8},{8,7},{9,10},{10,9},{11,... | collective-permute-start | bytes 786440 | tf_op jit(solution)/shard_map/ppermute | solution.py:51
  28.8 2.3 %collective-permute-start.5 = (f32[1,1024]{1,0:T(1,128)S(1)}, f32[1,1024]{1,0:T(1,128)S(1)}, u32[]{:S(2)}, u32[]{:S(2)}) collective-permute-start(f32[1,1024]{1,0:T(1,128)S(1)} %get-tuple-element.46), channel_id=1, source_target_pairs={{2,0},{3,1},{4,2},{5,3},{6,4},{7,5},{8,6},{9,7},{10,8},{11,9},{12,... | collective-permute-start | bytes 12296 | tf_op jit(solution)/shard_map/ppermute | solution.py:55
  31.3 4.1 %collective-permute-done.3.chip_ref = bf16[64,2048]{1,0:T(8,128)(2,1)S(1)} collective-permute-done((bf16[64,2048]{1,0:T(8,128)(2,1)S(1)}, bf16[64,2048]{1,0:T(8,128)(2,1)S(1)}, u32[]{:S(2)}, u32[]{:S(2)}) %collective-permute-start.3) | collective-permute-done | bytes 262176 | tf_op jit(solution)/shard_map/ppermute | solution.py:51
  37.5 1.7 %collective-permute-start.14 = (bf16[256,384]{1,0:T(8,128)(2,1)S(1)}, bf16[256,384]{1,0:T(8,128)(2,1)S(1)}, u32[]{:S(2)}, u32[]{:S(2)}) collective-permute-start(bf16[256,384]{1,0:T(8,128)(2,1)S(1)} %get-tuple-element.50.refs_8_), channel_id=1, source_target_pairs={{0,96},{32,0},{64,32},{96,64},{128,224},{160,128},{192,160},{224,1... | collective-permute-start | bytes 589832 | tf_op jit(solution)/shard_map/ppermute | solution.py:138
  39.1 2.0 %collective-permute-start.15 = (bf16[256,384]{1,0:T(8,128)(2,1)S(1)}, bf16[256,384]{1,0:T(8,128)(2,1)S(1)}, u32[]{:S(2)}, u32[]{:S(2)}) collective-permute-start(bf16[256,384]{1,0:T(8,128)(2,1)S(1)} %get-tuple-element.50.refs_8_), channel_id=1, source_target_pairs={{0,64},{32,96},{64,0},{96,32},{128,192},{160,224},{192,128},{224,1... | collective-permute-start | bytes 589832 | tf_op jit(solution)/shard_map/ppermute | solution.py:138
  42.8 1.8 %collective-permute-start.9 = (bf16[64,1024]{1,0:T(8,128)(2,1)S(1)}, bf16[64,1024]{1,0:T(8,128)(2,1)S(1)}, u32[]{:S(2)}, u32[]{:S(2)}) collective-permute-start(bf16[64,1024]{1,0:T(8,128)(2,1)S(1)} %shard_map.87), channel_id=1, source_target_pairs={{0,13},{1,4},{2,15},{3,6},{4,1},{5,8},{6,3},{7,10},{8,5},{9,12},{1... | collective-permute-start | bytes 393224 | tf_op jit(solution)/shard_map/ppermute | solution.py:46
  44.5 3.1 %collective-permute-done.13.refs_0_.refs_9_ = bf16[256,384]{1,0:T(8,128)(2,1)S(1)} collective-permute-done((bf16[256,384]{1,0:T(8,128)(2,1)S(1)}, bf16[256,384]{1,0:T(8,128)(2,1)S(1)}, u32[]{:S(2)}, u32[]{:S(2)}) %collective-permute-start.13) | collective-permute-done | bytes 196640 | tf_op jit(solution)/shard_map/ppermute | solution.py:138
  49.3 3.8 %collective-permute-done.15.refs_2_.refs_11_ = bf16[256,384]{1,0:T(8,128)(2,1)S(1)} collective-permute-done((bf16[256,384]{1,0:T(8,128)(2,1)S(1)}, bf16[256,384]{1,0:T(8,128)(2,1)S(1)}, u32[]{:S(2)}, u32[]{:S(2)}) %collective-permute-start.15) | collective-permute-done | bytes 196640 | tf_op jit(solution)/shard_map/ppermute | solution.py:138
  54.6 2.3 %shard_map.89 = (bf16[512,128]{1,0:T(8,128)(2,1)S(1)}, bf16[512,256]{1,0:T(8,128)(2,1)S(1)}, bf16[1024,384]{1,0:T(8,128)(2,1)S(1)}, bf16[128,128]{1,0:T(8,128)(2...) custom-call(bf16[64,1024]{1,0:T(8,128)(2,1)S(1)} %get-tuple-element.48.value_ref.r, ...), custom_call_target="tpu_custom_call" | custom-call | tf_op jit(solution)/shard_map/pallas_call | solution.py:362
  58.2 5.3 %collective-permute-start.18 = (bf16[128,128]{1,0:T(8,128)(2,1)S(1)}, bf16[128,128]{1,0:T(8,128)(2,1)S(1)}, u32[]{:S(2)}, u32[]{:S(2)}) collective-permute-start(bf16[128,128]{1,0:T(8,128)(2,1)S(1)} %get-tuple-element.55), channel_id=1, source_target_pairs={{0,8},{1,9},{2,10},{3,11},{4,12},{5,13},{6,14},{7,15},{8,0},{9,1},... | collective-permute-start | bytes 98312 | tf_op jit(solution)/shard_map/ppermute | solution.py:46
  63.5 2.4 %collective-permute-start.19 = (bf16[128,128]{1,0:T(8,128)(2,1)S(1)}, bf16[128,128]{1,0:T(8,128)(2,1)S(1)}, u32[]{:S(2)}, u32[]{:S(2)}) collective-permute-start(bf16[128,128]{1,0:T(8,128)(2,1)S(1)} %get-tuple-element.56), channel_id=1, source_target_pairs={{0,12},{1,13},{2,14},{3,15},{4,0},{5,1},{6,2},{7,3},{8,4},{9,5},{1... | collective-permute-start | bytes 98312 | tf_op jit(solution)/shard_map/ppermute | solution.py:46
  72.6 9.3 %collective-permute-done.25.refs_11_ = bf16[512,256]{1,0:T(8,128)(2,1)S(1)} collective-permute-done((bf16[512,256]{1,0:T(8,128)(2,1)S(1)}, bf16[512,256]{1,0:T(8,128)(2,1)S(1)}, u32[]{:S(2)}, u32[]{:S(2)}) %collective-permute-start.25) | collective-permute-done | bytes 262176 | tf_op jit(solution)/shard_map/ppermute | solution.py:46
  81.9 4.3 %shard_map.91 = (bf16[512,128]{1,0:T(8,128)(2,1)S(1)}, bf16[512,256]{1,0:T(8,128)(2,1)S(1)}, bf16[512,256]{1,0:T(8,128)(2,1)S(1)}, bf16[512,256]{1,0:T(8,128)(2,1)S(1)}, bf16[512,256]{1,0:T(8,128)(2,1)S(1)}) custom-call(bf16[512,128]{1,0:T(8,128)(2,1)S(1)} %get-tuple-element.52.refs_0_, bf16[128,128]{1,0:T(8,128)(2,1)S(1)} %get-tuple-element.53.refs_1_, ...), custom_call_target="tpu_custom_call" | custom-call | flops 1610612736 | bytes 2490368 | tf_op jit(solution)/shard_map/pallas_call | solution.py:459
  89.7 4.6 %collective-permute-done.27.refs_1_ = bf16[512,256]{1,0:T(8,128)(2,1)S(1)} collective-permute-done((bf16[512,256]{1,0:T(8,128)(2,1)S(1)}, bf16[512,256]{1,0:T(8,128)(2,1)S(1)}, u32[]{:S(2)}, u32[]{:S(2)}) %collective-permute-start.27) | collective-permute-done | bytes 262176 | tf_op jit(solution)/shard_map/ppermute | solution.py:46
  96.0 1.9 %collective-permute-done.30.swapped = bf16[256,1024]{1,0:T(8,128)(2,1)S(1)} collective-permute-done((bf16[256,1024]{1,0:T(8,128)(2,1)S(1)}, bf16[256,1024]{1,0:T(8,128)(2,1)S(1)}, u32[]{:S(2)}, u32[]{:S(2)}) %collective-permute-start.30) | collective-permute-done | bytes 524320 | tf_op jit(solution)/shard_map/ppermute | solution.py:46
  98.0 2.9 %collective-permute-start.32 = (bf16[64,1024]{1,0:T(8,128)(2,1)S(1)}, bf16[64,1024]{1,0:T(8,128)(2,1)S(1)}, u32[]{:S(2)}, u32[]{:S(2)}) collective-permute-start(bf16[64,1024]{1,0:T(8,128)(2,1)S(1)} %get-tuple-element.72), channel_id=1, source_target_pairs={{0,12},{1,5},{2,14},{3,7},{4,0},{5,9},{6,2},{7,11},{8,4},{9,13},{1... | collective-permute-start | bytes 393224 | tf_op jit(solution)/shard_map/ppermute | solution.py:46
  101.7 5.9 %collective-permute-done.32 = bf16[64,1024]{1,0:T(8,128)(2,1)S(1)} collective-permute-done((bf16[64,1024]{1,0:T(8,128)(2,1)S(1)}, bf16[64,1024]{1,0:T(8,128)(2,1)S(1)}, u32[]{:S(2)}, u32[]{:S(2)}) %collective-permute-start.32) | collective-permute-done | bytes 131104 | tf_op jit(solution)/shard_map/ppermute | solution.py:46
  107.6 1.7 %collective-permute-start.33 = (bf16[64,1024]{1,0:T(8,128)(2,1)S(1)}, bf16[64,1024]{1,0:T(8,128)(2,1)S(1)}, u32[]{:S(2)}, u32[]{:S(2)}) collective-permute-start(bf16[64,1024]{1,0:T(8,128)(2,1)S(1)} %add_convert_fusion.1), channel_id=1, source_target_pairs={{0,12},{1,5},{2,14},{3,7},{4,0},{5,9},{6,2},{7,11},{8,4},{9,13},{1... | collective-permute-start | bytes 393224 | tf_op jit(solution)/shard_map/ppermute | solution.py:46
  109.3 6.2 %collective-permute-done.33 = bf16[64,1024]{1,0:T(8,128)(2,1)S(1)} collective-permute-done((bf16[64,1024]{1,0:T(8,128)(2,1)S(1)}, bf16[64,1024]{1,0:T(8,128)(2,1)S(1)}, u32[]{:S(2)}, u32[]{:S(2)}) %collective-permute-start.33) | collective-permute-done | bytes 131104 | tf_op jit(solution)/shard_map/ppermute | solution.py:46
  115.8 6.0 %collective-permute-start.34 = (bf16[64,1024]{1,0:T(8,128)(2,1)S(1)}, bf16[64,1024]{1,0:T(8,128)(2,1)S(1)}, u32[]{:S(2)}, u32[]{:S(2)}) collective-permute-start(bf16[64,1024]{1,0:T(8,128)(2,1)S(1)} %divide_convert_fusion), channel_id=1, source_target_pairs={{1,2},{2,1},{3,4},{4,3},{5,6},{6,5},{7,8},{8,7},{9,10},{10,9},{11,... | collective-permute-start | bytes 393224 | tf_op jit(solution)/shard_map/ppermute | solution.py:51
  122.0 3.9 %collective-permute-done.34 = bf16[64,1024]{1,0:T(8,128)(2,1)S(1)} collective-permute-done((bf16[64,1024]{1,0:T(8,128)(2,1)S(1)}, bf16[64,1024]{1,0:T(8,128)(2,1)S(1)}, u32[]{:S(2)}, u32[]{:S(2)}) %collective-permute-start.34) | collective-permute-done | bytes 131104 | tf_op jit(solution)/shard_map/ppermute | solution.py:51
  (88 shorter events, 26.2 us)
Async XLA Ops:
  6.5 48.0 %all-gather.3.cloned.1.call-start = ((), (), s32[]{:S(2)}) async-start(), calls=%async_computation | async-start | bytes 1179648 | tf_op jit(solution)/shard_map/all_gather | solution.py:142
  8.2 10.4 %collective-permute-start.1 = (s32[1,64]{1,0:T(1,128)}, s32[1,64]{1,0:T(1,128)S(1)}, u32[]{:S(2)}, u32[]{:S(2)}) collective-permute-start(s32[1,64]{1,0:T(1,128)} %get-tuple-element.40.ready_ref), channel_id=1, source_target_pairs={{0,1},{1,0},{2,3},{3,2},{4,5},{5,4},{6,7},{7,6},{8,9},{9,8},{10,11... | collective-permute-start | bytes 776 | tf_op jit(solution)/shard_map/ppermute | solution.py:46
  8.3 10.3 %collective-permute-start = (s32[1,64]{1,0:T(1,128)}, s32[1,64]{1,0:T(1,128)S(1)}, u32[]{:S(2)}, u32[]{:S(2)}) collective-permute-start(s32[1,64]{1,0:T(1,128)} %get-tuple-element.40.ready_ref), channel_id=1, source_target_pairs={{1,2},{2,1},{3,4},{4,3},{5,6},{6,5},{7,8},{8,7},{9,10},{10,9},{11,... | collective-permute-start | bytes 776 | tf_op jit(solution)/shard_map/ppermute | solution.py:51
  18.5 12.7 %collective-permute-start.4 = (bf16[128,384]{1,0:T(8,128)(2,1)}, bf16[128,384]{1,0:T(8,128)(2,1)S(1)}, u32[]{:S(2)}, u32[]{:S(2)}) collective-permute-start(bf16[128,384]{1,0:T(8,128)(2,1)} %shard_map.84.refs_0_), channel_id=1, source_target_pairs={{0,128},{32,160},{64,192},{96,224},{128,0},{160,32},{192,64},{224,... | collective-permute-start | bytes 294920 | tf_op jit(solution)/shard_map/ppermute | solution.py:133
  21.6 9.7 %collective-permute-start.2 = (bf16[64,2048]{1,0:T(8,128)(2,1)S(1)}, bf16[64,2048]{1,0:T(8,128)(2,1)S(1)}, u32[]{:S(2)}, u32[]{:S(2)}) collective-permute-start(bf16[64,2048]{1,0:T(8,128)(2,1)S(1)} %get-tuple-element.41), channel_id=1, source_target_pairs={{0,1},{1,0},{2,3},{3,2},{4,5},{5,4},{6,7},{7,6},{8,9},{9,8},{10,11... | collective-permute-start | bytes 786440 | tf_op jit(solution)/shard_map/ppermute | solution.py:46
  21.7 13.6 %collective-permute-start.3 = (bf16[64,2048]{1,0:T(8,128)(2,1)S(1)}, bf16[64,2048]{1,0:T(8,128)(2,1)S(1)}, u32[]{:S(2)}, u32[]{:S(2)}) collective-permute-start(bf16[64,2048]{1,0:T(8,128)(2,1)S(1)} %get-tuple-element.42), channel_id=1, source_target_pairs={{1,2},{2,1},{3,4},{4,3},{5,6},{6,5},{7,8},{8,7},{9,10},{10,9},{11,... | collective-permute-start | bytes 786440 | tf_op jit(solution)/shard_map/ppermute | solution.py:51
  28.8 6.9 %collective-permute-start.5 = (f32[1,1024]{1,0:T(1,128)S(1)}, f32[1,1024]{1,0:T(1,128)S(1)}, u32[]{:S(2)}, u32[]{:S(2)}) collective-permute-start(f32[1,1024]{1,0:T(1,128)S(1)} %get-tuple-element.46), channel_id=1, source_target_pairs={{2,0},{3,1},{4,2},{5,3},{6,4},{7,5},{8,6},{9,7},{10,8},{11,9},{12,... | collective-permute-start | bytes 12296 | tf_op jit(solution)/shard_map/ppermute | solution.py:55
  35.6 7.2 %collective-permute-start.7 = (bf16[64,1024]{1,0:T(8,128)(2,1)S(1)}, bf16[64,1024]{1,0:T(8,128)(2,1)S(1)}, u32[]{:S(2)}, u32[]{:S(2)}) collective-permute-start(bf16[64,1024]{1,0:T(8,128)(2,1)S(1)} %get-tuple-element.48.value_ref.refs_0_), channel_id=1, source_target_pairs={{0,4},{1,13},{2,6},{3,15},{4,8},{5,1},{6,10},{7,3},{8,12},{9,5},{1... | collective-permute-start | bytes 393224 | tf_op jit(solution)/shard_map/ppermute | solution.py:46
  35.7 7.0 %collective-permute-start.8 = (bf16[64,1024]{1,0:T(8,128)(2,1)S(1)}, bf16[64,1024]{1,0:T(8,128)(2,1)S(1)}, u32[]{:S(2)}, u32[]{:S(2)}) collective-permute-start(bf16[64,1024]{1,0:T(8,128)(2,1)S(1)} %get-tuple-element.49.refs_12_), channel_id=1, source_target_pairs={{0,1},{1,0},{2,3},{3,2},{4,5},{5,4},{6,7},{7,6},{8,9},{9,8},{10,11... | collective-permute-start | bytes 393224 | tf_op jit(solution)/shard_map/ppermute | solution.py:46
  35.8 11.8 %collective-permute-start.13 = (bf16[256,384]{1,0:T(8,128)(2,1)S(1)}, bf16[256,384]{1,0:T(8,128)(2,1)S(1)}, u32[]{:S(2)}, u32[]{:S(2)}) collective-permute-start(bf16[256,384]{1,0:T(8,128)(2,1)S(1)} %get-tuple-element.50.refs_8_), channel_id=1, source_target_pairs={{0,32},{32,64},{64,96},{96,0},{128,160},{160,192},{192,224},{224,1... | collective-permute-start | bytes 589832 | tf_op jit(solution)/shard_map/ppermute | solution.py:138
  37.5 10.3 %collective-permute-start.14 = (bf16[256,384]{1,0:T(8,128)(2,1)S(1)}, bf16[256,384]{1,0:T(8,128)(2,1)S(1)}, u32[]{:S(2)}, u32[]{:S(2)}) collective-permute-start(bf16[256,384]{1,0:T(8,128)(2,1)S(1)} %get-tuple-element.50.refs_8_), channel_id=1, source_target_pairs={{0,96},{32,0},{64,32},{96,64},{128,224},{160,128},{192,160},{224,1... | collective-permute-start | bytes 589832 | tf_op jit(solution)/shard_map/ppermute | solution.py:138
  39.1 14.0 %collective-permute-start.15 = (bf16[256,384]{1,0:T(8,128)(2,1)S(1)}, bf16[256,384]{1,0:T(8,128)(2,1)S(1)}, u32[]{:S(2)}, u32[]{:S(2)}) collective-permute-start(bf16[256,384]{1,0:T(8,128)(2,1)S(1)} %get-tuple-element.50.refs_8_), channel_id=1, source_target_pairs={{0,64},{32,96},{64,0},{96,32},{128,192},{160,224},{192,128},{224,1... | collective-permute-start | bytes 589832 | tf_op jit(solution)/shard_map/ppermute | solution.py:138
  44.5 8.6 %collective-permute-start.12 = (bf16[64,1024]{1,0:T(8,128)(2,1)S(1)}, bf16[64,1024]{1,0:T(8,128)(2,1)S(1)}, u32[]{:S(2)}, u32[]{:S(2)}) collective-permute-start(bf16[64,1024]{1,0:T(8,128)(2,1)S(1)} %collective-permute-done.7.refs_0_.refs_2_), channel_id=1, source_target_pairs={{0,4},{1,13},{2,6},{3,15},{4,8},{5,1},{6,10},{7,3},{8,12},{9,5},{1... | collective-permute-start | bytes 393224 | tf_op jit(solution)/shard_map/ppermute | solution.py:46
  56.9 10.9 %collective-permute-start.17 = (bf16[128,128]{1,0:T(8,128)(2,1)S(1)}, bf16[128,128]{1,0:T(8,128)(2,1)S(1)}, u32[]{:S(2)}, u32[]{:S(2)}) collective-permute-start(bf16[128,128]{1,0:T(8,128)(2,1)S(1)} %get-tuple-element.54), channel_id=1, source_target_pairs={{0,4},{1,5},{2,6},{3,7},{4,8},{5,9},{6,10},{7,11},{8,12},{9,13},{1... | collective-permute-start | bytes 98312 | tf_op jit(solution)/shard_map/ppermute | solution.py:46
  58.2 9.6 %collective-permute-start.18 = (bf16[128,128]{1,0:T(8,128)(2,1)S(1)}, bf16[128,128]{1,0:T(8,128)(2,1)S(1)}, u32[]{:S(2)}, u32[]{:S(2)}) collective-permute-start(bf16[128,128]{1,0:T(8,128)(2,1)S(1)} %get-tuple-element.55), channel_id=1, source_target_pairs={{0,8},{1,9},{2,10},{3,11},{4,12},{5,13},{6,14},{7,15},{8,0},{9,1},... | collective-permute-start | bytes 98312 | tf_op jit(solution)/shard_map/ppermute | solution.py:46
  65.9 6.7 %collective-permute-start.24 = (bf16[512,256]{1,0:T(8,128)(2,1)S(1)}, bf16[512,256]{1,0:T(8,128)(2,1)S(1)}, u32[]{:S(2)}, u32[]{:S(2)}) collective-permute-start(bf16[512,256]{1,0:T(8,128)(2,1)S(1)} %get-tuple-element.57.value_ref.refs_9_), channel_id=1, source_target_pairs={{0,2},{1,3},{2,0},{3,1},{4,6},{5,7},{6,4},{7,5},{8,10},{9,11},{10,... | collective-permute-start | bytes 786440 | tf_op jit(solution)/shard_map/ppermute | solution.py:46
  66.6 15.4 %collective-permute-start.25 = (bf16[512,256]{1,0:T(8,128)(2,1)S(1)}, bf16[512,256]{1,0:T(8,128)(2,1)S(1)}, u32[]{:S(2)}, u32[]{:S(2)}) collective-permute-start(bf16[512,256]{1,0:T(8,128)(2,1)S(1)} %get-tuple-element.57.value_ref.refs_9_), channel_id=1, source_target_pairs={{0,16},{1,17},{2,18},{3,19},{4,20},{5,21},{6,22},{7,23},{8,24},{9,... | collective-permute-start | bytes 786440 | tf_op jit(solution)/shard_map/ppermute | solution.py:46
  68.7 13.3 %collective-permute-start.26 = (bf16[512,256]{1,0:T(8,128)(2,1)S(1)}, bf16[512,256]{1,0:T(8,128)(2,1)S(1)}, u32[]{:S(2)}, u32[]{:S(2)}) collective-permute-start(bf16[512,256]{1,0:T(8,128)(2,1)S(1)} %shard_map.90), channel_id=1, source_target_pairs={{0,18},{1,19},{2,16},{3,17},{4,22},{5,23},{6,20},{7,21},{8,26},{9,... | collective-permute-start | bytes 786440 | tf_op jit(solution)/shard_map/ppermute | solution.py:46
  86.2 8.0 %collective-permute-start.27 = (bf16[512,256]{1,0:T(8,128)(2,1)S(1)}, bf16[512,256]{1,0:T(8,128)(2,1)S(1)}, u32[]{:S(2)}, u32[]{:S(2)}) collective-permute-start(bf16[512,256]{1,0:T(8,128)(2,1)S(1)} %get-tuple-element.60), channel_id=1, source_target_pairs={{0,2},{1,3},{2,0},{3,1},{4,6},{5,7},{6,4},{7,5},{8,10},{9,11},{10,... | collective-permute-start | bytes 786440 | tf_op jit(solution)/shard_map/ppermute | solution.py:46
  87.1 7.2 %collective-permute-start.28 = (bf16[512,256]{1,0:T(8,128)(2,1)S(1)}, bf16[512,256]{1,0:T(8,128)(2,1)S(1)}, u32[]{:S(2)}, u32[]{:S(2)}) collective-permute-start(bf16[512,256]{1,0:T(8,128)(2,1)S(1)} %get-tuple-element.61), channel_id=1, source_target_pairs={{16,0},{17,1},{18,2},{19,3},{20,4},{21,5},{22,6},{23,7},{24,8},{25... | collective-permute-start | bytes 786440 | tf_op jit(solution)/shard_map/ppermute | solution.py:46
  98.0 9.5 %collective-permute-start.32 = (bf16[64,1024]{1,0:T(8,128)(2,1)S(1)}, bf16[64,1024]{1,0:T(8,128)(2,1)S(1)}, u32[]{:S(2)}, u32[]{:S(2)}) collective-permute-start(bf16[64,1024]{1,0:T(8,128)(2,1)S(1)} %get-tuple-element.72), channel_id=1, source_target_pairs={{0,12},{1,5},{2,14},{3,7},{4,0},{5,9},{6,2},{7,11},{8,4},{9,13},{1... | collective-permute-start | bytes 393224 | tf_op jit(solution)/shard_map/ppermute | solution.py:46
  100.9 8.4 %collective-permute-start.31 = (bf16[64,1024]{1,0:T(8,128)(2,1)S(1)}, bf16[64,1024]{1,0:T(8,128)(2,1)S(1)}, u32[]{:S(2)}, u32[]{:S(2)}) collective-permute-start(bf16[64,1024]{1,0:T(8,128)(2,1)S(1)} %get-tuple-element.70), channel_id=1, source_target_pairs={{0,13},{1,4},{2,15},{3,6},{4,1},{5,8},{6,3},{7,10},{8,5},{9,12},{1... | collective-permute-start | bytes 393224 | tf_op jit(solution)/shard_map/ppermute | solution.py:46
  107.6 7.9 %collective-permute-start.33 = (bf16[64,1024]{1,0:T(8,128)(2,1)S(1)}, bf16[64,1024]{1,0:T(8,128)(2,1)S(1)}, u32[]{:S(2)}, u32[]{:S(2)}) collective-permute-start(bf16[64,1024]{1,0:T(8,128)(2,1)S(1)} %add_convert_fusion.1), channel_id=1, source_target_pairs={{0,12},{1,5},{2,14},{3,7},{4,0},{5,9},{6,2},{7,11},{8,4},{9,13},{1... | collective-permute-start | bytes 393224 | tf_op jit(solution)/shard_map/ppermute | solution.py:46
  115.8 10.0 %collective-permute-start.34 = (bf16[64,1024]{1,0:T(8,128)(2,1)S(1)}, bf16[64,1024]{1,0:T(8,128)(2,1)S(1)}, u32[]{:S(2)}, u32[]{:S(2)}) collective-permute-start(bf16[64,1024]{1,0:T(8,128)(2,1)S(1)} %divide_convert_fusion), channel_id=1, source_target_pairs={{1,2},{2,1},{3,4},{4,3},{5,6},{6,5},{7,8},{8,7},{9,10},{10,9},{11,... | collective-permute-start | bytes 393224 | tf_op jit(solution)/shard_map/ppermute | solution.py:51
  (19 other events, 112.5 us)
Sparse Core Ops, SparseCore 0:
  9.1 44.1 all-gather.2

commit v15 on v13

--- a/solution.py
+++ b/solution.py
@@ -307,18 +307,33 @@
     )(dout, second)
 
 
+def dattended_kernel(own_ref, other_ref, weight, ready_ref, *refs):
+    outs, rows = refs[:TURNS], refs[TURNS]
+    fill(rows, [own_ref, other_ref])
+    two = outs[0].shape[1]
+    turn = here()[1]
+    for step, ref in enumerate(outs):
+        at = pl.multiple_of((turn + step) % TURNS * two, two)
+        ref[...] = contract_last(rows[...], weight[pl.ds(at, two), :]).astype(jnp.bfloat16)
+
+
+def dattended(own, other, halves, ready):
+    heads, half, width = halves.shape
+    rows = 2 * own.shape[0]
+    return pl.pallas_call(
+        dattended_kernel,
+        out_shape=(jax.ShapeDtypeStruct((rows, CORES * half), jnp.bfloat16),) * TURNS,
+        in_specs=[VMEM] * 3 + [ANY],
+        out_specs=(VMEM,) * TURNS,
+        scratch_shapes=[pltpu.VMEM((rows, width), jnp.bfloat16)],
+        compiler_params=room(8),
+    )(own, other, halves.reshape(heads * half, width), ready)
+
+
 def project_kernel(*refs):
-    pieces, weights, douts, halves = refs[:8], refs[8:12], refs[12:14], refs[14]
-    q_ref, kv_ref, w_ref, outs = *refs[15:18], refs[18:22]
-    rows, chip_rows, w_back, sems = refs[22:]
-    heads, half = halves.shape[:2]
-    started = []
-    for i in range(heads):
-        target = w_back.at[i * half : (i + 1) * half, :]
-        started.append(pltpu.make_async_copy(halves.at[i], target, sems.at[i]))
-        started[-1].start()
+    pieces, weights = refs[:8], refs[8:12]
+    q_ref, kv_ref, w_ref, rows = refs[12:]
     fill(rows, pieces)
-    fill(chip_rows, douts)
     dp = lax.axis_index("dp")
     x, y = dp // ROWS_Y, dp % ROWS_Y
     depth = weights[0].shape[0] // ROWS_X
@@ -331,34 +346,20 @@
     out = jnp.dot(rows[...], w_ref[...], preferred_element_type=F32).astype(jnp.bfloat16)
     q_ref[...] = out[:, :HEAD]
     kv_ref[...] = out[:, HEAD:]
-    for copy in started:
-        copy.wait()
-    turn = here()[1]
-    for step, ref in enumerate(outs):
-        at = pl.multiple_of((turn + step) % TURNS * CORES * half, CORES * half)
-        part = w_back[pl.ds(at, CORES * half), :]
-        ref[...] = contract_last(chip_rows[...], part).astype(jnp.bfloat16)
-
-
-def project(pieces, weights, douts, halves):
+
+
+def project(pieces, weights):
     seg, width = pieces[0].shape
     rows = seg * len(pieces)
-    heads, half = halves.shape[:2]
     bf16 = lambda *shape: jax.ShapeDtypeStruct(shape, jnp.bfloat16)
     return pl.pallas_call(
         project_kernel,
-        out_shape=(bf16(rows, HEAD), bf16(rows, 2 * HEAD), bf16(width, 3 * HEAD))
-        + (bf16(2 * seg, CORES * half),) * TURNS,
-        in_specs=[VMEM] * 14 + [ANY],
-        out_specs=(VMEM,) * (3 + TURNS),
-        scratch_shapes=[
-            pltpu.VMEM((rows, width), jnp.bfloat16),
-            pltpu.VMEM((2 * seg, width), jnp.bfloat16),
-            pltpu.VMEM((heads * half, width), jnp.bfloat16),
-            pltpu.SemaphoreType.DMA((heads,)),
-        ],
-        compiler_params=room(50),
-    )(*pieces, *weights, *douts, halves)
+        out_shape=(bf16(rows, HEAD), bf16(rows, 2 * HEAD), bf16(width, 3 * HEAD)),
+        in_specs=[VMEM] * 12,
+        out_specs=(VMEM,) * 3,
+        scratch_shapes=[pltpu.VMEM((rows, width), jnp.bfloat16)],
+        compiler_params=room(12),
+    )(*pieces, *weights)
 
 
 def place_dattended(core, seg, here_refs, there_refs, out_ref):
@@ -552,7 +553,8 @@
     dout, dout_b = whole_dout(dout, second)
     dout_there = other_core(dout_b)
     pieces = gathered_rows(normin, [dout_there], weights[1:])
-    q, own, w_full, *da = project(pieces, weights, (dout_b, dout_there), halves)
+    q, own, w_full = project(pieces, weights)
+    da = dattended(dout_b, dout_there, halves, w_full)
     far, beside = across(own, 0, False), other_pair(own)
     da_here = [da[0]] + [
         moved(da[i], lambda h, t, p, k, i=i: (h, t + i, p, k)) for i in range(1, TURNS)

time: 135 us -> 135 us (level)
  waiting for transfers between devices: 47.5 us -> 53.1 us
  starting transfers between devices: 57 us -> 52 us
    ppermute x3, starting transfers between devices: 24.3 us -> 20.2 us  [other_chip(): return lax.ppermute(value, 'ctx', pairs)]
    ppermute x3, waiting for transfers between devices: 7.89 us -> 10.9 us  [other_chip(): return lax.ppermute(value, 'ctx', pairs)]
    ppermute x28, waiting for transfers between devices: 32.7 us -> 35.3 us  [moved(): return lax.ppermute(value, 'ctx', pairs)]
    pallas_call x1, Pallas kernels: 2.33 us -> 0.8 us  [project(): pl.pallas_call(project_kernel, out_shape=(bf16(rows, HEAD), bf16(rows, 2...]
  transfers between devices with their start and end apart: 37 -> 37, of which waited for: 20 -> 21; matrix products, arithmetic and copies ran while one was open for 0% -> 0% of each run, Pallas kernels for 1% -> 2%
where the time goes in v15:
time: 135 us; the launch traced here: 134 us
  waiting for transfers between devices  53.1 us (39%)
  starting transfers between devices  52 us (39%)
  between operations  13.8 us (10%)
  Pallas kernels  10.1 us (7%)
  local copies, waits for them, and re-layouts  2.56 us (2%)
  matrix products  1.45 us (1%)
    ppermute x28, waiting for transfers between devices, moved(): return lax.ppermute(value, 'ctx', pairs)  35.3 us
    ppermute x28, starting transfers between devices, moved(): return lax.ppermute(value, 'ctx', pairs)  24.2 us
    ppermute x3, starting transfers between devices, other_chip(): return lax.ppermute(value, 'ctx', pairs)  20.2 us
    ppermute x3, waiting for transfers between devices, other_chip(): return lax.ppermute(value, 'ctx', pairs)  10.9 us
    ppermute x3, waiting for transfers between devices, shifted_y(): return lax.ppermute(value, 'dp', pairs)  6.89 us
    ppermute x3, starting transfers between devices, shifted_y(): return lax.ppermute(value, 'dp', pairs)  5.3 us
    pallas_call x1, Pallas kernels, attention(): pl.pallas_call(functools.partial(attention_kernel, 256, seg), out_shape=(...  4.31 us
  transfers between devices with their start and end apart: 37, of which 21 were waited for; matrix products, arithmetic and copies ran while one was open for 0% of the time, Pallas kernels for 2%

profile of v15, /device:TPU:6, one launch (start us, length us, event | category | flops | bytes accessed | tf_op | source)
XLA Modules:
  0.0 133.8 jit_solution(8749185109314905539)
XLA Ops:
  6.5 1.8 %shard_map.82 = (bf16[128,384]{1,0:T(8,128)(2,1)}, bf16[64,1024]{1,0:T(8,128)(2,1)}, s32[1,64]{1,0:T(1,128)}) custom-call(bf16[128,1024]{1,0:T(8,128)(2,1)} %q_ref.1, bf16[128,1024]{1,0:T(8,128)(2,1)} %k_ref.1, bf16[128,1024]{1,0:T(8,128)(2,1)} %v_ref.1, bf16[128,1024]{1,0:T(8,128)(2,1)} %o_ref.1, s32[1,64]{1,0:T(1,128)} %own_ref.1), custom_call_target="tpu_custom_call" | custom-call | tf_op jit(solution)/shard_map/pallas_call | solution.py:104
  8.4 8.7 %collective-permute-start = (s32[1,64]{1,0:T(1,128)}, s32[1,64]{1,0:T(1,128)S(1)}, u32[]{:S(2)}, u32[]{:S(2)}) collective-permute-start(s32[1,64]{1,0:T(1,128)} %get-tuple-element.41), channel_id=1, source_target_pairs={{1,2},{2,1},{3,4},{4,3},{5,6},{6,5},{7,8},{8,7},{9,10},{10,9},{11,... | collective-permute-start | bytes 776 | tf_op jit(solution)/shard_map/ppermute | solution.py:51
  19.8 1.7 %shard_map.83 = (bf16[64,2048]{1,0:T(8,128)(2,1)S(1)}, bf16[64,2048]{1,0:T(8,128)(2,1)S(1)}, f32[64,1024]{1,0:T(8,128)S(1)}, f32[64,1024]{1,0:T(8,128)S(1)}, f32[1,1024]{1,0:T(1,128)S(1)}) custom-call(s32[1,64]{1,0:T(1,128)S(1)} %copy-done.6, s32[1,64]{1,0:T(1,128)S(1)} %collective-permute-done.1.beside_ref, s32[1,64]{1,0:T(1,128)S(1)} %collective-permute-done.facing_ref, ...), custom_call_target="tpu_custom_call" | custom-call | tf_op jit(solution)/shard_map/pallas_call | solution.py:237
  21.6 7.1 %collective-permute-start.3 = (bf16[64,2048]{1,0:T(8,128)(2,1)S(1)}, bf16[64,2048]{1,0:T(8,128)(2,1)S(1)}, u32[]{:S(2)}, u32[]{:S(2)}) collective-permute-start(bf16[64,2048]{1,0:T(8,128)(2,1)S(1)} %get-tuple-element.43), channel_id=1, source_target_pairs={{1,2},{2,1},{3,4},{4,3},{5,6},{6,5},{7,8},{8,7},{9,10},{10,9},{11,... | collective-permute-start | bytes 786440 | tf_op jit(solution)/shard_map/ppermute | solution.py:51
  28.9 2.3 %collective-permute-start.5 = (f32[1,1024]{1,0:T(1,128)S(1)}, f32[1,1024]{1,0:T(1,128)S(1)}, u32[]{:S(2)}, u32[]{:S(2)}) collective-permute-start(f32[1,1024]{1,0:T(1,128)S(1)} %get-tuple-element.48), channel_id=1, source_target_pairs={{2,0},{3,1},{4,2},{5,3},{6,4},{7,5},{8,6},{9,7},{10,8},{11,9},{12,... | collective-permute-start | bytes 12296 | tf_op jit(solution)/shard_map/ppermute | solution.py:55
  31.3 4.1 %collective-permute-done.3.chip_ref = bf16[64,2048]{1,0:T(8,128)(2,1)S(1)} collective-permute-done((bf16[64,2048]{1,0:T(8,128)(2,1)S(1)}, bf16[64,2048]{1,0:T(8,128)(2,1)S(1)}, u32[]{:S(2)}, u32[]{:S(2)}) %collective-permute-start.3) | collective-permute-done | bytes 262176 | tf_op jit(solution)/shard_map/ppermute | solution.py:51
  39.2 2.0 %collective-permute-start.15 = (bf16[256,384]{1,0:T(8,128)(2,1)S(1)}, bf16[256,384]{1,0:T(8,128)(2,1)S(1)}, u32[]{:S(2)}, u32[]{:S(2)}) collective-permute-start(bf16[256,384]{1,0:T(8,128)(2,1)S(1)} %get-tuple-element.52.refs_8_), channel_id=1, source_target_pairs={{0,64},{32,96},{64,0},{96,32},{128,192},{160,224},{192,128},{224,1... | collective-permute-start | bytes 589832 | tf_op jit(solution)/shard_map/ppermute | solution.py:125
  42.8 1.8 %collective-permute-start.8 = (bf16[64,1024]{1,0:T(8,128)(2,1)S(1)}, bf16[64,1024]{1,0:T(8,128)(2,1)S(1)}, u32[]{:S(2)}, u32[]{:S(2)}) collective-permute-start(bf16[64,1024]{1,0:T(8,128)(2,1)S(1)} %shard_map.86), channel_id=1, source_target_pairs={{0,13},{1,4},{2,15},{3,6},{4,1},{5,8},{6,3},{7,10},{8,5},{9,12},{1... | collective-permute-start | bytes 393224 | tf_op jit(solution)/shard_map/ppermute | solution.py:46
  44.7 2.2 %collective-permute-done.13.refs_0_.refs_9_ = bf16[256,384]{1,0:T(8,128)(2,1)S(1)} collective-permute-done((bf16[256,384]{1,0:T(8,128)(2,1)S(1)}, bf16[256,384]{1,0:T(8,128)(2,1)S(1)}, u32[]{:S(2)}, u32[]{:S(2)}) %collective-permute-start.13) | collective-permute-done | bytes 196640 | tf_op jit(solution)/shard_map/ppermute | solution.py:125
  49.4 3.7 %collective-permute-done.15.refs_2_.refs_11_ = bf16[256,384]{1,0:T(8,128)(2,1)S(1)} collective-permute-done((bf16[256,384]{1,0:T(8,128)(2,1)S(1)}, bf16[256,384]{1,0:T(8,128)(2,1)S(1)}, u32[]{:S(2)}, u32[]{:S(2)}) %collective-permute-start.15) | collective-permute-done | bytes 196640 | tf_op jit(solution)/shard_map/ppermute | solution.py:125
  58.8 6.3 %collective-permute-start.18 = (bf16[128,128]{1,0:T(8,128)(2,1)S(1)}, bf16[128,128]{1,0:T(8,128)(2,1)S(1)}, u32[]{:S(2)}, u32[]{:S(2)}) collective-permute-start(bf16[128,128]{1,0:T(8,128)(2,1)S(1)} %get-tuple-element.58), channel_id=1, source_target_pairs={{0,8},{1,9},{2,10},{3,11},{4,12},{5,13},{6,14},{7,15},{8,0},{9,1},... | collective-permute-start | bytes 98312 | tf_op jit(solution)/shard_map/ppermute | solution.py:46
  65.1 3.4 %collective-permute-done.17.refs_0_.refs_2_ = bf16[128,128]{1,0:T(8,128)(2,1)S(1)} collective-permute-done((bf16[128,128]{1,0:T(8,128)(2,1)S(1)}, bf16[128,128]{1,0:T(8,128)(2,1)S(1)}, u32[]{:S(2)}, u32[]{:S(2)}) %collective-permute-start.17) | collective-permute-done | bytes 32800 | tf_op jit(solution)/shard_map/ppermute | solution.py:46
  68.6 1.7 %collective-permute-done.19.refs_2_.refs_4_ = bf16[128,128]{1,0:T(8,128)(2,1)S(1)} collective-permute-done((bf16[128,128]{1,0:T(8,128)(2,1)S(1)}, bf16[128,128]{1,0:T(8,128)(2,1)S(1)}, u32[]{:S(2)}, u32[]{:S(2)}) %collective-permute-start.19) | collective-permute-done | bytes 32800 | tf_op jit(solution)/shard_map/ppermute | solution.py:46
  73.6 8.2 %collective-permute-done.26.refs_12_ = bf16[512,256]{1,0:T(8,128)(2,1)S(1)} collective-permute-done((bf16[512,256]{1,0:T(8,128)(2,1)S(1)}, bf16[512,256]{1,0:T(8,128)(2,1)S(1)}, u32[]{:S(2)}, u32[]{:S(2)}) %collective-permute-start.26) | collective-permute-done | bytes 262176 | tf_op jit(solution)/shard_map/ppermute | solution.py:46
  81.8 4.3 %shard_map.92 = (bf16[512,128]{1,0:T(8,128)(2,1)S(1)}, bf16[512,256]{1,0:T(8,128)(2,1)S(1)}, bf16[512,256]{1,0:T(8,128)(2,1)S(1)}, bf16[512,256]{1,0:T(8,128)(2,1)S(1)}, bf16[512,256]{1,0:T(8,128)(2,1)S(1)}) custom-call(bf16[512,128]{1,0:T(8,128)(2,1)S(1)} %get-tuple-element.53.refs_0_, bf16[128,128]{1,0:T(8,128)(2,1)S(1)} %get-tuple-element.56.refs_1_, ...), custom_call_target="tpu_custom_call" | custom-call | flops 1610612736 | bytes 2490368 | tf_op jit(solution)/shard_map/pallas_call | solution.py:446
  90.1 5.0 %collective-permute-done.27.refs_1_ = bf16[512,256]{1,0:T(8,128)(2,1)S(1)} collective-permute-done((bf16[512,256]{1,0:T(8,128)(2,1)S(1)}, bf16[512,256]{1,0:T(8,128)(2,1)S(1)}, u32[]{:S(2)}, u32[]{:S(2)}) %collective-permute-start.27) | collective-permute-done | bytes 262176 | tf_op jit(solution)/shard_map/ppermute | solution.py:46
  95.1 2.3 %collective-permute-done.28.refs_2_ = bf16[512,256]{1,0:T(8,128)(2,1)S(1)} collective-permute-done((bf16[512,256]{1,0:T(8,128)(2,1)S(1)}, bf16[512,256]{1,0:T(8,128)(2,1)S(1)}, u32[]{:S(2)}, u32[]{:S(2)}) %collective-permute-start.28) | collective-permute-done | bytes 262176 | tf_op jit(solution)/shard_map/ppermute | solution.py:46
  98.2 1.9 %collective-permute-done.30.swapped = bf16[256,1024]{1,0:T(8,128)(2,1)S(1)} collective-permute-done((bf16[256,1024]{1,0:T(8,128)(2,1)S(1)}, bf16[256,1024]{1,0:T(8,128)(2,1)S(1)}, u32[]{:S(2)}, u32[]{:S(2)}) %collective-permute-start.30) | collective-permute-done | bytes 524320 | tf_op jit(solution)/shard_map/ppermute | solution.py:46
  100.2 3.2 %collective-permute-start.32 = (bf16[64,1024]{1,0:T(8,128)(2,1)S(1)}, bf16[64,1024]{1,0:T(8,128)(2,1)S(1)}, u32[]{:S(2)}, u32[]{:S(2)}) collective-permute-start(bf16[64,1024]{1,0:T(8,128)(2,1)S(1)} %get-tuple-element.74), channel_id=1, source_target_pairs={{0,12},{1,5},{2,14},{3,7},{4,0},{5,9},{6,2},{7,11},{8,4},{9,13},{1... | collective-permute-start | bytes 393224 | tf_op jit(solution)/shard_map/ppermute | solution.py:46
  103.9 5.1 %collective-permute-done.32 = bf16[64,1024]{1,0:T(8,128)(2,1)S(1)} collective-permute-done((bf16[64,1024]{1,0:T(8,128)(2,1)S(1)}, bf16[64,1024]{1,0:T(8,128)(2,1)S(1)}, u32[]{:S(2)}, u32[]{:S(2)}) %collective-permute-start.32) | collective-permute-done | bytes 131104 | tf_op jit(solution)/shard_map/ppermute | solution.py:46
  109.0 3.6 %collective-permute-start.33 = (bf16[64,1024]{1,0:T(8,128)(2,1)S(1)}, bf16[64,1024]{1,0:T(8,128)(2,1)S(1)}, u32[]{:S(2)}, u32[]{:S(2)}) collective-permute-start(bf16[64,1024]{1,0:T(8,128)(2,1)S(1)} %add_convert_fusion.1), channel_id=1, source_target_pairs={{0,12},{1,5},{2,14},{3,7},{4,0},{5,9},{6,2},{7,11},{8,4},{9,13},{1... | collective-permute-start | bytes 393224 | tf_op jit(solution)/shard_map/ppermute | solution.py:46
  112.7 2.4 %collective-permute-done.33 = bf16[64,1024]{1,0:T(8,128)(2,1)S(1)} collective-permute-done((bf16[64,1024]{1,0:T(8,128)(2,1)S(1)}, bf16[64,1024]{1,0:T(8,128)(2,1)S(1)}, u32[]{:S(2)}, u32[]{:S(2)}) %collective-permute-start.33) | collective-permute-done | bytes 131104 | tf_op jit(solution)/shard_map/ppermute | solution.py:46
  115.4 4.4 %collective-permute-start.34 = (bf16[64,1024]{1,0:T(8,128)(2,1)S(1)}, bf16[64,1024]{1,0:T(8,128)(2,1)S(1)}, u32[]{:S(2)}, u32[]{:S(2)}) collective-permute-start(bf16[64,1024]{1,0:T(8,128)(2,1)S(1)} %divide_convert_fusion), channel_id=1, source_target_pairs={{1,2},{2,1},{3,4},{4,3},{5,6},{6,5},{7,8},{8,7},{9,10},{10,9},{11,... | collective-permute-start | bytes 393224 | tf_op jit(solution)/shard_map/ppermute | solution.py:51
  119.9 5.5 %collective-permute-done.34 = bf16[64,1024]{1,0:T(8,128)(2,1)S(1)} collective-permute-done((bf16[64,1024]{1,0:T(8,128)(2,1)S(1)}, bf16[64,1024]{1,0:T(8,128)(2,1)S(1)}, u32[]{:S(2)}, u32[]{:S(2)}) %collective-permute-start.34) | collective-permute-done | bytes 131104 | tf_op jit(solution)/shard_map/ppermute | solution.py:51
  (91 shorter events, 27.4 us)
Async XLA Ops:
  6.5 50.5 %all-gather.3.cloned.1.call-start = ((), (), s32[]{:S(2)}) async-start(), calls=%async_computation | async-start | bytes 1179648 | tf_op jit(solution)/shard_map/all_gather | solution.py:129
  8.3 8.9 %collective-permute-start.1 = (s32[1,64]{1,0:T(1,128)}, s32[1,64]{1,0:T(1,128)S(1)}, u32[]{:S(2)}, u32[]{:S(2)}) collective-permute-start(s32[1,64]{1,0:T(1,128)} %get-tuple-element.41), channel_id=1, source_target_pairs={{0,1},{1,0},{2,3},{3,2},{4,5},{5,4},{6,7},{7,6},{8,9},{9,8},{10,11... | collective-permute-start | bytes 776 | tf_op jit(solution)/shard_map/ppermute | solution.py:46
  8.4 10.1 %collective-permute-start = (s32[1,64]{1,0:T(1,128)}, s32[1,64]{1,0:T(1,128)S(1)}, u32[]{:S(2)}, u32[]{:S(2)}) collective-permute-start(s32[1,64]{1,0:T(1,128)} %get-tuple-element.41), channel_id=1, source_target_pairs={{1,2},{2,1},{3,4},{4,3},{5,6},{6,5},{7,8},{8,7},{9,10},{10,9},{11,... | collective-permute-start | bytes 776 | tf_op jit(solution)/shard_map/ppermute | solution.py:51
  17.1 14.2 %collective-permute-start.4 = (bf16[128,384]{1,0:T(8,128)(2,1)}, bf16[128,384]{1,0:T(8,128)(2,1)S(1)}, u32[]{:S(2)}, u32[]{:S(2)}) collective-permute-start(bf16[128,384]{1,0:T(8,128)(2,1)} %get-tuple-element.46.refs_0_), channel_id=1, source_target_pairs={{0,128},{32,160},{64,192},{96,224},{128,0},{160,32},{192,64},{224,... | collective-permute-start | bytes 294920 | tf_op jit(solution)/shard_map/ppermute | solution.py:120
  21.5 9.8 %collective-permute-start.2 = (bf16[64,2048]{1,0:T(8,128)(2,1)S(1)}, bf16[64,2048]{1,0:T(8,128)(2,1)S(1)}, u32[]{:S(2)}, u32[]{:S(2)}) collective-permute-start(bf16[64,2048]{1,0:T(8,128)(2,1)S(1)} %get-tuple-element.42), channel_id=1, source_target_pairs={{0,1},{1,0},{2,3},{3,2},{4,5},{5,4},{6,7},{7,6},{8,9},{9,8},{10,11... | collective-permute-start | bytes 786440 | tf_op jit(solution)/shard_map/ppermute | solution.py:46
  21.6 13.8 %collective-permute-start.3 = (bf16[64,2048]{1,0:T(8,128)(2,1)S(1)}, bf16[64,2048]{1,0:T(8,128)(2,1)S(1)}, u32[]{:S(2)}, u32[]{:S(2)}) collective-permute-start(bf16[64,2048]{1,0:T(8,128)(2,1)S(1)} %get-tuple-element.43), channel_id=1, source_target_pairs={{1,2},{2,1},{3,4},{4,3},{5,6},{6,5},{7,8},{8,7},{9,10},{10,9},{11,... | collective-permute-start | bytes 786440 | tf_op jit(solution)/shard_map/ppermute | solution.py:51
  28.9 6.9 %collective-permute-start.5 = (f32[1,1024]{1,0:T(1,128)S(1)}, f32[1,1024]{1,0:T(1,128)S(1)}, u32[]{:S(2)}, u32[]{:S(2)}) collective-permute-start(f32[1,1024]{1,0:T(1,128)S(1)} %get-tuple-element.48), channel_id=1, source_target_pairs={{2,0},{3,1},{4,2},{5,3},{6,4},{7,5},{8,6},{9,7},{10,8},{11,9},{12,... | collective-permute-start | bytes 12296 | tf_op jit(solution)/shard_map/ppermute | solution.py:55
  35.7 7.2 %collective-permute-start.7 = (bf16[64,1024]{1,0:T(8,128)(2,1)S(1)}, bf16[64,1024]{1,0:T(8,128)(2,1)S(1)}, u32[]{:S(2)}, u32[]{:S(2)}) collective-permute-start(bf16[64,1024]{1,0:T(8,128)(2,1)S(1)} %get-tuple-element.50.value_ref.refs_0_), channel_id=1, source_target_pairs={{0,4},{1,13},{2,6},{3,15},{4,8},{5,1},{6,10},{7,3},{8,12},{9,5},{1... | collective-permute-start | bytes 393224 | tf_op jit(solution)/shard_map/ppermute | solution.py:46
  35.8 8.8 %collective-permute-start.11 = (bf16[64,1024]{1,0:T(8,128)(2,1)S(1)}, bf16[64,1024]{1,0:T(8,128)(2,1)S(1)}, u32[]{:S(2)}, u32[]{:S(2)}) collective-permute-start(bf16[64,1024]{1,0:T(8,128)(2,1)S(1)} %get-tuple-element.51.own_ref), channel_id=1, source_target_pairs={{0,1},{1,0},{2,3},{3,2},{4,5},{5,4},{6,7},{7,6},{8,9},{9,8},{10,11... | collective-permute-start | bytes 393224 | tf_op jit(solution)/shard_map/ppermute | solution.py:46
  35.9 11.0 %collective-permute-start.13 = (bf16[256,384]{1,0:T(8,128)(2,1)S(1)}, bf16[256,384]{1,0:T(8,128)(2,1)S(1)}, u32[]{:S(2)}, u32[]{:S(2)}) collective-permute-start(bf16[256,384]{1,0:T(8,128)(2,1)S(1)} %get-tuple-element.52.refs_8_), channel_id=1, source_target_pairs={{0,32},{32,64},{64,96},{96,0},{128,160},{160,192},{192,224},{224,1... | collective-permute-start | bytes 589832 | tf_op jit(solution)/shard_map/ppermute | solution.py:125
  37.6 10.4 %collective-permute-start.14 = (bf16[256,384]{1,0:T(8,128)(2,1)S(1)}, bf16[256,384]{1,0:T(8,128)(2,1)S(1)}, u32[]{:S(2)}, u32[]{:S(2)}) collective-permute-start(bf16[256,384]{1,0:T(8,128)(2,1)S(1)} %get-tuple-element.52.refs_8_), channel_id=1, source_target_pairs={{0,96},{32,0},{64,32},{96,64},{128,224},{160,128},{192,160},{224,1... | collective-permute-start | bytes 589832 | tf_op jit(solution)/shard_map/ppermute | solution.py:125
  39.2 13.9 %collective-permute-start.15 = (bf16[256,384]{1,0:T(8,128)(2,1)S(1)}, bf16[256,384]{1,0:T(8,128)(2,1)S(1)}, u32[]{:S(2)}, u32[]{:S(2)}) collective-permute-start(bf16[256,384]{1,0:T(8,128)(2,1)S(1)} %get-tuple-element.52.refs_8_), channel_id=1, source_target_pairs={{0,64},{32,96},{64,0},{96,32},{128,192},{160,224},{192,128},{224,1... | collective-permute-start | bytes 589832 | tf_op jit(solution)/shard_map/ppermute | solution.py:125
  44.6 8.5 %collective-permute-start.12 = (bf16[64,1024]{1,0:T(8,128)(2,1)S(1)}, bf16[64,1024]{1,0:T(8,128)(2,1)S(1)}, u32[]{:S(2)}, u32[]{:S(2)}) collective-permute-start(bf16[64,1024]{1,0:T(8,128)(2,1)S(1)} %shard_map.87), channel_id=1, source_target_pairs={{0,4},{1,13},{2,6},{3,15},{4,8},{5,1},{6,10},{7,3},{8,12},{9,5},{1... | collective-permute-start | bytes 393224 | tf_op jit(solution)/shard_map/ppermute | solution.py:46
  55.4 16.8 %collective-permute-start.24 = (bf16[512,256]{1,0:T(8,128)(2,1)S(1)}, bf16[512,256]{1,0:T(8,128)(2,1)S(1)}, u32[]{:S(2)}, u32[]{:S(2)}) collective-permute-start(bf16[512,256]{1,0:T(8,128)(2,1)S(1)} %get-tuple-element.60.value_ref.refs_9_), channel_id=1, source_target_pairs={{0,2},{1,3},{2,0},{3,1},{4,6},{5,7},{6,4},{7,5},{8,10},{9,11},{10,... | collective-permute-start | bytes 786440 | tf_op jit(solution)/shard_map/ppermute | solution.py:46
  55.5 16.8 %collective-permute-start.25 = (bf16[512,256]{1,0:T(8,128)(2,1)S(1)}, bf16[512,256]{1,0:T(8,128)(2,1)S(1)}, u32[]{:S(2)}, u32[]{:S(2)}) collective-permute-start(bf16[512,256]{1,0:T(8,128)(2,1)S(1)} %get-tuple-element.60.value_ref.refs_9_), channel_id=1, source_target_pairs={{0,16},{1,17},{2,18},{3,19},{4,20},{5,21},{6,22},{7,23},{8,24},{9,... | collective-permute-start | bytes 786440 | tf_op jit(solution)/shard_map/ppermute | solution.py:46
  58.7 9.9 %collective-permute-start.17 = (bf16[128,128]{1,0:T(8,128)(2,1)S(1)}, bf16[128,128]{1,0:T(8,128)(2,1)S(1)}, u32[]{:S(2)}, u32[]{:S(2)}) collective-permute-start(bf16[128,128]{1,0:T(8,128)(2,1)S(1)} %get-tuple-element.57), channel_id=1, source_target_pairs={{0,4},{1,5},{2,6},{3,7},{4,8},{5,9},{6,10},{7,11},{8,12},{9,13},{1... | collective-permute-start | bytes 98312 | tf_op jit(solution)/shard_map/ppermute | solution.py:46
  58.8 9.8 %collective-permute-start.18 = (bf16[128,128]{1,0:T(8,128)(2,1)S(1)}, bf16[128,128]{1,0:T(8,128)(2,1)S(1)}, u32[]{:S(2)}, u32[]{:S(2)}) collective-permute-start(bf16[128,128]{1,0:T(8,128)(2,1)S(1)} %get-tuple-element.58), channel_id=1, source_target_pairs={{0,8},{1,9},{2,10},{3,11},{4,12},{5,13},{6,14},{7,15},{8,0},{9,1},... | collective-permute-start | bytes 98312 | tf_op jit(solution)/shard_map/ppermute | solution.py:46
  70.3 11.5 %collective-permute-start.26 = (bf16[512,256]{1,0:T(8,128)(2,1)S(1)}, bf16[512,256]{1,0:T(8,128)(2,1)S(1)}, u32[]{:S(2)}, u32[]{:S(2)}) collective-permute-start(bf16[512,256]{1,0:T(8,128)(2,1)S(1)} %shard_map.91), channel_id=1, source_target_pairs={{0,18},{1,19},{2,16},{3,17},{4,22},{5,23},{6,20},{7,21},{8,26},{9,... | collective-permute-start | bytes 786440 | tf_op jit(solution)/shard_map/ppermute | solution.py:46
  86.1 9.0 %collective-permute-start.27 = (bf16[512,256]{1,0:T(8,128)(2,1)S(1)}, bf16[512,256]{1,0:T(8,128)(2,1)S(1)}, u32[]{:S(2)}, u32[]{:S(2)}) collective-permute-start(bf16[512,256]{1,0:T(8,128)(2,1)S(1)} %get-tuple-element.63), channel_id=1, source_target_pairs={{0,2},{1,3},{2,0},{3,1},{4,6},{5,7},{6,4},{7,5},{8,10},{9,11},{10,... | collective-permute-start | bytes 786440 | tf_op jit(solution)/shard_map/ppermute | solution.py:46
  87.3 10.1 %collective-permute-start.28 = (bf16[512,256]{1,0:T(8,128)(2,1)S(1)}, bf16[512,256]{1,0:T(8,128)(2,1)S(1)}, u32[]{:S(2)}, u32[]{:S(2)}) collective-permute-start(bf16[512,256]{1,0:T(8,128)(2,1)S(1)} %get-tuple-element.64), channel_id=1, source_target_pairs={{16,0},{17,1},{18,2},{19,3},{20,4},{21,5},{22,6},{23,7},{24,8},{25... | collective-permute-start | bytes 786440 | tf_op jit(solution)/shard_map/ppermute | solution.py:46
  88.6 8.8 %collective-permute-start.29 = (bf16[512,256]{1,0:T(8,128)(2,1)S(1)}, bf16[512,256]{1,0:T(8,128)(2,1)S(1)}, u32[]{:S(2)}, u32[]{:S(2)}) collective-permute-start(bf16[512,256]{1,0:T(8,128)(2,1)S(1)} %get-tuple-element.65), channel_id=1, source_target_pairs={{16,2},{17,3},{18,0},{19,1},{20,6},{21,7},{22,4},{23,5},{24,10},{2... | collective-permute-start | bytes 786440 | tf_op jit(solution)/shard_map/ppermute | solution.py:46
  100.2 8.8 %collective-permute-start.32 = (bf16[64,1024]{1,0:T(8,128)(2,1)S(1)}, bf16[64,1024]{1,0:T(8,128)(2,1)S(1)}, u32[]{:S(2)}, u32[]{:S(2)}) collective-permute-start(bf16[64,1024]{1,0:T(8,128)(2,1)S(1)} %get-tuple-element.74), channel_id=1, source_target_pairs={{0,12},{1,5},{2,14},{3,7},{4,0},{5,9},{6,2},{7,11},{8,4},{9,13},{1... | collective-permute-start | bytes 393224 | tf_op jit(solution)/shard_map/ppermute | solution.py:46
  103.4 9.3 %collective-permute-start.31 = (bf16[64,1024]{1,0:T(8,128)(2,1)S(1)}, bf16[64,1024]{1,0:T(8,128)(2,1)S(1)}, u32[]{:S(2)}, u32[]{:S(2)}) collective-permute-start(bf16[64,1024]{1,0:T(8,128)(2,1)S(1)} %get-tuple-element.72), channel_id=1, source_target_pairs={{0,13},{1,4},{2,15},{3,6},{4,1},{5,8},{6,3},{7,10},{8,5},{9,12},{1... | collective-permute-start | bytes 393224 | tf_op jit(solution)/shard_map/ppermute | solution.py:46
  115.4 10.0 %collective-permute-start.34 = (bf16[64,1024]{1,0:T(8,128)(2,1)S(1)}, bf16[64,1024]{1,0:T(8,128)(2,1)S(1)}, u32[]{:S(2)}, u32[]{:S(2)}) collective-permute-start(bf16[64,1024]{1,0:T(8,128)(2,1)S(1)} %divide_convert_fusion), channel_id=1, source_target_pairs={{1,2},{2,1},{3,4},{4,3},{5,6},{6,5},{7,8},{8,7},{9,10},{10,9},{11,... | collective-permute-start | bytes 393224 | tf_op jit(solution)/shard_map/ppermute | solution.py:51
  (20 other events, 115.6 us)
Sparse Core Ops, SparseCore 0:
  9.1 44.2 all-gather.2

commit v16 on v15

--- a/solution.py
+++ b/solution.py
@@ -559,7 +559,7 @@
     da_here = [da[0]] + [
         moved(da[i], lambda h, t, p, k, i=i: (h, t + i, p, k)) for i in range(1, TURNS)
     ]
-    cross = across(passed_on(own, *da_here[1:]), 0, True)
+    cross = across(passed_on(own, da_here[1], da_here[3]), 0, True)
     da_there = [other_core(piece) for piece in da_here]
     blocks = (own, beside, far, cross)
     dq, own, beside, far, cross = attention(q, da_here, da_there, blocks, seg)

time: 135 us -> 137 us (1.015)
  starting transfers between devices: 52 us -> 55.5 us
  waiting for transfers between devices: 53.1 us -> 51.6 us
    ppermute x3, waiting for transfers between devices: 10.9 us -> 8.89 us  [other_chip(): return lax.ppermute(value, 'ctx', pairs)]
    ppermute x3, starting transfers between devices: 20.2 us -> 22.2 us  [other_chip(): return lax.ppermute(value, 'ctx', pairs)]
    ppermute x28, starting transfers between devices: 24.2 us -> 25.6 us  [moved(): return lax.ppermute(value, 'ctx', pairs)]
  transfers between devices with their start and end apart: 37 -> 37, of which waited for: 21 -> 19; matrix products, arithmetic and copies ran while one was open for 0% -> 0% of each run, Pallas kernels for 2% -> 2%
where the time goes in v16:
time: 137 us; the launch traced here: 136 us
  starting transfers between devices  55.5 us (41%)
  waiting for transfers between devices  51.6 us (38%)
  between operations  13.8 us (10%)
  Pallas kernels  10.2 us (7%)
  local copies, waits for them, and re-layouts  2.56 us (2%)
  matrix products  1.46 us (1%)
    ppermute x28, waiting for transfers between devices, moved(): return lax.ppermute(value, 'ctx', pairs)  35.8 us
    ppermute x28, starting transfers between devices, moved(): return lax.ppermute(value, 'ctx', pairs)  25.6 us
    ppermute x3, starting transfers between devices, other_chip(): return lax.ppermute(value, 'ctx', pairs)  22.2 us
    ppermute x3, waiting for transfers between devices, other_chip(): return lax.ppermute(value, 'ctx', pairs)  8.89 us
    ppermute x3, waiting for transfers between devices, shifted_y(): return lax.ppermute(value, 'dp', pairs)  6.89 us
    ppermute x3, starting transfers between devices, shifted_y(): return lax.ppermute(value, 'dp', pairs)  5.3 us
    pallas_call x1, Pallas kernels, attention(): pl.pallas_call(functools.partial(attention_kernel, 256, seg), out_shape=(...  4.33 us
  transfers between devices with their start and end apart: 37, of which 19 were waited for; matrix products, arithmetic and copies ran while one was open for 0% of the time, Pallas kernels for 2%

profile of v16, /device:TPU:6, one launch (start us, length us, event | category | flops | bytes accessed | tf_op | source)
XLA Modules:
  0.0 135.8 jit_solution(91353840918652110)
XLA Ops:
  6.5 1.8 %shard_map.82 = (bf16[128,384]{1,0:T(8,128)(2,1)}, bf16[64,1024]{1,0:T(8,128)(2,1)}, s32[1,64]{1,0:T(1,128)}) custom-call(bf16[128,1024]{1,0:T(8,128)(2,1)} %q_ref.1, bf16[128,1024]{1,0:T(8,128)(2,1)} %k_ref.1, bf16[128,1024]{1,0:T(8,128)(2,1)} %v_ref.1, bf16[128,1024]{1,0:T(8,128)(2,1)} %o_ref.1, s32[1,64]{1,0:T(1,128)} %own_ref.1), custom_call_target="tpu_custom_call" | custom-call | tf_op jit(solution)/shard_map/pallas_call | solution.py:104
  8.4 8.7 %collective-permute-start = (s32[1,64]{1,0:T(1,128)}, s32[1,64]{1,0:T(1,128)S(1)}, u32[]{:S(2)}, u32[]{:S(2)}) collective-permute-start(s32[1,64]{1,0:T(1,128)} %get-tuple-element.41), channel_id=1, source_target_pairs={{1,2},{2,1},{3,4},{4,3},{5,6},{6,5},{7,8},{8,7},{9,10},{10,9},{11,... | collective-permute-start | bytes 776 | tf_op jit(solution)/shard_map/ppermute | solution.py:51
  21.6 7.1 %collective-permute-start.3 = (bf16[64,2048]{1,0:T(8,128)(2,1)S(1)}, bf16[64,2048]{1,0:T(8,128)(2,1)S(1)}, u32[]{:S(2)}, u32[]{:S(2)}) collective-permute-start(bf16[64,2048]{1,0:T(8,128)(2,1)S(1)} %get-tuple-element.43), channel_id=1, source_target_pairs={{1,2},{2,1},{3,4},{4,3},{5,6},{6,5},{7,8},{8,7},{9,10},{10,9},{11,... | collective-permute-start | bytes 786440 | tf_op jit(solution)/shard_map/ppermute | solution.py:51
  28.9 2.3 %collective-permute-start.5 = (f32[1,1024]{1,0:T(1,128)S(1)}, f32[1,1024]{1,0:T(1,128)S(1)}, u32[]{:S(2)}, u32[]{:S(2)}) collective-permute-start(f32[1,1024]{1,0:T(1,128)S(1)} %get-tuple-element.48), channel_id=1, source_target_pairs={{2,0},{3,1},{4,2},{5,3},{6,4},{7,5},{8,6},{9,7},{10,8},{11,9},{12,... | collective-permute-start | bytes 12296 | tf_op jit(solution)/shard_map/ppermute | solution.py:55
  31.3 4.1 %collective-permute-done.3.chip_ref = bf16[64,2048]{1,0:T(8,128)(2,1)S(1)} collective-permute-done((bf16[64,2048]{1,0:T(8,128)(2,1)S(1)}, bf16[64,2048]{1,0:T(8,128)(2,1)S(1)}, u32[]{:S(2)}, u32[]{:S(2)}) %collective-permute-start.3) | collective-permute-done | bytes 262176 | tf_op jit(solution)/shard_map/ppermute | solution.py:51
  39.2 2.0 %collective-permute-start.15 = (bf16[256,384]{1,0:T(8,128)(2,1)S(1)}, bf16[256,384]{1,0:T(8,128)(2,1)S(1)}, u32[]{:S(2)}, u32[]{:S(2)}) collective-permute-start(bf16[256,384]{1,0:T(8,128)(2,1)S(1)} %get-tuple-element.52.refs_8_), channel_id=1, source_target_pairs={{0,64},{32,96},{64,0},{96,32},{128,192},{160,224},{192,128},{224,1... | collective-permute-start | bytes 589832 | tf_op jit(solution)/shard_map/ppermute | solution.py:125
  42.8 1.8 %collective-permute-start.8 = (bf16[64,1024]{1,0:T(8,128)(2,1)S(1)}, bf16[64,1024]{1,0:T(8,128)(2,1)S(1)}, u32[]{:S(2)}, u32[]{:S(2)}) collective-permute-start(bf16[64,1024]{1,0:T(8,128)(2,1)S(1)} %shard_map.86), channel_id=1, source_target_pairs={{0,13},{1,4},{2,15},{3,6},{4,1},{5,8},{6,3},{7,10},{8,5},{9,12},{1... | collective-permute-start | bytes 393224 | tf_op jit(solution)/shard_map/ppermute | solution.py:46
  44.7 2.2 %collective-permute-done.13.refs_0_.refs_9_ = bf16[256,384]{1,0:T(8,128)(2,1)S(1)} collective-permute-done((bf16[256,384]{1,0:T(8,128)(2,1)S(1)}, bf16[256,384]{1,0:T(8,128)(2,1)S(1)}, u32[]{:S(2)}, u32[]{:S(2)}) %collective-permute-start.13) | collective-permute-done | bytes 196640 | tf_op jit(solution)/shard_map/ppermute | solution.py:125
  49.4 3.7 %collective-permute-done.15.refs_2_.refs_11_ = bf16[256,384]{1,0:T(8,128)(2,1)S(1)} collective-permute-done((bf16[256,384]{1,0:T(8,128)(2,1)S(1)}, bf16[256,384]{1,0:T(8,128)(2,1)S(1)}, u32[]{:S(2)}, u32[]{:S(2)}) %collective-permute-start.15) | collective-permute-done | bytes 196640 | tf_op jit(solution)/shard_map/ppermute | solution.py:125
  58.8 4.1 %collective-permute-start.19 = (bf16[128,128]{1,0:T(8,128)(2,1)S(1)}, bf16[128,128]{1,0:T(8,128)(2,1)S(1)}, u32[]{:S(2)}, u32[]{:S(2)}) collective-permute-start(bf16[128,128]{1,0:T(8,128)(2,1)S(1)} %get-tuple-element.59), channel_id=1, source_target_pairs={{0,12},{1,13},{2,14},{3,15},{4,0},{5,1},{6,2},{7,3},{8,4},{9,5},{1... | collective-permute-start | bytes 98312 | tf_op jit(solution)/shard_map/ppermute | solution.py:46
  62.9 4.3 %collective-permute-done.17.refs_0_.refs_2_ = bf16[128,128]{1,0:T(8,128)(2,1)S(1)} collective-permute-done((bf16[128,128]{1,0:T(8,128)(2,1)S(1)}, bf16[128,128]{1,0:T(8,128)(2,1)S(1)}, u32[]{:S(2)}, u32[]{:S(2)}) %collective-permute-start.17) | collective-permute-done | bytes 32800 | tf_op jit(solution)/shard_map/ppermute | solution.py:46
  68.5 2.9 %collective-permute-start.18 = (bf16[128,128]{1,0:T(8,128)(2,1)S(1)}, bf16[128,128]{1,0:T(8,128)(2,1)S(1)}, u32[]{:S(2)}, u32[]{:S(2)}) collective-permute-start(bf16[128,128]{1,0:T(8,128)(2,1)S(1)} %get-tuple-element.58), channel_id=1, source_target_pairs={{0,8},{1,9},{2,10},{3,11},{4,12},{5,13},{6,14},{7,15},{8,0},{9,1},... | collective-permute-start | bytes 98312 | tf_op jit(solution)/shard_map/ppermute | solution.py:46
  71.9 4.5 %collective-permute-done.18.refs_3_ = bf16[128,128]{1,0:T(8,128)(2,1)S(1)} collective-permute-done((bf16[128,128]{1,0:T(8,128)(2,1)S(1)}, bf16[128,128]{1,0:T(8,128)(2,1)S(1)}, u32[]{:S(2)}, u32[]{:S(2)}) %collective-permute-start.18) | collective-permute-done | bytes 32800 | tf_op jit(solution)/shard_map/ppermute | solution.py:46
  77.8 2.6 %collective-permute-done.26.refs_12_ = bf16[512,256]{1,0:T(8,128)(2,1)S(1)} collective-permute-done((bf16[512,256]{1,0:T(8,128)(2,1)S(1)}, bf16[512,256]{1,0:T(8,128)(2,1)S(1)}, u32[]{:S(2)}, u32[]{:S(2)}) %collective-permute-start.26) | collective-permute-done | bytes 262176 | tf_op jit(solution)/shard_map/ppermute | solution.py:46
  80.4 4.3 %shard_map.92 = (bf16[512,128]{1,0:T(8,128)(2,1)S(1)}, bf16[512,256]{1,0:T(8,128)(2,1)S(1)}, bf16[512,256]{1,0:T(8,128)(2,1)S(1)}, bf16[512,256]{1,0:T(8,128)(2,1)S(1)}, bf16[512,256]{1,0:T(8,128)(2,1)S(1)}) custom-call(bf16[512,128]{1,0:T(8,128)(2,1)S(1)} %get-tuple-element.53.refs_0_, bf16[128,128]{1,0:T(8,128)(2,1)S(1)} %get-tuple-element.56.refs_1_, ...), custom_call_target="tpu_custom_call" | custom-call | flops 1610612736 | bytes 2490368 | tf_op jit(solution)/shard_map/pallas_call | solution.py:446
  84.8 4.2 %collective-permute-start.28 = (bf16[512,256]{1,0:T(8,128)(2,1)S(1)}, bf16[512,256]{1,0:T(8,128)(2,1)S(1)}, u32[]{:S(2)}, u32[]{:S(2)}) collective-permute-start(bf16[512,256]{1,0:T(8,128)(2,1)S(1)} %get-tuple-element.64), channel_id=1, source_target_pairs={{16,0},{17,1},{18,2},{19,3},{20,4},{21,5},{22,6},{23,7},{24,8},{25... | collective-permute-start | bytes 786440 | tf_op jit(solution)/shard_map/ppermute | solution.py:46
  89.1 2.8 %collective-permute-start.29 = (bf16[512,256]{1,0:T(8,128)(2,1)S(1)}, bf16[512,256]{1,0:T(8,128)(2,1)S(1)}, u32[]{:S(2)}, u32[]{:S(2)}) collective-permute-start(bf16[512,256]{1,0:T(8,128)(2,1)S(1)} %get-tuple-element.65), channel_id=1, source_target_pairs={{16,2},{17,3},{18,0},{19,1},{20,6},{21,7},{22,4},{23,5},{24,10},{2... | collective-permute-start | bytes 786440 | tf_op jit(solution)/shard_map/ppermute | solution.py:46
  91.9 8.7 %collective-permute-done.28.refs_2_ = bf16[512,256]{1,0:T(8,128)(2,1)S(1)} collective-permute-done((bf16[512,256]{1,0:T(8,128)(2,1)S(1)}, bf16[512,256]{1,0:T(8,128)(2,1)S(1)}, u32[]{:S(2)}, u32[]{:S(2)}) %collective-permute-start.28) | collective-permute-done | bytes 262176 | tf_op jit(solution)/shard_map/ppermute | solution.py:46
  101.5 1.9 %collective-permute-done.30.swapped = bf16[256,1024]{1,0:T(8,128)(2,1)S(1)} collective-permute-done((bf16[256,1024]{1,0:T(8,128)(2,1)S(1)}, bf16[256,1024]{1,0:T(8,128)(2,1)S(1)}, u32[]{:S(2)}, u32[]{:S(2)}) %collective-permute-start.30) | collective-permute-done | bytes 524320 | tf_op jit(solution)/shard_map/ppermute | solution.py:46
  105.1 2.0 %collective-permute-start.31 = (bf16[64,1024]{1,0:T(8,128)(2,1)S(1)}, bf16[64,1024]{1,0:T(8,128)(2,1)S(1)}, u32[]{:S(2)}, u32[]{:S(2)}) collective-permute-start(bf16[64,1024]{1,0:T(8,128)(2,1)S(1)} %get-tuple-element.72), channel_id=1, source_target_pairs={{0,13},{1,4},{2,15},{3,6},{4,1},{5,8},{6,3},{7,10},{8,5},{9,12},{1... | collective-permute-start | bytes 393224 | tf_op jit(solution)/shard_map/ppermute | solution.py:46
  107.1 3.9 %collective-permute-done.32 = bf16[64,1024]{1,0:T(8,128)(2,1)S(1)} collective-permute-done((bf16[64,1024]{1,0:T(8,128)(2,1)S(1)}, bf16[64,1024]{1,0:T(8,128)(2,1)S(1)}, u32[]{:S(2)}, u32[]{:S(2)}) %collective-permute-start.32) | collective-permute-done | bytes 131104 | tf_op jit(solution)/shard_map/ppermute | solution.py:46
  113.6 3.5 %collective-permute-done.33 = bf16[64,1024]{1,0:T(8,128)(2,1)S(1)} collective-permute-done((bf16[64,1024]{1,0:T(8,128)(2,1)S(1)}, bf16[64,1024]{1,0:T(8,128)(2,1)S(1)}, u32[]{:S(2)}, u32[]{:S(2)}) %collective-permute-start.33) | collective-permute-done | bytes 131104 | tf_op jit(solution)/shard_map/ppermute | solution.py:46
  117.4 6.4 %collective-permute-start.34 = (bf16[64,1024]{1,0:T(8,128)(2,1)S(1)}, bf16[64,1024]{1,0:T(8,128)(2,1)S(1)}, u32[]{:S(2)}, u32[]{:S(2)}) collective-permute-start(bf16[64,1024]{1,0:T(8,128)(2,1)S(1)} %divide_convert_fusion), channel_id=1, source_target_pairs={{1,2},{2,1},{3,4},{4,3},{5,6},{6,5},{7,8},{8,7},{9,10},{10,9},{11,... | collective-permute-start | bytes 393224 | tf_op jit(solution)/shard_map/ppermute | solution.py:51
  123.9 3.5 %collective-permute-done.34 = bf16[64,1024]{1,0:T(8,128)(2,1)S(1)} collective-permute-done((bf16[64,1024]{1,0:T(8,128)(2,1)S(1)}, bf16[64,1024]{1,0:T(8,128)(2,1)S(1)}, u32[]{:S(2)}, u32[]{:S(2)}) %collective-permute-start.34) | collective-permute-done | bytes 131104 | tf_op jit(solution)/shard_map/ppermute | solution.py:51
  (91 shorter events, 28.6 us)
Async XLA Ops:
  6.5 50.5 %all-gather.3.cloned.1.call-start = ((), (), s32[]{:S(2)}) async-start(), calls=%async_computation | async-start | bytes 1179648 | tf_op jit(solution)/shard_map/all_gather | solution.py:129
  8.3 8.9 %collective-permute-start.1 = (s32[1,64]{1,0:T(1,128)}, s32[1,64]{1,0:T(1,128)S(1)}, u32[]{:S(2)}, u32[]{:S(2)}) collective-permute-start(s32[1,64]{1,0:T(1,128)} %get-tuple-element.41), channel_id=1, source_target_pairs={{0,1},{1,0},{2,3},{3,2},{4,5},{5,4},{6,7},{7,6},{8,9},{9,8},{10,11... | collective-permute-start | bytes 776 | tf_op jit(solution)/shard_map/ppermute | solution.py:46
  8.4 10.1 %collective-permute-start = (s32[1,64]{1,0:T(1,128)}, s32[1,64]{1,0:T(1,128)S(1)}, u32[]{:S(2)}, u32[]{:S(2)}) collective-permute-start(s32[1,64]{1,0:T(1,128)} %get-tuple-element.41), channel_id=1, source_target_pairs={{1,2},{2,1},{3,4},{4,3},{5,6},{6,5},{7,8},{8,7},{9,10},{10,9},{11,... | collective-permute-start | bytes 776 | tf_op jit(solution)/shard_map/ppermute | solution.py:51
  17.1 14.2 %collective-permute-start.4 = (bf16[128,384]{1,0:T(8,128)(2,1)}, bf16[128,384]{1,0:T(8,128)(2,1)S(1)}, u32[]{:S(2)}, u32[]{:S(2)}) collective-permute-start(bf16[128,384]{1,0:T(8,128)(2,1)} %get-tuple-element.46.refs_0_), channel_id=1, source_target_pairs={{0,128},{32,160},{64,192},{96,224},{128,0},{160,32},{192,64},{224,... | collective-permute-start | bytes 294920 | tf_op jit(solution)/shard_map/ppermute | solution.py:120
  21.5 9.8 %collective-permute-start.2 = (bf16[64,2048]{1,0:T(8,128)(2,1)S(1)}, bf16[64,2048]{1,0:T(8,128)(2,1)S(1)}, u32[]{:S(2)}, u32[]{:S(2)}) collective-permute-start(bf16[64,2048]{1,0:T(8,128)(2,1)S(1)} %get-tuple-element.42), channel_id=1, source_target_pairs={{0,1},{1,0},{2,3},{3,2},{4,5},{5,4},{6,7},{7,6},{8,9},{9,8},{10,11... | collective-permute-start | bytes 786440 | tf_op jit(solution)/shard_map/ppermute | solution.py:46
  21.6 13.8 %collective-permute-start.3 = (bf16[64,2048]{1,0:T(8,128)(2,1)S(1)}, bf16[64,2048]{1,0:T(8,128)(2,1)S(1)}, u32[]{:S(2)}, u32[]{:S(2)}) collective-permute-start(bf16[64,2048]{1,0:T(8,128)(2,1)S(1)} %get-tuple-element.43), channel_id=1, source_target_pairs={{1,2},{2,1},{3,4},{4,3},{5,6},{6,5},{7,8},{8,7},{9,10},{10,9},{11,... | collective-permute-start | bytes 786440 | tf_op jit(solution)/shard_map/ppermute | solution.py:51
  35.7 7.2 %collective-permute-start.7 = (bf16[64,1024]{1,0:T(8,128)(2,1)S(1)}, bf16[64,1024]{1,0:T(8,128)(2,1)S(1)}, u32[]{:S(2)}, u32[]{:S(2)}) collective-permute-start(bf16[64,1024]{1,0:T(8,128)(2,1)S(1)} %get-tuple-element.50.value_ref.refs_0_), channel_id=1, source_target_pairs={{0,4},{1,13},{2,6},{3,15},{4,8},{5,1},{6,10},{7,3},{8,12},{9,5},{1... | collective-permute-start | bytes 393224 | tf_op jit(solution)/shard_map/ppermute | solution.py:46
  35.8 8.8 %collective-permute-start.11 = (bf16[64,1024]{1,0:T(8,128)(2,1)S(1)}, bf16[64,1024]{1,0:T(8,128)(2,1)S(1)}, u32[]{:S(2)}, u32[]{:S(2)}) collective-permute-start(bf16[64,1024]{1,0:T(8,128)(2,1)S(1)} %get-tuple-element.51.own_ref), channel_id=1, source_target_pairs={{0,1},{1,0},{2,3},{3,2},{4,5},{5,4},{6,7},{7,6},{8,9},{9,8},{10,11... | collective-permute-start | bytes 393224 | tf_op jit(solution)/shard_map/ppermute | solution.py:46
  35.9 11.0 %collective-permute-start.13 = (bf16[256,384]{1,0:T(8,128)(2,1)S(1)}, bf16[256,384]{1,0:T(8,128)(2,1)S(1)}, u32[]{:S(2)}, u32[]{:S(2)}) collective-permute-start(bf16[256,384]{1,0:T(8,128)(2,1)S(1)} %get-tuple-element.52.refs_8_), channel_id=1, source_target_pairs={{0,32},{32,64},{64,96},{96,0},{128,160},{160,192},{192,224},{224,1... | collective-permute-start | bytes 589832 | tf_op jit(solution)/shard_map/ppermute | solution.py:125
  37.6 10.4 %collective-permute-start.14 = (bf16[256,384]{1,0:T(8,128)(2,1)S(1)}, bf16[256,384]{1,0:T(8,128)(2,1)S(1)}, u32[]{:S(2)}, u32[]{:S(2)}) collective-permute-start(bf16[256,384]{1,0:T(8,128)(2,1)S(1)} %get-tuple-element.52.refs_8_), channel_id=1, source_target_pairs={{0,96},{32,0},{64,32},{96,64},{128,224},{160,128},{192,160},{224,1... | collective-permute-start | bytes 589832 | tf_op jit(solution)/shard_map/ppermute | solution.py:125
  39.2 13.9 %collective-permute-start.15 = (bf16[256,384]{1,0:T(8,128)(2,1)S(1)}, bf16[256,384]{1,0:T(8,128)(2,1)S(1)}, u32[]{:S(2)}, u32[]{:S(2)}) collective-permute-start(bf16[256,384]{1,0:T(8,128)(2,1)S(1)} %get-tuple-element.52.refs_8_), channel_id=1, source_target_pairs={{0,64},{32,96},{64,0},{96,32},{128,192},{160,224},{192,128},{224,1... | collective-permute-start | bytes 589832 | tf_op jit(solution)/shard_map/ppermute | solution.py:125
  44.6 8.5 %collective-permute-start.12 = (bf16[64,1024]{1,0:T(8,128)(2,1)S(1)}, bf16[64,1024]{1,0:T(8,128)(2,1)S(1)}, u32[]{:S(2)}, u32[]{:S(2)}) collective-permute-start(bf16[64,1024]{1,0:T(8,128)(2,1)S(1)} %shard_map.87), channel_id=1, source_target_pairs={{0,4},{1,13},{2,6},{3,15},{4,8},{5,1},{6,10},{7,3},{8,12},{9,5},{1... | collective-permute-start | bytes 393224 | tf_op jit(solution)/shard_map/ppermute | solution.py:46
  55.4 15.9 %collective-permute-start.24 = (bf16[512,256]{1,0:T(8,128)(2,1)S(1)}, bf16[512,256]{1,0:T(8,128)(2,1)S(1)}, u32[]{:S(2)}, u32[]{:S(2)}) collective-permute-start(bf16[512,256]{1,0:T(8,128)(2,1)S(1)} %get-tuple-element.60.value_ref.refs_9_), channel_id=1, source_target_pairs={{0,2},{1,3},{2,0},{3,1},{4,6},{5,7},{6,4},{7,5},{8,10},{9,11},{10,... | collective-permute-start | bytes 786440 | tf_op jit(solution)/shard_map/ppermute | solution.py:46
  55.5 20.9 %collective-permute-start.25 = (bf16[512,256]{1,0:T(8,128)(2,1)S(1)}, bf16[512,256]{1,0:T(8,128)(2,1)S(1)}, u32[]{:S(2)}, u32[]{:S(2)}) collective-permute-start(bf16[512,256]{1,0:T(8,128)(2,1)S(1)} %get-tuple-element.60.value_ref.refs_9_), channel_id=1, source_target_pairs={{0,16},{1,17},{2,18},{3,19},{4,20},{5,21},{6,22},{7,23},{8,24},{9,... | collective-permute-start | bytes 786440 | tf_op jit(solution)/shard_map/ppermute | solution.py:46
  58.7 8.5 %collective-permute-start.17 = (bf16[128,128]{1,0:T(8,128)(2,1)S(1)}, bf16[128,128]{1,0:T(8,128)(2,1)S(1)}, u32[]{:S(2)}, u32[]{:S(2)}) collective-permute-start(bf16[128,128]{1,0:T(8,128)(2,1)S(1)} %get-tuple-element.57), channel_id=1, source_target_pairs={{0,4},{1,5},{2,6},{3,7},{4,8},{5,9},{6,10},{7,11},{8,12},{9,13},{1... | collective-permute-start | bytes 98312 | tf_op jit(solution)/shard_map/ppermute | solution.py:46
  58.8 8.4 %collective-permute-start.19 = (bf16[128,128]{1,0:T(8,128)(2,1)S(1)}, bf16[128,128]{1,0:T(8,128)(2,1)S(1)}, u32[]{:S(2)}, u32[]{:S(2)}) collective-permute-start(bf16[128,128]{1,0:T(8,128)(2,1)S(1)} %get-tuple-element.59), channel_id=1, source_target_pairs={{0,12},{1,13},{2,14},{3,15},{4,0},{5,1},{6,2},{7,3},{8,4},{9,5},{1... | collective-permute-start | bytes 98312 | tf_op jit(solution)/shard_map/ppermute | solution.py:46
  67.2 13.2 %collective-permute-start.26 = (bf16[512,256]{1,0:T(8,128)(2,1)S(1)}, bf16[512,256]{1,0:T(8,128)(2,1)S(1)}, u32[]{:S(2)}, u32[]{:S(2)}) collective-permute-start(bf16[512,256]{1,0:T(8,128)(2,1)S(1)} %shard_map.91), channel_id=1, source_target_pairs={{0,18},{1,19},{2,16},{3,17},{4,22},{5,23},{6,20},{7,21},{8,26},{9,... | collective-permute-start | bytes 786440 | tf_op jit(solution)/shard_map/ppermute | solution.py:46
  68.5 7.9 %collective-permute-start.18 = (bf16[128,128]{1,0:T(8,128)(2,1)S(1)}, bf16[128,128]{1,0:T(8,128)(2,1)S(1)}, u32[]{:S(2)}, u32[]{:S(2)}) collective-permute-start(bf16[128,128]{1,0:T(8,128)(2,1)S(1)} %get-tuple-element.58), channel_id=1, source_target_pairs={{0,8},{1,9},{2,10},{3,11},{4,12},{5,13},{6,14},{7,15},{8,0},{9,1},... | collective-permute-start | bytes 98312 | tf_op jit(solution)/shard_map/ppermute | solution.py:46
  84.7 7.2 %collective-permute-start.27 = (bf16[512,256]{1,0:T(8,128)(2,1)S(1)}, bf16[512,256]{1,0:T(8,128)(2,1)S(1)}, u32[]{:S(2)}, u32[]{:S(2)}) collective-permute-start(bf16[512,256]{1,0:T(8,128)(2,1)S(1)} %get-tuple-element.63), channel_id=1, source_target_pairs={{0,2},{1,3},{2,0},{3,1},{4,6},{5,7},{6,4},{7,5},{8,10},{9,11},{10,... | collective-permute-start | bytes 786440 | tf_op jit(solution)/shard_map/ppermute | solution.py:46
  84.8 15.8 %collective-permute-start.28 = (bf16[512,256]{1,0:T(8,128)(2,1)S(1)}, bf16[512,256]{1,0:T(8,128)(2,1)S(1)}, u32[]{:S(2)}, u32[]{:S(2)}) collective-permute-start(bf16[512,256]{1,0:T(8,128)(2,1)S(1)} %get-tuple-element.64), channel_id=1, source_target_pairs={{16,0},{17,1},{18,2},{19,3},{20,4},{21,5},{22,6},{23,7},{24,8},{25... | collective-permute-start | bytes 786440 | tf_op jit(solution)/shard_map/ppermute | solution.py:46
  89.1 11.5 %collective-permute-start.29 = (bf16[512,256]{1,0:T(8,128)(2,1)S(1)}, bf16[512,256]{1,0:T(8,128)(2,1)S(1)}, u32[]{:S(2)}, u32[]{:S(2)}) collective-permute-start(bf16[512,256]{1,0:T(8,128)(2,1)S(1)} %get-tuple-element.65), channel_id=1, source_target_pairs={{16,2},{17,3},{18,0},{19,1},{20,6},{21,7},{22,4},{23,5},{24,10},{2... | collective-permute-start | bytes 786440 | tf_op jit(solution)/shard_map/ppermute | solution.py:46
  103.5 7.6 %collective-permute-start.32 = (bf16[64,1024]{1,0:T(8,128)(2,1)S(1)}, bf16[64,1024]{1,0:T(8,128)(2,1)S(1)}, u32[]{:S(2)}, u32[]{:S(2)}) collective-permute-start(bf16[64,1024]{1,0:T(8,128)(2,1)S(1)} %get-tuple-element.74), channel_id=1, source_target_pairs={{0,12},{1,5},{2,14},{3,7},{4,0},{5,9},{6,2},{7,11},{8,4},{9,13},{1... | collective-permute-start | bytes 393224 | tf_op jit(solution)/shard_map/ppermute | solution.py:46
  105.1 8.5 %collective-permute-start.31 = (bf16[64,1024]{1,0:T(8,128)(2,1)S(1)}, bf16[64,1024]{1,0:T(8,128)(2,1)S(1)}, u32[]{:S(2)}, u32[]{:S(2)}) collective-permute-start(bf16[64,1024]{1,0:T(8,128)(2,1)S(1)} %get-tuple-element.72), channel_id=1, source_target_pairs={{0,13},{1,4},{2,15},{3,6},{4,1},{5,8},{6,3},{7,10},{8,5},{9,12},{1... | collective-permute-start | bytes 393224 | tf_op jit(solution)/shard_map/ppermute | solution.py:46
  117.4 10.0 %collective-permute-start.34 = (bf16[64,1024]{1,0:T(8,128)(2,1)S(1)}, bf16[64,1024]{1,0:T(8,128)(2,1)S(1)}, u32[]{:S(2)}, u32[]{:S(2)}) collective-permute-start(bf16[64,1024]{1,0:T(8,128)(2,1)S(1)} %divide_convert_fusion), channel_id=1, source_target_pairs={{1,2},{2,1},{3,4},{4,3},{5,6},{6,5},{7,8},{8,7},{9,10},{10,9},{11,... | collective-permute-start | bytes 393224 | tf_op jit(solution)/shard_map/ppermute | solution.py:51
  (20 other events, 123.9 us)
Sparse Core Ops, SparseCore 0:
  9.1 44.2 all-gather.2

commit v17 on v15

--- a/solution.py
+++ b/solution.py
@@ -444,7 +444,7 @@
     keys = sum(block.shape[0] for block in blocks)
     parts = tuple(jax.ShapeDtypeStruct(block.shape, jnp.bfloat16) for block in blocks)
     return pl.pallas_call(
-        functools.partial(attention_kernel, 256, seg),
+        functools.partial(attention_kernel, 512, seg),
         out_shape=(jax.ShapeDtypeStruct((queries, HEAD), jnp.bfloat16),) + parts,
         in_specs=[VMEM] * 13,
         out_specs=(VMEM,) * 5,
@@ -454,7 +454,7 @@
             pltpu.VMEM((HEAD, keys), F32),
             pltpu.VMEM((HEAD, keys), F32),
         ],
-        compiler_params=room(36),
+        compiler_params=room(48),
         cost_estimate=pl.CostEstimate(
             flops=12 * queries * keys * HEAD,
             bytes_accessed=2 * HEAD * (3 * queries + 4 * keys),

time: 135 us -> 135 us (level)
  no operation moved by 1% of the time
where the time goes in v17:
time: 135 us; the launch traced here: 134 us
  waiting for transfers between devices  53.2 us (39%)
  starting transfers between devices  51.9 us (38%)
  between operations  13.8 us (10%)
  Pallas kernels  9.98 us (7%)
  local copies, waits for them, and re-layouts  2.56 us (2%)
  matrix products  1.46 us (1%)
    ppermute x28, waiting for transfers between devices, moved(): return lax.ppermute(value, 'ctx', pairs)  35.2 us
    ppermute x28, starting transfers between devices, moved(): return lax.ppermute(value, 'ctx', pairs)  24.2 us
    ppermute x3, starting transfers between devices, other_chip(): return lax.ppermute(value, 'ctx', pairs)  20.1 us
    ppermute x3, waiting for transfers between devices, other_chip(): return lax.ppermute(value, 'ctx', pairs)  11 us
    ppermute x3, waiting for transfers between devices, shifted_y(): return lax.ppermute(value, 'dp', pairs)  6.89 us
    ppermute x3, starting transfers between devices, shifted_y(): return lax.ppermute(value, 'dp', pairs)  5.3 us
    pallas_call x1, Pallas kernels, attention(): pl.pallas_call(functools.partial(attention_kernel, 512, seg), out_shape=(...  4.14 us
  transfers between devices with their start and end apart: 37, of which 21 were waited for; matrix products, arithmetic and copies ran while one was open for 0% of the time, Pallas kernels for 2%

profile of v17, /device:TPU:6, one launch (start us, length us, event | category | flops | bytes accessed | tf_op | source)
XLA Modules:
  0.0 133.6 jit_solution(1661674090333238316)
XLA Ops:
  6.5 1.8 %shard_map.82 = (bf16[128,384]{1,0:T(8,128)(2,1)}, bf16[64,1024]{1,0:T(8,128)(2,1)}, s32[1,64]{1,0:T(1,128)}) custom-call(bf16[128,1024]{1,0:T(8,128)(2,1)} %q_ref.1, bf16[128,1024]{1,0:T(8,128)(2,1)} %k_ref.1, bf16[128,1024]{1,0:T(8,128)(2,1)} %v_ref.1, bf16[128,1024]{1,0:T(8,128)(2,1)} %o_ref.1, s32[1,64]{1,0:T(1,128)} %own_ref.1), custom_call_target="tpu_custom_call" | custom-call | tf_op jit(solution)/shard_map/pallas_call | solution.py:104
  8.4 8.7 %collective-permute-start = (s32[1,64]{1,0:T(1,128)}, s32[1,64]{1,0:T(1,128)S(1)}, u32[]{:S(2)}, u32[]{:S(2)}) collective-permute-start(s32[1,64]{1,0:T(1,128)} %get-tuple-element.41), channel_id=1, source_target_pairs={{1,2},{2,1},{3,4},{4,3},{5,6},{6,5},{7,8},{8,7},{9,10},{10,9},{11,... | collective-permute-start | bytes 776 | tf_op jit(solution)/shard_map/ppermute | solution.py:51
  19.8 1.7 %shard_map.83 = (bf16[64,2048]{1,0:T(8,128)(2,1)S(1)}, bf16[64,2048]{1,0:T(8,128)(2,1)S(1)}, f32[64,1024]{1,0:T(8,128)S(1)}, f32[64,1024]{1,0:T(8,128)S(1)}, f32[1,1024]{1,0:T(1,128)S(1)}) custom-call(s32[1,64]{1,0:T(1,128)S(1)} %copy-done.6, s32[1,64]{1,0:T(1,128)S(1)} %collective-permute-done.1.beside_ref, s32[1,64]{1,0:T(1,128)S(1)} %collective-permute-done.facing_ref, ...), custom_call_target="tpu_custom_call" | custom-call | tf_op jit(solution)/shard_map/pallas_call | solution.py:237
  21.6 7.1 %collective-permute-start.3 = (bf16[64,2048]{1,0:T(8,128)(2,1)S(1)}, bf16[64,2048]{1,0:T(8,128)(2,1)S(1)}, u32[]{:S(2)}, u32[]{:S(2)}) collective-permute-start(bf16[64,2048]{1,0:T(8,128)(2,1)S(1)} %get-tuple-element.43), channel_id=1, source_target_pairs={{1,2},{2,1},{3,4},{4,3},{5,6},{6,5},{7,8},{8,7},{9,10},{10,9},{11,... | collective-permute-start | bytes 786440 | tf_op jit(solution)/shard_map/ppermute | solution.py:51
  28.9 2.3 %collective-permute-start.5 = (f32[1,1024]{1,0:T(1,128)S(1)}, f32[1,1024]{1,0:T(1,128)S(1)}, u32[]{:S(2)}, u32[]{:S(2)}) collective-permute-start(f32[1,1024]{1,0:T(1,128)S(1)} %get-tuple-element.48), channel_id=1, source_target_pairs={{2,0},{3,1},{4,2},{5,3},{6,4},{7,5},{8,6},{9,7},{10,8},{11,9},{12,... | collective-permute-start | bytes 12296 | tf_op jit(solution)/shard_map/ppermute | solution.py:55
  31.3 4.1 %collective-permute-done.3.chip_ref = bf16[64,2048]{1,0:T(8,128)(2,1)S(1)} collective-permute-done((bf16[64,2048]{1,0:T(8,128)(2,1)S(1)}, bf16[64,2048]{1,0:T(8,128)(2,1)S(1)}, u32[]{:S(2)}, u32[]{:S(2)}) %collective-permute-start.3) | collective-permute-done | bytes 262176 | tf_op jit(solution)/shard_map/ppermute | solution.py:51
  39.2 2.0 %collective-permute-start.15 = (bf16[256,384]{1,0:T(8,128)(2,1)S(1)}, bf16[256,384]{1,0:T(8,128)(2,1)S(1)}, u32[]{:S(2)}, u32[]{:S(2)}) collective-permute-start(bf16[256,384]{1,0:T(8,128)(2,1)S(1)} %get-tuple-element.52.refs_8_), channel_id=1, source_target_pairs={{0,64},{32,96},{64,0},{96,32},{128,192},{160,224},{192,128},{224,1... | collective-permute-start | bytes 589832 | tf_op jit(solution)/shard_map/ppermute | solution.py:125
  42.8 1.8 %collective-permute-start.8 = (bf16[64,1024]{1,0:T(8,128)(2,1)S(1)}, bf16[64,1024]{1,0:T(8,128)(2,1)S(1)}, u32[]{:S(2)}, u32[]{:S(2)}) collective-permute-start(bf16[64,1024]{1,0:T(8,128)(2,1)S(1)} %shard_map.86), channel_id=1, source_target_pairs={{0,13},{1,4},{2,15},{3,6},{4,1},{5,8},{6,3},{7,10},{8,5},{9,12},{1... | collective-permute-start | bytes 393224 | tf_op jit(solution)/shard_map/ppermute | solution.py:46
  44.7 2.2 %collective-permute-done.13.refs_0_.refs_9_ = bf16[256,384]{1,0:T(8,128)(2,1)S(1)} collective-permute-done((bf16[256,384]{1,0:T(8,128)(2,1)S(1)}, bf16[256,384]{1,0:T(8,128)(2,1)S(1)}, u32[]{:S(2)}, u32[]{:S(2)}) %collective-permute-start.13) | collective-permute-done | bytes 196640 | tf_op jit(solution)/shard_map/ppermute | solution.py:125
  49.4 3.7 %collective-permute-done.15.refs_2_.refs_11_ = bf16[256,384]{1,0:T(8,128)(2,1)S(1)} collective-permute-done((bf16[256,384]{1,0:T(8,128)(2,1)S(1)}, bf16[256,384]{1,0:T(8,128)(2,1)S(1)}, u32[]{:S(2)}, u32[]{:S(2)}) %collective-permute-start.15) | collective-permute-done | bytes 196640 | tf_op jit(solution)/shard_map/ppermute | solution.py:125
  58.8 6.3 %collective-permute-start.18 = (bf16[128,128]{1,0:T(8,128)(2,1)S(1)}, bf16[128,128]{1,0:T(8,128)(2,1)S(1)}, u32[]{:S(2)}, u32[]{:S(2)}) collective-permute-start(bf16[128,128]{1,0:T(8,128)(2,1)S(1)} %get-tuple-element.58), channel_id=1, source_target_pairs={{0,8},{1,9},{2,10},{3,11},{4,12},{5,13},{6,14},{7,15},{8,0},{9,1},... | collective-permute-start | bytes 98312 | tf_op jit(solution)/shard_map/ppermute | solution.py:46
  65.1 3.4 %collective-permute-done.17.refs_0_.refs_2_ = bf16[128,128]{1,0:T(8,128)(2,1)S(1)} collective-permute-done((bf16[128,128]{1,0:T(8,128)(2,1)S(1)}, bf16[128,128]{1,0:T(8,128)(2,1)S(1)}, u32[]{:S(2)}, u32[]{:S(2)}) %collective-permute-start.17) | collective-permute-done | bytes 32800 | tf_op jit(solution)/shard_map/ppermute | solution.py:46
  68.6 1.7 %collective-permute-done.19.refs_2_.refs_4_ = bf16[128,128]{1,0:T(8,128)(2,1)S(1)} collective-permute-done((bf16[128,128]{1,0:T(8,128)(2,1)S(1)}, bf16[128,128]{1,0:T(8,128)(2,1)S(1)}, u32[]{:S(2)}, u32[]{:S(2)}) %collective-permute-start.19) | collective-permute-done | bytes 32800 | tf_op jit(solution)/shard_map/ppermute | solution.py:46
  73.6 8.2 %collective-permute-done.26.refs_12_ = bf16[512,256]{1,0:T(8,128)(2,1)S(1)} collective-permute-done((bf16[512,256]{1,0:T(8,128)(2,1)S(1)}, bf16[512,256]{1,0:T(8,128)(2,1)S(1)}, u32[]{:S(2)}, u32[]{:S(2)}) %collective-permute-start.26) | collective-permute-done | bytes 262176 | tf_op jit(solution)/shard_map/ppermute | solution.py:46
  81.8 4.1 %shard_map.92 = (bf16[512,128]{1,0:T(8,128)(2,1)S(1)}, bf16[512,256]{1,0:T(8,128)(2,1)S(1)}, bf16[512,256]{1,0:T(8,128)(2,1)S(1)}, bf16[512,256]{1,0:T(8,128)(2,1)S(1)}, bf16[512,256]{1,0:T(8,128)(2,1)S(1)}) custom-call(bf16[512,128]{1,0:T(8,128)(2,1)S(1)} %get-tuple-element.53.refs_0_, bf16[128,128]{1,0:T(8,128)(2,1)S(1)} %get-tuple-element.56.refs_1_, ...), custom_call_target="tpu_custom_call" | custom-call | flops 1610612736 | bytes 2490368 | tf_op jit(solution)/shard_map/pallas_call | solution.py:446
  89.9 5.0 %collective-permute-done.27.refs_1_ = bf16[512,256]{1,0:T(8,128)(2,1)S(1)} collective-permute-done((bf16[512,256]{1,0:T(8,128)(2,1)S(1)}, bf16[512,256]{1,0:T(8,128)(2,1)S(1)}, u32[]{:S(2)}, u32[]{:S(2)}) %collective-permute-start.27) | collective-permute-done | bytes 262176 | tf_op jit(solution)/shard_map/ppermute | solution.py:46
  94.9 2.3 %collective-permute-done.28.refs_2_ = bf16[512,256]{1,0:T(8,128)(2,1)S(1)} collective-permute-done((bf16[512,256]{1,0:T(8,128)(2,1)S(1)}, bf16[512,256]{1,0:T(8,128)(2,1)S(1)}, u32[]{:S(2)}, u32[]{:S(2)}) %collective-permute-start.28) | collective-permute-done | bytes 262176 | tf_op jit(solution)/shard_map/ppermute | solution.py:46
  98.0 1.9 %collective-permute-done.30.swapped = bf16[256,1024]{1,0:T(8,128)(2,1)S(1)} collective-permute-done((bf16[256,1024]{1,0:T(8,128)(2,1)S(1)}, bf16[256,1024]{1,0:T(8,128)(2,1)S(1)}, u32[]{:S(2)}, u32[]{:S(2)}) %collective-permute-start.30) | collective-permute-done | bytes 524320 | tf_op jit(solution)/shard_map/ppermute | solution.py:46
  100.0 3.2 %collective-permute-start.32 = (bf16[64,1024]{1,0:T(8,128)(2,1)S(1)}, bf16[64,1024]{1,0:T(8,128)(2,1)S(1)}, u32[]{:S(2)}, u32[]{:S(2)}) collective-permute-start(bf16[64,1024]{1,0:T(8,128)(2,1)S(1)} %get-tuple-element.74), channel_id=1, source_target_pairs={{0,12},{1,5},{2,14},{3,7},{4,0},{5,9},{6,2},{7,11},{8,4},{9,13},{1... | collective-permute-start | bytes 393224 | tf_op jit(solution)/shard_map/ppermute | solution.py:46
  103.7 5.1 %collective-permute-done.32 = bf16[64,1024]{1,0:T(8,128)(2,1)S(1)} collective-permute-done((bf16[64,1024]{1,0:T(8,128)(2,1)S(1)}, bf16[64,1024]{1,0:T(8,128)(2,1)S(1)}, u32[]{:S(2)}, u32[]{:S(2)}) %collective-permute-start.32) | collective-permute-done | bytes 131104 | tf_op jit(solution)/shard_map/ppermute | solution.py:46
  108.8 3.6 %collective-permute-start.33 = (bf16[64,1024]{1,0:T(8,128)(2,1)S(1)}, bf16[64,1024]{1,0:T(8,128)(2,1)S(1)}, u32[]{:S(2)}, u32[]{:S(2)}) collective-permute-start(bf16[64,1024]{1,0:T(8,128)(2,1)S(1)} %add_convert_fusion.1), channel_id=1, source_target_pairs={{0,12},{1,5},{2,14},{3,7},{4,0},{5,9},{6,2},{7,11},{8,4},{9,13},{1... | collective-permute-start | bytes 393224 | tf_op jit(solution)/shard_map/ppermute | solution.py:46
  112.5 2.4 %collective-permute-done.33 = bf16[64,1024]{1,0:T(8,128)(2,1)S(1)} collective-permute-done((bf16[64,1024]{1,0:T(8,128)(2,1)S(1)}, bf16[64,1024]{1,0:T(8,128)(2,1)S(1)}, u32[]{:S(2)}, u32[]{:S(2)}) %collective-permute-start.33) | collective-permute-done | bytes 131104 | tf_op jit(solution)/shard_map/ppermute | solution.py:46
  115.2 4.3 %collective-permute-start.34 = (bf16[64,1024]{1,0:T(8,128)(2,1)S(1)}, bf16[64,1024]{1,0:T(8,128)(2,1)S(1)}, u32[]{:S(2)}, u32[]{:S(2)}) collective-permute-start(bf16[64,1024]{1,0:T(8,128)(2,1)S(1)} %divide_convert_fusion), channel_id=1, source_target_pairs={{1,2},{2,1},{3,4},{4,3},{5,6},{6,5},{7,8},{8,7},{9,10},{10,9},{11,... | collective-permute-start | bytes 393224 | tf_op jit(solution)/shard_map/ppermute | solution.py:51
  119.6 5.6 %collective-permute-done.34 = bf16[64,1024]{1,0:T(8,128)(2,1)S(1)} collective-permute-done((bf16[64,1024]{1,0:T(8,128)(2,1)S(1)}, bf16[64,1024]{1,0:T(8,128)(2,1)S(1)}, u32[]{:S(2)}, u32[]{:S(2)}) %collective-permute-start.34) | collective-permute-done | bytes 131104 | tf_op jit(solution)/shard_map/ppermute | solution.py:51
  (91 shorter events, 27.4 us)
Async XLA Ops:
  6.5 50.5 %all-gather.3.cloned.1.call-start = ((), (), s32[]{:S(2)}) async-start(), calls=%async_computation | async-start | bytes 1179648 | tf_op jit(solution)/shard_map/all_gather | solution.py:129
  8.3 8.9 %collective-permute-start.1 = (s32[1,64]{1,0:T(1,128)}, s32[1,64]{1,0:T(1,128)S(1)}, u32[]{:S(2)}, u32[]{:S(2)}) collective-permute-start(s32[1,64]{1,0:T(1,128)} %get-tuple-element.41), channel_id=1, source_target_pairs={{0,1},{1,0},{2,3},{3,2},{4,5},{5,4},{6,7},{7,6},{8,9},{9,8},{10,11... | collective-permute-start | bytes 776 | tf_op jit(solution)/shard_map/ppermute | solution.py:46
  8.4 10.1 %collective-permute-start = (s32[1,64]{1,0:T(1,128)}, s32[1,64]{1,0:T(1,128)S(1)}, u32[]{:S(2)}, u32[]{:S(2)}) collective-permute-start(s32[1,64]{1,0:T(1,128)} %get-tuple-element.41), channel_id=1, source_target_pairs={{1,2},{2,1},{3,4},{4,3},{5,6},{6,5},{7,8},{8,7},{9,10},{10,9},{11,... | collective-permute-start | bytes 776 | tf_op jit(solution)/shard_map/ppermute | solution.py:51
  17.1 14.2 %collective-permute-start.4 = (bf16[128,384]{1,0:T(8,128)(2,1)}, bf16[128,384]{1,0:T(8,128)(2,1)S(1)}, u32[]{:S(2)}, u32[]{:S(2)}) collective-permute-start(bf16[128,384]{1,0:T(8,128)(2,1)} %get-tuple-element.46.refs_0_), channel_id=1, source_target_pairs={{0,128},{32,160},{64,192},{96,224},{128,0},{160,32},{192,64},{224,... | collective-permute-start | bytes 294920 | tf_op jit(solution)/shard_map/ppermute | solution.py:120
  21.5 9.8 %collective-permute-start.2 = (bf16[64,2048]{1,0:T(8,128)(2,1)S(1)}, bf16[64,2048]{1,0:T(8,128)(2,1)S(1)}, u32[]{:S(2)}, u32[]{:S(2)}) collective-permute-start(bf16[64,2048]{1,0:T(8,128)(2,1)S(1)} %get-tuple-element.42), channel_id=1, source_target_pairs={{0,1},{1,0},{2,3},{3,2},{4,5},{5,4},{6,7},{7,6},{8,9},{9,8},{10,11... | collective-permute-start | bytes 786440 | tf_op jit(solution)/shard_map/ppermute | solution.py:46
  21.6 13.8 %collective-permute-start.3 = (bf16[64,2048]{1,0:T(8,128)(2,1)S(1)}, bf16[64,2048]{1,0:T(8,128)(2,1)S(1)}, u32[]{:S(2)}, u32[]{:S(2)}) collective-permute-start(bf16[64,2048]{1,0:T(8,128)(2,1)S(1)} %get-tuple-element.43), channel_id=1, source_target_pairs={{1,2},{2,1},{3,4},{4,3},{5,6},{6,5},{7,8},{8,7},{9,10},{10,9},{11,... | collective-permute-start | bytes 786440 | tf_op jit(solution)/shard_map/ppermute | solution.py:51
  28.9 6.9 %collective-permute-start.5 = (f32[1,1024]{1,0:T(1,128)S(1)}, f32[1,1024]{1,0:T(1,128)S(1)}, u32[]{:S(2)}, u32[]{:S(2)}) collective-permute-start(f32[1,1024]{1,0:T(1,128)S(1)} %get-tuple-element.48), channel_id=1, source_target_pairs={{2,0},{3,1},{4,2},{5,3},{6,4},{7,5},{8,6},{9,7},{10,8},{11,9},{12,... | collective-permute-start | bytes 12296 | tf_op jit(solution)/shard_map/ppermute | solution.py:55
  35.7 7.2 %collective-permute-start.7 = (bf16[64,1024]{1,0:T(8,128)(2,1)S(1)}, bf16[64,1024]{1,0:T(8,128)(2,1)S(1)}, u32[]{:S(2)}, u32[]{:S(2)}) collective-permute-start(bf16[64,1024]{1,0:T(8,128)(2,1)S(1)} %get-tuple-element.50.value_ref.refs_0_), channel_id=1, source_target_pairs={{0,4},{1,13},{2,6},{3,15},{4,8},{5,1},{6,10},{7,3},{8,12},{9,5},{1... | collective-permute-start | bytes 393224 | tf_op jit(solution)/shard_map/ppermute | solution.py:46
  35.8 8.8 %collective-permute-start.11 = (bf16[64,1024]{1,0:T(8,128)(2,1)S(1)}, bf16[64,1024]{1,0:T(8,128)(2,1)S(1)}, u32[]{:S(2)}, u32[]{:S(2)}) collective-permute-start(bf16[64,1024]{1,0:T(8,128)(2,1)S(1)} %get-tuple-element.51.own_ref), channel_id=1, source_target_pairs={{0,1},{1,0},{2,3},{3,2},{4,5},{5,4},{6,7},{7,6},{8,9},{9,8},{10,11... | collective-permute-start | bytes 393224 | tf_op jit(solution)/shard_map/ppermute | solution.py:46
  35.9 11.0 %collective-permute-start.13 = (bf16[256,384]{1,0:T(8,128)(2,1)S(1)}, bf16[256,384]{1,0:T(8,128)(2,1)S(1)}, u32[]{:S(2)}, u32[]{:S(2)}) collective-permute-start(bf16[256,384]{1,0:T(8,128)(2,1)S(1)} %get-tuple-element.52.refs_8_), channel_id=1, source_target_pairs={{0,32},{32,64},{64,96},{96,0},{128,160},{160,192},{192,224},{224,1... | collective-permute-start | bytes 589832 | tf_op jit(solution)/shard_map/ppermute | solution.py:125
  37.6 10.4 %collective-permute-start.14 = (bf16[256,384]{1,0:T(8,128)(2,1)S(1)}, bf16[256,384]{1,0:T(8,128)(2,1)S(1)}, u32[]{:S(2)}, u32[]{:S(2)}) collective-permute-start(bf16[256,384]{1,0:T(8,128)(2,1)S(1)} %get-tuple-element.52.refs_8_), channel_id=1, source_target_pairs={{0,96},{32,0},{64,32},{96,64},{128,224},{160,128},{192,160},{224,1... | collective-permute-start | bytes 589832 | tf_op jit(solution)/shard_map/ppermute | solution.py:125
  39.2 13.9 %collective-permute-start.15 = (bf16[256,384]{1,0:T(8,128)(2,1)S(1)}, bf16[256,384]{1,0:T(8,128)(2,1)S(1)}, u32[]{:S(2)}, u32[]{:S(2)}) collective-permute-start(bf16[256,384]{1,0:T(8,128)(2,1)S(1)} %get-tuple-element.52.refs_8_), channel_id=1, source_target_pairs={{0,64},{32,96},{64,0},{96,32},{128,192},{160,224},{192,128},{224,1... | collective-permute-start | bytes 589832 | tf_op jit(solution)/shard_map/ppermute | solution.py:125
  44.6 8.5 %collective-permute-start.12 = (bf16[64,1024]{1,0:T(8,128)(2,1)S(1)}, bf16[64,1024]{1,0:T(8,128)(2,1)S(1)}, u32[]{:S(2)}, u32[]{:S(2)}) collective-permute-start(bf16[64,1024]{1,0:T(8,128)(2,1)S(1)} %shard_map.87), channel_id=1, source_target_pairs={{0,4},{1,13},{2,6},{3,15},{4,8},{5,1},{6,10},{7,3},{8,12},{9,5},{1... | collective-permute-start | bytes 393224 | tf_op jit(solution)/shard_map/ppermute | solution.py:46
  55.4 16.8 %collective-permute-start.24 = (bf16[512,256]{1,0:T(8,128)(2,1)S(1)}, bf16[512,256]{1,0:T(8,128)(2,1)S(1)}, u32[]{:S(2)}, u32[]{:S(2)}) collective-permute-start(bf16[512,256]{1,0:T(8,128)(2,1)S(1)} %get-tuple-element.60.value_ref.refs_9_), channel_id=1, source_target_pairs={{0,2},{1,3},{2,0},{3,1},{4,6},{5,7},{6,4},{7,5},{8,10},{9,11},{10,... | collective-permute-start | bytes 786440 | tf_op jit(solution)/shard_map/ppermute | solution.py:46
  55.5 16.8 %collective-permute-start.25 = (bf16[512,256]{1,0:T(8,128)(2,1)S(1)}, bf16[512,256]{1,0:T(8,128)(2,1)S(1)}, u32[]{:S(2)}, u32[]{:S(2)}) collective-permute-start(bf16[512,256]{1,0:T(8,128)(2,1)S(1)} %get-tuple-element.60.value_ref.refs_9_), channel_id=1, source_target_pairs={{0,16},{1,17},{2,18},{3,19},{4,20},{5,21},{6,22},{7,23},{8,24},{9,... | collective-permute-start | bytes 786440 | tf_op jit(solution)/shard_map/ppermute | solution.py:46
  58.7 9.9 %collective-permute-start.17 = (bf16[128,128]{1,0:T(8,128)(2,1)S(1)}, bf16[128,128]{1,0:T(8,128)(2,1)S(1)}, u32[]{:S(2)}, u32[]{:S(2)}) collective-permute-start(bf16[128,128]{1,0:T(8,128)(2,1)S(1)} %get-tuple-element.57), channel_id=1, source_target_pairs={{0,4},{1,5},{2,6},{3,7},{4,8},{5,9},{6,10},{7,11},{8,12},{9,13},{1... | collective-permute-start | bytes 98312 | tf_op jit(solution)/shard_map/ppermute | solution.py:46
  58.8 9.8 %collective-permute-start.18 = (bf16[128,128]{1,0:T(8,128)(2,1)S(1)}, bf16[128,128]{1,0:T(8,128)(2,1)S(1)}, u32[]{:S(2)}, u32[]{:S(2)}) collective-permute-start(bf16[128,128]{1,0:T(8,128)(2,1)S(1)} %get-tuple-element.58), channel_id=1, source_target_pairs={{0,8},{1,9},{2,10},{3,11},{4,12},{5,13},{6,14},{7,15},{8,0},{9,1},... | collective-permute-start | bytes 98312 | tf_op jit(solution)/shard_map/ppermute | solution.py:46
  70.3 11.5 %collective-permute-start.26 = (bf16[512,256]{1,0:T(8,128)(2,1)S(1)}, bf16[512,256]{1,0:T(8,128)(2,1)S(1)}, u32[]{:S(2)}, u32[]{:S(2)}) collective-permute-start(bf16[512,256]{1,0:T(8,128)(2,1)S(1)} %shard_map.91), channel_id=1, source_target_pairs={{0,18},{1,19},{2,16},{3,17},{4,22},{5,23},{6,20},{7,21},{8,26},{9,... | collective-permute-start | bytes 786440 | tf_op jit(solution)/shard_map/ppermute | solution.py:46
  85.9 8.9 %collective-permute-start.27 = (bf16[512,256]{1,0:T(8,128)(2,1)S(1)}, bf16[512,256]{1,0:T(8,128)(2,1)S(1)}, u32[]{:S(2)}, u32[]{:S(2)}) collective-permute-start(bf16[512,256]{1,0:T(8,128)(2,1)S(1)} %get-tuple-element.63), channel_id=1, source_target_pairs={{0,2},{1,3},{2,0},{3,1},{4,6},{5,7},{6,4},{7,5},{8,10},{9,11},{10,... | collective-permute-start | bytes 786440 | tf_op jit(solution)/shard_map/ppermute | solution.py:46
  87.1 10.1 %collective-permute-start.28 = (bf16[512,256]{1,0:T(8,128)(2,1)S(1)}, bf16[512,256]{1,0:T(8,128)(2,1)S(1)}, u32[]{:S(2)}, u32[]{:S(2)}) collective-permute-start(bf16[512,256]{1,0:T(8,128)(2,1)S(1)} %get-tuple-element.64), channel_id=1, source_target_pairs={{16,0},{17,1},{18,2},{19,3},{20,4},{21,5},{22,6},{23,7},{24,8},{25... | collective-permute-start | bytes 786440 | tf_op jit(solution)/shard_map/ppermute | solution.py:46
  88.4 8.8 %collective-permute-start.29 = (bf16[512,256]{1,0:T(8,128)(2,1)S(1)}, bf16[512,256]{1,0:T(8,128)(2,1)S(1)}, u32[]{:S(2)}, u32[]{:S(2)}) collective-permute-start(bf16[512,256]{1,0:T(8,128)(2,1)S(1)} %get-tuple-element.65), channel_id=1, source_target_pairs={{16,2},{17,3},{18,0},{19,1},{20,6},{21,7},{22,4},{23,5},{24,10},{2... | collective-permute-start | bytes 786440 | tf_op jit(solution)/shard_map/ppermute | solution.py:46
  100.0 8.8 %collective-permute-start.32 = (bf16[64,1024]{1,0:T(8,128)(2,1)S(1)}, bf16[64,1024]{1,0:T(8,128)(2,1)S(1)}, u32[]{:S(2)}, u32[]{:S(2)}) collective-permute-start(bf16[64,1024]{1,0:T(8,128)(2,1)S(1)} %get-tuple-element.74), channel_id=1, source_target_pairs={{0,12},{1,5},{2,14},{3,7},{4,0},{5,9},{6,2},{7,11},{8,4},{9,13},{1... | collective-permute-start | bytes 393224 | tf_op jit(solution)/shard_map/ppermute | solution.py:46
  103.2 9.3 %collective-permute-start.31 = (bf16[64,1024]{1,0:T(8,128)(2,1)S(1)}, bf16[64,1024]{1,0:T(8,128)(2,1)S(1)}, u32[]{:S(2)}, u32[]{:S(2)}) collective-permute-start(bf16[64,1024]{1,0:T(8,128)(2,1)S(1)} %get-tuple-element.72), channel_id=1, source_target_pairs={{0,13},{1,4},{2,15},{3,6},{4,1},{5,8},{6,3},{7,10},{8,5},{9,12},{1... | collective-permute-start | bytes 393224 | tf_op jit(solution)/shard_map/ppermute | solution.py:46
  115.2 10.0 %collective-permute-start.34 = (bf16[64,1024]{1,0:T(8,128)(2,1)S(1)}, bf16[64,1024]{1,0:T(8,128)(2,1)S(1)}, u32[]{:S(2)}, u32[]{:S(2)}) collective-permute-start(bf16[64,1024]{1,0:T(8,128)(2,1)S(1)} %divide_convert_fusion), channel_id=1, source_target_pairs={{1,2},{2,1},{3,4},{4,3},{5,6},{6,5},{7,8},{8,7},{9,10},{10,9},{11,... | collective-permute-start | bytes 393224 | tf_op jit(solution)/shard_map/ppermute | solution.py:51
  (20 other events, 115.7 us)
Sparse Core Ops, SparseCore 0:
  9.1 44.2 all-gather.2
